TPU v7x, 32 devices: a whole 2x2x4 slice. The times are simulated.
32 devices in a mesh: group: 2 (over y), pix: 16 (over z, x, core).
Axes of the slice: x: 2, y: 2, z: 4, core: 2. Of those that a mesh axis runs over, the one named last changes fastest.
Arguments:
- images: bfloat16 [256, 2, 120, 840], P(('group', 'pix')), parts along dimension 0, may hold values from -170 to 170
- valid_mask: int32 [256, 840], P(('group', 'pix')), parts along dimension 0, may hold values from 0 to 1
Outputs:
- look_coherence: bfloat16 [128, 40, 2, 120, 120], P(('group', 'pix')), parts along dimension 0
- slab_coherence: float32 [4, 120, 120], P('group'), parts along dimension 0
There are 2 independent parts, one for each index of `group`. A program takes and returns all parts, laid end to end along the dimension named above; each array names one. Nothing has to cross between parts.
All inputs are finite; a program needn't handle non-finite values.
Results may differ from a plain program's by a relative error of at most 0.001.
Values may be sent and summed in bfloat16 or wider, within the bound.
No kernel may reach another device: no remote copies, remote signals or barrier semaphores. Data moves between devices by JAX's collectives and lax.ppermute only.
A program may use at most 128 MiB of HBM per device.

v0:
```python
import jax
import jax.numpy as jnp
from jax import lax
from jax.sharding import PartitionSpec as P

floor_power = 30.0


def extended(block, sides, width):
    for axis, dim in sides:
        count = lax.axis_size(axis)
        forward = [(i, i + 1) for i in range(count - 1)]
        backward = [(target, source) for source, target in forward]
        low = lax.ppermute(
            lax.slice_in_dim(block, block.shape[dim] - width, None, axis=dim), axis, forward
        )
        high = lax.ppermute(lax.slice_in_dim(block, 0, width, axis=dim), axis, backward)
        block = jnp.concatenate([low, block, high], axis=dim)
    return block


def split_parts(grams):
    real_part = grams[..., 0, :, 0, :] + grams[..., 1, :, 1, :]
    imag_part = grams[..., 1, :, 0, :] - grams[..., 0, :, 1, :]
    return (real_part, imag_part)


def coherence(real_part, imag_part, with_floor):
    powers = jnp.diagonal(real_part, axis1=-2, axis2=-1)
    if with_floor:
        powers = jnp.maximum(powers, floor_power)
    scaled = jnp.sqrt(powers[..., :, None] * powers[..., None, :])
    return jnp.stack([real_part / scaled, imag_part / scaled], axis=-3)


def shards(images, valid_mask):
    masked = images * valid_mask[:, None, None, :].astype(jnp.bfloat16)
    row_count = masked.shape[0]
    acq_count = masked.shape[2]
    look_cols = masked.shape[3] // 21
    padded = extended(masked, (("pix", 0),), 3)
    local_grams = jnp.einsum("rkic,rhjc->kihj", masked, masked, preferred_element_type=jnp.float32)
    local_real, local_imag = split_parts(local_grams)
    slab_real, slab_imag = lax.psum((local_real, local_imag), "pix")
    slab_coherence = coherence(slab_real, slab_imag, False)

    def one_look(look_index):
        window_data = lax.dynamic_slice_in_dim(padded, 2 * look_index, 7, 0)
        blocks = window_data.reshape(7, 2, acq_count, look_cols, 21)
        grams = jnp.einsum("rkilq,rhjlq->lkihj", blocks, blocks, preferred_element_type=jnp.float32)
        real_part, imag_part = split_parts(grams)
        return coherence(real_part, imag_part, True).astype(jnp.bfloat16)

    look_coherence = lax.map(one_look, jnp.arange(row_count // 2, dtype=jnp.int32))
    return (look_coherence, slab_coherence)


def solution(mesh):
    in_specs = (P(("group", "pix"), None, None, None), P(("group", "pix"), None))
    out_specs = (P(("group", "pix"), None, None, None, None), P("group", None, None))
    return jax.shard_map(shards, mesh=mesh, in_specs=in_specs, out_specs=out_specs, check_vma=False)
```

profile of v0, /device:TPU:1, one launch (start us, length us, event | category | flops | bytes accessed | tf_op | source)
XLA Modules:
  0.0 277.5 jit_solution(11654129077096014013)
XLA Ops:
  7.2 9.9 %copy.19 = bf16[8,2,120,840]{2,1,3,0:T(2,128)(2,1)} copy(bf16[8,2,120,840]{3,2,1,0:T(8,128)(2,1)} %param.4) | data formatting | bytes 6451200 | tf_op args[0]
  17.1 16.5 %broadcast_multiply_fusion = bf16[8,2,120,840]{2,1,3,0:T(2,128)(2,1)S(1)} fusion(bf16[8,2,120,840]{2,1,3,0:T(2,128)(2,1)} %copy.19, bf16[8,840]{1,0:T(8,128)(2,1)S(1)} %convert_element_type.12), kind=kLoop, calls=%fused_computation.27 | loop fusion | flops 1612800 | bytes 6464640 | tf_op jit(solution)/shard_map/mul | solution.py:37
  37.0 4.5 %collective-permute-start = (bf16[3,2,120,840]{2,1,3,0:T(2,128)(2,1)}, bf16[3,2,120,840]{2,1,3,0:T(2,128)(2,1)}, u32[]{:S(2)}, u32[]{:S(2)}) collective-permute-start(bf16[3,2,120,840]{2,1,3,0:T(2,128)(2,1)} %get-tuple-element.41), channel_id=1, source_target_pairs={{0,1},{1,2},{2,3},{3,4},{4,5},{5,6},{6,7},{7,8},{8,9},{9,10},{10,1... | collective-permute-start | bytes 3628808 | tf_op jit(solution)/shard_map/ppermute | solution.py:14
  43.6 6.8 %copy.21 = bf16[8,2,120,840]{3,2,0,1:T(8,128)(2,1)} copy(bf16[8,2,120,840]{2,1,3,0:T(2,128)(2,1)S(1)} %broadcast_multiply_fusion) | data formatting | bytes 6451200 | tf_op jit(solution)/shard_map/mul | solution.py:37
  50.4 16.6 %fusion.21 = bf16[8,2,120,840,1]{2,1,3,0,4:T(2,128)(2,1)S(1)} fusion(bf16[8,2,120,840]{2,1,3,0:T(2,128)(2,1)} %copy.19, bf16[8,840]{1,0:T(8,128)(2,1)S(1)} %convert_element_type.12), kind=kLoop, calls=%fused_computation.39 | loop fusion | flops 1612800 | bytes 6464640 | tf_op jit(solution)/shard_map/mul | solution.py:37
  68.9 89.1 %all-reduce.3.cloned.1.call-done = (f32[120,120]{1,0:T(8,128)}, f32[120,120]{1,0:T(8,128)}) async-done(((f32[120,120]{1,0:T(8,128)}, f32[120,120]{1,0:T(8,128)}), (f32[120,120]{1,0:T(8,128)}, f32[120,120]{1,0:T(8,128)})) %all-reduce.3.cloned.1.call-update) | async-done | bytes 115216 | tf_op jit(solution)/shard_map/psum | solution.py:44
  161.9 12.2 %pad_maximum_fusion.1 = bf16[14,2,120,840]{2,1,3,0:T(2,128)(2,1)} fusion(bf16[3,2,120,840]{2,1,3,0:T(2,128)(2,1)} %collective-permute-done.1, bf16[8,2,120,840]{2,1,3,0:T(2,128)(2,1)S(1)} %broadcast_multiply_fusion, bf16[3,2,120,840]{2,1,3,0:T(2,128)(2,1)} %collective-permute-done), kind=kLoop, calls=%fused_computation.23 | loop fusion | flops 5644800 | bytes 11289600 | tf_op jit(solution)/shard_map/concatenate | solution.py:18
  174.1 96.6 %while.10 = (s32[]{:T(128)}, bf16[4,40,2,120,120]{4,3,2,1,0:T(8,128)(2,1)}, s32[4]{0:T(128)S(1)}, bf16[14,2,120,840]{2,1,3,0:T(2,128)(2,1)}, s32[]{:T(128)}, /*index=5*/s32[1]{0:T(128)}, s32[]{:T(128)}, s32[]{:T(128)}) while((s32[]{:T(128)}, bf16[4,40,2,120,120]{4,3,2,1,0:T(8,128)(2,1)}, s32[4]{0:T(128)S(1)}, ...), condition=%wide.region_1.0_spmd, body=%wide.region_0.0_spmd.sunk | while | flops 683141312 | bytes 82507088 | solution.py:54
  175.3 3.9 %constant_dynamic-slice_fusion.2 = bf16[7,2,120,840]{2,1,3,0:T(2,128)(2,1)S(1)} fusion(bf16[14,2,120,840]{2,1,3,0:T(2,128)(2,1)} %get-tuple-element.95, s32[]{:T(128)S(6)} %select_n.12), kind=kLoop, calls=%fused_computation.22.clone.1 | loop fusion | bytes 5644804 | tf_op jit(solution)/shard_map/while/body/eval_jaxpr/dynamic_slice | solution.py:48
  181.1 3.8 %copy-done = f32[40,2,120,2,120]{4,2,3,1,0:T(8,128)} copy-done((f32[40,2,120,2,120]{4,2,3,1,0:T(8,128)}, f32[40,2,120,2,120]{4,2,3,1,0:T(8,128)S(1)}, u32[]{:S(2)}) %copy-start) | copy-done | bytes 9216024 | tf_op jit(solution)/shard_map/while
  185.1 4.5 %copy.55 = f32[40,120,120]{0,2,1:T(8,128)} copy(f32[40,120,120]{2,1,0:T(8,128)S(1)} %fusion.28) | data formatting | bytes 4608000 | tf_op jit(solution)/shard_map/while/body/eval_jaxpr/add | solution.py:23
  191.9 4.4 %fusion.29 = (bf16[1,40,1,120,120]{4,3,1,2,0:T(8,128)(2,1)S(1)}, bf16[1,40,1,120,120]{4,3,1,2,0:T(8,128)(2,1)S(1)}) fusion(f32[40,120]{1,0:T(8,128)S(1)} %copy.56, f32[40,2,120,2,120]{4,2,3,1,0:T(8,128)} %copy-done), kind=kLoop, calls=%fused_computation.17.clone.1 | loop fusion | flops 4032000 | bytes 11560960 | tf_op jit(solution)/shard_map/while/body/eval_jaxpr/stack | solution.py:33
  199.5 3.9 %constant_dynamic-slice_fusion.2 = bf16[7,2,120,840]{2,1,3,0:T(2,128)(2,1)S(1)} fusion(bf16[14,2,120,840]{2,1,3,0:T(2,128)(2,1)} %get-tuple-element.95, s32[]{:T(128)S(6)} %select_n.12), kind=kLoop, calls=%fused_computation.22.clone.1 | loop fusion | bytes 5644804 | tf_op jit(solution)/shard_map/while/body/eval_jaxpr/dynamic_slice | solution.py:48
  205.2 3.8 %copy-done = f32[40,2,120,2,120]{4,2,3,1,0:T(8,128)} copy-done((f32[40,2,120,2,120]{4,2,3,1,0:T(8,128)}, f32[40,2,120,2,120]{4,2,3,1,0:T(8,128)S(1)}, u32[]{:S(2)}) %copy-start) | copy-done | bytes 9216024 | tf_op jit(solution)/shard_map/while
  209.3 4.5 %copy.55 = f32[40,120,120]{0,2,1:T(8,128)} copy(f32[40,120,120]{2,1,0:T(8,128)S(1)} %fusion.28) | data formatting | bytes 4608000 | tf_op jit(solution)/shard_map/while/body/eval_jaxpr/add | solution.py:23
  216.0 4.4 %fusion.29 = (bf16[1,40,1,120,120]{4,3,1,2,0:T(8,128)(2,1)S(1)}, bf16[1,40,1,120,120]{4,3,1,2,0:T(8,128)(2,1)S(1)}) fusion(f32[40,120]{1,0:T(8,128)S(1)} %copy.56, f32[40,2,120,2,120]{4,2,3,1,0:T(8,128)} %copy-done), kind=kLoop, calls=%fused_computation.17.clone.1 | loop fusion | flops 4032000 | bytes 11560960 | tf_op jit(solution)/shard_map/while/body/eval_jaxpr/stack | solution.py:33
  223.6 3.9 %constant_dynamic-slice_fusion.2 = bf16[7,2,120,840]{2,1,3,0:T(2,128)(2,1)S(1)} fusion(bf16[14,2,120,840]{2,1,3,0:T(2,128)(2,1)} %get-tuple-element.95, s32[]{:T(128)S(6)} %select_n.12), kind=kLoop, calls=%fused_computation.22.clone.1 | loop fusion | bytes 5644804 | tf_op jit(solution)/shard_map/while/body/eval_jaxpr/dynamic_slice | solution.py:48
  229.4 3.8 %copy-done = f32[40,2,120,2,120]{4,2,3,1,0:T(8,128)} copy-done((f32[40,2,120,2,120]{4,2,3,1,0:T(8,128)}, f32[40,2,120,2,120]{4,2,3,1,0:T(8,128)S(1)}, u32[]{:S(2)}) %copy-start) | copy-done | bytes 9216024 | tf_op jit(solution)/shard_map/while
  233.4 4.5 %copy.55 = f32[40,120,120]{0,2,1:T(8,128)} copy(f32[40,120,120]{2,1,0:T(8,128)S(1)} %fusion.28) | data formatting | bytes 4608000 | tf_op jit(solution)/shard_map/while/body/eval_jaxpr/add | solution.py:23
  240.2 4.4 %fusion.29 = (bf16[1,40,1,120,120]{4,3,1,2,0:T(8,128)(2,1)S(1)}, bf16[1,40,1,120,120]{4,3,1,2,0:T(8,128)(2,1)S(1)}) fusion(f32[40,120]{1,0:T(8,128)S(1)} %copy.56, f32[40,2,120,2,120]{4,2,3,1,0:T(8,128)} %copy-done), kind=kLoop, calls=%fused_computation.17.clone.1 | loop fusion | flops 4032000 | bytes 11560960 | tf_op jit(solution)/shard_map/while/body/eval_jaxpr/stack | solution.py:33
  247.8 3.9 %constant_dynamic-slice_fusion.2 = bf16[7,2,120,840]{2,1,3,0:T(2,128)(2,1)S(1)} fusion(bf16[14,2,120,840]{2,1,3,0:T(2,128)(2,1)} %get-tuple-element.95, s32[]{:T(128)S(6)} %select_n.12), kind=kLoop, calls=%fused_computation.22.clone.1 | loop fusion | bytes 5644804 | tf_op jit(solution)/shard_map/while/body/eval_jaxpr/dynamic_slice | solution.py:48
  253.5 3.8 %copy-done = f32[40,2,120,2,120]{4,2,3,1,0:T(8,128)} copy-done((f32[40,2,120,2,120]{4,2,3,1,0:T(8,128)}, f32[40,2,120,2,120]{4,2,3,1,0:T(8,128)S(1)}, u32[]{:S(2)}) %copy-start) | copy-done | bytes 9216024 | tf_op jit(solution)/shard_map/while
  257.5 4.5 %copy.55 = f32[40,120,120]{0,2,1:T(8,128)} copy(f32[40,120,120]{2,1,0:T(8,128)S(1)} %fusion.28) | data formatting | bytes 4608000 | tf_op jit(solution)/shard_map/while/body/eval_jaxpr/add | solution.py:23
  264.3 4.4 %fusion.29 = (bf16[1,40,1,120,120]{4,3,1,2,0:T(8,128)(2,1)S(1)}, bf16[1,40,1,120,120]{4,3,1,2,0:T(8,128)(2,1)S(1)}) fusion(f32[40,120]{1,0:T(8,128)S(1)} %copy.56, f32[40,2,120,2,120]{4,2,3,1,0:T(8,128)} %copy-done), kind=kLoop, calls=%fused_computation.17.clone.1 | loop fusion | flops 4032000 | bytes 11560960 | tf_op jit(solution)/shard_map/while/body/eval_jaxpr/stack | solution.py:33
  (55 shorter events, 38.8 us)
Async XLA Ops:
  7.2 10.0 %copy-start.2 = (s32[8,840]{1,0:T(8,128)S(1)}, s32[8,840]{1,0:T(8,128)}, u32[]{:S(2)}) copy-start(s32[8,840]{1,0:T(8,128)} %param.5) | copy-start | bytes 80644
  7.2 150.9 %all-reduce.3.cloned.1.call-start = ((), (), s32[]{:S(2)}) async-start(), calls=%async_computation | async-start | bytes 245760 | tf_op jit(solution)/shard_map/psum | solution.py:44
  37.0 124.9 %collective-permute-start = (bf16[3,2,120,840]{2,1,3,0:T(2,128)(2,1)}, bf16[3,2,120,840]{2,1,3,0:T(2,128)(2,1)}, u32[]{:S(2)}, u32[]{:S(2)}) collective-permute-start(bf16[3,2,120,840]{2,1,3,0:T(2,128)(2,1)} %get-tuple-element.41), channel_id=1, source_target_pairs={{0,1},{1,2},{2,3},{3,4},{4,5},{5,6},{6,7},{7,8},{8,9},{9,10},{10,1... | collective-permute-start | bytes 3628808 | tf_op jit(solution)/shard_map/ppermute | solution.py:14
  41.5 120.4 %collective-permute-start.1 = (bf16[3,2,120,840]{2,1,3,0:T(2,128)(2,1)}, bf16[3,2,120,840]{2,1,3,0:T(2,128)(2,1)}, u32[]{:S(2)}, u32[]{:S(2)}) collective-permute-start(bf16[3,2,120,840]{2,1,3,0:T(2,128)(2,1)} %get-tuple-element.42), channel_id=1, source_target_pairs={{1,0},{2,1},{3,2},{4,3},{5,4},{6,5},{7,6},{8,7},{9,8},{10,9},{11,1... | collective-permute-start | bytes 3628808 | tf_op jit(solution)/shard_map/ppermute | solution.py:17
  50.4 16.7 %copy-start.1 = (bf16[8,2,120,840]{3,2,0,1:T(8,128)(2,1)S(1)}, bf16[8,2,120,840]{3,2,0,1:T(8,128)(2,1)}, u32[]{:S(2)}) copy-start(bf16[8,2,120,840]{3,2,0,1:T(8,128)(2,1)} %copy.21) | copy-start | bytes 9676804
  181.1 3.8 %copy-start = (f32[40,2,120,2,120]{4,2,3,1,0:T(8,128)}, f32[40,2,120,2,120]{4,2,3,1,0:T(8,128)S(1)}, u32[]{:S(2)}) copy-start(f32[40,2,120,2,120]{4,2,3,1,0:T(8,128)S(1)} %convolution_bitcast_fusion.2) | copy-start | bytes 27648004 | tf_op jit(solution)/shard_map/while
  205.2 3.8 %copy-start = (f32[40,2,120,2,120]{4,2,3,1,0:T(8,128)}, f32[40,2,120,2,120]{4,2,3,1,0:T(8,128)S(1)}, u32[]{:S(2)}) copy-start(f32[40,2,120,2,120]{4,2,3,1,0:T(8,128)S(1)} %convolution_bitcast_fusion.2) | copy-start | bytes 27648004 | tf_op jit(solution)/shard_map/while
  229.3 3.8 %copy-start = (f32[40,2,120,2,120]{4,2,3,1,0:T(8,128)}, f32[40,2,120,2,120]{4,2,3,1,0:T(8,128)S(1)}, u32[]{:S(2)}) copy-start(f32[40,2,120,2,120]{4,2,3,1,0:T(8,128)S(1)} %convolution_bitcast_fusion.2) | copy-start | bytes 27648004 | tf_op jit(solution)/shard_map/while
  253.5 3.8 %copy-start = (f32[40,2,120,2,120]{4,2,3,1,0:T(8,128)}, f32[40,2,120,2,120]{4,2,3,1,0:T(8,128)S(1)}, u32[]{:S(2)}) copy-start(f32[40,2,120,2,120]{4,2,3,1,0:T(8,128)S(1)} %convolution_bitcast_fusion.2) | copy-start | bytes 27648004 | tf_op jit(solution)/shard_map/while
Sparse Core Ops, SparseCore 0:
  69.0 88.9 all-reduce.2
where the time goes:
time: 279 us; the launch traced here: 278 us
  waiting for transfers between devices  89.1 us (32%)
  local copies, waits for them, and re-layouts  82.5 us (30%)
  other arithmetic  74.1 us (27%)
  between operations  14.1 us (5%)
  matrix products  8.36 us (3%)
  starting transfers between devices  6.64 us (2%)
    psum x1, waiting for transfers between devices, shards(): slab_real, slab_imag = lax.psum((local_real, local_imag), 'pix')  89.1 us
    mul x2, other arithmetic, shards(): masked = images * valid_mask[:, None, None, :].astype(jnp.bfloat16)  33.2 us
    another operation x6, other arithmetic, coherence(): return jnp.stack([real_part / scaled, imag_part / scaled], axis=-3)  19.3 us
    add x4, local copies, waits for them, and re-layouts, split_parts(): real_part = grams[..., 0, :, 0, :] + grams[..., 1, :, 1, :]  17.8 us
    dynamic_slice x4, local copies, waits for them, and re-layouts, one_look(): window_data = lax.dynamic_slice_in_dim(padded, 2 * look_index, 7, 0)  15.7 us
    while x8, local copies, waits for them, and re-layouts  15.1 us
    concatenate x1, other arithmetic, extended(): block = jnp.concatenate([low, block, high], axis=dim)  12.2 us
    gather x5, local copies, waits for them, and re-layouts, coherence(): powers = jnp.diagonal(real_part, axis1=-2, axis2=-1)  11.2 us
  transfers between devices with their start and end apart: 3, of which 1 were waited for; matrix products, arithmetic and copies ran while one was open for 10% of the time, Pallas kernels for 0%

commit v1 on v0

v1 whole, which is shorter than its diff:
```python
import functools
import jax
import jax.numpy as jnp
from jax import lax
from jax.experimental import pallas as pl
from jax.experimental.pallas import tpu as pltpu
from jax.sharding import PartitionSpec as P

floor_power = 30.0

LOOK = 21
LANES = 128
PER = LANES // LOOK
SPAN = PER * LOOK
ROWS = 8
SKEW = (5, 0, 1, 2, 3, 4, 1, 2)
BEFORE, AFTER = 3, 2
NT = (((1,), (1,)), ((), ()))


def skew_kernel(first, columns, has_sum, *refs):
    if has_sum:
        prev_ref, cur_ref, mask_prev_ref, mask_cur_ref, sum_ref, top_ref, mid_ref, low_ref, gram_ref, z_ref, acc_ref = refs
    else:
        prev_ref, cur_ref, mask_prev_ref, mask_cur_ref, top_ref, mid_ref, low_ref, gram_ref, z_ref, acc_ref = refs
    step = pl.program_id(0)
    g = step + first
    count = cur_ref.shape[2]

    @pl.when(step == 0)
    def _():
        z_ref[...] = jnp.zeros_like(z_ref)
        acc_ref[...] = jnp.zeros_like(acc_ref)

    lane = lax.broadcasted_iota(jnp.int32, (1, LANES), 1)
    from_prev = lane >= LANES - 2 * g
    place = jnp.where(from_prev, lane + 2 * g - LANES, lane + 2 * g)
    used = (place < SPAN) & (SPAN * g + place < columns)
    mask = jnp.where(from_prev, mask_prev_ref[...], mask_cur_ref[...])
    keep = jnp.where(used, mask, 0).astype(jnp.float32)
    prev_keep = jnp.broadcast_to(from_prev.astype(jnp.float32), (count, LANES)).astype(jnp.bfloat16) != 0
    zero = jnp.zeros((count, LANES), jnp.bfloat16)
    for r in range(ROWS):
        keep_r = jnp.broadcast_to(keep[r : r + 1], (count, LANES)).astype(jnp.bfloat16) != 0
        for k in range(2):
            row = jnp.where(prev_keep, prev_ref[r, k], cur_ref[r, k])
            row = jnp.where(keep_r, row, zero)
            row = pltpu.roll(row, 2 * g + LOOK * SKEW[r], 1)
            z_ref[pl.ds(k * LANES, count), pl.ds(r * LANES, LANES)] = row
            if r < AFTER:
                top_ref[0, r, k] = row
            elif r >= ROWS - BEFORE:
                low_ref[0, r - (ROWS - BEFORE), k] = row
            else:
                mid_ref[0, r - AFTER, k] = row
    z = z_ref[...]
    acc_ref[...] += lax.dot_general(z, z, NT, preferred_element_type=jnp.float32)

    @pl.when(step == pl.num_programs(0) - 1)
    def _():
        real = acc_ref[:LANES, :LANES] + acc_ref[LANES:, LANES:]
        imag = acc_ref[LANES:, :LANES] - acc_ref[:LANES, LANES:]
        i = lax.broadcasted_iota(jnp.int32, real.shape, 0)
        j = lax.broadcasted_iota(jnp.int32, real.shape, 1)
        packed = jnp.where(i <= j, real, imag)
        if has_sum:
            packed = packed + sum_ref[...]
        gram_ref[...] = packed


def skewed(images, valid_mask, first, groups, total):
    count, columns = images.shape[2:]
    block = (ROWS, 2, count, LANES)

    def rows_out(n):
        return jax.ShapeDtypeStruct((groups, n, 2, count, LANES), jnp.bfloat16)

    def rows_spec(n):
        return pl.BlockSpec((1, n, 2, count, LANES), lambda s: (s, 0, 0, 0, 0))

    middle = ROWS - AFTER - BEFORE
    in_specs = [
        pl.BlockSpec(block, lambda s: (0, 0, 0, jnp.maximum(s + first - 1, 0))),
        pl.BlockSpec(block, lambda s: (0, 0, 0, s + first)),
        pl.BlockSpec((ROWS, LANES), lambda s: (0, jnp.maximum(s + first - 1, 0))),
        pl.BlockSpec((ROWS, LANES), lambda s: (0, s + first)),
    ]
    operands = [images, images, valid_mask, valid_mask]
    if total is not None:
        in_specs.append(pl.BlockSpec((LANES, LANES), lambda s: (0, 0)))
        operands.append(total)
    return pl.pallas_call(
        functools.partial(skew_kernel, first, columns, total is not None),
        grid=(groups,),
        in_specs=in_specs,
        out_specs=[
            rows_spec(AFTER),
            rows_spec(middle),
            rows_spec(BEFORE),
            pl.BlockSpec((LANES, LANES), lambda s: (0, 0)),
        ],
        out_shape=[
            rows_out(AFTER),
            rows_out(middle),
            rows_out(BEFORE),
            jax.ShapeDtypeStruct((LANES, LANES), jnp.float32),
        ],
        scratch_shapes=[
            pltpu.VMEM((2 * LANES, ROWS * LANES), jnp.bfloat16),
            pltpu.VMEM((2 * LANES, 2 * LANES), jnp.float32),
        ],
        compiler_params=pltpu.CompilerParams(vmem_limit_bytes=48 * 2**20),
        cost_estimate=pl.CostEstimate(
            flops=2 * groups * 256 * 256 * 1024, bytes_accessed=groups * 3 * ROWS * 2 * count * LANES * 2, transcendentals=0
        ),
        name="skew",
    )(*operands)


def looks_kernel(aliased, *refs):
    if aliased:
        before_ref, top_ref, mid_ref, low_ref, after_ref, _, out_ref, w_ref, m_ref = refs
    else:
        before_ref, top_ref, mid_ref, low_ref, after_ref, out_ref, w_ref, m_ref = refs
    count = top_ref.shape[3]

    @pl.when(pl.program_id(0) == 0)
    def _():
        w_ref[...] = jnp.zeros_like(w_ref)
        m_ref[...] = jnp.zeros_like(m_ref)

    rows = {}
    for r in range(ROWS):
        if r < AFTER:
            rows[r] = top_ref.at[0, r]
        elif r >= ROWS - BEFORE:
            rows[r] = low_ref.at[0, r - (ROWS - BEFORE)]
        else:
            rows[r] = mid_ref.at[0, r - AFTER]
    for r in range(BEFORE):
        rows[r - BEFORE] = before_ref.at[0, r]
    for r in range(AFTER):
        rows[ROWS + r] = after_ref.at[0, r]

    lane = lax.broadcasted_iota(jnp.int32, (1, LANES), 1)

    def lanes_of(turn):
        place = lane + (-LOOK * turn) % LANES
        place = jnp.where(place >= LANES, place - LANES, place)
        return place < LOOK

    def widened(which):
        return jnp.broadcast_to(which.astype(jnp.float32), (count, LANES)).astype(jnp.bfloat16) != 0

    single = [lanes_of(t) for t in range(2 * PER - 1)]
    wide = [widened(s) for s in single]
    zero = jnp.zeros((count, LANES), jnp.bfloat16)

    def turn(l, r):
        return l + SKEW[r % ROWS]

    def gathered(l, k, which):
        out = zero
        for r in which:
            out = jnp.where(wide[turn(l, r)], rows[r][k], out)
        return out

    def kept(l, value, which):
        select = single[turn(l, which[0])]
        for r in which[1:]:
            select = select | single[turn(l, r)]
        return jnp.where(widened(select), value, zero)

    i = lax.broadcasted_iota(jnp.int32, (count, LANES), 0)
    j = lax.broadcasted_iota(jnp.int32, (count, LANES), 1)
    eye = i == j

    def normalised(real, imag, w, l):
        power = jnp.sum(jnp.where(eye, real, 0.0), axis=0, keepdims=True)
        across = lax.rsqrt(jnp.maximum(power, floor_power))
        down = jnp.sum(jnp.where(eye, across, 0.0), axis=1, keepdims=True)
        out_ref[w, l, 0] = (real * down * across).astype(jnp.bfloat16)[:, :count]
        out_ref[w, l, 1] = (imag * down * across).astype(jnp.bfloat16)[:, :count]

    for l in range(PER):
        common = [gathered(l, k, (1, 2, 3, 4, 5)) for k in range(2)]
        for half in range(2):
            outer_rows = (-3, -2, -1, 0) if half == 0 else (6, 7, 8, 9)
            slot = (2 * l + half) % 2
            for k in range(2):
                outer = gathered(l, k, outer_rows)
                w_ref[slot, k, pl.ds(0, count), pl.ds(0, LANES)] = common[k]
                w_ref[slot, k, pl.ds(0, count), pl.ds(LANES, LANES)] = outer
                if half == 0:
                    pairs = ((kept(l, common[k], (1, 2, 3)), outer), (common[k], kept(l, outer, (-1, 0))))
                else:
                    pairs = ((common[k], kept(l, outer, (6, 7))), (kept(l, common[k], (3, 4, 5)), outer))
                for w, (inner, rest) in enumerate(pairs):
                    m_ref[slot, w, k, pl.ds(0, count), pl.ds(0, LANES)] = inner
                    m_ref[slot, w, k, pl.ds(0, count), pl.ds(LANES, LANES)] = rest
            gram = lax.dot_general(
                m_ref[slot].reshape(4 * LANES, 2 * LANES),
                w_ref[slot].reshape(2 * LANES, 2 * LANES),
                NT,
                preferred_element_type=jnp.float32,
            )
            for w in range(2):
                base = 2 * w * LANES
                re = gram[base : base + count]
                im = gram[base + LANES : base + LANES + count]
                real = re[:, :LANES] + im[:, LANES:]
                imag = im[:, :LANES] - re[:, LANES:]
                normalised(real, imag, 2 * half + w, l)


def looked(before, parts, after, first, looks, previous):
    top, mid, low = parts
    groups, _, _, count, _ = top.shape

    def spec(array):
        return pl.BlockSpec((1,) + array.shape[1:], lambda s: (s, 0, 0, 0, 0))

    operands = [before, top, mid, low, after]
    in_specs = [spec(a) for a in operands]
    aliases = {}
    if previous is not None:
        aliases = {len(operands): 0}
        operands.append(previous)
        in_specs.append(pl.BlockSpec(memory_space=pl.ANY))
    return pl.pallas_call(
        functools.partial(looks_kernel, previous is not None),
        grid=(groups,),
        in_specs=in_specs,
        out_specs=pl.BlockSpec((ROWS // 2, PER, 2, count, count), lambda s: (0, s + first, 0, 0, 0)),
        out_shape=jax.ShapeDtypeStruct((ROWS // 2, looks, 2, count, count), jnp.bfloat16),
        input_output_aliases=aliases,
        scratch_shapes=[
            pltpu.VMEM((2, 2, LANES, 2 * LANES), jnp.bfloat16),
            pltpu.VMEM((2, 2, 2, LANES, 2 * LANES), jnp.bfloat16),
        ],
        compiler_params=pltpu.CompilerParams(vmem_limit_bytes=48 * 2**20),
        cost_estimate=pl.CostEstimate(
            flops=2 * groups * PER * 2 * 512 * 256 * 256, bytes_accessed=groups * 2 * 10**6, transcendentals=0
        ),
        name="looks",
    )(*operands)


def slab_kernel(packed_ref, out_ref):
    packed = packed_ref[...]
    flipped = packed.T
    i = lax.broadcasted_iota(jnp.int32, packed.shape, 0)
    j = lax.broadcasted_iota(jnp.int32, packed.shape, 1)
    real = jnp.where(i <= j, packed, flipped)
    imag = jnp.where(i > j, packed, jnp.where(i < j, -flipped, 0.0))
    powers = jnp.where(i == j, packed, 0.0)
    scaled = jnp.sqrt(jnp.sum(powers, axis=1, keepdims=True) * jnp.sum(powers, axis=0, keepdims=True))
    count = out_ref.shape[1]
    out_ref[0] = (real / scaled)[:count, :count]
    out_ref[1] = (imag / scaled)[:count, :count]


def axis_sum(value, axis):
    size = lax.axis_size(axis)
    stride = 1
    while size > stride:
        left = size // stride
        if left % 2:
            return lax.psum(value, axis)
        radix = 4 if left % 4 == 0 else 2
        got = []
        for shift in range(1, radix):
            pairs = []
            for i in range(size):
                place = (i // stride) % radix
                pairs.append((i, i + ((place + shift) % radix - place) * stride))
            got.append(lax.ppermute(value, axis, pairs))
        if radix == 4:
            value = (value + got[1]) + (got[0] + got[2])
        else:
            value = value + got[0]
        stride *= radix
    return value


def shards(images, valid_mask):
    count, columns = images.shape[2:]
    looks = columns // LOOK
    groups = -(-looks // PER)
    cuts = [0, -(-groups // 2), groups]
    size = lax.axis_size("pix")
    forward = [(i, i + 1) for i in range(size - 1)]
    backward = [(i + 1, i) for i in range(size - 1)]
    pieces = []
    total = None
    for start, stop in zip(cuts[:-1], cuts[1:]):
        top, mid, low, total = skewed(images, valid_mask, start, stop - start, total)
        before = lax.ppermute(low, "pix", forward)
        after = lax.ppermute(top, "pix", backward)
        pieces.append((start, (top, mid, low), before, after))
    total = axis_sum(total, "pix")
    slab_coherence = pl.pallas_call(
        slab_kernel, out_shape=jax.ShapeDtypeStruct((2, count, count), jnp.float32), name="slab"
    )(total)
    out = None
    for start, parts, before, after in pieces:
        out = looked(before, parts, after, start, looks, out)
    return (out, slab_coherence)


def solution(mesh):
    in_specs = (P(("group", "pix"), None, None, None), P(("group", "pix"), None))
    out_specs = (P(("group", "pix"), None, None, None, None), P("group", None, None))
    return jax.shard_map(shards, mesh=mesh, in_specs=in_specs, out_specs=out_specs, check_vma=False)
```

time: 279 us -> 61.1 us (0.22)
  local copies, waits for them, and re-layouts: 82.5 us -> 2.71 us
  waiting for transfers between devices: 89.1 us -> 11.5 us
  other arithmetic: 74.1 us -> 0.66 us
  Pallas kernels: 0 us -> 26.1 us
  between operations: 14.1 us -> 0.7 us
  starting transfers between devices: 6.64 us -> 19 us
  matrix products: 8.36 us -> 0 us
    psum x1 -> x0, waiting for transfers between devices: 89.1 us -> none  [shards(): slab_real, slab_imag = lax.psum((local_real, local_imag), 'pix')]
    mul x2 -> x0, other arithmetic: 33.2 us -> none  [shards(): masked = images * valid_mask[:, None, None, :].astype(jnp.bfloat16)]
    pallas_call x0 -> x5, Pallas kernels: none -> 26.1 us  [the longest x2 18.4 us: looked(): pl.pallas_call(functools.partial(looks_kernel, previous is not None), gri...]
    another operation x6 -> x0, other arithmetic: 19.3 us -> none  [coherence(): return jnp.stack([real_part / scaled, imag_part / scaled], axis=-3)]
    dynamic_slice x8 -> x0, local copies, waits for them, and re-layouts: 18.1 us -> none  [the longest x4 15.7 us: one_look(): window_data = lax.dynamic_slice_in_dim(padded, 2 * look_index, 7, 0)]
    add x4 -> x0, local copies, waits for them, and re-layouts: 17.8 us -> none  [split_parts(): real_part = grams[..., 0, :, 0, :] + grams[..., 1, :, 1, :]]
    while x8 -> x0, local copies, waits for them, and re-layouts: 15.1 us -> none
    ppermute x2 -> x10, starting transfers between devices: 6.6 us -> 19 us  [the longest x2 9.2 us: shards(): before = lax.ppermute(low, 'pix', forward)]
  transfers between devices with their start and end apart: 3 -> 10, of which waited for: 1 -> 3; matrix products, arithmetic and copies ran while one was open for 10% -> 1% of each run, Pallas kernels for 0% -> 24%
where the time goes in v1:
time: 61.1 us; the launch traced here: 60.7 us
  Pallas kernels  26.1 us (43%)
  starting transfers between devices  19 us (31%)
  waiting for transfers between devices  11.5 us (19%)
  local copies, waits for them, and re-layouts  2.71 us (4%)
  between operations  0.7 us (1%)
  other arithmetic  0.66 us (1%)
    pallas_call x2, Pallas kernels, looked(): pl.pallas_call(functools.partial(looks_kernel, previous is not None), gri...  18.4 us
    ppermute x6, waiting for transfers between devices, axis_sum(): got.append(lax.ppermute(value, axis, pairs))  11.5 us
    ppermute x2, starting transfers between devices, shards(): before = lax.ppermute(low, 'pix', forward)  9.2 us
    pallas_call x2, Pallas kernels, skewed(): pl.pallas_call(functools.partial(skew_kernel, first, columns, total is no...  6.11 us
    ppermute x6, starting transfers between devices, axis_sum(): got.append(lax.ppermute(value, axis, pairs))  5.62 us
    ppermute x2, starting transfers between devices, shards(): after = lax.ppermute(top, 'pix', backward)  4.18 us
    unnamed x4, local copies, waits for them, and re-layouts  2.71 us
    pallas_call x1, Pallas kernels, shards(): pl.pallas_call(slab_kernel, out_shape=jax.ShapeDtypeStruct((2, count, cou...  1.63 us
  transfers between devices with their start and end apart: 10, of which 3 were waited for; matrix products, arithmetic and copies ran while one was open for 1% of the time, Pallas kernels for 24%

profile of v1, /device:TPU:1, one launch (start us, length us, event | category | flops | bytes accessed | tf_op | source)
XLA Modules:
  0.0 60.7 jit_solution(3435236986347089373)
XLA Ops:
  0.6 2.0 %copy-done = bf16[8,2,120,840]{3,2,1,0:T(8,128)(2,1)S(1)} copy-done((bf16[8,2,120,840]{3,2,1,0:T(8,128)(2,1)S(1)}, bf16[8,2,120,840]{3,2,1,0:T(8,128)(2,1)}, u32[]{:S(2)}) %copy-start) | copy-done | bytes 3225624
  2.6 0.7 %copy-done.1 = s32[8,840]{1,0:T(8,128)S(1)} copy-done((s32[8,840]{1,0:T(8,128)S(1)}, s32[8,840]{1,0:T(8,128)}, u32[]{:S(2)}) %copy-start.1) | copy-done | bytes 26904
  3.4 3.3 %skew.2 = (bf16[4,2,2,120,128]{4,3,2,1,0:T(8,128)(2,1)}, bf16[4,3,2,120,128]{4,3,2,1,0:T(8,128)(2,1)S(1)}, bf16[4,3,2,120,128]{4,3,2,1,0:T(8,128)(2,1)S(1)}, f32[128,128]{1,0:T(8,128)S(1)}) custom-call(bf16[8,2,120,840]{3,2,1,0:T(8,128)(2,1)S(1)} %copy-done, bf16[8,2,120,840]{3,2,1,0:T(8,128)(2,1)S(1)} %copy-done, s32[8,840]{1,0:T(8,128)S(1)} %copy-done.1, ...), custom_call_target="tpu_custom_call" | custom-call | flops 536870912 | bytes 5898240 | tf_op jit(solution)/shard_map/skew/pallas_call | solution.py:92
  6.7 4.5 %collective-permute-start.2 = (bf16[4,3,2,120,128]{4,3,2,1,0:T(8,128)(2,1)S(1)}, bf16[4,3,2,120,128]{4,3,2,1,0:T(8,128)(2,1)S(1)}, u32[]{:S(2)}, u32[]{:S(2)}) collective-permute-start(bf16[4,3,2,120,128]{4,3,2,1,0:T(8,128)(2,1)S(1)} %get-tuple-element.14.refs_3_), channel_id=1, source_target_pairs={{0,1},{1,2},{2,3},{3,4},{4,5},{5,6},{6,7},{7,8},{8,9},{9,10},{10,1... | collective-permute-start | bytes 2211848 | tf_op jit(solution)/shard_map/ppermute | solution.py:298
  11.2 2.8 %skew.3 = (bf16[3,2,2,120,128]{4,3,2,1,0:T(8,128)(2,1)}, bf16[3,3,2,120,128]{4,3,2,1,0:T(8,128)(2,1)S(1)}, bf16[3,3,2,120,128]{4,3,2,1,0:T(8,128)(2,1)S(1)}, f32[128,128]{1,0:T(8,128)S(1)}) custom-call(bf16[8,2,120,840]{3,2,1,0:T(8,128)(2,1)S(1)} %copy-done, bf16[8,2,120,840]{3,2,1,0:T(8,128)(2,1)S(1)} %copy-done, s32[8,840]{1,0:T(8,128)S(1)} %copy-done.1, ...), custom_call_target="tpu_custom_call" | custom-call | flops 402653184 | bytes 4423680 | tf_op jit(solution)/shard_map/skew/pallas_call | solution.py:92
  14.0 0.0 collective-permute-start.5
  14.0 0.5 collective-permute-start.6
  14.5 1.3 %collective-permute-start.4 = (f32[128,128]{1,0:T(8,128)S(1)}, f32[128,128]{1,0:T(8,128)S(1)}, u32[]{:S(2)}, u32[]{:S(2)}) collective-permute-start(f32[128,128]{1,0:T(8,128)S(1)} %get-tuple-element.17), channel_id=1, source_target_pairs={{0,2},{1,3},{2,0},{3,1},{4,6},{5,7},{6,4},{7,5},{8,10},{9,11},{10,... | collective-permute-start | bytes 196616 | tf_op jit(solution)/shard_map/ppermute | solution.py:277
  15.8 2.3 %collective-permute-start.3 = (bf16[4,2,2,120,128]{4,3,2,1,0:T(8,128)(2,1)}, bf16[4,2,2,120,128]{4,3,2,1,0:T(8,128)(2,1)}, u32[]{:S(2)}, u32[]{:S(2)}) collective-permute-start(bf16[4,2,2,120,128]{4,3,2,1,0:T(8,128)(2,1)} %get-tuple-element.15.refs_1_), channel_id=1, source_target_pairs={{1,0},{2,1},{3,2},{4,3},{5,4},{6,5},{7,6},{8,7},{9,8},{10,9},{11,1... | collective-permute-start | bytes 1474568 | tf_op jit(solution)/shard_map/ppermute | solution.py:299
  18.0 8.9 %collective-permute-done.5 = f32[128,128]{1,0:T(8,128)S(1)} collective-permute-done((f32[128,128]{1,0:T(8,128)S(1)}, f32[128,128]{1,0:T(8,128)S(1)}, u32[]{:S(2)}, u32[]{:S(2)}) %collective-permute-start.5) | collective-permute-done | bytes 65568 | tf_op jit(solution)/shard_map/ppermute | solution.py:277
  26.9 0.0 collective-permute-done.6
  27.0 0.7 %collective-permute-done.4 = f32[128,128]{1,0:T(8,128)S(1)} collective-permute-done((f32[128,128]{1,0:T(8,128)S(1)}, f32[128,128]{1,0:T(8,128)S(1)}, u32[]{:S(2)}, u32[]{:S(2)}) %collective-permute-start.4) | collective-permute-done | bytes 65568 | tf_op jit(solution)/shard_map/ppermute | solution.py:277
  27.7 1.3 %collective-permute-start.8 = (f32[128,128]{1,0:T(8,128)S(1)}, f32[128,128]{1,0:T(8,128)S(1)}, u32[]{:S(2)}, u32[]{:S(2)}) collective-permute-start(f32[128,128]{1,0:T(8,128)S(1)} %add_add_fusion.1), channel_id=1, source_target_pairs={{0,4},{1,5},{2,6},{3,7},{4,8},{5,9},{6,10},{7,11},{8,12},{9,13},{1... | collective-permute-start | bytes 196616 | tf_op jit(solution)/shard_map/ppermute | solution.py:277
  29.0 2.0 %collective-permute-start.9 = (f32[128,128]{1,0:T(8,128)S(1)}, f32[128,128]{1,0:T(8,128)S(1)}, u32[]{:S(2)}, u32[]{:S(2)}) collective-permute-start(f32[128,128]{1,0:T(8,128)S(1)} %add_add_fusion.1), channel_id=1, source_target_pairs={{0,12},{1,13},{2,14},{3,15},{4,0},{5,1},{6,2},{7,3},{8,4},{9,5},{1... | collective-permute-start | bytes 196616 | tf_op jit(solution)/shard_map/ppermute | solution.py:277
  31.0 0.5 collective-permute-start.7
  31.5 1.9 %collective-permute-done.8 = f32[128,128]{1,0:T(8,128)S(1)} collective-permute-done((f32[128,128]{1,0:T(8,128)S(1)}, f32[128,128]{1,0:T(8,128)S(1)}, u32[]{:S(2)}, u32[]{:S(2)}) %collective-permute-start.8) | collective-permute-done | bytes 65568 | tf_op jit(solution)/shard_map/ppermute | solution.py:277
  33.4 4.7 %collective-permute-start = (bf16[3,3,2,120,128]{4,3,2,1,0:T(8,128)(2,1)S(1)}, bf16[3,3,2,120,128]{4,3,2,1,0:T(8,128)(2,1)}, u32[]{:S(2)}, u32[]{:S(2)}) collective-permute-start(bf16[3,3,2,120,128]{4,3,2,1,0:T(8,128)(2,1)S(1)} %get-tuple-element.11.refs_3_), channel_id=1, source_target_pairs={{0,1},{1,2},{2,3},{3,4},{4,5},{5,6},{6,7},{7,8},{8,9},{9,10},{10,1... | collective-permute-start | bytes 1658888 | tf_op jit(solution)/shard_map/ppermute | solution.py:298
  38.1 0.0 collective-permute-done.9
  38.1 1.9 %collective-permute-start.1 = (bf16[3,2,2,120,128]{4,3,2,1,0:T(8,128)(2,1)}, bf16[3,2,2,120,128]{4,3,2,1,0:T(8,128)(2,1)}, u32[]{:S(2)}, u32[]{:S(2)}) collective-permute-start(bf16[3,2,2,120,128]{4,3,2,1,0:T(8,128)(2,1)} %get-tuple-element.12.refs_1_), channel_id=1, source_target_pairs={{1,0},{2,1},{3,2},{4,3},{5,4},{6,5},{7,6},{8,7},{9,8},{10,9},{11,1... | collective-permute-start | bytes 1105928 | tf_op jit(solution)/shard_map/ppermute | solution.py:299
  40.0 0.0 collective-permute-done.7
  40.1 0.6 %add_add_fusion.packed_ref = f32[128,128]{1,0:T(8,128)} fusion(f32[128,128]{1,0:T(8,128)S(1)} %collective-permute-done.8, f32[128,128]{1,0:T(8,128)S(1)} %collective-permute-done.9, f32[128,128]{1,0:T(8,128)S(1)} %add_add_fusion.1, f32[128,128]{1,0:T(8,128)S(1)} %collective-permute-done.7), kind=kLoop, calls=%fused_computation | loop fusion | flops 49152 | bytes 327680 | tf_op jit(solution)/shard_map/add | solution.py:279
  40.7 1.6 %slab.1 = f32[2,120,120]{2,1,0:T(8,128)} custom-call(f32[128,128]{1,0:T(8,128)} %add_add_fusion.packed_ref), custom_call_target="tpu_custom_call" | custom-call | tf_op jit(solution)/shard_map/slab/pallas_call | solution.py:302
  42.3 10.3 %looks.2.refs_5_ = bf16[4,40,2,120,120]{4,3,2,1,0:T(8,128)(2,1)} custom-call(bf16[4,3,2,120,128]{4,3,2,1,0:T(8,128)(2,1)S(1)} %collective-permute-done.2.refs_0_, bf16[4,2,2,120,128]{4,3,2,1,0:T(8,128)(2,1)} %get-tuple-element.15.refs_1_, bf16[4,3,2,120,128]{4,3,2,1,0:T(8,128)(2,1)S(1)} %get-tuple-element.16.refs_2_, ...), custom_call_target="tpu_custom_call" | custom-call | flops 3221225472 | bytes 8000000 | tf_op jit(solution)/shard_map/looks/pallas_call | solution.py:230
  52.6 8.1 %looks.3 = bf16[4,40,2,120,120]{4,3,2,1,0:T(8,128)(2,1)} custom-call(bf16[3,3,2,120,128]{4,3,2,1,0:T(8,128)(2,1)} %collective-permute-done.refs_0_, bf16[3,2,2,120,128]{4,3,2,1,0:T(8,128)(2,1)} %get-tuple-element.12.refs_1_, bf16[3,3,2,120,128]{4,3,2,1,0:T(8,128)(2,1)S(1)} %get-tuple-element.13.refs_2_, ...), custom_call_target="tpu_custom_call", output_to_operand_aliasing={{}: (5, {})} | custom-call | flops 2415919104 | bytes 6000000 | tf_op jit(solution)/shard_map/looks/pallas_call | solution.py:230
  (7 shorter events, 0.0 us)
Async XLA Ops:
  0.6 2.0 %copy-start = (bf16[8,2,120,840]{3,2,1,0:T(8,128)(2,1)S(1)}, bf16[8,2,120,840]{3,2,1,0:T(8,128)(2,1)}, u32[]{:S(2)}) copy-start(bf16[8,2,120,840]{3,2,1,0:T(8,128)(2,1)} %refs_1_.3) | copy-start | bytes 9676804
  2.6 0.7 %copy-start.1 = (s32[8,840]{1,0:T(8,128)S(1)}, s32[8,840]{1,0:T(8,128)}, u32[]{:S(2)}) copy-start(s32[8,840]{1,0:T(8,128)} %refs_3_.3) | copy-start | bytes 80644
  6.7 35.7 %collective-permute-start.2 = (bf16[4,3,2,120,128]{4,3,2,1,0:T(8,128)(2,1)S(1)}, bf16[4,3,2,120,128]{4,3,2,1,0:T(8,128)(2,1)S(1)}, u32[]{:S(2)}, u32[]{:S(2)}) collective-permute-start(bf16[4,3,2,120,128]{4,3,2,1,0:T(8,128)(2,1)S(1)} %get-tuple-element.14.refs_3_), channel_id=1, source_target_pairs={{0,1},{1,2},{2,3},{3,4},{4,5},{5,6},{6,7},{7,8},{8,9},{9,10},{10,1... | collective-permute-start | bytes 2211848 | tf_op jit(solution)/shard_map/ppermute | solution.py:298
  14.0 13.0 %collective-permute-start.5 = (f32[128,128]{1,0:T(8,128)S(1)}, f32[128,128]{1,0:T(8,128)S(1)}, u32[]{:S(2)}, u32[]{:S(2)}) collective-permute-start(f32[128,128]{1,0:T(8,128)S(1)} %get-tuple-element.17), channel_id=1, source_target_pairs={{0,1},{1,2},{2,3},{3,0},{4,5},{5,6},{6,7},{7,4},{8,9},{9,10},{10,1... | collective-permute-start | bytes 196616 | tf_op jit(solution)/shard_map/ppermute | solution.py:277
  14.0 13.0 %collective-permute-start.6 = (f32[128,128]{1,0:T(8,128)S(1)}, f32[128,128]{1,0:T(8,128)S(1)}, u32[]{:S(2)}, u32[]{:S(2)}) collective-permute-start(f32[128,128]{1,0:T(8,128)S(1)} %get-tuple-element.17), channel_id=1, source_target_pairs={{0,3},{1,0},{2,1},{3,2},{4,7},{5,4},{6,5},{7,6},{8,11},{9,8},{10,9... | collective-permute-start | bytes 196616 | tf_op jit(solution)/shard_map/ppermute | solution.py:277
  14.5 13.2 %collective-permute-start.4 = (f32[128,128]{1,0:T(8,128)S(1)}, f32[128,128]{1,0:T(8,128)S(1)}, u32[]{:S(2)}, u32[]{:S(2)}) collective-permute-start(f32[128,128]{1,0:T(8,128)S(1)} %get-tuple-element.17), channel_id=1, source_target_pairs={{0,2},{1,3},{2,0},{3,1},{4,6},{5,7},{6,4},{7,5},{8,10},{9,11},{10,... | collective-permute-start | bytes 196616 | tf_op jit(solution)/shard_map/ppermute | solution.py:277
  15.8 26.6 %collective-permute-start.3 = (bf16[4,2,2,120,128]{4,3,2,1,0:T(8,128)(2,1)}, bf16[4,2,2,120,128]{4,3,2,1,0:T(8,128)(2,1)}, u32[]{:S(2)}, u32[]{:S(2)}) collective-permute-start(bf16[4,2,2,120,128]{4,3,2,1,0:T(8,128)(2,1)} %get-tuple-element.15.refs_1_), channel_id=1, source_target_pairs={{1,0},{2,1},{3,2},{4,3},{5,4},{6,5},{7,6},{8,7},{9,8},{10,9},{11,1... | collective-permute-start | bytes 1474568 | tf_op jit(solution)/shard_map/ppermute | solution.py:299
  27.7 5.7 %collective-permute-start.8 = (f32[128,128]{1,0:T(8,128)S(1)}, f32[128,128]{1,0:T(8,128)S(1)}, u32[]{:S(2)}, u32[]{:S(2)}) collective-permute-start(f32[128,128]{1,0:T(8,128)S(1)} %add_add_fusion.1), channel_id=1, source_target_pairs={{0,4},{1,5},{2,6},{3,7},{4,8},{5,9},{6,10},{7,11},{8,12},{9,13},{1... | collective-permute-start | bytes 196616 | tf_op jit(solution)/shard_map/ppermute | solution.py:277
  29.0 9.1 %collective-permute-start.9 = (f32[128,128]{1,0:T(8,128)S(1)}, f32[128,128]{1,0:T(8,128)S(1)}, u32[]{:S(2)}, u32[]{:S(2)}) collective-permute-start(f32[128,128]{1,0:T(8,128)S(1)} %add_add_fusion.1), channel_id=1, source_target_pairs={{0,12},{1,13},{2,14},{3,15},{4,0},{5,1},{6,2},{7,3},{8,4},{9,5},{1... | collective-permute-start | bytes 196616 | tf_op jit(solution)/shard_map/ppermute | solution.py:277
  31.0 9.1 %collective-permute-start.7 = (f32[128,128]{1,0:T(8,128)S(1)}, f32[128,128]{1,0:T(8,128)S(1)}, u32[]{:S(2)}, u32[]{:S(2)}) collective-permute-start(f32[128,128]{1,0:T(8,128)S(1)} %add_add_fusion.1), channel_id=1, source_target_pairs={{0,8},{1,9},{2,10},{3,11},{4,12},{5,13},{6,14},{7,15},{8,0},{9,1},... | collective-permute-start | bytes 196616 | tf_op jit(solution)/shard_map/ppermute | solution.py:277
  33.4 19.2 %collective-permute-start = (bf16[3,3,2,120,128]{4,3,2,1,0:T(8,128)(2,1)S(1)}, bf16[3,3,2,120,128]{4,3,2,1,0:T(8,128)(2,1)}, u32[]{:S(2)}, u32[]{:S(2)}) collective-permute-start(bf16[3,3,2,120,128]{4,3,2,1,0:T(8,128)(2,1)S(1)} %get-tuple-element.11.refs_3_), channel_id=1, source_target_pairs={{0,1},{1,2},{2,3},{3,4},{4,5},{5,6},{6,7},{7,8},{8,9},{9,10},{10,1... | collective-permute-start | bytes 1658888 | tf_op jit(solution)/shard_map/ppermute | solution.py:298
  38.1 14.5 %collective-permute-start.1 = (bf16[3,2,2,120,128]{4,3,2,1,0:T(8,128)(2,1)}, bf16[3,2,2,120,128]{4,3,2,1,0:T(8,128)(2,1)}, u32[]{:S(2)}, u32[]{:S(2)}) collective-permute-start(bf16[3,2,2,120,128]{4,3,2,1,0:T(8,128)(2,1)} %get-tuple-element.12.refs_1_), channel_id=1, source_target_pairs={{1,0},{2,1},{3,2},{4,3},{5,4},{6,5},{7,6},{8,7},{9,8},{10,9},{11,1... | collective-permute-start | bytes 1105928 | tf_op jit(solution)/shard_map/ppermute | solution.py:299

commit v2 on v1

--- a/solution.py
+++ b/solution.py
@@ -18,43 +18,140 @@
 NT = (((1,), (1,)), ((), ()))
 
 
-def skew_kernel(first, columns, has_sum, *refs):
-    if has_sum:
-        prev_ref, cur_ref, mask_prev_ref, mask_cur_ref, sum_ref, top_ref, mid_ref, low_ref, gram_ref, z_ref, acc_ref = refs
-    else:
-        prev_ref, cur_ref, mask_prev_ref, mask_cur_ref, top_ref, mid_ref, low_ref, gram_ref, z_ref, acc_ref = refs
+def turned(image, mask, skew, columns, put):
+    count = image[0].shape[0]
+    zero = jnp.zeros((count, LANES), jnp.bfloat16)
+    lane = lax.broadcasted_iota(jnp.int32, (1, LANES), 1)
+
+    def tile(value, g):
+        start, stop = g * LANES, min((g + 1) * LANES, columns)
+        part = value[:, start:stop]
+        if stop - start < LANES:
+            rest = jnp.zeros((part.shape[0], LANES - (stop - start)), part.dtype)
+            part = jnp.concatenate([part, rest], axis=1)
+        return part
+
+    def widened(which):
+        return jnp.broadcast_to(which.astype(jnp.float32), (count, LANES)).astype(jnp.bfloat16) != 0
+
+    tiles = -(-columns // LANES)
+    for g in range(-(-columns // SPAN)):
+        slide = (LANES - SPAN) * g
+        place = (lane + slide) % LANES
+        used = (place < SPAN) & (SPAN * g + place < columns)
+        prior = lane >= LANES - slide
+        sides = [t for t in (g - 1, g) if 0 <= t < tiles]
+
+        def joined(value):
+            parts = [tile(value, t) for t in sides]
+            if len(parts) == 1:
+                return parts[0]
+            which = prior if value.shape[0] == 1 else widened(prior)
+            return jnp.where(which, parts[0], parts[1])
+
+        keep = widened(used & (joined(mask) != 0))
+        for k in range(2):
+            row = jnp.where(keep, joined(image[k]), zero)
+            put(g, k, pltpu.roll(row, slide + LOOK * skew, 1))
+
+
+def pick(table, step):
+    value = table[0]
+    for i, entry in enumerate(table[1:]):
+        value = jnp.where(step > i, entry, value)
+    return value
+
+
+def edge_kernel(cuts, image_ref, mask_ref, *outs):
     step = pl.program_id(0)
-    g = step + first
-    count = cur_ref.shape[2]
+    low_refs, top_refs = outs[: len(cuts) - 1], outs[len(cuts) - 1 :]
+    row = lax.rem(step + ROWS - BEFORE, ROWS)
+    mask = mask_ref[pl.ds(row, 1), :]
+    skew = pick(SKEW[ROWS - BEFORE :] + SKEW[:AFTER], step)
+
+    def work(refs):
+        def put(g, k, value):
+            c = max(i for i in range(len(cuts) - 1) if cuts[i] <= g)
+            refs[c][g - cuts[c], 0, k] = value
+
+        turned([image_ref.at[0, 0], image_ref.at[0, 1]], mask, skew, mask.shape[1], put)
+
+    @pl.when(step < BEFORE)
+    def _():
+        work(low_refs)
+
+    @pl.when(step >= BEFORE)
+    def _():
+        work(top_refs)
+
+
+def edges(images, valid_mask, cuts):
+    count, columns = images.shape[2:]
+    sizes = [b - a for a, b in zip(cuts[:-1], cuts[1:])]
+
+    def shape(n, rows):
+        return jax.ShapeDtypeStruct((n, rows, 2, count, LANES), jnp.bfloat16)
+
+    def spec(n, index):
+        return pl.BlockSpec((n, 1, 2, count, LANES), lambda s: (0, index(s), 0, 0, 0))
+
+    outs = pl.pallas_call(
+        functools.partial(edge_kernel, cuts),
+        grid=(BEFORE + AFTER,),
+        in_specs=[
+            pl.BlockSpec((1, 2, count, columns), lambda s: (lax.rem(s + ROWS - BEFORE, ROWS), 0, 0, 0)),
+            pl.BlockSpec((ROWS, columns), lambda s: (0, 0)),
+        ],
+        out_specs=[spec(n, lambda s: jnp.minimum(s, BEFORE - 1)) for n in sizes]
+        + [spec(n, lambda s: jnp.maximum(s - BEFORE, 0)) for n in sizes],
+        out_shape=[shape(n, BEFORE) for n in sizes] + [shape(n, AFTER) for n in sizes],
+        cost_estimate=pl.CostEstimate(flops=10**6, bytes_accessed=4 * 10**6, transcendentals=0),
+        name="edges",
+    )(images, valid_mask)
+    return outs[: len(sizes)], outs[len(sizes) :]
+
+
+def middle_kernel(cuts, image_ref, mask_ref, *refs):
+    step = pl.program_id(0)
+    pieces = len(cuts) - 1
+    low_refs, top_refs = refs[:pieces], refs[pieces : 2 * pieces]
+    mid_ref, gram_ref, z_ref, acc_ref = refs[2 * pieces :]
+    groups = cuts[-1]
+    count = image_ref.shape[2]
 
     @pl.when(step == 0)
     def _():
         z_ref[...] = jnp.zeros_like(z_ref)
         acc_ref[...] = jnp.zeros_like(acc_ref)
 
-    lane = lax.broadcasted_iota(jnp.int32, (1, LANES), 1)
-    from_prev = lane >= LANES - 2 * g
-    place = jnp.where(from_prev, lane + 2 * g - LANES, lane + 2 * g)
-    used = (place < SPAN) & (SPAN * g + place < columns)
-    mask = jnp.where(from_prev, mask_prev_ref[...], mask_cur_ref[...])
-    keep = jnp.where(used, mask, 0).astype(jnp.float32)
-    prev_keep = jnp.broadcast_to(from_prev.astype(jnp.float32), (count, LANES)).astype(jnp.bfloat16) != 0
-    zero = jnp.zeros((count, LANES), jnp.bfloat16)
-    for r in range(ROWS):
-        keep_r = jnp.broadcast_to(keep[r : r + 1], (count, LANES)).astype(jnp.bfloat16) != 0
-        for k in range(2):
-            row = jnp.where(prev_keep, prev_ref[r, k], cur_ref[r, k])
-            row = jnp.where(keep_r, row, zero)
-            row = pltpu.roll(row, 2 * g + LOOK * SKEW[r], 1)
-            z_ref[pl.ds(k * LANES, count), pl.ds(r * LANES, LANES)] = row
-            if r < AFTER:
-                top_ref[0, r, k] = row
-            elif r >= ROWS - BEFORE:
-                low_ref[0, r - (ROWS - BEFORE), k] = row
-            else:
-                mid_ref[0, r - AFTER, k] = row
-    z = z_ref[...]
-    acc_ref[...] += lax.dot_general(z, z, NT, preferred_element_type=jnp.float32)
+    row = step + AFTER
+    mask = mask_ref[pl.ds(row, 1), :]
+
+    def place(at, g, k, value):
+        z_ref[pl.ds(k * LANES, count), pl.ds((at * groups + g) * LANES, LANES)] = value
+
+    def put(g, k, value):
+        mid_ref[g, 0, k] = value
+        place(0, g, k, value)
+
+    turned([image_ref.at[0, 0], image_ref.at[0, 1]], mask, pick(SKEW[AFTER : ROWS - BEFORE], step), mask.shape[1], put)
+    for c in range(pieces):
+        for g in range(cuts[c], cuts[c + 1]):
+            for k in range(2):
+                place(1, g, k, low_refs[c][g - cuts[c], 0, k])
+                place(2, g, k, top_refs[c][g - cuts[c], 0, k])
+
+    def add(rows):
+        z = z_ref[:, : rows * groups * LANES]
+        acc_ref[...] += lax.dot_general(z, z, NT, preferred_element_type=jnp.float32)
+
+    @pl.when(step < AFTER)
+    def _():
+        add(3)
+
+    @pl.when(step >= AFTER)
+    def _():
+        add(2)
 
     @pl.when(step == pl.num_programs(0) - 1)
     def _():
@@ -62,59 +159,41 @@
         imag = acc_ref[LANES:, :LANES] - acc_ref[:LANES, LANES:]
         i = lax.broadcasted_iota(jnp.int32, real.shape, 0)
         j = lax.broadcasted_iota(jnp.int32, real.shape, 1)
-        packed = jnp.where(i <= j, real, imag)
-        if has_sum:
-            packed = packed + sum_ref[...]
-        gram_ref[...] = packed
-
-
-def skewed(images, valid_mask, first, groups, total):
+        gram_ref[...] = jnp.where(i <= j, real, imag)
+
+
+def middle(images, valid_mask, lows, tops, cuts):
     count, columns = images.shape[2:]
-    block = (ROWS, 2, count, LANES)
-
-    def rows_out(n):
-        return jax.ShapeDtypeStruct((groups, n, 2, count, LANES), jnp.bfloat16)
-
-    def rows_spec(n):
-        return pl.BlockSpec((1, n, 2, count, LANES), lambda s: (s, 0, 0, 0, 0))
-
-    middle = ROWS - AFTER - BEFORE
-    in_specs = [
-        pl.BlockSpec(block, lambda s: (0, 0, 0, jnp.maximum(s + first - 1, 0))),
-        pl.BlockSpec(block, lambda s: (0, 0, 0, s + first)),
-        pl.BlockSpec((ROWS, LANES), lambda s: (0, jnp.maximum(s + first - 1, 0))),
-        pl.BlockSpec((ROWS, LANES), lambda s: (0, s + first)),
-    ]
-    operands = [images, images, valid_mask, valid_mask]
-    if total is not None:
-        in_specs.append(pl.BlockSpec((LANES, LANES), lambda s: (0, 0)))
-        operands.append(total)
+    groups = cuts[-1]
+    rows = ROWS - AFTER - BEFORE
+
+    def spec(array, last):
+        return pl.BlockSpec((array.shape[0], 1, 2, count, LANES), lambda s: (0, jnp.minimum(s, last), 0, 0, 0))
+
     return pl.pallas_call(
-        functools.partial(skew_kernel, first, columns, total is not None),
-        grid=(groups,),
-        in_specs=in_specs,
+        functools.partial(middle_kernel, cuts),
+        grid=(rows,),
+        in_specs=[
+            pl.BlockSpec((1, 2, count, columns), lambda s: (s + AFTER, 0, 0, 0)),
+            pl.BlockSpec((ROWS, columns), lambda s: (0, 0)),
+        ]
+        + [spec(a, BEFORE - 1) for a in lows]
+        + [spec(a, AFTER - 1) for a in tops],
         out_specs=[
-            rows_spec(AFTER),
-            rows_spec(middle),
-            rows_spec(BEFORE),
+            pl.BlockSpec((groups, 1, 2, count, LANES), lambda s: (0, s, 0, 0, 0)),
             pl.BlockSpec((LANES, LANES), lambda s: (0, 0)),
         ],
         out_shape=[
-            rows_out(AFTER),
-            rows_out(middle),
-            rows_out(BEFORE),
+            jax.ShapeDtypeStruct((groups, rows, 2, count, LANES), jnp.bfloat16),
             jax.ShapeDtypeStruct((LANES, LANES), jnp.float32),
         ],
         scratch_shapes=[
-            pltpu.VMEM((2 * LANES, ROWS * LANES), jnp.bfloat16),
+            pltpu.VMEM((2 * LANES, 3 * groups * LANES), jnp.bfloat16),
             pltpu.VMEM((2 * LANES, 2 * LANES), jnp.float32),
         ],
-        compiler_params=pltpu.CompilerParams(vmem_limit_bytes=48 * 2**20),
-        cost_estimate=pl.CostEstimate(
-            flops=2 * groups * 256 * 256 * 1024, bytes_accessed=groups * 3 * ROWS * 2 * count * LANES * 2, transcendentals=0
-        ),
-        name="skew",
-    )(*operands)
+        cost_estimate=pl.CostEstimate(flops=10**9, bytes_accessed=5 * 10**6, transcendentals=0),
+        name="middle",
+    )(images, valid_mask, *lows, *tops)
 
 
 def looks_kernel(aliased, *refs):
@@ -217,11 +296,11 @@
     top, mid, low = parts
     groups, _, _, count, _ = top.shape
 
-    def spec(array):
-        return pl.BlockSpec((1,) + array.shape[1:], lambda s: (s, 0, 0, 0, 0))
+    def spec(array, offset):
+        return pl.BlockSpec((1,) + array.shape[1:], lambda s: (s + offset, 0, 0, 0, 0))
 
     operands = [before, top, mid, low, after]
-    in_specs = [spec(a) for a in operands]
+    in_specs = [spec(a, first if a is mid else 0) for a in operands]
     aliases = {}
     if previous is not None:
         aliases = {len(operands): 0}
@@ -238,7 +317,6 @@
             pltpu.VMEM((2, 2, LANES, 2 * LANES), jnp.bfloat16),
             pltpu.VMEM((2, 2, 2, LANES, 2 * LANES), jnp.bfloat16),
         ],
-        compiler_params=pltpu.CompilerParams(vmem_limit_bytes=48 * 2**20),
         cost_estimate=pl.CostEstimate(
             flops=2 * groups * PER * 2 * 512 * 256 * 256, bytes_accessed=groups * 2 * 10**6, transcendentals=0
         ),
@@ -262,49 +340,35 @@
 
 def axis_sum(value, axis):
     size = lax.axis_size(axis)
-    stride = 1
-    while size > stride:
-        left = size // stride
-        if left % 2:
-            return lax.psum(value, axis)
-        radix = 4 if left % 4 == 0 else 2
-        got = []
-        for shift in range(1, radix):
-            pairs = []
-            for i in range(size):
-                place = (i // stride) % radix
-                pairs.append((i, i + ((place + shift) % radix - place) * stride))
-            got.append(lax.ppermute(value, axis, pairs))
-        if radix == 4:
-            value = (value + got[1]) + (got[0] + got[2])
-        else:
-            value = value + got[0]
-        stride *= radix
-    return value
+    rows, columns = value.shape
+    if rows % size:
+        return lax.psum(value, axis)
+    parts = lax.all_to_all(value.reshape(size, rows // size, columns), axis, 0, 0)
+    mine = jnp.sum(parts, axis=0, keepdims=True)
+    return lax.all_to_all(jnp.broadcast_to(mine, parts.shape), axis, 0, 0).reshape(rows, columns)
 
 
 def shards(images, valid_mask):
     count, columns = images.shape[2:]
     looks = columns // LOOK
     groups = -(-looks // PER)
-    cuts = [0, -(-groups // 2), groups]
+    cuts = (0, -(-groups // 2), groups)
     size = lax.axis_size("pix")
     forward = [(i, i + 1) for i in range(size - 1)]
     backward = [(i + 1, i) for i in range(size - 1)]
-    pieces = []
-    total = None
-    for start, stop in zip(cuts[:-1], cuts[1:]):
-        top, mid, low, total = skewed(images, valid_mask, start, stop - start, total)
-        before = lax.ppermute(low, "pix", forward)
-        after = lax.ppermute(top, "pix", backward)
-        pieces.append((start, (top, mid, low), before, after))
+    lows, tops = edges(images, valid_mask, cuts)
+    befores, afters = [], []
+    for low, top in zip(lows, tops):
+        befores.append(lax.ppermute(low, "pix", forward))
+        afters.append(lax.ppermute(top, "pix", backward))
+    mid, total = middle(images, valid_mask, lows, tops, cuts)
     total = axis_sum(total, "pix")
     slab_coherence = pl.pallas_call(
         slab_kernel, out_shape=jax.ShapeDtypeStruct((2, count, count), jnp.float32), name="slab"
     )(total)
     out = None
-    for start, parts, before, after in pieces:
-        out = looked(before, parts, after, start, looks, out)
+    for c, start in enumerate(cuts[:-1]):
+        out = looked(befores[c], (tops[c], mid, lows[c]), afters[c], start, looks, out)
     return (out, slab_coherence)
 
 

time: 61.1 us -> 69.4 us (1.14)
  the two profiles are of different devices: /device:TPU:1 before, /device:TPU:0 now
where the time goes in v2:
time: 69.4 us; the launch traced here: 68.9 us
  Pallas kernels  30.5 us (44%)
  starting transfers between devices  14.1 us (20%)
  blocking collectives  14.1 us (20%)
  waiting for transfers between devices  5.61 us (8%)
  local copies, waits for them, and re-layouts  3.89 us (6%)
  between operations  0.7 us (1%)
    pallas_call x2, Pallas kernels, looked(): pl.pallas_call(functools.partial(looks_kernel, previous is not None), gri...  18.7 us
    all_to_all x1, blocking collectives, axis_sum(): lax.all_to_all(value.reshape(size, rows // size, columns), axis, 0, 0)  14.1 us
    ppermute x2, starting transfers between devices, shards(): befores.append(lax.ppermute(low, 'pix', forward))  7.52 us
    all_to_all x1, waiting for transfers between devices, axis_sum(): lax.all_to_all(jnp.broadcast_to(mine, parts.shape), axis, 0, 0)  5.6 us
    pallas_call x1, Pallas kernels, middle(): pl.pallas_call(functools.partial(middle_kernel, cuts), grid=(rows,), in_s...  5.28 us
    pallas_call x1, Pallas kernels, edges(): pl.pallas_call(functools.partial(edge_kernel, cuts), grid=(BEFORE + AFTER...  4.91 us
    all_to_all x1, starting transfers between devices, axis_sum(): lax.all_to_all(jnp.broadcast_to(mine, parts.shape), axis, 0, 0)  3.99 us
    unnamed x10, local copies, waits for them, and re-layouts  3.25 us
  transfers between devices with their start and end apart: 5, of which 1 were waited for; matrix products, arithmetic and copies ran while one was open for 1% of the time, Pallas kernels for 25%

profile of v2, /device:TPU:0, one launch (start us, length us, event | category | flops | bytes accessed | tf_op | source)
XLA Modules:
  0.0 68.9 jit_solution(18025591251391979667)
XLA Ops:
  0.6 4.9 %edges.1 = (bf16[4,3,2,120,128]{4,3,2,1,0:T(8,128)(2,1)}, bf16[3,3,2,120,128]{4,3,2,1,0:T(8,128)(2,1)}, bf16[4,2,2,120,128]{4,3,2,1,0:T(8,128)(2,1)}, bf16[3,2,2,120,128]{4,3,2,1,0:T(8,128)(2,1)}) custom-call(bf16[8,2,120,840]{3,2,1,0:T(8,128)(2,1)} %image_ref.3, s32[8,840]{1,0:T(8,128)} %mask_ref.3), custom_call_target="tpu_custom_call" | custom-call | flops 1000000 | bytes 4000000 | tf_op jit(solution)/shard_map/edges/pallas_call | solution.py:98
  5.5 2.4 %collective-permute-start.2 = (bf16[4,3,2,120,128]{4,3,2,1,0:T(8,128)(2,1)}, bf16[4,3,2,120,128]{4,3,2,1,0:T(8,128)(2,1)S(1)}, u32[]{:S(2)}, u32[]{:S(2)}) collective-permute-start(bf16[4,3,2,120,128]{4,3,2,1,0:T(8,128)(2,1)} %get-tuple-element.10.refs_0_.refs_3_), channel_id=1, source_target_pairs={{0,1},{1,2},{2,3},{3,4},{4,5},{5,6},{6,7},{7,8},{8,9},{9,10},{10,1... | collective-permute-start | bytes 2211848 | tf_op jit(solution)/shard_map/ppermute | solution.py:362
  7.9 1.3 %collective-permute-start.3 = (bf16[4,2,2,120,128]{4,3,2,1,0:T(8,128)(2,1)}, bf16[4,2,2,120,128]{4,3,2,1,0:T(8,128)(2,1)S(1)}, u32[]{:S(2)}, u32[]{:S(2)}) collective-permute-start(bf16[4,2,2,120,128]{4,3,2,1,0:T(8,128)(2,1)} %get-tuple-element.11.refs_2_.refs_1_), channel_id=1, source_target_pairs={{1,0},{2,1},{3,2},{4,3},{5,4},{6,5},{7,6},{8,7},{9,8},{10,9},{11,1... | collective-permute-start | bytes 1474568 | tf_op jit(solution)/shard_map/ppermute | solution.py:363
  9.2 5.1 %collective-permute-start = (bf16[3,3,2,120,128]{4,3,2,1,0:T(8,128)(2,1)}, bf16[3,3,2,120,128]{4,3,2,1,0:T(8,128)(2,1)S(1)}, u32[]{:S(2)}, u32[]{:S(2)}) collective-permute-start(bf16[3,3,2,120,128]{4,3,2,1,0:T(8,128)(2,1)} %get-tuple-element.8.refs_1_.refs_3_), channel_id=1, source_target_pairs={{0,1},{1,2},{2,3},{3,4},{4,5},{5,6},{6,7},{7,8},{8,9},{9,10},{10,1... | collective-permute-start | bytes 1658888 | tf_op jit(solution)/shard_map/ppermute | solution.py:362
  14.4 5.3 %middle.1 = (bf16[7,3,2,120,128]{4,3,2,1,0:T(8,128)(2,1)}, f32[128,128]{1,0:T(8,128)}) custom-call(bf16[8,2,120,840]{3,2,1,0:T(8,128)(2,1)} %image_ref.3, s32[8,840]{1,0:T(8,128)} %mask_ref.3, bf16[4,3,2,120,128]{4,3,2,1,0:T(8,128)(2,1)} %get-tuple-element.10.refs_0_.refs_3_, bf16[3,3,2,120,128]{4,3,2,1,0:T(8,128)(2,1)} %get-tuple-element.8.refs_1_.refs_3_, ...), custom_call_target="tpu_custom_call" | custom-call | flops 1000000000 | bytes 5000000 | tf_op jit(solution)/shard_map/middle/pallas_call | solution.py:173
  19.6 14.1 %all_to_all.10 = f32[16,8,128]{2,1,0:T(8,128)S(1)} all-to-all(f32[16,8,128]{2,1,0:T(8,128)} %bitcast.3), channel_id=1, replica_groups=mesh['group'=2,'pix'=16] {'pix'}, dimensions={0} | all-to-all | bytes 131072 | tf_op jit(solution)/shard_map/all_to_all | solution.py:346
  33.7 0.6 broadcast_in_dim.2
  34.4 4.0 %all-to-all-start.1 = ((f32[16,8,128]{2,1,0:T(8,128)}), f32[16,8,128]{2,1,0:T(8,128)S(1)}, u32[]{:S(2)}, u32[]{:S(2)}) async-start(f32[16,8,128]{2,1,0:T(8,128)} %broadcast_in_dim.2), calls=%async_computation.1 | async-start | bytes 131072 | tf_op jit(solution)/shard_map/all_to_all | solution.py:348
  38.4 1.3 %collective-permute-start.1 = (bf16[3,2,2,120,128]{4,3,2,1,0:T(8,128)(2,1)}, bf16[3,2,2,120,128]{4,3,2,1,0:T(8,128)(2,1)S(1)}, u32[]{:S(2)}, u32[]{:S(2)}) collective-permute-start(bf16[3,2,2,120,128]{4,3,2,1,0:T(8,128)(2,1)} %get-tuple-element.9.refs_3_.refs_1_), channel_id=1, source_target_pairs={{1,0},{2,1},{3,2},{4,3},{5,4},{6,5},{7,6},{8,7},{9,8},{10,9},{11,1... | collective-permute-start | bytes 1105928 | tf_op jit(solution)/shard_map/ppermute | solution.py:363
  39.7 5.6 %all-to-all-done.1 = f32[16,8,128]{2,1,0:T(8,128)S(1)} async-done(((f32[16,8,128]{2,1,0:T(8,128)}), f32[16,8,128]{2,1,0:T(8,128)S(1)}, u32[]{:S(2)}, u32[]{:S(2)}) %all-to-all-start.1) | async-done | bytes 65568 | tf_op jit(solution)/shard_map/all_to_all | solution.py:348
  45.3 0.0 copy-start.4
  45.3 0.6 copy-done.4
  45.9 1.6 %slab.1 = f32[2,120,120]{2,1,0:T(8,128)} custom-call(f32[128,128]{1,0:T(8,128)} %bitcast.2), custom_call_target="tpu_custom_call" | custom-call | tf_op jit(solution)/shard_map/slab/pallas_call | solution.py:366
  47.5 0.0 collective-permute-done.3.refs_4_
  47.5 0.0 collective-permute-done.2.refs_0_
  47.5 0.0 copy-start
  47.5 0.8 %copy-done.2 = bf16[4,2,2,120,128]{4,3,2,1,0:T(8,128)(2,1)} copy-done((bf16[4,2,2,120,128]{4,3,2,1,0:T(8,128)(2,1)}, bf16[4,2,2,120,128]{4,3,2,1,0:T(8,128)(2,1)S(1)}, u32[]{:S(2)}) %copy-start.2) | copy-done | bytes 491544
  48.3 0.3 copy-done
  48.6 10.4 %looks.2.refs_5_ = bf16[4,40,2,120,120]{4,3,2,1,0:T(8,128)(2,1)} custom-call(bf16[4,3,2,120,128]{4,3,2,1,0:T(8,128)(2,1)} %copy-done, bf16[4,2,2,120,128]{4,3,2,1,0:T(8,128)(2,1)} %get-tuple-element.11.refs_2_.refs_1_, bf16[7,3,2,120,128]{4,3,2,1,0:T(8,128)(2,1)} %get-tuple-element.12.refs_2_, ...), custom_call_target="tpu_custom_call" | custom-call | flops 3221225472 | bytes 8000000 | tf_op jit(solution)/shard_map/looks/pallas_call | solution.py:309
  59.0 0.0 collective-permute-done.1.refs_4_
  59.0 0.0 collective-permute-done.refs_0_
  59.0 0.8 %copy-done.3 = bf16[3,2,2,120,128]{4,3,2,1,0:T(8,128)(2,1)} copy-done((bf16[3,2,2,120,128]{4,3,2,1,0:T(8,128)(2,1)}, bf16[3,2,2,120,128]{4,3,2,1,0:T(8,128)(2,1)S(1)}, u32[]{:S(2)}) %copy-start.3) | copy-done | bytes 368664
  59.8 0.8 %copy-done.1 = bf16[3,3,2,120,128]{4,3,2,1,0:T(8,128)(2,1)} copy-done((bf16[3,3,2,120,128]{4,3,2,1,0:T(8,128)(2,1)}, bf16[3,3,2,120,128]{4,3,2,1,0:T(8,128)(2,1)S(1)}, u32[]{:S(2)}) %copy-start.1) | copy-done | bytes 552984
  60.6 8.3 %looks.3 = bf16[4,40,2,120,120]{4,3,2,1,0:T(8,128)(2,1)} custom-call(bf16[3,3,2,120,128]{4,3,2,1,0:T(8,128)(2,1)} %copy-done.1, bf16[3,2,2,120,128]{4,3,2,1,0:T(8,128)(2,1)} %get-tuple-element.9.refs_3_.refs_1_, bf16[7,3,2,120,128]{4,3,2,1,0:T(8,128)(2,1)} %get-tuple-element.12.refs_2_, ...), custom_call_target="tpu_custom_call", output_to_operand_aliasing={{}: (5, {})} | custom-call | flops 2415919104 | bytes 6000000 | tf_op jit(solution)/shard_map/looks/pallas_call | solution.py:309
  (4 shorter events, 0.0 us)
Async XLA Ops:
  5.5 42.0 %collective-permute-start.2 = (bf16[4,3,2,120,128]{4,3,2,1,0:T(8,128)(2,1)}, bf16[4,3,2,120,128]{4,3,2,1,0:T(8,128)(2,1)S(1)}, u32[]{:S(2)}, u32[]{:S(2)}) collective-permute-start(bf16[4,3,2,120,128]{4,3,2,1,0:T(8,128)(2,1)} %get-tuple-element.10.refs_0_.refs_3_), channel_id=1, source_target_pairs={{0,1},{1,2},{2,3},{3,4},{4,5},{5,6},{6,7},{7,8},{8,9},{9,10},{10,1... | collective-permute-start | bytes 2211848 | tf_op jit(solution)/shard_map/ppermute | solution.py:362
  7.9 39.6 %collective-permute-start.3 = (bf16[4,2,2,120,128]{4,3,2,1,0:T(8,128)(2,1)}, bf16[4,2,2,120,128]{4,3,2,1,0:T(8,128)(2,1)S(1)}, u32[]{:S(2)}, u32[]{:S(2)}) collective-permute-start(bf16[4,2,2,120,128]{4,3,2,1,0:T(8,128)(2,1)} %get-tuple-element.11.refs_2_.refs_1_), channel_id=1, source_target_pairs={{1,0},{2,1},{3,2},{4,3},{5,4},{6,5},{7,6},{8,7},{9,8},{10,9},{11,1... | collective-permute-start | bytes 1474568 | tf_op jit(solution)/shard_map/ppermute | solution.py:363
  9.2 49.8 %collective-permute-start = (bf16[3,3,2,120,128]{4,3,2,1,0:T(8,128)(2,1)}, bf16[3,3,2,120,128]{4,3,2,1,0:T(8,128)(2,1)S(1)}, u32[]{:S(2)}, u32[]{:S(2)}) collective-permute-start(bf16[3,3,2,120,128]{4,3,2,1,0:T(8,128)(2,1)} %get-tuple-element.8.refs_1_.refs_3_), channel_id=1, source_target_pairs={{0,1},{1,2},{2,3},{3,4},{4,5},{5,6},{6,7},{7,8},{8,9},{9,10},{10,1... | collective-permute-start | bytes 1658888 | tf_op jit(solution)/shard_map/ppermute | solution.py:362
  34.4 10.9 %all-to-all-start.1 = ((f32[16,8,128]{2,1,0:T(8,128)}), f32[16,8,128]{2,1,0:T(8,128)S(1)}, u32[]{:S(2)}, u32[]{:S(2)}) async-start(f32[16,8,128]{2,1,0:T(8,128)} %broadcast_in_dim.2), calls=%async_computation.1 | async-start | bytes 131072 | tf_op jit(solution)/shard_map/all_to_all | solution.py:348
  38.4 20.6 %collective-permute-start.1 = (bf16[3,2,2,120,128]{4,3,2,1,0:T(8,128)(2,1)}, bf16[3,2,2,120,128]{4,3,2,1,0:T(8,128)(2,1)S(1)}, u32[]{:S(2)}, u32[]{:S(2)}) collective-permute-start(bf16[3,2,2,120,128]{4,3,2,1,0:T(8,128)(2,1)} %get-tuple-element.9.refs_3_.refs_1_), channel_id=1, source_target_pairs={{1,0},{2,1},{3,2},{4,3},{5,4},{6,5},{7,6},{8,7},{9,8},{10,9},{11,1... | collective-permute-start | bytes 1105928 | tf_op jit(solution)/shard_map/ppermute | solution.py:363
  45.3 0.6 copy-start.4
  47.5 0.8 %copy-start.2 = (bf16[4,2,2,120,128]{4,3,2,1,0:T(8,128)(2,1)}, bf16[4,2,2,120,128]{4,3,2,1,0:T(8,128)(2,1)S(1)}, u32[]{:S(2)}) copy-start(bf16[4,2,2,120,128]{4,3,2,1,0:T(8,128)(2,1)S(1)} %collective-permute-done.3.refs_4_) | copy-start | bytes 1474564
  47.5 1.1 %copy-start = (bf16[4,3,2,120,128]{4,3,2,1,0:T(8,128)(2,1)}, bf16[4,3,2,120,128]{4,3,2,1,0:T(8,128)(2,1)S(1)}, u32[]{:S(2)}) copy-start(bf16[4,3,2,120,128]{4,3,2,1,0:T(8,128)(2,1)S(1)} %collective-permute-done.2.refs_0_) | copy-start | bytes 2211844
  59.0 0.8 %copy-start.3 = (bf16[3,2,2,120,128]{4,3,2,1,0:T(8,128)(2,1)}, bf16[3,2,2,120,128]{4,3,2,1,0:T(8,128)(2,1)S(1)}, u32[]{:S(2)}) copy-start(bf16[3,2,2,120,128]{4,3,2,1,0:T(8,128)(2,1)S(1)} %collective-permute-done.1.refs_4_) | copy-start | bytes 1105924
  59.8 0.8 %copy-start.1 = (bf16[3,3,2,120,128]{4,3,2,1,0:T(8,128)(2,1)}, bf16[3,3,2,120,128]{4,3,2,1,0:T(8,128)(2,1)S(1)}, u32[]{:S(2)}) copy-start(bf16[3,3,2,120,128]{4,3,2,1,0:T(8,128)(2,1)S(1)} %collective-permute-done.refs_0_) | copy-start | bytes 1658884

commit v3 on v0

v3 whole, which is shorter than its diff:
```python
import functools
import jax
import jax.numpy as jnp
from jax import lax
from jax.experimental import pallas as pl
from jax.experimental.pallas import tpu as pltpu
from jax.sharding import PartitionSpec as P

floor_power = 30.0

LOOK = 21
LANES = 128
PER = LANES // LOOK
SPAN = PER * LOOK
ROWS = 8
SKEW = (5, 0, 1, 2, 3, 4, 1, 2)
BEFORE, AFTER = 3, 2
NT = (((1,), (1,)), ((), ()))


def turned(image, mask, skew, columns, put):
    count = image[0].shape[0]
    zero = jnp.zeros((count, LANES), jnp.bfloat16)
    lane = lax.broadcasted_iota(jnp.int32, (1, LANES), 1)

    def tile(value, g):
        start, stop = g * LANES, min((g + 1) * LANES, columns)
        part = value[:, start:stop]
        if stop - start < LANES:
            rest = jnp.zeros((part.shape[0], LANES - (stop - start)), part.dtype)
            part = jnp.concatenate([part, rest], axis=1)
        return part

    def widened(which):
        return jnp.broadcast_to(which.astype(jnp.float32), (count, LANES)).astype(jnp.bfloat16) != 0

    tiles = -(-columns // LANES)
    for g in range(-(-columns // SPAN)):
        slide = (LANES - SPAN) * g
        place = (lane + slide) % LANES
        used = (place < SPAN) & (SPAN * g + place < columns)
        prior = lane >= LANES - slide
        sides = [t for t in (g - 1, g) if 0 <= t < tiles]

        def joined(value):
            parts = [tile(value, t) for t in sides]
            if len(parts) == 1:
                return parts[0]
            which = prior if value.shape[0] == 1 else widened(prior)
            return jnp.where(which, parts[0], parts[1])

        keep = widened(used & (joined(mask) != 0))
        for k in range(2):
            row = jnp.where(keep, joined(image[k]), zero)
            put(g, k, pltpu.roll(row, slide + LOOK * skew, 1))


def edge_kernel(image_ref, mask_ref, top_ref, low_ref, rows_ref, top_out, low_out, in_sems, out_sems):
    order = [(r, top_out, top_ref, r) for r in range(AFTER)]
    order += [(ROWS - BEFORE + r, low_out, low_ref, r) for r in range(BEFORE)]
    fetches = []
    for at, (row, _, _, _) in enumerate(order):
        fetch = pltpu.make_async_copy(image_ref.at[row], rows_ref.at[at], in_sems.at[at])
        fetch.start()
        fetches.append(fetch)
    stores = []
    for at, (row, out, target, i) in enumerate(order):
        fetches[at].wait()

        def put(g, k, value):
            out[i, g, k] = value

        rows = [rows_ref.at[at, 0], rows_ref.at[at, 1]]
        turned(rows, mask_ref[row : row + 1, :], SKEW[row], mask_ref.shape[1], put)
        store = pltpu.make_async_copy(out.at[i], target.at[i], out_sems.at[at])
        store.start()
        stores.append(store)
    for store in stores:
        store.wait()


def edges(images, valid_mask, groups):
    count, columns = images.shape[2:]

    def shape(rows):
        return (rows, groups, 2, count, LANES)

    return pl.pallas_call(
        edge_kernel,
        in_specs=[pl.BlockSpec(memory_space=pl.ANY), pl.BlockSpec(memory_space=pltpu.VMEM)],
        out_specs=[pl.BlockSpec(memory_space=pl.ANY)] * 2,
        out_shape=[jax.ShapeDtypeStruct(shape(rows), jnp.bfloat16) for rows in (AFTER, BEFORE)],
        scratch_shapes=[
            pltpu.VMEM((BEFORE + AFTER, 2, count, columns), jnp.bfloat16),
            pltpu.VMEM(shape(AFTER), jnp.bfloat16),
            pltpu.VMEM(shape(BEFORE), jnp.bfloat16),
            pltpu.SemaphoreType.DMA((BEFORE + AFTER,)),
            pltpu.SemaphoreType.DMA((BEFORE + AFTER,)),
        ],
        cost_estimate=pl.CostEstimate(flops=10**6, bytes_accessed=4 * 10**6, transcendentals=0),
        name="edges",
    )(images, valid_mask)


def middle_kernel(image_ref, mask_ref, top_ref, low_ref, mid_ref, gram_ref, rows_ref, z_ref, in_sems):
    count = image_ref.shape[2]
    groups = low_ref.shape[1]
    middle_rows = ROWS - BEFORE - AFTER
    fetches = []
    for at in range(middle_rows):
        fetch = pltpu.make_async_copy(image_ref.at[AFTER + at], rows_ref.at[at], in_sems.at[at])
        fetch.start()
        fetches.append(fetch)
    z_ref[...] = jnp.zeros_like(z_ref)

    def place(at, g, k, value):
        z_ref[at, pl.ds(k * LANES, count), pl.ds(g * LANES, LANES)] = value

    for i in range(AFTER):
        for g in range(groups):
            for k in range(2):
                place(i, g, k, top_ref[i, g, k])
    for i in range(BEFORE):
        for g in range(groups):
            for k in range(2):
                place(AFTER + i, g, k, low_ref[i, g, k])
    for at in range(middle_rows):
        row = AFTER + at
        fetches[at].wait()

        def put(g, k, value):
            mid_ref[at, g, k] = value
            place(AFTER + BEFORE + at, g, k, value)

        turned([rows_ref.at[at, 0], rows_ref.at[at, 1]], mask_ref[row : row + 1, :], SKEW[row], mask_ref.shape[1], put)
    total = None
    for r in range(ROWS):
        z = z_ref[r]
        part = lax.dot_general(z, z, NT, preferred_element_type=jnp.float32)
        total = part if total is None else total + part
    real = total[:LANES, :LANES] + total[LANES:, LANES:]
    imag = total[LANES:, :LANES] - total[:LANES, LANES:]
    i = lax.broadcasted_iota(jnp.int32, real.shape, 0)
    j = lax.broadcasted_iota(jnp.int32, real.shape, 1)
    gram_ref[...] = jnp.where(i <= j, real, imag)


def middle(images, valid_mask, top, low):
    count, columns = images.shape[2:]
    groups = low.shape[1]
    rows = ROWS - AFTER - BEFORE
    vmem = pl.BlockSpec(memory_space=pltpu.VMEM)
    return pl.pallas_call(
        middle_kernel,
        in_specs=[pl.BlockSpec(memory_space=pl.ANY), vmem, vmem, vmem],
        out_specs=[vmem, vmem],
        out_shape=[
            jax.ShapeDtypeStruct((rows, groups, 2, count, LANES), jnp.bfloat16),
            jax.ShapeDtypeStruct((LANES, LANES), jnp.float32),
        ],
        scratch_shapes=[
            pltpu.VMEM((rows, 2, count, columns), jnp.bfloat16),
            pltpu.VMEM((ROWS, 2 * LANES, groups * LANES), jnp.bfloat16),
            pltpu.SemaphoreType.DMA((rows,)),
        ],
        cost_estimate=pl.CostEstimate(flops=10**9, bytes_accessed=5 * 10**6, transcendentals=0),
        name="middle",
    )(images, valid_mask, top, low)


def added(terms):
    if len(terms) == 4:
        return (terms[0] + terms[2]) + (terms[1] + terms[3])
    return functools.reduce(jnp.add, terms)


def slab_values(terms):
    packed = added(terms)
    flipped = packed.T
    i = lax.broadcasted_iota(jnp.int32, packed.shape, 0)
    j = lax.broadcasted_iota(jnp.int32, packed.shape, 1)
    real = jnp.where(i <= j, packed, flipped)
    imag = jnp.where(i > j, packed, jnp.where(i < j, -flipped, 0.0))
    powers = jnp.where(i == j, packed, 0.0)
    scaled = jnp.sqrt(jnp.sum(powers, axis=1, keepdims=True) * jnp.sum(powers, axis=0, keepdims=True))
    return real / scaled, imag / scaled


INNER = (1, 2, 3, 4, 5)
HALVES = (
    ((-3, -2, -1, 0), (((1, 2, 3), None), (None, (-1, 0)))),
    ((6, 7, 8, 9), ((None, (6, 7)), ((3, 4, 5), None))),
)


def looks_kernel(half, aliased, terms, *refs):
    other_ref, top_ref, mid_ref, low_ref = refs[:4]
    refs = refs[4 + aliased :]
    term_refs, refs = refs[:terms], refs[terms:]
    if terms:
        out_ref, slab_ref, w_ref, m_ref = refs
    else:
        out_ref, w_ref, m_ref = refs
    count = top_ref.shape[3]

    @pl.when(pl.program_id(0) == 0)
    def _():
        w_ref[...] = jnp.zeros_like(w_ref)
        m_ref[...] = jnp.zeros_like(m_ref)
        if terms:
            real, imag = slab_values([t[...] for t in term_refs])
            slab_ref[0] = real[:count, :count]
            slab_ref[1] = imag[:count, :count]

    rows = {}
    for r in range(ROWS):
        if r < AFTER:
            rows[r] = top_ref.at[r, 0]
        elif r >= ROWS - BEFORE:
            rows[r] = low_ref.at[r - (ROWS - BEFORE), 0]
        else:
            rows[r] = mid_ref.at[r - AFTER, 0]
    for r in range(other_ref.shape[0]):
        rows[ROWS + r if half else r - BEFORE] = other_ref.at[r, 0]

    lane = lax.broadcasted_iota(jnp.int32, (1, LANES), 1)

    def lanes_of(turn):
        place = lane + (-LOOK * turn) % LANES
        place = jnp.where(place >= LANES, place - LANES, place)
        return place < LOOK

    def widened(which):
        return jnp.broadcast_to(which.astype(jnp.float32), (count, LANES)).astype(jnp.bfloat16) != 0

    single = [lanes_of(t) for t in range(2 * PER - 1)]
    wide = [widened(s) for s in single]
    zero = jnp.zeros((count, LANES), jnp.bfloat16)

    def turn(l, r):
        return l + SKEW[r % ROWS]

    def gathered(l, k, which):
        out = zero
        for r in which:
            out = jnp.where(wide[turn(l, r)], rows[r][k], out)
        return out

    def kept(l, value, which):
        if which is None:
            return value
        select = single[turn(l, which[0])]
        for r in which[1:]:
            select = select | single[turn(l, r)]
        return jnp.where(widened(select), value, zero)

    i = lax.broadcasted_iota(jnp.int32, (count, LANES), 0)
    j = lax.broadcasted_iota(jnp.int32, (count, LANES), 1)
    eye = i == j

    def normalised(real, imag, w, l):
        power = jnp.sum(jnp.where(eye, real, 0.0), axis=0, keepdims=True)
        across = lax.rsqrt(jnp.maximum(power, floor_power))
        down = jnp.sum(jnp.where(eye, across, 0.0), axis=1, keepdims=True)
        out_ref[w, l, 0] = (real * down * across).astype(jnp.bfloat16)[:, :count]
        out_ref[w, l, 1] = (imag * down * across).astype(jnp.bfloat16)[:, :count]

    outer_rows, windows = HALVES[half]
    for l in range(PER):
        slot = l % 2
        for k in range(2):
            inner = gathered(l, k, INNER)
            outer = gathered(l, k, outer_rows)
            w_ref[slot, k, pl.ds(0, count), pl.ds(0, LANES)] = inner
            w_ref[slot, k, pl.ds(0, count), pl.ds(LANES, LANES)] = outer
            for w, (inner_rows, rest_rows) in enumerate(windows):
                m_ref[slot, w, k, pl.ds(0, count), pl.ds(0, LANES)] = kept(l, inner, inner_rows)
                m_ref[slot, w, k, pl.ds(0, count), pl.ds(LANES, LANES)] = kept(l, outer, rest_rows)
        gram = lax.dot_general(
            m_ref[slot].reshape(4 * LANES, 2 * LANES),
            w_ref[slot].reshape(2 * LANES, 2 * LANES),
            NT,
            preferred_element_type=jnp.float32,
        )
        for w in range(2):
            base = 2 * w * LANES
            re = gram[base : base + count]
            im = gram[base + LANES : base + LANES + count]
            normalised(re[:, :LANES] + im[:, LANES:], im[:, :LANES] - re[:, LANES:], w, l)


def looked(half, other, top, mid, low, looks, previous, terms):
    groups, _, count, _ = top.shape[1:]

    def spec(array):
        return pl.BlockSpec((array.shape[0], 1) + array.shape[2:], lambda s: (0, s, 0, 0, 0))

    operands = [other, top, mid, low]
    in_specs = [spec(a) for a in operands]
    aliases = {}
    if previous is not None:
        aliases = {len(operands): 0}
        operands.append(previous)
        in_specs.append(pl.BlockSpec(memory_space=pl.ANY))
    for term in terms:
        operands.append(term)
        in_specs.append(pl.BlockSpec(term.shape, lambda s: (0, 0)))
    out_specs = [pl.BlockSpec((2, PER, 2, count, count), lambda s: (half, s, 0, 0, 0))]
    out_shape = [jax.ShapeDtypeStruct((ROWS // 2, looks, 2, count, count), jnp.bfloat16)]
    if terms:
        out_specs.append(pl.BlockSpec((2, count, count), lambda s: (0, 0, 0)))
        out_shape.append(jax.ShapeDtypeStruct((2, count, count), jnp.float32))
    return pl.pallas_call(
        functools.partial(looks_kernel, half, previous is not None, len(terms)),
        grid=(groups,),
        in_specs=in_specs,
        out_specs=out_specs,
        out_shape=out_shape,
        input_output_aliases=aliases,
        scratch_shapes=[
            pltpu.VMEM((2, 2, LANES, 2 * LANES), jnp.bfloat16),
            pltpu.VMEM((2, 2, 2, LANES, 2 * LANES), jnp.bfloat16),
        ],
        compiler_params=pltpu.CompilerParams(vmem_limit_bytes=32 * 2**20),
        cost_estimate=pl.CostEstimate(
            flops=groups * PER * 2 * 512 * 256 * 256, bytes_accessed=groups * 10**6, transcendentals=0
        ),
        name="looks",
    )(*operands)


def axis_terms(value, axis):
    size = lax.axis_size(axis)
    stride = 1
    terms = [value]
    while size > stride:
        left = size // stride
        if left % 2:
            return [lax.psum(value, axis)]
        radix = 4 if left % 4 == 0 else 2
        part = added(terms)
        terms = [part]
        for shift in range(1, radix):
            pairs = []
            for i in range(size):
                place = (i // stride) % radix
                pairs.append((i, i + ((place + shift) % radix - place) * stride))
            terms.append(lax.ppermute(part, axis, pairs))
        stride *= radix
    return terms


def shards(images, valid_mask):
    looks = images.shape[3] // LOOK
    groups = -(-looks // PER)
    size = lax.axis_size("pix")
    top, low = edges(images, valid_mask, groups)
    after = lax.ppermute(top, "pix", [(i + 1, i) for i in range(size - 1)])
    before = lax.ppermute(low, "pix", [(i, i + 1) for i in range(size - 1)])
    mid, total = middle(images, valid_mask, top, low)
    terms = axis_terms(total, "pix")
    (out,) = looked(1, after, top, mid, low, looks, None, [])
    out, slab = looked(0, before, top, mid, low, looks, out, terms)
    return (out, slab)


def solution(mesh):
    in_specs = (P(("group", "pix"), None, None, None), P(("group", "pix"), None))
    out_specs = (P(("group", "pix"), None, None, None, None), P("group", None, None))
    return jax.shard_map(shards, mesh=mesh, in_specs=in_specs, out_specs=out_specs, check_vma=False)
```

time: 279 us -> 63.6 us (0.23)
  the two profiles are of different devices: /device:TPU:1 before, /device:TPU:0 now
where the time goes in v3:
time: 63.6 us; the launch traced here: 63.2 us
  Pallas kernels  27.3 us (43%)
  starting transfers between devices  24.6 us (39%)
  waiting for transfers between devices  8.36 us (13%)
  local copies, waits for them, and re-layouts  1.31 us (2%)
  other arithmetic  0.86 us (1%)
  between operations  0.71 us (1%)
    ppermute x6, starting transfers between devices, axis_terms(): terms.append(lax.ppermute(part, axis, pairs))  20.8 us
    pallas_call x2, Pallas kernels, looked(): pl.pallas_call(functools.partial(looks_kernel, half, previous is not None...  18.6 us
    ppermute x6, waiting for transfers between devices, axis_terms(): terms.append(lax.ppermute(part, axis, pairs))  8.35 us
    pallas_call x1, Pallas kernels, middle(): pl.pallas_call(middle_kernel, in_specs=[pl.BlockSpec(memory_space=pl.ANY)...  5.07 us
    pallas_call x1, Pallas kernels, edges(): pl.pallas_call(edge_kernel, in_specs=[pl.BlockSpec(memory_space=pl.ANY),...  3.57 us
    ppermute x1, starting transfers between devices, shards(): before = lax.ppermute(low, 'pix', [(i, i + 1) for i in range(size - 1)])  2.57 us
    unnamed x6, local copies, waits for them, and re-layouts  1.31 us
    ppermute x1, starting transfers between devices, shards(): after = lax.ppermute(top, 'pix', [(i + 1, i) for i in range(size - 1)])  1.29 us
  transfers between devices with their start and end apart: 8, of which 2 were waited for; matrix products, arithmetic and copies ran while one was open for 1% of the time, Pallas kernels for 23%

profile of v3, /device:TPU:0, one launch (start us, length us, event | category | flops | bytes accessed | tf_op | source)
XLA Modules:
  0.0 63.2 jit_solution(11529436060907636330)
XLA Ops:
  0.6 3.6 %edges.1 = (bf16[2,7,2,120,128]{4,3,2,1,0:T(8,128)(2,1)}, bf16[3,7,2,120,128]{4,3,2,1,0:T(8,128)(2,1)}) custom-call(bf16[8,2,120,840]{3,2,1,0:T(8,128)(2,1)} %image_ref.3, s32[8,840]{1,0:T(8,128)} %mask_ref.3), custom_call_target="tpu_custom_call" | custom-call | flops 1000000 | bytes 4000000 | tf_op jit(solution)/shard_map/edges/pallas_call | solution.py:88
  4.2 0.0 copy-start
  4.2 2.6 %collective-permute-start = (bf16[3,7,2,120,128]{4,3,2,1,0:T(8,128)(2,1)}, bf16[3,7,2,120,128]{4,3,2,1,0:T(8,128)(2,1)S(1)}, u32[]{:S(2)}, u32[]{:S(2)}) collective-permute-start(bf16[3,7,2,120,128]{4,3,2,1,0:T(8,128)(2,1)} %get-tuple-element.6.low_ref.refs_3_), channel_id=1, source_target_pairs={{0,1},{1,2},{2,3},{3,4},{4,5},{5,6},{6,7},{7,8},{8,9},{9,10},{10,1... | collective-permute-start | bytes 3870728 | tf_op jit(solution)/shard_map/ppermute | solution.py:359
  6.8 1.3 %collective-permute-start.1 = (bf16[2,7,2,120,128]{4,3,2,1,0:T(8,128)(2,1)}, bf16[2,7,2,120,128]{4,3,2,1,0:T(8,128)(2,1)}, u32[]{:S(2)}, u32[]{:S(2)}) collective-permute-start(bf16[2,7,2,120,128]{4,3,2,1,0:T(8,128)(2,1)} %get-tuple-element.7.top_ref.refs_1_), channel_id=1, source_target_pairs={{1,0},{2,1},{3,2},{4,3},{5,4},{6,5},{7,6},{8,7},{9,8},{10,9},{11,1... | collective-permute-start | bytes 2580488 | tf_op jit(solution)/shard_map/ppermute | solution.py:358
  8.1 5.1 %middle.1 = (bf16[3,7,2,120,128]{4,3,2,1,0:T(8,128)(2,1)}, f32[128,128]{1,0:T(8,128)}) custom-call(bf16[8,2,120,840]{3,2,1,0:T(8,128)(2,1)} %image_ref.3, s32[8,840]{1,0:T(8,128)} %mask_ref.3, bf16[2,7,2,120,128]{4,3,2,1,0:T(8,128)(2,1)} %get-tuple-element.7.top_ref.refs_1_, bf16[3,7,2,120,128]{4,3,2,1,0:T(8,128)(2,1)} %get-tuple-element.6.low_ref.refs_3_), custom_call_target="tpu_custom_call" | custom-call | flops 1000000000 | bytes 5000000 | tf_op jit(solution)/shard_map/middle/pallas_call | solution.py:153
  13.2 4.4 %collective-permute-start.4 = (f32[128,128]{1,0:T(8,128)}, f32[128,128]{1,0:T(8,128)S(1)}, u32[]{:S(2)}, u32[]{:S(2)}) collective-permute-start(f32[128,128]{1,0:T(8,128)} %get-tuple-element.9), channel_id=1, source_target_pairs={{0,3},{1,0},{2,1},{3,2},{4,7},{5,4},{6,5},{7,6},{8,11},{9,8},{10,9... | collective-permute-start | bytes 196616 | tf_op jit(solution)/shard_map/ppermute | solution.py:348
  17.5 0.0 collective-permute-start.3
  17.5 1.0 %collective-permute-start.2 = (f32[128,128]{1,0:T(8,128)}, f32[128,128]{1,0:T(8,128)S(1)}, u32[]{:S(2)}, u32[]{:S(2)}) collective-permute-start(f32[128,128]{1,0:T(8,128)} %get-tuple-element.9), channel_id=1, source_target_pairs={{0,2},{1,3},{2,0},{3,1},{4,6},{5,7},{6,4},{7,5},{8,10},{9,11},{10,... | collective-permute-start | bytes 196616 | tf_op jit(solution)/shard_map/ppermute | solution.py:348
  18.5 6.9 %collective-permute-done.4 = f32[128,128]{1,0:T(8,128)S(1)} collective-permute-done((f32[128,128]{1,0:T(8,128)}, f32[128,128]{1,0:T(8,128)S(1)}, u32[]{:S(2)}, u32[]{:S(2)}) %collective-permute-start.4) | collective-permute-done | bytes 65568 | tf_op jit(solution)/shard_map/ppermute | solution.py:348
  25.5 0.0 collective-permute-done.3
  25.5 1.4 %collective-permute-done.2 = f32[128,128]{1,0:T(8,128)S(1)} collective-permute-done((f32[128,128]{1,0:T(8,128)}, f32[128,128]{1,0:T(8,128)S(1)}, u32[]{:S(2)}, u32[]{:S(2)}) %collective-permute-start.2) | collective-permute-done | bytes 65568 | tf_op jit(solution)/shard_map/ppermute | solution.py:348
  26.9 0.9 %add_add_fusion.refs_5_ = f32[128,128]{1,0:T(8,128)S(1)} fusion(f32[128,128]{1,0:T(8,128)S(1)} %collective-permute-done.3, f32[128,128]{1,0:T(8,128)S(1)} %collective-permute-done.4, f32[128,128]{1,0:T(8,128)} %get-tuple-element.9, f32[128,128]{1,0:T(8,128)S(1)} %collective-permute-done.2), kind=kLoop, calls=%fused_computation | loop fusion | flops 49152 | bytes 327680 | tf_op jit(solution)/shard_map/add | solution.py:173
  27.7 14.4 %collective-permute-start.7 = (f32[128,128]{1,0:T(8,128)S(1)}, f32[128,128]{1,0:T(8,128)S(1)}, u32[]{:S(2)}, u32[]{:S(2)}) collective-permute-start(f32[128,128]{1,0:T(8,128)S(1)} %add_add_fusion.refs_5_), channel_id=1, source_target_pairs={{0,12},{1,13},{2,14},{3,15},{4,0},{5,1},{6,2},{7,3},{8,4},{9,5},{1... | collective-permute-start | bytes 196616 | tf_op jit(solution)/shard_map/ppermute | solution.py:348
  42.2 0.0 collective-permute-start.6
  42.2 1.0 %collective-permute-start.5 = (f32[128,128]{1,0:T(8,128)S(1)}, f32[128,128]{1,0:T(8,128)S(1)}, u32[]{:S(2)}, u32[]{:S(2)}) collective-permute-start(f32[128,128]{1,0:T(8,128)S(1)} %add_add_fusion.refs_5_), channel_id=1, source_target_pairs={{0,4},{1,5},{2,6},{3,7},{4,8},{5,9},{6,10},{7,11},{8,12},{9,13},{1... | collective-permute-start | bytes 196616 | tf_op jit(solution)/shard_map/ppermute | solution.py:348
  43.2 0.0 collective-permute-done.1.refs_0_
  43.2 0.0 copy-start.2
  43.2 1.3 %copy-done.2 = bf16[3,7,2,120,128]{4,3,2,1,0:T(8,128)(2,1)S(1)} copy-done((bf16[3,7,2,120,128]{4,3,2,1,0:T(8,128)(2,1)S(1)}, bf16[3,7,2,120,128]{4,3,2,1,0:T(8,128)(2,1)}, u32[]{:S(2)}) %copy-start.2) | copy-done | bytes 1290264
  44.5 9.6 %looks.2.refs_4_ = bf16[4,40,2,120,120]{4,3,2,1,0:T(8,128)(2,1)} custom-call(bf16[2,7,2,120,128]{4,3,2,1,0:T(8,128)(2,1)} %collective-permute-done.1.refs_0_, bf16[2,7,2,120,128]{4,3,2,1,0:T(8,128)(2,1)S(1)} %copy-done.1, bf16[3,7,2,120,128]{4,3,2,1,0:T(8,128)(2,1)S(1)} %copy-done.2, bf16[3,7,2,120,128]{4,3,2,1,0:T(8,128)(2,1)S(1)} %copy-done), custom_call_target="tpu_custom_call" | custom-call | flops 2818572288 | bytes 7000000 | tf_op jit(solution)/shard_map/looks/pallas_call | solution.py:313
  54.1 0.0 collective-permute-done.7.refs_8_
  54.1 0.0 collective-permute-done.6.refs_7_
  54.1 0.0 collective-permute-done.5.refs_6_
  54.1 0.0 collective-permute-done.refs_0_
  54.1 9.1 %looks.3 = (bf16[4,40,2,120,120]{4,3,2,1,0:T(8,128)(2,1)}, f32[2,120,120]{2,1,0:T(8,128)}) custom-call(bf16[3,7,2,120,128]{4,3,2,1,0:T(8,128)(2,1)S(1)} %collective-permute-done.refs_0_, bf16[2,7,2,120,128]{4,3,2,1,0:T(8,128)(2,1)S(1)} %copy-done.1, bf16[3,7,2,120,128]{4,3,2,1,0:T(8,128)(2,1)S(1)} %copy-done.2, ...), custom_call_target="tpu_custom_call", output_to_operand_aliasing={{0}: (4, {})} | custom-call | flops 2818572288 | bytes 7000000 | tf_op jit(solution)/shard_map/looks/pallas_call | solution.py:313
  (3 shorter events, 0.0 us)
Async XLA Ops:
  4.2 39.0 %copy-start = (bf16[3,7,2,120,128]{4,3,2,1,0:T(8,128)(2,1)S(1)}, bf16[3,7,2,120,128]{4,3,2,1,0:T(8,128)(2,1)}, u32[]{:S(2)}) copy-start(bf16[3,7,2,120,128]{4,3,2,1,0:T(8,128)(2,1)} %get-tuple-element.6.low_ref.refs_3_) | copy-start | bytes 3870724
  4.2 39.0 %copy-start.1 = (bf16[2,7,2,120,128]{4,3,2,1,0:T(8,128)(2,1)S(1)}, bf16[2,7,2,120,128]{4,3,2,1,0:T(8,128)(2,1)}, u32[]{:S(2)}) copy-start(bf16[2,7,2,120,128]{4,3,2,1,0:T(8,128)(2,1)} %get-tuple-element.7.top_ref.refs_1_) | copy-start | bytes 2580484
  4.2 49.9 %collective-permute-start = (bf16[3,7,2,120,128]{4,3,2,1,0:T(8,128)(2,1)}, bf16[3,7,2,120,128]{4,3,2,1,0:T(8,128)(2,1)S(1)}, u32[]{:S(2)}, u32[]{:S(2)}) collective-permute-start(bf16[3,7,2,120,128]{4,3,2,1,0:T(8,128)(2,1)} %get-tuple-element.6.low_ref.refs_3_), channel_id=1, source_target_pairs={{0,1},{1,2},{2,3},{3,4},{4,5},{5,6},{6,7},{7,8},{8,9},{9,10},{10,1... | collective-permute-start | bytes 3870728 | tf_op jit(solution)/shard_map/ppermute | solution.py:359
  6.8 36.4 %collective-permute-start.1 = (bf16[2,7,2,120,128]{4,3,2,1,0:T(8,128)(2,1)}, bf16[2,7,2,120,128]{4,3,2,1,0:T(8,128)(2,1)}, u32[]{:S(2)}, u32[]{:S(2)}) collective-permute-start(bf16[2,7,2,120,128]{4,3,2,1,0:T(8,128)(2,1)} %get-tuple-element.7.top_ref.refs_1_), channel_id=1, source_target_pairs={{1,0},{2,1},{3,2},{4,3},{5,4},{6,5},{7,6},{8,7},{9,8},{10,9},{11,1... | collective-permute-start | bytes 2580488 | tf_op jit(solution)/shard_map/ppermute | solution.py:358
  13.2 12.3 %collective-permute-start.4 = (f32[128,128]{1,0:T(8,128)}, f32[128,128]{1,0:T(8,128)S(1)}, u32[]{:S(2)}, u32[]{:S(2)}) collective-permute-start(f32[128,128]{1,0:T(8,128)} %get-tuple-element.9), channel_id=1, source_target_pairs={{0,3},{1,0},{2,1},{3,2},{4,7},{5,4},{6,5},{7,6},{8,11},{9,8},{10,9... | collective-permute-start | bytes 196616 | tf_op jit(solution)/shard_map/ppermute | solution.py:348
  17.5 7.9 %collective-permute-start.3 = (f32[128,128]{1,0:T(8,128)}, f32[128,128]{1,0:T(8,128)S(1)}, u32[]{:S(2)}, u32[]{:S(2)}) collective-permute-start(f32[128,128]{1,0:T(8,128)} %get-tuple-element.9), channel_id=1, source_target_pairs={{0,1},{1,2},{2,3},{3,0},{4,5},{5,6},{6,7},{7,4},{8,9},{9,10},{10,1... | collective-permute-start | bytes 196616 | tf_op jit(solution)/shard_map/ppermute | solution.py:348
  17.5 9.3 %collective-permute-start.2 = (f32[128,128]{1,0:T(8,128)}, f32[128,128]{1,0:T(8,128)S(1)}, u32[]{:S(2)}, u32[]{:S(2)}) collective-permute-start(f32[128,128]{1,0:T(8,128)} %get-tuple-element.9), channel_id=1, source_target_pairs={{0,2},{1,3},{2,0},{3,1},{4,6},{5,7},{6,4},{7,5},{8,10},{9,11},{10,... | collective-permute-start | bytes 196616 | tf_op jit(solution)/shard_map/ppermute | solution.py:348
  27.7 26.4 %collective-permute-start.7 = (f32[128,128]{1,0:T(8,128)S(1)}, f32[128,128]{1,0:T(8,128)S(1)}, u32[]{:S(2)}, u32[]{:S(2)}) collective-permute-start(f32[128,128]{1,0:T(8,128)S(1)} %add_add_fusion.refs_5_), channel_id=1, source_target_pairs={{0,12},{1,13},{2,14},{3,15},{4,0},{5,1},{6,2},{7,3},{8,4},{9,5},{1... | collective-permute-start | bytes 196616 | tf_op jit(solution)/shard_map/ppermute | solution.py:348
  42.2 11.9 %collective-permute-start.6 = (f32[128,128]{1,0:T(8,128)S(1)}, f32[128,128]{1,0:T(8,128)S(1)}, u32[]{:S(2)}, u32[]{:S(2)}) collective-permute-start(f32[128,128]{1,0:T(8,128)S(1)} %add_add_fusion.refs_5_), channel_id=1, source_target_pairs={{0,8},{1,9},{2,10},{3,11},{4,12},{5,13},{6,14},{7,15},{8,0},{9,1},... | collective-permute-start | bytes 196616 | tf_op jit(solution)/shard_map/ppermute | solution.py:348
  42.2 11.9 %collective-permute-start.5 = (f32[128,128]{1,0:T(8,128)S(1)}, f32[128,128]{1,0:T(8,128)S(1)}, u32[]{:S(2)}, u32[]{:S(2)}) collective-permute-start(f32[128,128]{1,0:T(8,128)S(1)} %add_add_fusion.refs_5_), channel_id=1, source_target_pairs={{0,4},{1,5},{2,6},{3,7},{4,8},{5,9},{6,10},{7,11},{8,12},{9,13},{1... | collective-permute-start | bytes 196616 | tf_op jit(solution)/shard_map/ppermute | solution.py:348
  43.2 1.3 %copy-start.2 = (bf16[3,7,2,120,128]{4,3,2,1,0:T(8,128)(2,1)S(1)}, bf16[3,7,2,120,128]{4,3,2,1,0:T(8,128)(2,1)}, u32[]{:S(2)}) copy-start(bf16[3,7,2,120,128]{4,3,2,1,0:T(8,128)(2,1)} %get-tuple-element.8.refs_2_) | copy-start | bytes 3870724

commit v4 on v3

--- a/solution.py
+++ b/solution.py
@@ -55,82 +55,66 @@
             put(g, k, pltpu.roll(row, slide + LOOK * skew, 1))
 
 
-def edge_kernel(image_ref, mask_ref, top_ref, low_ref, rows_ref, top_out, low_out, in_sems, out_sems):
-    order = [(r, top_out, top_ref, r) for r in range(AFTER)]
-    order += [(ROWS - BEFORE + r, low_out, low_ref, r) for r in range(BEFORE)]
+def edge_kernel(image_ref, mask_ref, top_ref, rows_ref, sems):
     fetches = []
-    for at, (row, _, _, _) in enumerate(order):
-        fetch = pltpu.make_async_copy(image_ref.at[row], rows_ref.at[at], in_sems.at[at])
-        fetch.start()
-        fetches.append(fetch)
-    stores = []
-    for at, (row, out, target, i) in enumerate(order):
-        fetches[at].wait()
+    for r in range(AFTER):
+        fetches.append(pltpu.make_async_copy(image_ref.at[r], rows_ref.at[r], sems.at[r]))
+        fetches[r].start()
+    for r in range(AFTER):
+        fetches[r].wait()
 
         def put(g, k, value):
-            out[i, g, k] = value
-
-        rows = [rows_ref.at[at, 0], rows_ref.at[at, 1]]
-        turned(rows, mask_ref[row : row + 1, :], SKEW[row], mask_ref.shape[1], put)
-        store = pltpu.make_async_copy(out.at[i], target.at[i], out_sems.at[at])
-        store.start()
-        stores.append(store)
-    for store in stores:
-        store.wait()
-
-
-def edges(images, valid_mask, groups):
+            top_ref[r, g, k] = value
+
+        turned([rows_ref.at[r, 0], rows_ref.at[r, 1]], mask_ref[r : r + 1, :], SKEW[r], mask_ref.shape[1], put)
+
+
+def edge(images, valid_mask, groups):
     count, columns = images.shape[2:]
-
-    def shape(rows):
-        return (rows, groups, 2, count, LANES)
-
+    vmem = pl.BlockSpec(memory_space=pltpu.VMEM)
     return pl.pallas_call(
         edge_kernel,
-        in_specs=[pl.BlockSpec(memory_space=pl.ANY), pl.BlockSpec(memory_space=pltpu.VMEM)],
-        out_specs=[pl.BlockSpec(memory_space=pl.ANY)] * 2,
-        out_shape=[jax.ShapeDtypeStruct(shape(rows), jnp.bfloat16) for rows in (AFTER, BEFORE)],
+        in_specs=[pl.BlockSpec(memory_space=pltpu.HBM), vmem],
+        out_specs=vmem,
+        out_shape=jax.ShapeDtypeStruct((AFTER, groups, 2, count, LANES), jnp.bfloat16),
         scratch_shapes=[
-            pltpu.VMEM((BEFORE + AFTER, 2, count, columns), jnp.bfloat16),
-            pltpu.VMEM(shape(AFTER), jnp.bfloat16),
-            pltpu.VMEM(shape(BEFORE), jnp.bfloat16),
-            pltpu.SemaphoreType.DMA((BEFORE + AFTER,)),
-            pltpu.SemaphoreType.DMA((BEFORE + AFTER,)),
+            pltpu.VMEM((AFTER, 2, count, columns), jnp.bfloat16),
+            pltpu.SemaphoreType.DMA((AFTER,)),
         ],
-        cost_estimate=pl.CostEstimate(flops=10**6, bytes_accessed=4 * 10**6, transcendentals=0),
-        name="edges",
+        compiler_params=pltpu.CompilerParams(vmem_limit_bytes=61 * 2**20),
+        cost_estimate=pl.CostEstimate(flops=10**6, bytes_accessed=2 * 10**6, transcendentals=0),
+        name="edge",
     )(images, valid_mask)
 
 
-def middle_kernel(image_ref, mask_ref, top_ref, low_ref, mid_ref, gram_ref, rows_ref, z_ref, in_sems):
+def rest_kernel(cut, image_ref, mask_ref, top_ref, mid_ref, low0_ref, low1_ref, gram_ref, rows_ref, z_ref, sems):
     count = image_ref.shape[2]
-    groups = low_ref.shape[1]
-    middle_rows = ROWS - BEFORE - AFTER
+    groups = top_ref.shape[1]
+    order = list(range(ROWS - BEFORE, ROWS)) + list(range(AFTER, ROWS - BEFORE))
     fetches = []
-    for at in range(middle_rows):
-        fetch = pltpu.make_async_copy(image_ref.at[AFTER + at], rows_ref.at[at], in_sems.at[at])
-        fetch.start()
-        fetches.append(fetch)
+    for at, row in enumerate(order):
+        fetches.append(pltpu.make_async_copy(image_ref.at[row], rows_ref.at[at], sems.at[at]))
+        fetches[at].start()
     z_ref[...] = jnp.zeros_like(z_ref)
 
-    def place(at, g, k, value):
-        z_ref[at, pl.ds(k * LANES, count), pl.ds(g * LANES, LANES)] = value
-
-    for i in range(AFTER):
+    def place(row, g, k, value):
+        z_ref[row, pl.ds(k * LANES, count), pl.ds(g * LANES, LANES)] = value
+
+    for r in range(AFTER):
         for g in range(groups):
             for k in range(2):
-                place(i, g, k, top_ref[i, g, k])
-    for i in range(BEFORE):
-        for g in range(groups):
-            for k in range(2):
-                place(AFTER + i, g, k, low_ref[i, g, k])
-    for at in range(middle_rows):
-        row = AFTER + at
+                place(r, g, k, top_ref[r, g, k])
+    for at, row in enumerate(order):
         fetches[at].wait()
 
         def put(g, k, value):
-            mid_ref[at, g, k] = value
-            place(AFTER + BEFORE + at, g, k, value)
+            if row < ROWS - BEFORE:
+                mid_ref[row - AFTER, g, k] = value
+            elif g < cut:
+                low0_ref[row - (ROWS - BEFORE), g, k] = value
+            else:
+                low1_ref[row - (ROWS - BEFORE), g - cut, k] = value
+            place(row, g, k, value)
 
         turned([rows_ref.at[at, 0], rows_ref.at[at, 1]], mask_ref[row : row + 1, :], SKEW[row], mask_ref.shape[1], put)
     total = None
@@ -145,27 +129,50 @@
     gram_ref[...] = jnp.where(i <= j, real, imag)
 
 
-def middle(images, valid_mask, top, low):
+def rest(images, valid_mask, top, cut):
     count, columns = images.shape[2:]
-    groups = low.shape[1]
-    rows = ROWS - AFTER - BEFORE
+    groups = top.shape[1]
     vmem = pl.BlockSpec(memory_space=pltpu.VMEM)
+
+    def shape(rows, n):
+        return jax.ShapeDtypeStruct((rows, n, 2, count, LANES), jnp.bfloat16)
+
     return pl.pallas_call(
-        middle_kernel,
-        in_specs=[pl.BlockSpec(memory_space=pl.ANY), vmem, vmem, vmem],
-        out_specs=[vmem, vmem],
+        functools.partial(rest_kernel, cut),
+        in_specs=[pl.BlockSpec(memory_space=pltpu.HBM), vmem, vmem],
+        out_specs=[vmem] * 4,
         out_shape=[
-            jax.ShapeDtypeStruct((rows, groups, 2, count, LANES), jnp.bfloat16),
+            shape(ROWS - AFTER - BEFORE, groups),
+            shape(BEFORE, cut),
+            shape(BEFORE, groups - cut),
             jax.ShapeDtypeStruct((LANES, LANES), jnp.float32),
         ],
         scratch_shapes=[
-            pltpu.VMEM((rows, 2, count, columns), jnp.bfloat16),
+            pltpu.VMEM((ROWS - AFTER, 2, count, columns), jnp.bfloat16),
             pltpu.VMEM((ROWS, 2 * LANES, groups * LANES), jnp.bfloat16),
-            pltpu.SemaphoreType.DMA((rows,)),
+            pltpu.SemaphoreType.DMA((ROWS - AFTER,)),
         ],
+        compiler_params=pltpu.CompilerParams(vmem_limit_bytes=58 * 2**20),
         cost_estimate=pl.CostEstimate(flops=10**9, bytes_accessed=5 * 10**6, transcendentals=0),
-        name="middle",
-    )(images, valid_mask, top, low)
+        name="rest",
+    )(images, valid_mask, top)
+
+
+def again_kernel(in_ref, out_ref):
+    out_ref[...] = in_ref[...]
+
+
+def again(array):
+    vmem = pl.BlockSpec(memory_space=pltpu.VMEM)
+    return pl.pallas_call(
+        again_kernel,
+        in_specs=[vmem],
+        out_specs=vmem,
+        out_shape=jax.ShapeDtypeStruct(array.shape, array.dtype),
+        compiler_params=pltpu.CompilerParams(vmem_limit_bytes=16 * 2**20),
+        cost_estimate=pl.CostEstimate(flops=0, bytes_accessed=2 * 10**6, transcendentals=0),
+        name="again",
+    )(array)
 
 
 def added(terms):
@@ -289,11 +296,12 @@
             normalised(re[:, :LANES] + im[:, LANES:], im[:, :LANES] - re[:, LANES:], w, l)
 
 
-def looked(half, other, top, mid, low, looks, previous, terms):
-    groups, _, count, _ = top.shape[1:]
+def looked(half, other, top, mid, low, first, looks, previous, terms):
+    groups, _, count, _ = other.shape[1:]
 
     def spec(array):
-        return pl.BlockSpec((array.shape[0], 1) + array.shape[2:], lambda s: (0, s, 0, 0, 0))
+        offset = 0 if array.shape[1] == groups else first
+        return pl.BlockSpec((array.shape[0], 1) + array.shape[2:], lambda s: (0, s + offset, 0, 0, 0))
 
     operands = [other, top, mid, low]
     in_specs = [spec(a) for a in operands]
@@ -305,7 +313,7 @@
     for term in terms:
         operands.append(term)
         in_specs.append(pl.BlockSpec(term.shape, lambda s: (0, 0)))
-    out_specs = [pl.BlockSpec((2, PER, 2, count, count), lambda s: (half, s, 0, 0, 0))]
+    out_specs = [pl.BlockSpec((2, PER, 2, count, count), lambda s: (half, s + first, 0, 0, 0))]
     out_shape = [jax.ShapeDtypeStruct((ROWS // 2, looks, 2, count, count), jnp.bfloat16)]
     if terms:
         out_specs.append(pl.BlockSpec((2, count, count), lambda s: (0, 0, 0)))
@@ -354,13 +362,18 @@
     looks = images.shape[3] // LOOK
     groups = -(-looks // PER)
     size = lax.axis_size("pix")
-    top, low = edges(images, valid_mask, groups)
+    cut = -(-groups // 2)
+    forward = [(i, i + 1) for i in range(size - 1)]
+    top = edge(images, valid_mask, groups)
     after = lax.ppermute(top, "pix", [(i + 1, i) for i in range(size - 1)])
-    before = lax.ppermute(low, "pix", [(i, i + 1) for i in range(size - 1)])
-    mid, total = middle(images, valid_mask, top, low)
+    mid, low0, low1, total = rest(images, valid_mask, top, cut)
+    before0 = lax.ppermute(low0, "pix", forward)
     terms = axis_terms(total, "pix")
-    (out,) = looked(1, after, top, mid, low, looks, None, [])
-    out, slab = looked(0, before, top, mid, low, looks, out, terms)
+    before1 = lax.ppermute(again(low1), "pix", forward)
+    low = jnp.concatenate([low0, low1], axis=1)
+    (out,) = looked(1, after, top, mid, low, 0, looks, None, [])
+    (out,) = looked(0, before0, top, mid, low0, 0, looks, out, [])
+    out, slab = looked(0, before1, top, mid, low1, cut, looks, out, terms)
     return (out, slab)
 
 

time: 63.6 us -> 56.3 us (0.89)
  waiting for transfers between devices: 8.36 us -> 1.54 us
  local copies, waits for them, and re-layouts: 1.31 us -> 0.02 us
  other arithmetic: 0.86 us -> 1.55 us
    ppermute x1 -> x2, starting transfers between devices: 2.57 us -> 13.5 us  [the longest x1 10.5 us: shards(): before1 = lax.ppermute(again(low1), 'pix', forward)]
    ppermute x6, starting transfers between devices: 20.8 us -> 10.2 us  [axis_terms(): terms.append(lax.ppermute(part, axis, pairs))]
    ppermute x6, waiting for transfers between devices: 8.35 us -> 1.53 us  [axis_terms(): terms.append(lax.ppermute(part, axis, pairs))]
    concatenate x0 -> x1, other arithmetic: none -> 1.53 us  [shards(): low = jnp.concatenate([low0, low1], axis=1)]
    unnamed x6 -> x10, local copies, waits for them, and re-layouts: 1.31 us -> 0.02 us
    add x1, other arithmetic: 0.86 us -> 0.02 us  [added(): return terms[0] + terms[2] + (terms[1] + terms[3])]
    pallas_call x2 -> x3, Pallas kernels: 8.64 us -> 8.25 us  [the longest x1 5.16 us: rest(): pl.pallas_call(functools.partial(rest_kernel, cut), in_specs=[pl.BlockSpe...]
    pallas_call x2 -> x3, Pallas kernels: 18.6 us -> 18.8 us  [looked(): pl.pallas_call(functools.partial(looks_kernel, half, previous is not None...]
  transfers between devices with their start and end apart: 8 -> 9, of which waited for: 2 -> 1; matrix products, arithmetic and copies ran while one was open for 1% -> 3% of each run, Pallas kernels for 23% -> 35%
where the time goes in v4:
time: 56.3 us; the launch traced here: 56 us
  Pallas kernels  27 us (48%)
  starting transfers between devices  25.1 us (45%)
  other arithmetic  1.55 us (3%)
  waiting for transfers between devices  1.54 us (3%)
  between operations  0.75 us (1%)
    pallas_call x3, Pallas kernels, looked(): pl.pallas_call(functools.partial(looks_kernel, half, previous is not None...  18.8 us
    ppermute x1, starting transfers between devices, shards(): before1 = lax.ppermute(again(low1), 'pix', forward)  10.5 us
    ppermute x6, starting transfers between devices, axis_terms(): terms.append(lax.ppermute(part, axis, pairs))  10.2 us
    pallas_call x1, Pallas kernels, rest(): pl.pallas_call(functools.partial(rest_kernel, cut), in_specs=[pl.BlockSpe...  5.16 us
    ppermute x1, starting transfers between devices, shards(): before0 = lax.ppermute(low0, 'pix', forward)  3.08 us
    pallas_call x1, Pallas kernels, edge(): pl.pallas_call(edge_kernel, in_specs=[pl.BlockSpec(memory_space=pltpu.HBM...  3.06 us
    concatenate x1, other arithmetic, shards(): low = jnp.concatenate([low0, low1], axis=1)  1.53 us
    ppermute x6, waiting for transfers between devices, axis_terms(): terms.append(lax.ppermute(part, axis, pairs))  1.53 us
  transfers between devices with their start and end apart: 9, of which 1 were waited for; matrix products, arithmetic and copies ran while one was open for 3% of the time, Pallas kernels for 35%

profile of v4, /device:TPU:0, one launch (start us, length us, event | category | flops | bytes accessed | tf_op | source)
XLA Modules:
  0.0 56.0 jit_solution(10624455435350132142)
XLA Ops:
  0.6 3.1 %edge.1.top_ref.refs_1_ = bf16[2,7,2,120,128]{4,3,2,1,0:T(8,128)(2,1)} custom-call(bf16[8,2,120,840]{3,2,1,0:T(8,128)(2,1)} %image_ref.3, s32[8,840]{1,0:T(8,128)} %mask_ref.3), custom_call_target="tpu_custom_call" | custom-call | flops 1000000 | bytes 2000000 | tf_op jit(solution)/shard_map/edge/pallas_call | solution.py:75
  3.7 1.3 %collective-permute-start.2 = (bf16[2,7,2,120,128]{4,3,2,1,0:T(8,128)(2,1)}, bf16[2,7,2,120,128]{4,3,2,1,0:T(8,128)(2,1)S(1)}, u32[]{:S(2)}, u32[]{:S(2)}) collective-permute-start(bf16[2,7,2,120,128]{4,3,2,1,0:T(8,128)(2,1)} %edge.1.top_ref.refs_1_), channel_id=1, source_target_pairs={{1,0},{2,1},{3,2},{4,3},{5,4},{6,5},{7,6},{8,7},{9,8},{10,9},{11,1... | collective-permute-start | bytes 2580488 | tf_op jit(solution)/shard_map/ppermute | solution.py:368
  5.0 5.2 %rest.1 = (bf16[3,7,2,120,128]{4,3,2,1,0:T(8,128)(2,1)}, bf16[3,4,2,120,128]{4,3,2,1,0:T(8,128)(2,1)}, bf16[3,3,2,120,128]{4,3,2,1,0:T(8,128)(2,1)}, f32[128,128]{1,0:T(8,128)}) custom-call(bf16[8,2,120,840]{3,2,1,0:T(8,128)(2,1)} %image_ref.3, s32[8,840]{1,0:T(8,128)} %mask_ref.3, bf16[2,7,2,120,128]{4,3,2,1,0:T(8,128)(2,1)} %edge.1.top_ref.refs_1_), custom_call_target="tpu_custom_call" | custom-call | flops 1000000000 | bytes 5000000 | tf_op jit(solution)/shard_map/rest/pallas_call | solution.py:140
  10.2 3.1 %collective-permute-start.1 = (bf16[3,4,2,120,128]{4,3,2,1,0:T(8,128)(2,1)}, bf16[3,4,2,120,128]{4,3,2,1,0:T(8,128)(2,1)S(1)}, u32[]{:S(2)}, u32[]{:S(2)}) collective-permute-start(bf16[3,4,2,120,128]{4,3,2,1,0:T(8,128)(2,1)} %get-tuple-element.8.refs_3_), channel_id=1, source_target_pairs={{0,1},{1,2},{2,3},{3,4},{4,5},{5,6},{6,7},{7,8},{8,9},{9,10},{10,1... | collective-permute-start | bytes 2211848 | tf_op jit(solution)/shard_map/ppermute | solution.py:370
  13.2 3.0 %collective-permute-start.3 = (f32[128,128]{1,0:T(8,128)}, f32[128,128]{1,0:T(8,128)S(1)}, u32[]{:S(2)}, u32[]{:S(2)}) collective-permute-start(f32[128,128]{1,0:T(8,128)} %get-tuple-element.9), channel_id=1, source_target_pairs={{0,2},{1,3},{2,0},{3,1},{4,6},{5,7},{6,4},{7,5},{8,10},{9,11},{10,... | collective-permute-start | bytes 196616 | tf_op jit(solution)/shard_map/ppermute | solution.py:356
  16.2 1.7 %collective-permute-start.4 = (f32[128,128]{1,0:T(8,128)}, f32[128,128]{1,0:T(8,128)S(1)}, u32[]{:S(2)}, u32[]{:S(2)}) collective-permute-start(f32[128,128]{1,0:T(8,128)} %get-tuple-element.9), channel_id=1, source_target_pairs={{0,1},{1,2},{2,3},{3,0},{4,5},{5,6},{6,7},{7,4},{8,9},{9,10},{10,1... | collective-permute-start | bytes 196616 | tf_op jit(solution)/shard_map/ppermute | solution.py:356
  17.9 0.0 collective-permute-start.5
  18.0 1.5 %pad_maximum_fusion.refs_3_ = bf16[3,7,2,120,128]{4,3,2,1,0:T(8,128)(2,1)S(1)} fusion(bf16[3,3,2,120,128]{4,3,2,1,0:T(8,128)(2,1)} %get-tuple-element.6.in_ref.refs_3_, bf16[3,4,2,120,128]{4,3,2,1,0:T(8,128)(2,1)} %get-tuple-element.8.refs_3_), kind=kLoop, calls=%fused_computation | loop fusion | flops 645120 | bytes 2580480 | tf_op jit(solution)/shard_map/concatenate | solution.py:373
  19.6 1.5 %collective-permute-done.3 = f32[128,128]{1,0:T(8,128)S(1)} collective-permute-done((f32[128,128]{1,0:T(8,128)}, f32[128,128]{1,0:T(8,128)S(1)}, u32[]{:S(2)}, u32[]{:S(2)}) %collective-permute-start.3) | collective-permute-done | bytes 65568 | tf_op jit(solution)/shard_map/ppermute | solution.py:356
  21.1 10.5 %collective-permute-start = (bf16[3,3,2,120,128]{4,3,2,1,0:T(8,128)(2,1)S(1)}, bf16[3,3,2,120,128]{4,3,2,1,0:T(8,128)(2,1)S(1)}, u32[]{:S(2)}, u32[]{:S(2)}) collective-permute-start(bf16[3,3,2,120,128]{4,3,2,1,0:T(8,128)(2,1)S(1)} %again.1), channel_id=1, source_target_pairs={{0,1},{1,2},{2,3},{3,4},{4,5},{5,6},{6,7},{7,8},{8,9},{9,10},{10,1... | collective-permute-start | bytes 1658888 | tf_op jit(solution)/shard_map/ppermute | solution.py:372
  31.5 0.0 collective-permute-done.4
  31.5 0.0 collective-permute-done.5
  31.6 1.6 %collective-permute-start.6 = (f32[128,128]{1,0:T(8,128)S(1)}, f32[128,128]{1,0:T(8,128)S(1)}, u32[]{:S(2)}, u32[]{:S(2)}) collective-permute-start(f32[128,128]{1,0:T(8,128)S(1)} %add_add_fusion.refs_5_), channel_id=1, source_target_pairs={{0,4},{1,5},{2,6},{3,7},{4,8},{5,9},{6,10},{7,11},{8,12},{9,13},{1... | collective-permute-start | bytes 196616 | tf_op jit(solution)/shard_map/ppermute | solution.py:356
  33.2 2.5 %collective-permute-start.7 = (f32[128,128]{1,0:T(8,128)S(1)}, f32[128,128]{1,0:T(8,128)S(1)}, u32[]{:S(2)}, u32[]{:S(2)}) collective-permute-start(f32[128,128]{1,0:T(8,128)S(1)} %add_add_fusion.refs_5_), channel_id=1, source_target_pairs={{0,8},{1,9},{2,10},{3,11},{4,12},{5,13},{6,14},{7,15},{8,0},{9,1},... | collective-permute-start | bytes 196616 | tf_op jit(solution)/shard_map/ppermute | solution.py:356
  35.7 0.0 collective-permute-done.2.refs_0_
  35.7 1.4 %collective-permute-start.8 = (f32[128,128]{1,0:T(8,128)S(1)}, f32[128,128]{1,0:T(8,128)S(1)}, u32[]{:S(2)}, u32[]{:S(2)}) collective-permute-start(f32[128,128]{1,0:T(8,128)S(1)} %add_add_fusion.refs_5_), channel_id=1, source_target_pairs={{0,12},{1,13},{2,14},{3,15},{4,0},{5,1},{6,2},{7,3},{8,4},{9,5},{1... | collective-permute-start | bytes 196616 | tf_op jit(solution)/shard_map/ppermute | solution.py:356
  37.1 8.8 %looks.3.refs_4_ = bf16[4,40,2,120,120]{4,3,2,1,0:T(8,128)(2,1)} custom-call(bf16[2,7,2,120,128]{4,3,2,1,0:T(8,128)(2,1)S(1)} %collective-permute-done.2.refs_0_, bf16[2,7,2,120,128]{4,3,2,1,0:T(8,128)(2,1)S(1)} %copy-done, bf16[3,7,2,120,128]{4,3,2,1,0:T(8,128)(2,1)S(1)} %copy-done.1, bf16[3,7,2,120,128]{4,3,2,1,0:T(8,128)(2,1)S(1)} %pad_maximum_fusion.refs_3_), custom_call_target="tpu_custom_call" | custom-call | flops 2818572288 | bytes 7000000 | tf_op jit(solution)/shard_map/looks/pallas_call | solution.py:321
  45.9 0.0 collective-permute-done.1.refs_0_
  46.0 5.5 %looks.4.refs_4_ = bf16[4,40,2,120,120]{4,3,2,1,0:T(8,128)(2,1)} custom-call(bf16[3,4,2,120,128]{4,3,2,1,0:T(8,128)(2,1)S(1)} %collective-permute-done.1.refs_0_, bf16[2,7,2,120,128]{4,3,2,1,0:T(8,128)(2,1)S(1)} %copy-done, bf16[3,7,2,120,128]{4,3,2,1,0:T(8,128)(2,1)S(1)} %copy-done.1, ...), custom_call_target="tpu_custom_call", output_to_operand_aliasing={{}: (4, {})} | custom-call | flops 1610612736 | bytes 4000000 | tf_op jit(solution)/shard_map/looks/pallas_call | solution.py:321
  51.5 0.0 collective-permute-done.6.refs_6_
  51.5 0.0 collective-permute-done.7.refs_7_
  51.5 0.0 collective-permute-done.8.refs_8_
  51.5 0.0 collective-permute-done.refs_0_
  51.5 4.5 %looks.5 = (bf16[4,40,2,120,120]{4,3,2,1,0:T(8,128)(2,1)}, f32[2,120,120]{2,1,0:T(8,128)}) custom-call(bf16[3,3,2,120,128]{4,3,2,1,0:T(8,128)(2,1)S(1)} %collective-permute-done.refs_0_, bf16[2,7,2,120,128]{4,3,2,1,0:T(8,128)(2,1)S(1)} %copy-done, bf16[3,7,2,120,128]{4,3,2,1,0:T(8,128)(2,1)S(1)} %copy-done.1, ...), custom_call_target="tpu_custom_call", output_to_operand_aliasing={{0}: (4, {})} | custom-call | flops 1207959552 | bytes 3000000 | tf_op jit(solution)/shard_map/looks/pallas_call | solution.py:321
  (12 shorter events, 0.1 us)
Async XLA Ops:
  3.7 32.0 %collective-permute-start.2 = (bf16[2,7,2,120,128]{4,3,2,1,0:T(8,128)(2,1)}, bf16[2,7,2,120,128]{4,3,2,1,0:T(8,128)(2,1)S(1)}, u32[]{:S(2)}, u32[]{:S(2)}) collective-permute-start(bf16[2,7,2,120,128]{4,3,2,1,0:T(8,128)(2,1)} %edge.1.top_ref.refs_1_), channel_id=1, source_target_pairs={{1,0},{2,1},{3,2},{4,3},{5,4},{6,5},{7,6},{8,7},{9,8},{10,9},{11,1... | collective-permute-start | bytes 2580488 | tf_op jit(solution)/shard_map/ppermute | solution.py:368
  10.2 35.8 %collective-permute-start.1 = (bf16[3,4,2,120,128]{4,3,2,1,0:T(8,128)(2,1)}, bf16[3,4,2,120,128]{4,3,2,1,0:T(8,128)(2,1)S(1)}, u32[]{:S(2)}, u32[]{:S(2)}) collective-permute-start(bf16[3,4,2,120,128]{4,3,2,1,0:T(8,128)(2,1)} %get-tuple-element.8.refs_3_), channel_id=1, source_target_pairs={{0,1},{1,2},{2,3},{3,4},{4,5},{5,6},{6,7},{7,8},{8,9},{9,10},{10,1... | collective-permute-start | bytes 2211848 | tf_op jit(solution)/shard_map/ppermute | solution.py:370
  13.2 7.8 %collective-permute-start.3 = (f32[128,128]{1,0:T(8,128)}, f32[128,128]{1,0:T(8,128)S(1)}, u32[]{:S(2)}, u32[]{:S(2)}) collective-permute-start(f32[128,128]{1,0:T(8,128)} %get-tuple-element.9), channel_id=1, source_target_pairs={{0,2},{1,3},{2,0},{3,1},{4,6},{5,7},{6,4},{7,5},{8,10},{9,11},{10,... | collective-permute-start | bytes 196616 | tf_op jit(solution)/shard_map/ppermute | solution.py:356
  16.2 15.3 %collective-permute-start.4 = (f32[128,128]{1,0:T(8,128)}, f32[128,128]{1,0:T(8,128)S(1)}, u32[]{:S(2)}, u32[]{:S(2)}) collective-permute-start(f32[128,128]{1,0:T(8,128)} %get-tuple-element.9), channel_id=1, source_target_pairs={{0,1},{1,2},{2,3},{3,0},{4,5},{5,6},{6,7},{7,4},{8,9},{9,10},{10,1... | collective-permute-start | bytes 196616 | tf_op jit(solution)/shard_map/ppermute | solution.py:356
  17.9 13.6 %collective-permute-start.5 = (f32[128,128]{1,0:T(8,128)}, f32[128,128]{1,0:T(8,128)S(1)}, u32[]{:S(2)}, u32[]{:S(2)}) collective-permute-start(f32[128,128]{1,0:T(8,128)} %get-tuple-element.9), channel_id=1, source_target_pairs={{0,3},{1,0},{2,1},{3,2},{4,7},{5,4},{6,5},{7,6},{8,11},{9,8},{10,9... | collective-permute-start | bytes 196616 | tf_op jit(solution)/shard_map/ppermute | solution.py:356
  18.0 1.5 %copy-start.2 = (bf16[3,3,2,120,128]{4,3,2,1,0:T(8,128)(2,1)S(1)}, bf16[3,3,2,120,128]{4,3,2,1,0:T(8,128)(2,1)}, u32[]{:S(2)}) copy-start(bf16[3,3,2,120,128]{4,3,2,1,0:T(8,128)(2,1)} %get-tuple-element.6.in_ref.refs_3_) | copy-start | bytes 1658884
  18.0 13.6 %copy-start.4 = (f32[128,128]{1,0:T(8,128)S(1)}, f32[128,128]{1,0:T(8,128)}, u32[]{:S(2)}) copy-start(f32[128,128]{1,0:T(8,128)} %get-tuple-element.9) | copy-start | bytes 196612
  18.0 19.2 %copy-start.1 = (bf16[3,7,2,120,128]{4,3,2,1,0:T(8,128)(2,1)S(1)}, bf16[3,7,2,120,128]{4,3,2,1,0:T(8,128)(2,1)}, u32[]{:S(2)}) copy-start(bf16[3,7,2,120,128]{4,3,2,1,0:T(8,128)(2,1)} %get-tuple-element.7.refs_2_) | copy-start | bytes 3870724
  19.5 17.6 %copy-start = (bf16[2,7,2,120,128]{4,3,2,1,0:T(8,128)(2,1)S(1)}, bf16[2,7,2,120,128]{4,3,2,1,0:T(8,128)(2,1)}, u32[]{:S(2)}) copy-start(bf16[2,7,2,120,128]{4,3,2,1,0:T(8,128)(2,1)} %edge.1.top_ref.refs_1_) | copy-start | bytes 2580484
  21.1 30.4 %collective-permute-start = (bf16[3,3,2,120,128]{4,3,2,1,0:T(8,128)(2,1)S(1)}, bf16[3,3,2,120,128]{4,3,2,1,0:T(8,128)(2,1)S(1)}, u32[]{:S(2)}, u32[]{:S(2)}) collective-permute-start(bf16[3,3,2,120,128]{4,3,2,1,0:T(8,128)(2,1)S(1)} %again.1), channel_id=1, source_target_pairs={{0,1},{1,2},{2,3},{3,4},{4,5},{5,6},{6,7},{7,8},{8,9},{9,10},{10,1... | collective-permute-start | bytes 1658888 | tf_op jit(solution)/shard_map/ppermute | solution.py:372
  31.6 19.9 %collective-permute-start.6 = (f32[128,128]{1,0:T(8,128)S(1)}, f32[128,128]{1,0:T(8,128)S(1)}, u32[]{:S(2)}, u32[]{:S(2)}) collective-permute-start(f32[128,128]{1,0:T(8,128)S(1)} %add_add_fusion.refs_5_), channel_id=1, source_target_pairs={{0,4},{1,5},{2,6},{3,7},{4,8},{5,9},{6,10},{7,11},{8,12},{9,13},{1... | collective-permute-start | bytes 196616 | tf_op jit(solution)/shard_map/ppermute | solution.py:356
  33.2 18.3 %collective-permute-start.7 = (f32[128,128]{1,0:T(8,128)S(1)}, f32[128,128]{1,0:T(8,128)S(1)}, u32[]{:S(2)}, u32[]{:S(2)}) collective-permute-start(f32[128,128]{1,0:T(8,128)S(1)} %add_add_fusion.refs_5_), channel_id=1, source_target_pairs={{0,8},{1,9},{2,10},{3,11},{4,12},{5,13},{6,14},{7,15},{8,0},{9,1},... | collective-permute-start | bytes 196616 | tf_op jit(solution)/shard_map/ppermute | solution.py:356
  35.7 15.8 %collective-permute-start.8 = (f32[128,128]{1,0:T(8,128)S(1)}, f32[128,128]{1,0:T(8,128)S(1)}, u32[]{:S(2)}, u32[]{:S(2)}) collective-permute-start(f32[128,128]{1,0:T(8,128)S(1)} %add_add_fusion.refs_5_), channel_id=1, source_target_pairs={{0,12},{1,13},{2,14},{3,15},{4,0},{5,1},{6,2},{7,3},{8,4},{9,5},{1... | collective-permute-start | bytes 196616 | tf_op jit(solution)/shard_map/ppermute | solution.py:356
  37.1 8.8 %copy-start.3 = (bf16[3,4,2,120,128]{4,3,2,1,0:T(8,128)(2,1)S(1)}, bf16[3,4,2,120,128]{4,3,2,1,0:T(8,128)(2,1)}, u32[]{:S(2)}) copy-start(bf16[3,4,2,120,128]{4,3,2,1,0:T(8,128)(2,1)} %get-tuple-element.8.refs_3_) | copy-start | bytes 2211844

commit v5 on v3

v5 whole, which is shorter than its diff:
```python
import functools
import jax
import jax.numpy as jnp
from jax import lax
from jax.experimental import pallas as pl
from jax.experimental.pallas import tpu as pltpu
from jax.sharding import PartitionSpec as P

floor_power = 30.0

LOOK = 21
LANES = 128
TILE = 16
PER = LANES // LOOK
SPAN = PER * LOOK
ROWS = 8
SKEW = (5, 0, 1, 2, 3, 4, 1, 2)
BEFORE, AFTER = 3, 2
NT = (((1,), (1,)), ((), ()))


def turned(image, mask, skew, columns, put):
    count = image[0].shape[0]
    zero = jnp.zeros((count, LANES), jnp.bfloat16)
    lane = lax.broadcasted_iota(jnp.int32, (1, LANES), 1)

    def tile(value, g):
        start, stop = g * LANES, min((g + 1) * LANES, columns)
        part = value[:, start:stop]
        if stop - start < LANES:
            rest = jnp.zeros((part.shape[0], LANES - (stop - start)), part.dtype)
            part = jnp.concatenate([part, rest], axis=1)
        return part

    def widened(which):
        return jnp.broadcast_to(which.astype(jnp.float32), (count, LANES)).astype(jnp.bfloat16) != 0

    tiles = -(-columns // LANES)
    for g in range(-(-columns // SPAN)):
        slide = (LANES - SPAN) * g
        place = (lane + slide) % LANES
        used = (place < SPAN) & (SPAN * g + place < columns)
        prior = lane >= LANES - slide
        sides = [t for t in (g - 1, g) if 0 <= t < tiles]

        def joined(value):
            parts = [tile(value, t) for t in sides]
            if len(parts) == 1:
                return parts[0]
            which = prior if value.shape[0] == 1 else widened(prior)
            return jnp.where(which, parts[0], parts[1])

        keep = widened(used & (joined(mask) != 0))
        for k in range(2):
            row = jnp.where(keep, joined(image[k]), zero)
            put(g, k, pltpu.roll(row, slide + LOOK * skew, 1))


def fetched(image_ref, mask_ref, rows_ref, masks_ref, sems, order):
    copies = [pltpu.make_async_copy(mask_ref, masks_ref, sems.at[len(order)])]
    for at, row in enumerate(order):
        copies.append(pltpu.make_async_copy(image_ref.at[row], rows_ref.at[at], sems.at[at]))
    for copy in copies:
        copy.start()
    return copies[0], copies[1:]


def rows_kernel(jobs, behind, image_ref, mask_ref, *refs):
    order = [row for row, _ in jobs]
    count = sum(len(targets) for _, targets in jobs)
    rows_ref, masks_ref, turned_ref, in_sems, out_sems = refs[-5:]
    outs = refs[behind:-5]
    mask_copy, fetches = fetched(image_ref, mask_ref, rows_ref, masks_ref, in_sems, order)
    mask_copy.wait()
    stores = []
    for at, (row, targets) in enumerate(jobs):
        fetches[at].wait()

        def put(g, k, value):
            turned_ref[at, g, k] = value

        turned([rows_ref.at[at, 0], rows_ref.at[at, 1]], masks_ref[row : row + 1, :], SKEW[row], masks_ref.shape[1], put)
        for out, i, start, stop in targets:
            store = pltpu.make_async_copy(turned_ref.at[at, start:stop], outs[out].at[i], out_sems.at[len(stores)])
            store.start()
            stores.append(store)
    for store in stores:
        store.wait()


def turned_rows(images, valid_mask, jobs, groups, shapes, name, behind=()):
    count, columns = images.shape[2:]
    far = pl.BlockSpec(memory_space=pl.ANY)
    stores = sum(len(targets) for _, targets in jobs)
    return pl.pallas_call(
        functools.partial(rows_kernel, jobs, len(behind)),
        in_specs=[far, far] + [far] * len(behind),
        out_specs=[far] * len(shapes),
        out_shape=[jax.ShapeDtypeStruct((rows, n, 2, count, LANES), jnp.bfloat16) for rows, n in shapes],
        scratch_shapes=[
            pltpu.VMEM((len(jobs), 2, count, columns), jnp.bfloat16),
            pltpu.VMEM(valid_mask.shape, jnp.int32),
            pltpu.VMEM((len(jobs), groups, 2, count, LANES), jnp.bfloat16),
            pltpu.SemaphoreType.DMA((len(jobs) + 1,)),
            pltpu.SemaphoreType.DMA((stores,)),
        ],
        compiler_params=pltpu.CompilerParams(vmem_limit_bytes=61 * 2**20),
        cost_estimate=pl.CostEstimate(flops=10**6, bytes_accessed=len(jobs) * 10**6, transcendentals=0),
        name=name,
    )(images, valid_mask, *behind)


def gram_kernel(image_ref, mask_ref, gram_ref, rows_ref, masks_ref, z_ref, sems):
    count, columns = image_ref.shape[2:]
    mask_copy, fetches = fetched(image_ref, mask_ref, rows_ref, masks_ref, sems, range(ROWS))
    z_ref[...] = jnp.zeros_like(z_ref)
    mask_copy.wait()
    zero = jnp.zeros((count, columns), jnp.bfloat16)
    total = None
    for r in range(ROWS):
        keep = masks_ref[r : r + 1, :] != 0
        keep = jnp.broadcast_to(keep.astype(jnp.float32), (count, columns)).astype(jnp.bfloat16) != 0
        fetches[r].wait()
        for k in range(2):
            z_ref[r % 2, pl.ds(k * LANES, count), pl.ds(0, columns)] = jnp.where(keep, rows_ref[r, k], zero)
        z = z_ref[r % 2]
        part = lax.dot_general(z, z, NT, preferred_element_type=jnp.float32)
        total = part if total is None else total + part
    real = total[:LANES, :LANES] + total[LANES:, LANES:]
    imag = total[LANES:, :LANES] - total[:LANES, LANES:]
    i = lax.broadcasted_iota(jnp.int32, real.shape, 0)
    j = lax.broadcasted_iota(jnp.int32, real.shape, 1)
    gram_ref[...] = jnp.where(i <= j, real, imag)


def local_gram(images, valid_mask):
    count, columns = images.shape[2:]
    far = pl.BlockSpec(memory_space=pl.ANY)
    return pl.pallas_call(
        gram_kernel,
        in_specs=[far, far],
        out_specs=pl.BlockSpec(memory_space=pltpu.VMEM),
        out_shape=jax.ShapeDtypeStruct((LANES, LANES), jnp.float32),
        scratch_shapes=[
            pltpu.VMEM(images.shape, jnp.bfloat16),
            pltpu.VMEM(valid_mask.shape, jnp.int32),
            pltpu.VMEM((2, 2 * LANES, -(-columns // LANES) * LANES), jnp.bfloat16),
            pltpu.SemaphoreType.DMA((ROWS + 1,)),
        ],
        compiler_params=pltpu.CompilerParams(vmem_limit_bytes=61 * 2**20),
        cost_estimate=pl.CostEstimate(flops=10**9, bytes_accessed=5 * 10**6, transcendentals=0),
        name="gram",
    )(images, valid_mask)


def added(terms):
    if len(terms) == 4:
        return (terms[0] + terms[2]) + (terms[1] + terms[3])
    return functools.reduce(jnp.add, terms)


def slab_values(terms):
    packed = added(terms)
    flipped = packed.T
    i = lax.broadcasted_iota(jnp.int32, packed.shape, 0)
    j = lax.broadcasted_iota(jnp.int32, packed.shape, 1)
    real = jnp.where(i <= j, packed, flipped)
    imag = jnp.where(i > j, packed, jnp.where(i < j, -flipped, 0.0))
    powers = jnp.where(i == j, packed, 0.0)
    scaled = jnp.sqrt(jnp.sum(powers, axis=1, keepdims=True) * jnp.sum(powers, axis=0, keepdims=True))
    return real / scaled, imag / scaled


INNER = (1, 2, 3, 4, 5)
HALVES = (
    ((-3, -2, -1, 0), (((1, 2, 3), None), (None, (-1, 0)))),
    ((6, 7, 8, 9), ((None, (6, 7)), ((3, 4, 5), None))),
)


def looks_kernel(half, aliased, terms, *refs):
    other_ref, top_ref, mid_ref, low_ref = refs[:4]
    refs = refs[4 + aliased :]
    term_refs, refs = refs[:terms], refs[terms:]
    out_ref, extra_ref, w_ref = refs
    count = top_ref.shape[3]

    @pl.when(pl.program_id(0) == 0)
    def _():
        w_ref[...] = jnp.zeros_like(w_ref)
        if terms:
            real, imag = slab_values([t[...] for t in term_refs])
            extra_ref[0] = real[:count, :count]
            extra_ref[1] = imag[:count, :count]
        else:
            extra_ref[...] = jnp.zeros_like(extra_ref)

    rows = {}
    for r in range(ROWS):
        if r < AFTER:
            rows[r] = top_ref.at[r, 0]
        elif r >= ROWS - BEFORE:
            rows[r] = low_ref.at[r - (ROWS - BEFORE), 0]
        else:
            rows[r] = mid_ref.at[r - AFTER, 0]
    for r in range(other_ref.shape[0]):
        rows[ROWS + r if half else r - BEFORE] = other_ref.at[r, 0]

    lane = lax.broadcasted_iota(jnp.int32, (1, LANES), 1)

    def lanes_of(turn):
        place = lane + (-LOOK * turn) % LANES
        place = jnp.where(place >= LANES, place - LANES, place)
        return place < LOOK

    def widened(which):
        return jnp.broadcast_to(which.astype(jnp.float32), (count, LANES)).astype(jnp.bfloat16) != 0

    single = [lanes_of(t) for t in range(2 * PER - 1)]
    wide = [widened(s) for s in single]
    zero = jnp.zeros((count, LANES), jnp.bfloat16)

    def turn(l, r):
        return l + SKEW[r % ROWS]

    def gathered(l, k, which):
        out = zero
        for r in which:
            out = jnp.where(wide[turn(l, r)], rows[r][k], out)
        return out

    def kept(l, which):
        select = jnp.ones((1, LANES), jnp.bool_)
        if which is not None:
            select = single[turn(l, which[0])]
            for r in which[1:]:
                select = select | single[turn(l, r)]
        return select.astype(jnp.float32)

    i = lax.broadcasted_iota(jnp.int32, (count, LANES), 0)
    j = lax.broadcasted_iota(jnp.int32, (count, LANES), 1)
    eye = i == j

    def normalised(real, imag, w, l):
        power = jnp.sum(jnp.where(eye, real, 0.0), axis=0, keepdims=True)
        across = lax.rsqrt(jnp.maximum(power, floor_power))
        down = jnp.sum(jnp.where(eye, across, 0.0), axis=1, keepdims=True)
        out_ref[w, l, 0] = (real * down * across).astype(jnp.bfloat16)[:, :count]
        out_ref[w, l, 1] = (imag * down * across).astype(jnp.bfloat16)[:, :count]

    outer_rows, windows = HALVES[half]
    for l in range(PER):
        slot = l % 2
        for k in range(2):
            w_ref[slot, k, pl.ds(0, count), pl.ds(0, LANES)] = gathered(l, k, INNER)
            w_ref[slot, k, pl.ds(0, count), pl.ds(LANES, LANES)] = gathered(l, k, outer_rows)
        every = w_ref[slot].reshape(2 * LANES, 2 * LANES)
        nothing = jnp.zeros_like(every)
        reads = []
        for inner_rows, rest_rows in windows:
            lanes = jnp.concatenate([kept(l, inner_rows), kept(l, rest_rows)], axis=1)
            lanes = jnp.broadcast_to(lanes, every.shape).astype(jnp.bfloat16) != 0
            read = jnp.where(lanes, every, nothing)
            for start in range(0, LANES, TILE):
                reads.append(read[start : start + TILE])
                reads.append(read[LANES + start : LANES + start + TILE])
        gram = lax.dot_general(jnp.concatenate(reads, axis=0), every, NT, preferred_element_type=jnp.float32)
        for w in range(2):
            real, imag = [], []
            for start in range(0, LANES, TILE):
                base = 2 * (w * LANES + start)
                re, im = gram[base : base + TILE], gram[base + TILE : base + 2 * TILE]
                real.append(re[:, :LANES] + im[:, LANES:])
                imag.append(im[:, :LANES] - re[:, LANES:])
            normalised(jnp.concatenate(real, axis=0)[:count], jnp.concatenate(imag, axis=0)[:count], w, l)


def looked(half, other, top, mid, low, first, looks, previous, terms):
    groups, _, count, _ = other.shape[1:]

    def spec(array):
        offset = 0 if array.shape[1] == groups else first
        return pl.BlockSpec((array.shape[0], 1) + array.shape[2:], lambda s: (0, s + offset, 0, 0, 0))

    operands = [other, top, mid, low]
    in_specs = [spec(a) for a in operands]
    aliases = {}
    if previous is not None:
        aliases = {len(operands): 0}
        operands.append(previous)
        in_specs.append(pl.BlockSpec(memory_space=pl.ANY))
    for term in terms:
        operands.append(term)
        in_specs.append(pl.BlockSpec(term.shape, lambda s: (0, 0)))
    extra = (2, count, count) if terms else (LANES, LANES)
    out_specs = [
        pl.BlockSpec((2, PER, 2, count, count), lambda s: (half, s + first, 0, 0, 0)),
        pl.BlockSpec(extra, lambda s: (0,) * len(extra)),
    ]
    out_shape = [
        jax.ShapeDtypeStruct((ROWS // 2, looks, 2, count, count), jnp.bfloat16),
        jax.ShapeDtypeStruct(extra, jnp.float32),
    ]
    return pl.pallas_call(
        functools.partial(looks_kernel, half, previous is not None, len(terms)),
        grid=(groups,),
        in_specs=in_specs,
        out_specs=out_specs,
        out_shape=out_shape,
        input_output_aliases=aliases,
        scratch_shapes=[
            pltpu.VMEM((2, 2, LANES, 2 * LANES), jnp.bfloat16),
        ],
        compiler_params=pltpu.CompilerParams(vmem_limit_bytes=32 * 2**20),
        cost_estimate=pl.CostEstimate(
            flops=groups * PER * 2 * 512 * 256 * 256, bytes_accessed=groups * 10**6, transcendentals=0
        ),
        name="looks",
    )(*operands)


def radices(size):
    found = []
    while size % 4 == 0:
        found.append(4)
        size //= 4
    if size == 2:
        found.append(2)
        size = 1
    return found if size == 1 else None


def round_terms(value, axis, stride, radix):
    size = lax.axis_size(axis)
    terms = [value]
    for shift in range(1, radix):
        pairs = []
        for i in range(size):
            place = (i // stride) % radix
            pairs.append((i, i + ((place + shift) % radix - place) * stride))
        terms.append(lax.ppermute(value, axis, pairs))
    return terms


def shards(images, valid_mask):
    looks = images.shape[3] // LOOK
    groups = -(-looks // PER)
    cut = -(-groups // 2)
    size = lax.axis_size("pix")
    forward = [(i, i + 1) for i in range(size - 1)]
    backward = [(i + 1, i) for i in range(size - 1)]
    (top,) = turned_rows(
        images, valid_mask, [(r, ((0, r, 0, groups),)) for r in range(AFTER)], groups, [(AFTER, groups)], "first_rows"
    )
    after = lax.ppermute(top, "pix", backward)

    total = local_gram(images, valid_mask)
    steps = radices(size)
    if steps:
        terms = round_terms(total, "pix", 1, steps[0])
    else:
        terms = [lax.psum(total, "pix")]

    jobs = []
    for r in range(BEFORE):
        jobs.append((ROWS - BEFORE + r, ((0, r, 0, cut), (1, r, cut, groups), (2, r, 0, groups))))
    for r in range(ROWS - BEFORE - AFTER):
        jobs.append((AFTER + r, ((3, r, 0, groups),)))
    shapes = [(BEFORE, cut), (BEFORE, groups - cut), (BEFORE, groups), (ROWS - BEFORE - AFTER, groups)]
    low0, low1, low, mid = turned_rows(images, valid_mask, jobs, groups, shapes, "last_rows", (total,))
    before0 = lax.ppermute(low0, "pix", forward)
    before1 = lax.ppermute(low1, "pix", forward)

    out, zeros = looked(1, after, top, mid, low, 0, looks, None, [])
    if steps:
        stride = steps[0]
        for radix in steps[1:]:
            terms = round_terms(added(terms) + zeros, "pix", stride, radix)
            stride *= radix
    out, _ = looked(0, before0, top, mid, low, 0, looks, out, [])
    out, slab = looked(0, before1, top, mid, low, cut, looks, out, terms)
    return (out, slab)


def solution(mesh):
    in_specs = (P(("group", "pix"), None, None, None), P(("group", "pix"), None))
    out_specs = (P(("group", "pix"), None, None, None, None), P("group", None, None))
    return jax.shard_map(shards, mesh=mesh, in_specs=in_specs, out_specs=out_specs, check_vma=False)
```

time: 63.6 us -> 51.7 us (0.81)
  waiting for transfers between devices: 8.36 us -> 0.17 us
  starting transfers between devices: 24.6 us -> 20.1 us
  local copies, waits for them, and re-layouts: 1.31 us -> 3.78 us
  other arithmetic: 0.86 us -> 0.02 us
  Pallas kernels: 27.3 us -> 26.6 us
    ppermute x8 -> x9, waiting for transfers between devices: 8.36 us -> 0.17 us  [the longest x6 0.16 us: round_terms(): terms.append(lax.ppermute(value, axis, pairs))]
    ppermute x8 -> x9, starting transfers between devices: 24.6 us -> 20.1 us  [the longest x6 12.3 us: round_terms(): terms.append(lax.ppermute(value, axis, pairs))]
    unnamed x6 -> x10, local copies, waits for them, and re-layouts: 1.31 us -> 3.78 us
    pallas_call x2 -> x3, Pallas kernels: 18.6 us -> 16.3 us  [looked(): pl.pallas_call(functools.partial(looks_kernel, half, previous is not None...]
    pallas_call x2 -> x3, Pallas kernels: 8.64 us -> 10.2 us  [the longest x2 5.58 us: turned_rows(): pl.pallas_call(functools.partial(rows_kernel, jobs, len(behind)), in_spec...]
    add x1, other arithmetic: 0.86 us -> 0.02 us  [shards(): terms = round_terms(added(terms) + zeros, 'pix', stride, radix)]
  transfers between devices with their start and end apart: 8 -> 9, of which waited for: 2 -> 1; matrix products, arithmetic and copies ran while one was open for 1% -> 0% of each run, Pallas kernels for 23% -> 40%
where the time goes in v5:
time: 51.7 us; the launch traced here: 51.4 us
  Pallas kernels  26.6 us (51%)
  starting transfers between devices  20.1 us (39%)
  local copies, waits for them, and re-layouts  3.78 us (7%)
  between operations  0.73 us (1%)
    pallas_call x3, Pallas kernels, looked(): pl.pallas_call(functools.partial(looks_kernel, half, previous is not None...  16.3 us
    ppermute x6, starting transfers between devices, round_terms(): terms.append(lax.ppermute(value, axis, pairs))  12.3 us
    pallas_call x2, Pallas kernels, turned_rows(): pl.pallas_call(functools.partial(rows_kernel, jobs, len(behind)), in_spec...  5.58 us
    pallas_call x1, Pallas kernels, local_gram(): pl.pallas_call(gram_kernel, in_specs=[far, far], out_specs=pl.BlockSpec(m...  4.64 us
    unnamed x10, local copies, waits for them, and re-layouts  3.78 us
    ppermute x1, starting transfers between devices, shards(): before1 = lax.ppermute(low1, 'pix', forward)  3.33 us
    ppermute x1, starting transfers between devices, shards(): before0 = lax.ppermute(low0, 'pix', forward)  3.07 us
    ppermute x1, starting transfers between devices, shards(): after = lax.ppermute(top, 'pix', backward)  1.42 us
  transfers between devices with their start and end apart: 9, of which 1 were waited for; matrix products, arithmetic and copies ran while one was open for 0% of the time, Pallas kernels for 40%

profile of v5, /device:TPU:0, one launch (start us, length us, event | category | flops | bytes accessed | tf_op | source)
XLA Modules:
  0.0 51.4 jit_solution(5138144459268993601)
XLA Ops:
  0.6 2.2 %first_rows.1.refs_1_ = bf16[2,7,2,120,128]{4,3,2,1,0:T(8,128)(2,1)} custom-call(bf16[8,2,120,840]{3,2,1,0:T(8,128)(2,1)} %image_ref.5, s32[8,840]{1,0:T(8,128)} %mask_ref.5), custom_call_target="tpu_custom_call" | custom-call | flops 1000000 | bytes 2000000 | tf_op jit(solution)/shard_map/first_rows/pallas_call | solution.py:95
  2.9 1.4 %collective-permute-start.2 = (bf16[2,7,2,120,128]{4,3,2,1,0:T(8,128)(2,1)}, bf16[2,7,2,120,128]{4,3,2,1,0:T(8,128)(2,1)S(1)}, u32[]{:S(2)}, u32[]{:S(2)}) collective-permute-start(bf16[2,7,2,120,128]{4,3,2,1,0:T(8,128)(2,1)} %first_rows.1.refs_1_), channel_id=1, source_target_pairs={{1,0},{2,1},{3,2},{4,3},{5,4},{6,5},{7,6},{8,7},{9,8},{10,9},{11,1... | collective-permute-start | bytes 2580488 | tf_op jit(solution)/shard_map/ppermute | solution.py:355
  4.3 4.6 %gram.1.refs_0_ = f32[128,128]{1,0:T(8,128)} custom-call(bf16[8,2,120,840]{3,2,1,0:T(8,128)(2,1)} %image_ref.5, s32[8,840]{1,0:T(8,128)} %mask_ref.5), custom_call_target="tpu_custom_call" | custom-call | flops 1000000000 | bytes 5000000 | tf_op jit(solution)/shard_map/gram/pallas_call | solution.py:139
  9.0 0.0 copy-start.4
  9.0 3.3 %last_rows.1 = (bf16[3,4,2,120,128]{4,3,2,1,0:T(8,128)(2,1)}, bf16[3,3,2,120,128]{4,3,2,1,0:T(8,128)(2,1)}, bf16[3,7,2,120,128]{4,3,2,1,0:T(8,128)(2,1)}, bf16[3,7,2,120,128]{4,3,2,1,0:T(8,128)(2,1)}) custom-call(bf16[8,2,120,840]{3,2,1,0:T(8,128)(2,1)} %image_ref.5, s32[8,840]{1,0:T(8,128)} %mask_ref.5, f32[128,128]{1,0:T(8,128)} %gram.1.refs_0_), custom_call_target="tpu_custom_call" | custom-call | flops 1000000 | bytes 6000000 | tf_op jit(solution)/shard_map/last_rows/pallas_call | solution.py:95
  12.3 3.1 %collective-permute-start.1 = (bf16[3,4,2,120,128]{4,3,2,1,0:T(8,128)(2,1)}, bf16[3,4,2,120,128]{4,3,2,1,0:T(8,128)(2,1)S(1)}, u32[]{:S(2)}, u32[]{:S(2)}) collective-permute-start(bf16[3,4,2,120,128]{4,3,2,1,0:T(8,128)(2,1)} %get-tuple-element.12), channel_id=1, source_target_pairs={{0,1},{1,2},{2,3},{3,4},{4,5},{5,6},{6,7},{7,8},{8,9},{9,10},{10,1... | collective-permute-start | bytes 2211848 | tf_op jit(solution)/shard_map/ppermute | solution.py:371
  15.4 4.5 %collective-permute-start.5 = (f32[128,128]{1,0:T(8,128)}, f32[128,128]{1,0:T(8,128)S(1)}, u32[]{:S(2)}, u32[]{:S(2)}) collective-permute-start(f32[128,128]{1,0:T(8,128)} %gram.1.refs_0_), channel_id=1, source_target_pairs={{0,3},{1,0},{2,1},{3,2},{4,7},{5,4},{6,5},{7,6},{8,11},{9,8},{10,9... | collective-permute-start | bytes 196616 | tf_op jit(solution)/shard_map/ppermute | solution.py:341
  19.9 0.0 collective-permute-start.4
  19.9 0.5 collective-permute-start.3
  20.4 0.0 collective-permute-done.2.refs_0_
  20.4 3.3 %collective-permute-start = (bf16[3,3,2,120,128]{4,3,2,1,0:T(8,128)(2,1)}, bf16[3,3,2,120,128]{4,3,2,1,0:T(8,128)(2,1)S(1)}, u32[]{:S(2)}, u32[]{:S(2)}) collective-permute-start(bf16[3,3,2,120,128]{4,3,2,1,0:T(8,128)(2,1)} %get-tuple-element.9), channel_id=1, source_target_pairs={{0,1},{1,2},{2,3},{3,4},{4,5},{5,6},{6,7},{7,8},{8,9},{9,10},{10,1... | collective-permute-start | bytes 1658888 | tf_op jit(solution)/shard_map/ppermute | solution.py:372
  23.7 1.1 %copy-done = bf16[2,7,2,120,128]{4,3,2,1,0:T(8,128)(2,1)S(1)} copy-done((bf16[2,7,2,120,128]{4,3,2,1,0:T(8,128)(2,1)S(1)}, bf16[2,7,2,120,128]{4,3,2,1,0:T(8,128)(2,1)}, u32[]{:S(2)}) %copy-start) | copy-done | bytes 860184
  24.9 1.3 %copy-done.2 = bf16[3,7,2,120,128]{4,3,2,1,0:T(8,128)(2,1)S(1)} copy-done((bf16[3,7,2,120,128]{4,3,2,1,0:T(8,128)(2,1)S(1)}, bf16[3,7,2,120,128]{4,3,2,1,0:T(8,128)(2,1)}, u32[]{:S(2)}) %copy-start.2) | copy-done | bytes 1290264
  26.2 1.3 %copy-done.3 = bf16[3,7,2,120,128]{4,3,2,1,0:T(8,128)(2,1)S(1)} copy-done((bf16[3,7,2,120,128]{4,3,2,1,0:T(8,128)(2,1)S(1)}, bf16[3,7,2,120,128]{4,3,2,1,0:T(8,128)(2,1)}, u32[]{:S(2)}) %copy-start.3) | copy-done | bytes 1290264
  27.5 7.6 %looks.3 = (bf16[4,40,2,120,120]{4,3,2,1,0:T(8,128)(2,1)}, f32[128,128]{1,0:T(8,128)S(1)}) custom-call(bf16[2,7,2,120,128]{4,3,2,1,0:T(8,128)(2,1)S(1)} %collective-permute-done.2.refs_0_, bf16[2,7,2,120,128]{4,3,2,1,0:T(8,128)(2,1)S(1)} %copy-done, bf16[3,7,2,120,128]{4,3,2,1,0:T(8,128)(2,1)S(1)} %copy-done.3, bf16[3,7,2,120,128]{4,3,2,1,0:T(8,128)(2,1)S(1)} %copy-done.2), custom_call_target="tpu_custom_call" | custom-call | flops 2818572288 | bytes 7000000 | tf_op jit(solution)/shard_map/looks/pallas_call | solution.py:304
  35.1 0.0 collective-permute-done.5
  35.1 0.0 collective-permute-done.3
  35.1 5.8 %collective-permute-start.8 = (f32[128,128]{1,0:T(8,128)S(1)}, f32[128,128]{1,0:T(8,128)S(1)}, u32[]{:S(2)}, u32[]{:S(2)}) collective-permute-start(f32[128,128]{1,0:T(8,128)S(1)} %add_add_fusion.refs_5_), channel_id=1, source_target_pairs={{0,12},{1,13},{2,14},{3,15},{4,0},{5,1},{6,2},{7,3},{8,4},{9,5},{1... | collective-permute-start | bytes 196616 | tf_op jit(solution)/shard_map/ppermute | solution.py:341
  40.9 1.5 %collective-permute-start.6 = (f32[128,128]{1,0:T(8,128)S(1)}, f32[128,128]{1,0:T(8,128)S(1)}, u32[]{:S(2)}, u32[]{:S(2)}) collective-permute-start(f32[128,128]{1,0:T(8,128)S(1)} %add_add_fusion.refs_5_), channel_id=1, source_target_pairs={{0,4},{1,5},{2,6},{3,7},{4,8},{5,9},{6,10},{7,11},{8,12},{9,13},{1... | collective-permute-start | bytes 196616 | tf_op jit(solution)/shard_map/ppermute | solution.py:341
  42.4 4.9 %looks.4 = (bf16[4,40,2,120,120]{4,3,2,1,0:T(8,128)(2,1)}, f32[128,128]{1,0:T(8,128)}) custom-call(bf16[3,4,2,120,128]{4,3,2,1,0:T(8,128)(2,1)S(1)} %collective-permute-done.1.refs_0_, bf16[2,7,2,120,128]{4,3,2,1,0:T(8,128)(2,1)S(1)} %copy-done.1, bf16[3,7,2,120,128]{4,3,2,1,0:T(8,128)(2,1)S(1)} %copy-done.3, ...), custom_call_target="tpu_custom_call", output_to_operand_aliasing={{0}: (4, {})} | custom-call | flops 1610612736 | bytes 4000000 | tf_op jit(solution)/shard_map/looks/pallas_call | solution.py:304
  47.3 0.0 collective-permute-done.refs_0_
  47.3 0.0 collective-permute-done.8.refs_8_
  47.3 0.2 collective-permute-done.7.refs_7_
  47.5 3.9 %looks.5 = (bf16[4,40,2,120,120]{4,3,2,1,0:T(8,128)(2,1)}, f32[2,120,120]{2,1,0:T(8,128)}) custom-call(bf16[3,3,2,120,128]{4,3,2,1,0:T(8,128)(2,1)S(1)} %collective-permute-done.refs_0_, bf16[2,7,2,120,128]{4,3,2,1,0:T(8,128)(2,1)S(1)} %copy-done.1, bf16[3,7,2,120,128]{4,3,2,1,0:T(8,128)(2,1)S(1)} %copy-done.3, ...), custom_call_target="tpu_custom_call", output_to_operand_aliasing={{0}: (4, {})} | custom-call | flops 1207959552 | bytes 3000000 | tf_op jit(solution)/shard_map/looks/pallas_call | solution.py:304
  (11 shorter events, 0.0 us)
Async XLA Ops:
  2.9 39.6 %copy-start.1 = (bf16[2,7,2,120,128]{4,3,2,1,0:T(8,128)(2,1)S(1)}, bf16[2,7,2,120,128]{4,3,2,1,0:T(8,128)(2,1)}, u32[]{:S(2)}) copy-start(bf16[2,7,2,120,128]{4,3,2,1,0:T(8,128)(2,1)} %first_rows.1.refs_1_) | copy-start | bytes 2580484
  2.9 17.5 %collective-permute-start.2 = (bf16[2,7,2,120,128]{4,3,2,1,0:T(8,128)(2,1)}, bf16[2,7,2,120,128]{4,3,2,1,0:T(8,128)(2,1)S(1)}, u32[]{:S(2)}, u32[]{:S(2)}) collective-permute-start(bf16[2,7,2,120,128]{4,3,2,1,0:T(8,128)(2,1)} %first_rows.1.refs_1_), channel_id=1, source_target_pairs={{1,0},{2,1},{3,2},{4,3},{5,4},{6,5},{7,6},{8,7},{9,8},{10,9},{11,1... | collective-permute-start | bytes 2580488 | tf_op jit(solution)/shard_map/ppermute | solution.py:355
  9.0 26.1 %copy-start.4 = (f32[128,128]{1,0:T(8,128)S(1)}, f32[128,128]{1,0:T(8,128)}, u32[]{:S(2)}) copy-start(f32[128,128]{1,0:T(8,128)} %gram.1.refs_0_) | copy-start | bytes 196612
  12.3 30.1 %collective-permute-start.1 = (bf16[3,4,2,120,128]{4,3,2,1,0:T(8,128)(2,1)}, bf16[3,4,2,120,128]{4,3,2,1,0:T(8,128)(2,1)S(1)}, u32[]{:S(2)}, u32[]{:S(2)}) collective-permute-start(bf16[3,4,2,120,128]{4,3,2,1,0:T(8,128)(2,1)} %get-tuple-element.12), channel_id=1, source_target_pairs={{0,1},{1,2},{2,3},{3,4},{4,5},{5,6},{6,7},{7,8},{8,9},{9,10},{10,1... | collective-permute-start | bytes 2211848 | tf_op jit(solution)/shard_map/ppermute | solution.py:371
  15.4 19.7 %collective-permute-start.5 = (f32[128,128]{1,0:T(8,128)}, f32[128,128]{1,0:T(8,128)S(1)}, u32[]{:S(2)}, u32[]{:S(2)}) collective-permute-start(f32[128,128]{1,0:T(8,128)} %gram.1.refs_0_), channel_id=1, source_target_pairs={{0,3},{1,0},{2,1},{3,2},{4,7},{5,4},{6,5},{7,6},{8,11},{9,8},{10,9... | collective-permute-start | bytes 196616 | tf_op jit(solution)/shard_map/ppermute | solution.py:341
  19.9 15.1 %collective-permute-start.4 = (f32[128,128]{1,0:T(8,128)}, f32[128,128]{1,0:T(8,128)S(1)}, u32[]{:S(2)}, u32[]{:S(2)}) collective-permute-start(f32[128,128]{1,0:T(8,128)} %gram.1.refs_0_), channel_id=1, source_target_pairs={{0,1},{1,2},{2,3},{3,0},{4,5},{5,6},{6,7},{7,4},{8,9},{9,10},{10,1... | collective-permute-start | bytes 196616 | tf_op jit(solution)/shard_map/ppermute | solution.py:341
  19.9 15.1 %collective-permute-start.3 = (f32[128,128]{1,0:T(8,128)}, f32[128,128]{1,0:T(8,128)S(1)}, u32[]{:S(2)}, u32[]{:S(2)}) collective-permute-start(f32[128,128]{1,0:T(8,128)} %gram.1.refs_0_), channel_id=1, source_target_pairs={{0,2},{1,3},{2,0},{3,1},{4,6},{5,7},{6,4},{7,5},{8,10},{9,11},{10,... | collective-permute-start | bytes 196616 | tf_op jit(solution)/shard_map/ppermute | solution.py:341
  20.4 26.9 %collective-permute-start = (bf16[3,3,2,120,128]{4,3,2,1,0:T(8,128)(2,1)}, bf16[3,3,2,120,128]{4,3,2,1,0:T(8,128)(2,1)S(1)}, u32[]{:S(2)}, u32[]{:S(2)}) collective-permute-start(bf16[3,3,2,120,128]{4,3,2,1,0:T(8,128)(2,1)} %get-tuple-element.9), channel_id=1, source_target_pairs={{0,1},{1,2},{2,3},{3,4},{4,5},{5,6},{6,7},{7,8},{8,9},{9,10},{10,1... | collective-permute-start | bytes 1658888 | tf_op jit(solution)/shard_map/ppermute | solution.py:372
  23.7 1.2 %copy-start = (bf16[2,7,2,120,128]{4,3,2,1,0:T(8,128)(2,1)S(1)}, bf16[2,7,2,120,128]{4,3,2,1,0:T(8,128)(2,1)}, u32[]{:S(2)}) copy-start(bf16[2,7,2,120,128]{4,3,2,1,0:T(8,128)(2,1)} %first_rows.1.refs_1_) | copy-start | bytes 2580484
  24.9 1.3 %copy-start.2 = (bf16[3,7,2,120,128]{4,3,2,1,0:T(8,128)(2,1)S(1)}, bf16[3,7,2,120,128]{4,3,2,1,0:T(8,128)(2,1)}, u32[]{:S(2)}) copy-start(bf16[3,7,2,120,128]{4,3,2,1,0:T(8,128)(2,1)} %get-tuple-element.11.refs_3_) | copy-start | bytes 3870724
  26.2 1.3 %copy-start.3 = (bf16[3,7,2,120,128]{4,3,2,1,0:T(8,128)(2,1)S(1)}, bf16[3,7,2,120,128]{4,3,2,1,0:T(8,128)(2,1)}, u32[]{:S(2)}) copy-start(bf16[3,7,2,120,128]{4,3,2,1,0:T(8,128)(2,1)} %get-tuple-element.10.refs_2_) | copy-start | bytes 3870724
  35.1 12.2 %collective-permute-start.8 = (f32[128,128]{1,0:T(8,128)S(1)}, f32[128,128]{1,0:T(8,128)S(1)}, u32[]{:S(2)}, u32[]{:S(2)}) collective-permute-start(f32[128,128]{1,0:T(8,128)S(1)} %add_add_fusion.refs_5_), channel_id=1, source_target_pairs={{0,12},{1,13},{2,14},{3,15},{4,0},{5,1},{6,2},{7,3},{8,4},{9,5},{1... | collective-permute-start | bytes 196616 | tf_op jit(solution)/shard_map/ppermute | solution.py:341
  40.9 6.5 %collective-permute-start.7 = (f32[128,128]{1,0:T(8,128)S(1)}, f32[128,128]{1,0:T(8,128)S(1)}, u32[]{:S(2)}, u32[]{:S(2)}) collective-permute-start(f32[128,128]{1,0:T(8,128)S(1)} %add_add_fusion.refs_5_), channel_id=1, source_target_pairs={{0,8},{1,9},{2,10},{3,11},{4,12},{5,13},{6,14},{7,15},{8,0},{9,1},... | collective-permute-start | bytes 196616 | tf_op jit(solution)/shard_map/ppermute | solution.py:341
  40.9 6.5 %collective-permute-start.6 = (f32[128,128]{1,0:T(8,128)S(1)}, f32[128,128]{1,0:T(8,128)S(1)}, u32[]{:S(2)}, u32[]{:S(2)}) collective-permute-start(f32[128,128]{1,0:T(8,128)S(1)} %add_add_fusion.refs_5_), channel_id=1, source_target_pairs={{0,4},{1,5},{2,6},{3,7},{4,8},{5,9},{6,10},{7,11},{8,12},{9,13},{1... | collective-permute-start | bytes 196616 | tf_op jit(solution)/shard_map/ppermute | solution.py:341

commit v6 on v5

v6 whole, which is shorter than its diff:
```python
import functools
import jax
import jax.numpy as jnp
from jax import lax
from jax.experimental import pallas as pl
from jax.experimental.pallas import tpu as pltpu
from jax.sharding import PartitionSpec as P

floor_power = 30.0

LOOK = 21
LANES = 128
TILE = 16
PER = LANES // LOOK
SPAN = PER * LOOK
ROWS = 8
SKEW = (5, 0, 1, 2, 3, 4, 1, 2)
BEFORE, AFTER = 3, 2
NT = (((1,), (1,)), ((), ()))


def turned(image, mask, skew, columns, put):
    count = image[0].shape[0]
    zero = jnp.zeros((count, LANES), jnp.bfloat16)
    lane = lax.broadcasted_iota(jnp.int32, (1, LANES), 1)

    def tile(value, g):
        start, stop = g * LANES, min((g + 1) * LANES, columns)
        part = value[:, start:stop]
        if stop - start < LANES:
            rest = jnp.zeros((part.shape[0], LANES - (stop - start)), part.dtype)
            part = jnp.concatenate([part, rest], axis=1)
        return part

    def widened(which):
        return jnp.broadcast_to(which.astype(jnp.float32), (count, LANES)).astype(jnp.bfloat16) != 0

    tiles = -(-columns // LANES)
    for g in range(-(-columns // SPAN)):
        slide = (LANES - SPAN) * g
        place = (lane + slide) % LANES
        used = (place < SPAN) & (SPAN * g + place < columns)
        prior = lane >= LANES - slide
        sides = [t for t in (g - 1, g) if 0 <= t < tiles]

        def joined(value):
            parts = [tile(value, t) for t in sides]
            if len(parts) == 1:
                return parts[0]
            which = prior if value.shape[0] == 1 else widened(prior)
            return jnp.where(which, parts[0], parts[1])

        keep = widened(used & (joined(mask) != 0))
        for k in range(2):
            row = jnp.where(keep, joined(image[k]), zero)
            put(g, k, pltpu.roll(row, slide + LOOK * skew, 1))


def fetched(image_ref, mask_ref, rows_ref, masks_ref, sems, order):
    mask_copy = pltpu.make_async_copy(mask_ref, masks_ref, sems.at[len(order)])
    mask_copy.start()
    copies = [pltpu.make_async_copy(image_ref.at[row], rows_ref.at[at], sems.at[at]) for at, row in enumerate(order)]
    for copy in copies:
        copy.start()
    mask_copy.wait()
    return copies


EDGE = tuple(range(AFTER)) + tuple(range(ROWS - BEFORE, ROWS))


def edge_kernel(image_ref, mask_ref, top_ref, low_ref, rows_ref, masks_ref, turned_ref, in_sems, out_sems):
    fetches = fetched(image_ref, mask_ref, rows_ref, masks_ref, in_sems, EDGE)
    stores = []
    for at, row in enumerate(EDGE):
        fetches[at].wait()

        def put(g, k, value):
            turned_ref[at, g, k] = value

        turned([rows_ref.at[at, 0], rows_ref.at[at, 1]], masks_ref[row : row + 1, :], SKEW[row], masks_ref.shape[1], put)
        target = top_ref.at[row] if row < AFTER else low_ref.at[row - (ROWS - BEFORE)]
        store = pltpu.make_async_copy(turned_ref.at[at], target, out_sems.at[at])
        store.start()
        stores.append(store)
    for store in stores:
        store.wait()


def rows_shape(rows, groups, count):
    return jax.ShapeDtypeStruct((rows, groups, 2, count, LANES), jnp.bfloat16)


def edge_rows(images, valid_mask, groups):
    count = images.shape[2]
    far = pl.BlockSpec(memory_space=pl.ANY)
    return pl.pallas_call(
        edge_kernel,
        in_specs=[far, far],
        out_specs=[far, far],
        out_shape=[rows_shape(AFTER, groups, count), rows_shape(BEFORE, groups, count)],
        scratch_shapes=[
            pltpu.VMEM((len(EDGE),) + images.shape[1:], jnp.bfloat16),
            pltpu.VMEM(valid_mask.shape, jnp.int32),
            pltpu.VMEM((len(EDGE), groups, 2, count, LANES), jnp.bfloat16),
            pltpu.SemaphoreType.DMA((len(EDGE) + 1,)),
            pltpu.SemaphoreType.DMA((len(EDGE),)),
        ],
        compiler_params=pltpu.CompilerParams(vmem_limit_bytes=61 * 2**20),
        cost_estimate=pl.CostEstimate(flops=10**6, bytes_accessed=4 * 10**6, transcendentals=0),
        name="edge_rows",
    )(images, valid_mask)


def middle_kernel(image_ref, mask_ref, edge_ref, mid_ref, gram_ref, rows_ref, masks_ref, turned_ref, z_ref, in_sems, out_sems):
    groups = mid_ref.shape[1]
    count, columns = image_ref.shape[2:]
    order = tuple(range(AFTER, ROWS - BEFORE)) + EDGE
    fetches = fetched(image_ref, mask_ref, rows_ref, masks_ref, in_sems, order)
    z_ref[...] = jnp.zeros_like(z_ref)
    zero = jnp.zeros((count, columns), jnp.bfloat16)
    stores = []
    total = None
    wide = groups * LANES
    for at, row in enumerate(order):
        fetches[at].wait()
        mask = masks_ref[row : row + 1, :]
        if AFTER <= row < ROWS - BEFORE:

            def put(g, k, value):
                turned_ref[at, g, k] = value
                z_ref[pl.ds(k * LANES, count), pl.ds(at * wide + g * LANES, LANES)] = value

            turned([rows_ref.at[at, 0], rows_ref.at[at, 1]], mask, SKEW[row], columns, put)
            store = pltpu.make_async_copy(turned_ref.at[at], mid_ref.at[row - AFTER], out_sems.at[at])
            store.start()
            stores.append(store)
        else:
            keep = jnp.broadcast_to((mask != 0).astype(jnp.float32), (count, columns)).astype(jnp.bfloat16) != 0
            for k in range(2):
                z_ref[pl.ds(k * LANES, count), pl.ds(at * wide, columns)] = jnp.where(keep, rows_ref[at, k], zero)
        if at % 2:
            z = z_ref[:, pl.ds((at - 1) * wide, 2 * wide)]
            part = lax.dot_general(z, z, NT, preferred_element_type=jnp.float32)
            total = part if total is None else total + part
    real = total[:LANES, :LANES] + total[LANES:, LANES:]
    imag = total[LANES:, :LANES] - total[:LANES, LANES:]
    i = lax.broadcasted_iota(jnp.int32, real.shape, 0)
    j = lax.broadcasted_iota(jnp.int32, real.shape, 1)
    gram_ref[...] = jnp.where(i <= j, real, imag)
    for store in stores:
        store.wait()


def middle_rows(images, valid_mask, low):
    count = images.shape[2]
    groups = low.shape[1]
    rows = ROWS - AFTER - BEFORE
    far = pl.BlockSpec(memory_space=pl.ANY)
    return pl.pallas_call(
        middle_kernel,
        in_specs=[far, far, far],
        out_specs=[far, pl.BlockSpec(memory_space=pltpu.VMEM)],
        out_shape=[rows_shape(rows, groups, count), jax.ShapeDtypeStruct((LANES, LANES), jnp.float32)],
        scratch_shapes=[
            pltpu.VMEM(images.shape, jnp.bfloat16),
            pltpu.VMEM(valid_mask.shape, jnp.int32),
            pltpu.VMEM((rows, groups, 2, count, LANES), jnp.bfloat16),
            pltpu.VMEM((2 * LANES, ROWS * groups * LANES), jnp.bfloat16),
            pltpu.SemaphoreType.DMA((ROWS + 1,)),
            pltpu.SemaphoreType.DMA((rows,)),
        ],
        compiler_params=pltpu.CompilerParams(vmem_limit_bytes=61 * 2**20),
        cost_estimate=pl.CostEstimate(flops=10**9, bytes_accessed=5 * 10**6, transcendentals=0),
        name="middle_rows",
    )(images, valid_mask, low)


def added(terms):
    if len(terms) == 4:
        return (terms[0] + terms[2]) + (terms[1] + terms[3])
    return functools.reduce(jnp.add, terms)


def slab_values(terms):
    packed = added(terms)
    flipped = packed.T
    i = lax.broadcasted_iota(jnp.int32, packed.shape, 0)
    j = lax.broadcasted_iota(jnp.int32, packed.shape, 1)
    real = jnp.where(i <= j, packed, flipped)
    imag = jnp.where(i > j, packed, jnp.where(i < j, -flipped, 0.0))
    powers = jnp.where(i == j, packed, 0.0)
    scaled = jnp.sqrt(jnp.sum(powers, axis=1, keepdims=True) * jnp.sum(powers, axis=0, keepdims=True))
    return real / scaled, imag / scaled


INNER = (1, 2, 3, 4, 5)
HALVES = (
    ((-3, -2, -1, 0), (((1, 2, 3), None), (None, (-1, 0)))),
    ((6, 7, 8, 9), ((None, (6, 7)), ((3, 4, 5), None))),
)


def looks_kernel(half, aliased, terms, slab, *refs):
    other_ref, top_ref, mid_ref, low_ref = refs[:4]
    refs = refs[4 + aliased :]
    term_refs, refs = refs[:terms], refs[terms:]
    out_ref, extra_ref, w_ref = refs
    count = top_ref.shape[3]

    @pl.when(pl.program_id(0) == 0)
    def _():
        w_ref[...] = jnp.zeros_like(w_ref)
        if slab:
            real, imag = slab_values([t[...] for t in term_refs])
            extra_ref[0] = real[:count, :count]
            extra_ref[1] = imag[:count, :count]
        elif terms:
            extra_ref[...] = added([t[...] for t in term_refs])
        else:
            extra_ref[...] = jnp.zeros_like(extra_ref)

    rows = {}
    for r in range(ROWS):
        if r < AFTER:
            rows[r] = top_ref.at[r, 0]
        elif r >= ROWS - BEFORE:
            rows[r] = low_ref.at[r - (ROWS - BEFORE), 0]
        else:
            rows[r] = mid_ref.at[r - AFTER, 0]
    for r in range(other_ref.shape[0]):
        rows[ROWS + r if half else r - BEFORE] = other_ref.at[r, 0]

    lane = lax.broadcasted_iota(jnp.int32, (1, LANES), 1)

    def lanes_of(turn):
        place = lane + (-LOOK * turn) % LANES
        place = jnp.where(place >= LANES, place - LANES, place)
        return place < LOOK

    def widened(which):
        return jnp.broadcast_to(which.astype(jnp.float32), (count, LANES)).astype(jnp.bfloat16) != 0

    single = [lanes_of(t) for t in range(2 * PER - 1)]
    wide = [widened(s) for s in single]

    def turn(l, r):
        return l + SKEW[r % ROWS]

    def gathered(l, k, which):
        out = rows[which[0]][k]
        for r in which[1:]:
            out = jnp.where(wide[turn(l, r)], rows[r][k], out)
        return out

    def kept(l, which):
        select = single[turn(l, which[0])]
        for r in which[1:]:
            select = select | single[turn(l, r)]
        return select.astype(jnp.float32)

    eight = (8, LANES)
    along = lax.broadcasted_iota(jnp.int32, eight, 1)
    on_eye = along % 8 == lax.broadcasted_iota(jnp.int32, eight, 0)
    block = along // 8

    def normalised(real, imag, w, l):
        picked = real[:8]
        for v in range(1, count // 8):
            picked = jnp.where(block == v, real[8 * v : 8 * v + 8], picked)
        power = jnp.sum(jnp.where(on_eye, picked, 0.0), axis=0, keepdims=True)
        across = lax.rsqrt(jnp.maximum(power, floor_power))
        diagonal = jnp.where(on_eye, across, 0.0)
        spread = jnp.concatenate([jnp.where(block == v, diagonal, 0.0) for v in range(count // 8)], axis=0)
        scale = jnp.sum(spread, axis=1, keepdims=True) * across
        out_ref[w, l, 0] = (real * scale).astype(jnp.bfloat16)[:, :count]
        out_ref[w, l, 1] = (imag * scale).astype(jnp.bfloat16)[:, :count]

    outer_rows, windows = HALVES[half]
    for l in range(PER):
        slot = l % 2
        for k in range(2):
            w_ref[slot, k, pl.ds(0, count), pl.ds(0, LANES)] = gathered(l, k, INNER)
            w_ref[slot, k, pl.ds(0, count), pl.ds(LANES, LANES)] = gathered(l, k, outer_rows)
        every = w_ref[slot].reshape(2 * LANES, 2 * LANES)
        nothing = jnp.zeros_like(every)
        reads = []
        for inner_rows, rest_rows in windows:
            lanes = jnp.concatenate([kept(l, inner_rows or INNER), kept(l, rest_rows or outer_rows)], axis=1)
            lanes = jnp.broadcast_to(lanes, every.shape).astype(jnp.bfloat16) != 0
            read = jnp.where(lanes, every, nothing)
            for start in range(0, LANES, TILE):
                reads.append(read[start : start + TILE])
                reads.append(read[LANES + start : LANES + start + TILE])
        gram = lax.dot_general(jnp.concatenate(reads, axis=0), every, NT, preferred_element_type=jnp.float32)
        for w in range(2):
            real, imag = [], []
            for start in range(0, LANES, TILE):
                base = 2 * (w * LANES + start)
                re, im = gram[base : base + TILE], gram[base + TILE : base + 2 * TILE]
                real.append(re[:, :LANES] + im[:, LANES:])
                imag.append(im[:, :LANES] - re[:, LANES:])
            normalised(jnp.concatenate(real, axis=0)[:count], jnp.concatenate(imag, axis=0)[:count], w, l)


def looked(half, other, top, mid, low, first, groups, looks, previous, terms, slab):
    count = other.shape[3]

    def spec(array):
        return pl.BlockSpec((array.shape[0], 1) + array.shape[2:], lambda s: (0, s + first, 0, 0, 0))

    operands = [other, top, mid, low]
    in_specs = [spec(a) for a in operands]
    aliases = {}
    if previous is not None:
        aliases = {len(operands): 0}
        operands.append(previous)
        in_specs.append(pl.BlockSpec(memory_space=pl.ANY))
    for term in terms:
        operands.append(term)
        in_specs.append(pl.BlockSpec(term.shape, lambda s: (0, 0)))
    extra = (2, count, count) if slab else (LANES, LANES)
    out_specs = [
        pl.BlockSpec((2, PER, 2, count, count), lambda s: (half, s + first, 0, 0, 0)),
        pl.BlockSpec(extra, lambda s: (0,) * len(extra)),
    ]
    out_shape = [
        jax.ShapeDtypeStruct((ROWS // 2, looks, 2, count, count), jnp.bfloat16),
        jax.ShapeDtypeStruct(extra, jnp.float32),
    ]
    return pl.pallas_call(
        functools.partial(looks_kernel, half, previous is not None, len(terms), slab),
        grid=(groups,),
        in_specs=in_specs,
        out_specs=out_specs,
        out_shape=out_shape,
        input_output_aliases=aliases,
        scratch_shapes=[
            pltpu.VMEM((2, 2, LANES, 2 * LANES), jnp.bfloat16),
        ],
        compiler_params=pltpu.CompilerParams(vmem_limit_bytes=51 * 2**20),
        cost_estimate=pl.CostEstimate(
            flops=20 * groups * PER * 2 * 512 * 256 * 256, bytes_accessed=groups * 10**6, transcendentals=0
        ),
        name="looks",
    )(*operands)


def rounds(size):
    found = []
    stride = 1
    while stride < size:
        radix = 4 if size // stride % 4 == 0 else 2
        if size // stride % radix:
            return None
        found.append((stride, radix))
        stride *= radix
    return found[::-1]


def round_terms(value, axis, stride, radix):
    size = lax.axis_size(axis)
    terms = [value]
    for shift in range(1, radix):
        pairs = []
        for i in range(size):
            place = (i // stride) % radix
            pairs.append((i, i + ((place + shift) % radix - place) * stride))
        terms.append(lax.ppermute(value, axis, pairs))
    return terms


def shards(images, valid_mask):
    looks = images.shape[3] // LOOK
    groups = -(-looks // PER)
    cut = -(-groups // 2)
    size = lax.axis_size("pix")
    forward = [(i, i + 1) for i in range(size - 1)]
    backward = [(i + 1, i) for i in range(size - 1)]
    top, low = edge_rows(images, valid_mask, groups)
    after = lax.ppermute(top, "pix", backward)
    before = lax.ppermute(low, "pix", forward)
    mid, total = middle_rows(images, valid_mask, low)
    steps = rounds(size)
    if steps is None:
        terms, steps = [lax.psum(total, "pix")], []
    else:
        terms = round_terms(total, "pix", *steps[0]) if steps else [total]
    out, total = looked(1, after, top, mid, low, 0, groups, looks, None, terms, False)
    terms = [total]
    for step in steps[1:]:
        terms = round_terms(added(terms), "pix", *step)
    out, _ = looked(0, before, top, mid, low, 0, cut, looks, out, [], False)
    out, slab = looked(0, before, top, mid, low, cut, groups - cut, looks, out, terms, True)
    return (out, slab)


def solution(mesh):
    in_specs = (P(("group", "pix"), None, None, None), P(("group", "pix"), None))
    out_specs = (P(("group", "pix"), None, None, None, None), P("group", None, None))
    return jax.shard_map(shards, mesh=mesh, in_specs=in_specs, out_specs=out_specs, check_vma=False)
```

time: 51.7 us -> 50 us (0.967)
  the two profiles are of different devices: /device:TPU:0 before, /device:TPU:1 now
where the time goes in v6:
time: 50 us; the launch traced here: 49.5 us
  Pallas kernels  27.7 us (55%)
  starting transfers between devices  18.5 us (37%)
  waiting for transfers between devices  1.73 us (3%)
  local copies, waits for them, and re-layouts  0.85 us (2%)
  between operations  0.72 us (1%)
    pallas_call x3, Pallas kernels, looked(): pl.pallas_call(functools.partial(looks_kernel, half, previous is not None...  19.9 us
    ppermute x6, starting transfers between devices, round_terms(): terms.append(lax.ppermute(value, axis, pairs))  12.5 us
    pallas_call x1, Pallas kernels, middle_rows(): pl.pallas_call(middle_kernel, in_specs=[far, far, far], out_specs=[far, p...  4.93 us
    ppermute x1, starting transfers between devices, shards(): before = lax.ppermute(low, 'pix', forward)  3.84 us
    pallas_call x1, Pallas kernels, edge_rows(): pl.pallas_call(edge_kernel, in_specs=[far, far], out_specs=[far, far], ou...  2.86 us
    ppermute x1, starting transfers between devices, shards(): after = lax.ppermute(top, 'pix', backward)  2.1 us
    ppermute x6, waiting for transfers between devices, round_terms(): terms.append(lax.ppermute(value, axis, pairs))  1.73 us
  transfers between devices with their start and end apart: 8, of which 1 were waited for; matrix products, arithmetic and copies ran while one was open for 0% of the time, Pallas kernels for 40%

profile of v6, /device:TPU:1, one launch (start us, length us, event | category | flops | bytes accessed | tf_op | source)
XLA Modules:
  0.0 49.5 jit_solution(8494692099927743025)
XLA Ops:
  0.6 2.9 %edge_rows.1 = (bf16[2,7,2,120,128]{4,3,2,1,0:T(8,128)(2,1)}, bf16[3,7,2,120,128]{4,3,2,1,0:T(8,128)(2,1)}) custom-call(bf16[8,2,120,840]{3,2,1,0:T(8,128)(2,1)} %image_ref.3, s32[8,840]{1,0:T(8,128)} %mask_ref.3), custom_call_target="tpu_custom_call" | custom-call | flops 1000000 | bytes 4000000 | tf_op jit(solution)/shard_map/edge_rows/pallas_call | solution.py:97
  3.5 0.0 copy-start
  3.5 2.1 %collective-permute-start.1 = (bf16[2,7,2,120,128]{4,3,2,1,0:T(8,128)(2,1)}, bf16[2,7,2,120,128]{4,3,2,1,0:T(8,128)(2,1)S(1)}, u32[]{:S(2)}, u32[]{:S(2)}) collective-permute-start(bf16[2,7,2,120,128]{4,3,2,1,0:T(8,128)(2,1)} %get-tuple-element.10.refs_1_), channel_id=1, source_target_pairs={{1,0},{2,1},{3,2},{4,3},{5,4},{6,5},{7,6},{8,7},{9,8},{10,9},{11,1... | collective-permute-start | bytes 2580488 | tf_op jit(solution)/shard_map/ppermute | solution.py:381
  5.6 4.9 %middle_rows.1 = (bf16[3,7,2,120,128]{4,3,2,1,0:T(8,128)(2,1)}, f32[128,128]{1,0:T(8,128)}) custom-call(bf16[8,2,120,840]{3,2,1,0:T(8,128)(2,1)} %image_ref.3, s32[8,840]{1,0:T(8,128)} %mask_ref.3, bf16[3,7,2,120,128]{4,3,2,1,0:T(8,128)(2,1)} %get-tuple-element.9.edge_ref.refs_3_), custom_call_target="tpu_custom_call" | custom-call | flops 1000000000 | bytes 5000000 | tf_op jit(solution)/shard_map/middle_rows/pallas_call | solution.py:160
  10.6 4.8 %collective-permute-start.4 = (f32[128,128]{1,0:T(8,128)}, f32[128,128]{1,0:T(8,128)S(1)}, u32[]{:S(2)}, u32[]{:S(2)}) collective-permute-start(f32[128,128]{1,0:T(8,128)} %get-tuple-element.12.refs_4_), channel_id=1, source_target_pairs={{0,12},{1,13},{2,14},{3,15},{4,0},{5,1},{6,2},{7,3},{8,4},{9,5},{1... | collective-permute-start | bytes 196616 | tf_op jit(solution)/shard_map/ppermute | solution.py:369
  15.4 0.0 collective-permute-start.3
  15.4 0.5 collective-permute-start.2
  15.8 3.8 %collective-permute-start = (bf16[3,7,2,120,128]{4,3,2,1,0:T(8,128)(2,1)S(1)}, bf16[3,7,2,120,128]{4,3,2,1,0:T(8,128)(2,1)S(1)}, u32[]{:S(2)}, u32[]{:S(2)}) collective-permute-start(bf16[3,7,2,120,128]{4,3,2,1,0:T(8,128)(2,1)S(1)} %copy-done.2), channel_id=1, source_target_pairs={{0,1},{1,2},{2,3},{3,4},{4,5},{5,6},{6,7},{7,8},{8,9},{9,10},{10,1... | collective-permute-start | bytes 3870728 | tf_op jit(solution)/shard_map/ppermute | solution.py:382
  19.7 0.0 collective-permute-done.4.refs_7_
  19.7 1.7 %collective-permute-done.3.refs_6_ = f32[128,128]{1,0:T(8,128)S(1)} collective-permute-done((f32[128,128]{1,0:T(8,128)}, f32[128,128]{1,0:T(8,128)S(1)}, u32[]{:S(2)}, u32[]{:S(2)}) %collective-permute-start.3) | collective-permute-done | bytes 65568 | tf_op jit(solution)/shard_map/ppermute | solution.py:369
  21.4 0.0 collective-permute-done.2.refs_5_
  21.4 0.0 collective-permute-done.1.refs_0_
  21.4 0.0 copy-start.1
  21.4 0.8 %copy-done.1 = f32[128,128]{1,0:T(8,128)S(1)} copy-done((f32[128,128]{1,0:T(8,128)S(1)}, f32[128,128]{1,0:T(8,128)}, u32[]{:S(2)}) %copy-start.1) | copy-done | bytes 65560
  22.3 9.1 %looks.3 = (bf16[4,40,2,120,120]{4,3,2,1,0:T(8,128)(2,1)}, f32[128,128]{1,0:T(8,128)S(1)}) custom-call(bf16[2,7,2,120,128]{4,3,2,1,0:T(8,128)(2,1)S(1)} %collective-permute-done.1.refs_0_, bf16[2,7,2,120,128]{4,3,2,1,0:T(8,128)(2,1)S(1)} %copy-done, bf16[3,7,2,120,128]{4,3,2,1,0:T(8,128)(2,1)} %get-tuple-element.11.refs_2_, ...), custom_call_target="tpu_custom_call" | custom-call | flops 56371445760 | bytes 7000000 | tf_op jit(solution)/shard_map/looks/pallas_call | solution.py:331
  31.4 5.6 %collective-permute-start.7 = (f32[128,128]{1,0:T(8,128)S(1)}, f32[128,128]{1,0:T(8,128)S(1)}, u32[]{:S(2)}, u32[]{:S(2)}) collective-permute-start(f32[128,128]{1,0:T(8,128)S(1)} %get-tuple-element.15.refs_5_), channel_id=1, source_target_pairs={{0,3},{1,0},{2,1},{3,2},{4,7},{5,4},{6,5},{7,6},{8,11},{9,8},{10,9... | collective-permute-start | bytes 196616 | tf_op jit(solution)/shard_map/ppermute | solution.py:369
  37.0 0.0 collective-permute-start.6
  37.0 1.6 %collective-permute-start.5 = (f32[128,128]{1,0:T(8,128)S(1)}, f32[128,128]{1,0:T(8,128)S(1)}, u32[]{:S(2)}, u32[]{:S(2)}) collective-permute-start(f32[128,128]{1,0:T(8,128)S(1)} %get-tuple-element.15.refs_5_), channel_id=1, source_target_pairs={{0,1},{1,2},{2,3},{3,0},{4,5},{5,6},{6,7},{7,4},{8,9},{9,10},{10,1... | collective-permute-start | bytes 196616 | tf_op jit(solution)/shard_map/ppermute | solution.py:369
  38.6 0.0 collective-permute-done.refs_0_
  38.6 5.9 %looks.4 = (bf16[4,40,2,120,120]{4,3,2,1,0:T(8,128)(2,1)}, f32[128,128]{1,0:T(8,128)}) custom-call(bf16[3,7,2,120,128]{4,3,2,1,0:T(8,128)(2,1)S(1)} %collective-permute-done.refs_0_, bf16[2,7,2,120,128]{4,3,2,1,0:T(8,128)(2,1)S(1)} %copy-done, bf16[3,7,2,120,128]{4,3,2,1,0:T(8,128)(2,1)} %get-tuple-element.11.refs_2_, ...), custom_call_target="tpu_custom_call", output_to_operand_aliasing={{0}: (4, {})} | custom-call | flops 32212254720 | bytes 4000000 | tf_op jit(solution)/shard_map/looks/pallas_call | solution.py:331
  44.5 0.0 collective-permute-done.7.refs_8_
  44.5 0.0 collective-permute-done.6.refs_7_
  44.5 0.0 collective-permute-done.5.refs_6_
  44.5 5.0 %looks.5 = (bf16[4,40,2,120,120]{4,3,2,1,0:T(8,128)(2,1)}, f32[2,120,120]{2,1,0:T(8,128)}) custom-call(bf16[3,7,2,120,128]{4,3,2,1,0:T(8,128)(2,1)S(1)} %collective-permute-done.refs_0_, bf16[2,7,2,120,128]{4,3,2,1,0:T(8,128)(2,1)S(1)} %copy-done, bf16[3,7,2,120,128]{4,3,2,1,0:T(8,128)(2,1)} %get-tuple-element.11.refs_2_, ...), custom_call_target="tpu_custom_call", output_to_operand_aliasing={{0}: (4, {})} | custom-call | flops 24159191040 | bytes 3000000 | tf_op jit(solution)/shard_map/looks/pallas_call | solution.py:331
  (3 shorter events, 0.0 us)
Async XLA Ops:
  3.5 12.3 %copy-start.2 = (bf16[3,7,2,120,128]{4,3,2,1,0:T(8,128)(2,1)S(1)}, bf16[3,7,2,120,128]{4,3,2,1,0:T(8,128)(2,1)}, u32[]{:S(2)}) copy-start(bf16[3,7,2,120,128]{4,3,2,1,0:T(8,128)(2,1)} %get-tuple-element.9.edge_ref.refs_3_) | copy-start | bytes 3870724
  3.5 17.9 %copy-start = (bf16[2,7,2,120,128]{4,3,2,1,0:T(8,128)(2,1)S(1)}, bf16[2,7,2,120,128]{4,3,2,1,0:T(8,128)(2,1)}, u32[]{:S(2)}) copy-start(bf16[2,7,2,120,128]{4,3,2,1,0:T(8,128)(2,1)} %get-tuple-element.10.refs_1_) | copy-start | bytes 2580484
  3.5 17.9 %collective-permute-start.1 = (bf16[2,7,2,120,128]{4,3,2,1,0:T(8,128)(2,1)}, bf16[2,7,2,120,128]{4,3,2,1,0:T(8,128)(2,1)S(1)}, u32[]{:S(2)}, u32[]{:S(2)}) collective-permute-start(bf16[2,7,2,120,128]{4,3,2,1,0:T(8,128)(2,1)} %get-tuple-element.10.refs_1_), channel_id=1, source_target_pairs={{1,0},{2,1},{3,2},{4,3},{5,4},{6,5},{7,6},{8,7},{9,8},{10,9},{11,1... | collective-permute-start | bytes 2580488 | tf_op jit(solution)/shard_map/ppermute | solution.py:381
  10.6 9.1 %collective-permute-start.4 = (f32[128,128]{1,0:T(8,128)}, f32[128,128]{1,0:T(8,128)S(1)}, u32[]{:S(2)}, u32[]{:S(2)}) collective-permute-start(f32[128,128]{1,0:T(8,128)} %get-tuple-element.12.refs_4_), channel_id=1, source_target_pairs={{0,12},{1,13},{2,14},{3,15},{4,0},{5,1},{6,2},{7,3},{8,4},{9,5},{1... | collective-permute-start | bytes 196616 | tf_op jit(solution)/shard_map/ppermute | solution.py:369
  15.4 6.0 %collective-permute-start.3 = (f32[128,128]{1,0:T(8,128)}, f32[128,128]{1,0:T(8,128)S(1)}, u32[]{:S(2)}, u32[]{:S(2)}) collective-permute-start(f32[128,128]{1,0:T(8,128)} %get-tuple-element.12.refs_4_), channel_id=1, source_target_pairs={{0,8},{1,9},{2,10},{3,11},{4,12},{5,13},{6,14},{7,15},{8,0},{9,1},... | collective-permute-start | bytes 196616 | tf_op jit(solution)/shard_map/ppermute | solution.py:369
  15.4 6.0 %collective-permute-start.2 = (f32[128,128]{1,0:T(8,128)}, f32[128,128]{1,0:T(8,128)S(1)}, u32[]{:S(2)}, u32[]{:S(2)}) collective-permute-start(f32[128,128]{1,0:T(8,128)} %get-tuple-element.12.refs_4_), channel_id=1, source_target_pairs={{0,4},{1,5},{2,6},{3,7},{4,8},{5,9},{6,10},{7,11},{8,12},{9,13},{1... | collective-permute-start | bytes 196616 | tf_op jit(solution)/shard_map/ppermute | solution.py:369
  15.8 22.8 %collective-permute-start = (bf16[3,7,2,120,128]{4,3,2,1,0:T(8,128)(2,1)S(1)}, bf16[3,7,2,120,128]{4,3,2,1,0:T(8,128)(2,1)S(1)}, u32[]{:S(2)}, u32[]{:S(2)}) collective-permute-start(bf16[3,7,2,120,128]{4,3,2,1,0:T(8,128)(2,1)S(1)} %copy-done.2), channel_id=1, source_target_pairs={{0,1},{1,2},{2,3},{3,4},{4,5},{5,6},{6,7},{7,8},{8,9},{9,10},{10,1... | collective-permute-start | bytes 3870728 | tf_op jit(solution)/shard_map/ppermute | solution.py:382
  21.4 0.8 %copy-start.1 = (f32[128,128]{1,0:T(8,128)S(1)}, f32[128,128]{1,0:T(8,128)}, u32[]{:S(2)}) copy-start(f32[128,128]{1,0:T(8,128)} %get-tuple-element.12.refs_4_) | copy-start | bytes 196612
  31.4 13.1 %collective-permute-start.7 = (f32[128,128]{1,0:T(8,128)S(1)}, f32[128,128]{1,0:T(8,128)S(1)}, u32[]{:S(2)}, u32[]{:S(2)}) collective-permute-start(f32[128,128]{1,0:T(8,128)S(1)} %get-tuple-element.15.refs_5_), channel_id=1, source_target_pairs={{0,3},{1,0},{2,1},{3,2},{4,7},{5,4},{6,5},{7,6},{8,11},{9,8},{10,9... | collective-permute-start | bytes 196616 | tf_op jit(solution)/shard_map/ppermute | solution.py:369
  37.0 7.5 %collective-permute-start.6 = (f32[128,128]{1,0:T(8,128)S(1)}, f32[128,128]{1,0:T(8,128)S(1)}, u32[]{:S(2)}, u32[]{:S(2)}) collective-permute-start(f32[128,128]{1,0:T(8,128)S(1)} %get-tuple-element.15.refs_5_), channel_id=1, source_target_pairs={{0,2},{1,3},{2,0},{3,1},{4,6},{5,7},{6,4},{7,5},{8,10},{9,11},{10,... | collective-permute-start | bytes 196616 | tf_op jit(solution)/shard_map/ppermute | solution.py:369
  37.0 7.5 %collective-permute-start.5 = (f32[128,128]{1,0:T(8,128)S(1)}, f32[128,128]{1,0:T(8,128)S(1)}, u32[]{:S(2)}, u32[]{:S(2)}) collective-permute-start(f32[128,128]{1,0:T(8,128)S(1)} %get-tuple-element.15.refs_5_), channel_id=1, source_target_pairs={{0,1},{1,2},{2,3},{3,0},{4,5},{5,6},{6,7},{7,4},{8,9},{9,10},{10,1... | collective-permute-start | bytes 196616 | tf_op jit(solution)/shard_map/ppermute | solution.py:369

commit v7 on v6

--- a/solution.py
+++ b/solution.py
@@ -69,7 +69,7 @@
 EDGE = tuple(range(AFTER)) + tuple(range(ROWS - BEFORE, ROWS))
 
 
-def edge_kernel(image_ref, mask_ref, top_ref, low_ref, rows_ref, masks_ref, turned_ref, in_sems, out_sems):
+def edge_kernel(image_ref, mask_ref, top_ref, low_ref, _, rows_ref, masks_ref, turned_ref, in_sems, out_sems):
     fetches = fetched(image_ref, mask_ref, rows_ref, masks_ref, in_sems, EDGE)
     stores = []
     for at, row in enumerate(EDGE):
@@ -97,8 +97,12 @@
     return pl.pallas_call(
         edge_kernel,
         in_specs=[far, far],
-        out_specs=[far, far],
-        out_shape=[rows_shape(AFTER, groups, count), rows_shape(BEFORE, groups, count)],
+        out_specs=[far] * 3,
+        out_shape=[
+            rows_shape(AFTER, groups, count),
+            rows_shape(BEFORE, groups, count),
+            jax.ShapeDtypeStruct((8, LANES), jnp.float32),
+        ],
         scratch_shapes=[
             pltpu.VMEM((len(EDGE),) + images.shape[1:], jnp.bfloat16),
             pltpu.VMEM(valid_mask.shape, jnp.int32),
@@ -112,7 +116,7 @@
     )(images, valid_mask)
 
 
-def middle_kernel(image_ref, mask_ref, edge_ref, mid_ref, gram_ref, rows_ref, masks_ref, turned_ref, z_ref, in_sems, out_sems):
+def middle_kernel(image_ref, mask_ref, _, mid_ref, gram_ref, rows_ref, masks_ref, turned_ref, z_ref, in_sems, out_sems):
     groups = mid_ref.shape[1]
     count, columns = image_ref.shape[2:]
     order = tuple(range(AFTER, ROWS - BEFORE)) + EDGE
@@ -152,9 +156,8 @@
         store.wait()
 
 
-def middle_rows(images, valid_mask, low):
+def middle_rows(images, valid_mask, groups, behind):
     count = images.shape[2]
-    groups = low.shape[1]
     rows = ROWS - AFTER - BEFORE
     far = pl.BlockSpec(memory_space=pl.ANY)
     return pl.pallas_call(
@@ -170,10 +173,10 @@
             pltpu.SemaphoreType.DMA((ROWS + 1,)),
             pltpu.SemaphoreType.DMA((rows,)),
         ],
-        compiler_params=pltpu.CompilerParams(vmem_limit_bytes=61 * 2**20),
+        compiler_params=pltpu.CompilerParams(vmem_limit_bytes=52 * 2**20),
         cost_estimate=pl.CostEstimate(flops=10**9, bytes_accessed=5 * 10**6, transcendentals=0),
         name="middle_rows",
-    )(images, valid_mask, low)
+    )(images, valid_mask, behind)
 
 
 def added(terms):
@@ -338,7 +341,7 @@
         scratch_shapes=[
             pltpu.VMEM((2, 2, LANES, 2 * LANES), jnp.bfloat16),
         ],
-        compiler_params=pltpu.CompilerParams(vmem_limit_bytes=51 * 2**20),
+        compiler_params=pltpu.CompilerParams(vmem_limit_bytes=48 * 2**20),
         cost_estimate=pl.CostEstimate(
             flops=20 * groups * PER * 2 * 512 * 256 * 256, bytes_accessed=groups * 10**6, transcendentals=0
         ),
@@ -377,19 +380,18 @@
     size = lax.axis_size("pix")
     forward = [(i, i + 1) for i in range(size - 1)]
     backward = [(i + 1, i) for i in range(size - 1)]
-    top, low = edge_rows(images, valid_mask, groups)
+    top, low, edge_done = edge_rows(images, valid_mask, groups)
     after = lax.ppermute(top, "pix", backward)
     before = lax.ppermute(low, "pix", forward)
-    mid, total = middle_rows(images, valid_mask, low)
+    mid, total = middle_rows(images, valid_mask, groups, edge_done)
     steps = rounds(size)
     if steps is None:
         terms, steps = [lax.psum(total, "pix")], []
     else:
         terms = round_terms(total, "pix", *steps[0]) if steps else [total]
-    out, total = looked(1, after, top, mid, low, 0, groups, looks, None, terms, False)
-    terms = [total]
+    out, zeros = looked(1, after, top, mid, low, 0, groups, looks, None, [], False)
     for step in steps[1:]:
-        terms = round_terms(added(terms), "pix", *step)
+        terms = round_terms(added(terms) + zeros, "pix", *step)
     out, _ = looked(0, before, top, mid, low, 0, cut, looks, out, [], False)
     out, slab = looked(0, before, top, mid, low, cut, groups - cut, looks, out, terms, True)
     return (out, slab)

time: 50 us -> 46.7 us (0.934)
  the two profiles are of different devices: /device:TPU:1 before, /device:TPU:8 now
where the time goes in v7:
time: 46.7 us; the launch traced here: 46.5 us
  Pallas kernels  23.3 us (50%)
  starting transfers between devices  13.7 us (29%)
  waiting for transfers between devices  8.1 us (17%)
  between operations  0.75 us (2%)
  local copies, waits for them, and re-layouts  0.7 us (1%)
    pallas_call x3, Pallas kernels, looked(): pl.pallas_call(functools.partial(looks_kernel, half, previous is not None...  15.5 us
    ppermute x6, starting transfers between devices, round_terms(): terms.append(lax.ppermute(value, axis, pairs))  8.93 us
    ppermute x1, waiting for transfers between devices, shards(): before = lax.ppermute(low, 'pix', forward)  8.08 us
    pallas_call x1, Pallas kernels, middle_rows(): pl.pallas_call(middle_kernel, in_specs=[far, far, far], out_specs=[far, p...  4.95 us
    ppermute x1, starting transfers between devices, shards(): after = lax.ppermute(top, 'pix', backward)  2.86 us
    pallas_call x1, Pallas kernels, edge_rows(): pl.pallas_call(edge_kernel, in_specs=[far, far], out_specs=[far] * 3, out...  2.84 us
    ppermute x1, starting transfers between devices, shards(): before = lax.ppermute(low, 'pix', forward)  1.91 us
  transfers between devices with their start and end apart: 8, of which 1 were waited for; matrix products, arithmetic and copies ran while one was open for 0% of the time, Pallas kernels for 36%

profile of v7, /device:TPU:8, one launch (start us, length us, event | category | flops | bytes accessed | tf_op | source)
XLA Modules:
  0.0 46.5 jit_solution(11314825088616233410)
XLA Ops:
  0.6 2.8 %edge_rows.1 = (bf16[2,7,2,120,128]{4,3,2,1,0:T(8,128)(2,1)}, bf16[3,7,2,120,128]{4,3,2,1,0:T(8,128)(2,1)}, f32[8,128]{1,0:T(8,128)}) custom-call(bf16[8,2,120,840]{3,2,1,0:T(8,128)(2,1)} %image_ref.3, s32[8,840]{1,0:T(8,128)} %mask_ref.3), custom_call_target="tpu_custom_call" | custom-call | flops 1000000 | bytes 4000000 | tf_op jit(solution)/shard_map/edge_rows/pallas_call | solution.py:97
  3.5 0.0 copy-start.1
  3.5 2.9 %collective-permute-start.1 = (bf16[2,7,2,120,128]{4,3,2,1,0:T(8,128)(2,1)}, bf16[2,7,2,120,128]{4,3,2,1,0:T(8,128)(2,1)S(1)}, u32[]{:S(2)}, u32[]{:S(2)}) collective-permute-start(bf16[2,7,2,120,128]{4,3,2,1,0:T(8,128)(2,1)} %get-tuple-element.11.refs_1_), channel_id=1, source_target_pairs={{1,0},{2,1},{3,2},{4,3},{5,4},{6,5},{7,6},{8,7},{9,8},{10,9},{11,1... | collective-permute-start | bytes 2580488 | tf_op jit(solution)/shard_map/ppermute | solution.py:384
  6.4 0.0 copy-start.3
  6.4 0.7 %copy-done.3 = f32[8,128]{1,0:T(8,128)S(1)} copy-done((f32[8,128]{1,0:T(8,128)S(1)}, f32[8,128]{1,0:T(8,128)}, u32[]{:S(2)}) %copy-start.3) | copy-done | bytes 4120
  7.1 5.0 %middle_rows.1 = (bf16[3,7,2,120,128]{4,3,2,1,0:T(8,128)(2,1)S(1)}, f32[128,128]{1,0:T(8,128)S(1)}) custom-call(bf16[8,2,120,840]{3,2,1,0:T(8,128)(2,1)} %image_ref.3, s32[8,840]{1,0:T(8,128)S(1)} %copy-done, f32[8,128]{1,0:T(8,128)S(1)} %copy-done.3), custom_call_target="tpu_custom_call" | custom-call | flops 1000000000 | bytes 5000000 | tf_op jit(solution)/shard_map/middle_rows/pallas_call | solution.py:163
  12.0 0.1 collective-permute-start.4
  12.1 2.0 %collective-permute-start.3 = (f32[128,128]{1,0:T(8,128)S(1)}, f32[128,128]{1,0:T(8,128)S(1)}, u32[]{:S(2)}, u32[]{:S(2)}) collective-permute-start(f32[128,128]{1,0:T(8,128)S(1)} %get-tuple-element.16), channel_id=1, source_target_pairs={{0,4},{1,5},{2,6},{3,7},{4,8},{5,9},{6,10},{7,11},{8,12},{9,13},{1... | collective-permute-start | bytes 196616 | tf_op jit(solution)/shard_map/ppermute | solution.py:372
  14.1 4.4 %collective-permute-start.2 = (f32[128,128]{1,0:T(8,128)S(1)}, f32[128,128]{1,0:T(8,128)S(1)}, u32[]{:S(2)}, u32[]{:S(2)}) collective-permute-start(f32[128,128]{1,0:T(8,128)S(1)} %get-tuple-element.16), channel_id=1, source_target_pairs={{0,8},{1,9},{2,10},{3,11},{4,12},{5,13},{6,14},{7,15},{8,0},{9,1},... | collective-permute-start | bytes 196616 | tf_op jit(solution)/shard_map/ppermute | solution.py:372
  18.5 1.9 %collective-permute-start = (bf16[3,7,2,120,128]{4,3,2,1,0:T(8,128)(2,1)S(1)}, bf16[3,7,2,120,128]{4,3,2,1,0:T(8,128)(2,1)S(1)}, u32[]{:S(2)}, u32[]{:S(2)}) collective-permute-start(bf16[3,7,2,120,128]{4,3,2,1,0:T(8,128)(2,1)S(1)} %copy-done.1), channel_id=1, source_target_pairs={{0,1},{1,2},{2,3},{3,4},{4,5},{5,6},{6,7},{7,8},{8,9},{9,10},{10,1... | collective-permute-start | bytes 3870728 | tf_op jit(solution)/shard_map/ppermute | solution.py:385
  20.4 0.0 collective-permute-done.1.refs_0_
  20.4 7.2 %looks.3 = (bf16[4,40,2,120,120]{4,3,2,1,0:T(8,128)(2,1)}, f32[128,128]{1,0:T(8,128)S(1)}) custom-call(bf16[2,7,2,120,128]{4,3,2,1,0:T(8,128)(2,1)S(1)} %collective-permute-done.1.refs_0_, bf16[2,7,2,120,128]{4,3,2,1,0:T(8,128)(2,1)S(1)} %copy-done.2, bf16[3,7,2,120,128]{4,3,2,1,0:T(8,128)(2,1)S(1)} %get-tuple-element.13.refs_2_, ...), custom_call_target="tpu_custom_call" | custom-call | flops 56371445760 | bytes 7000000 | tf_op jit(solution)/shard_map/looks/pallas_call | solution.py:334
  27.6 0.0 collective-permute-done.4
  27.6 0.0 collective-permute-done.3
  27.6 0.0 collective-permute-done.2
  27.6 2.2 %collective-permute-start.7 = (f32[128,128]{1,0:T(8,128)S(1)}, f32[128,128]{1,0:T(8,128)S(1)}, u32[]{:S(2)}, u32[]{:S(2)}) collective-permute-start(f32[128,128]{1,0:T(8,128)S(1)} %add_add_fusion.refs_5_), channel_id=1, source_target_pairs={{0,3},{1,0},{2,1},{3,2},{4,7},{5,4},{6,5},{7,6},{8,11},{9,8},{10,9... | collective-permute-start | bytes 196616 | tf_op jit(solution)/shard_map/ppermute | solution.py:372
  29.8 0.3 collective-permute-start.6
  30.1 0.0 collective-permute-start.5
  30.1 8.1 %collective-permute-done.refs_0_ = bf16[3,7,2,120,128]{4,3,2,1,0:T(8,128)(2,1)S(1)} collective-permute-done((bf16[3,7,2,120,128]{4,3,2,1,0:T(8,128)(2,1)S(1)}, bf16[3,7,2,120,128]{4,3,2,1,0:T(8,128)(2,1)S(1)}, u32[]{:S(2)}, u32[]{:S(2)}) %collective-permute-start) | collective-permute-done | bytes 1290272 | tf_op jit(solution)/shard_map/ppermute | solution.py:385
  38.2 4.5 %looks.4 = (bf16[4,40,2,120,120]{4,3,2,1,0:T(8,128)(2,1)}, f32[128,128]{1,0:T(8,128)}) custom-call(bf16[3,7,2,120,128]{4,3,2,1,0:T(8,128)(2,1)S(1)} %collective-permute-done.refs_0_, bf16[2,7,2,120,128]{4,3,2,1,0:T(8,128)(2,1)S(1)} %copy-done.2, bf16[3,7,2,120,128]{4,3,2,1,0:T(8,128)(2,1)S(1)} %get-tuple-element.13.refs_2_, ...), custom_call_target="tpu_custom_call", output_to_operand_aliasing={{0}: (4, {})} | custom-call | flops 32212254720 | bytes 4000000 | tf_op jit(solution)/shard_map/looks/pallas_call | solution.py:334
  42.8 0.0 collective-permute-done.7.refs_8_
  42.8 0.0 collective-permute-done.6.refs_7_
  42.8 0.0 collective-permute-done.5.refs_6_
  42.8 3.7 %looks.5 = (bf16[4,40,2,120,120]{4,3,2,1,0:T(8,128)(2,1)}, f32[2,120,120]{2,1,0:T(8,128)}) custom-call(bf16[3,7,2,120,128]{4,3,2,1,0:T(8,128)(2,1)S(1)} %collective-permute-done.refs_0_, bf16[2,7,2,120,128]{4,3,2,1,0:T(8,128)(2,1)S(1)} %copy-done.2, bf16[3,7,2,120,128]{4,3,2,1,0:T(8,128)(2,1)S(1)} %get-tuple-element.13.refs_2_, ...), custom_call_target="tpu_custom_call", output_to_operand_aliasing={{0}: (4, {})} | custom-call | flops 24159191040 | bytes 3000000 | tf_op jit(solution)/shard_map/looks/pallas_call | solution.py:334
  (6 shorter events, 0.0 us)
Async XLA Ops:
  0.6 5.7 %copy-start = (s32[8,840]{1,0:T(8,128)S(1)}, s32[8,840]{1,0:T(8,128)}, u32[]{:S(2)}) copy-start(s32[8,840]{1,0:T(8,128)} %mask_ref.3) | copy-start | bytes 80644
  3.5 15.0 %copy-start.1 = (bf16[3,7,2,120,128]{4,3,2,1,0:T(8,128)(2,1)S(1)}, bf16[3,7,2,120,128]{4,3,2,1,0:T(8,128)(2,1)}, u32[]{:S(2)}) copy-start(bf16[3,7,2,120,128]{4,3,2,1,0:T(8,128)(2,1)} %get-tuple-element.10.refs_3_) | copy-start | bytes 3870724
  3.5 16.9 %copy-start.2 = (bf16[2,7,2,120,128]{4,3,2,1,0:T(8,128)(2,1)S(1)}, bf16[2,7,2,120,128]{4,3,2,1,0:T(8,128)(2,1)}, u32[]{:S(2)}) copy-start(bf16[2,7,2,120,128]{4,3,2,1,0:T(8,128)(2,1)} %get-tuple-element.11.refs_1_) | copy-start | bytes 2580484
  3.5 16.9 %collective-permute-start.1 = (bf16[2,7,2,120,128]{4,3,2,1,0:T(8,128)(2,1)}, bf16[2,7,2,120,128]{4,3,2,1,0:T(8,128)(2,1)S(1)}, u32[]{:S(2)}, u32[]{:S(2)}) collective-permute-start(bf16[2,7,2,120,128]{4,3,2,1,0:T(8,128)(2,1)} %get-tuple-element.11.refs_1_), channel_id=1, source_target_pairs={{1,0},{2,1},{3,2},{4,3},{5,4},{6,5},{7,6},{8,7},{9,8},{10,9},{11,1... | collective-permute-start | bytes 2580488 | tf_op jit(solution)/shard_map/ppermute | solution.py:384
  6.4 0.7 %copy-start.3 = (f32[8,128]{1,0:T(8,128)S(1)}, f32[8,128]{1,0:T(8,128)}, u32[]{:S(2)}) copy-start(f32[8,128]{1,0:T(8,128)} %get-tuple-element.12._) | copy-start | bytes 12292
  12.0 15.6 %collective-permute-start.4 = (f32[128,128]{1,0:T(8,128)S(1)}, f32[128,128]{1,0:T(8,128)S(1)}, u32[]{:S(2)}, u32[]{:S(2)}) collective-permute-start(f32[128,128]{1,0:T(8,128)S(1)} %get-tuple-element.16), channel_id=1, source_target_pairs={{0,12},{1,13},{2,14},{3,15},{4,0},{5,1},{6,2},{7,3},{8,4},{9,5},{1... | collective-permute-start | bytes 196616 | tf_op jit(solution)/shard_map/ppermute | solution.py:372
  12.1 15.5 %collective-permute-start.3 = (f32[128,128]{1,0:T(8,128)S(1)}, f32[128,128]{1,0:T(8,128)S(1)}, u32[]{:S(2)}, u32[]{:S(2)}) collective-permute-start(f32[128,128]{1,0:T(8,128)S(1)} %get-tuple-element.16), channel_id=1, source_target_pairs={{0,4},{1,5},{2,6},{3,7},{4,8},{5,9},{6,10},{7,11},{8,12},{9,13},{1... | collective-permute-start | bytes 196616 | tf_op jit(solution)/shard_map/ppermute | solution.py:372
  14.1 13.5 %collective-permute-start.2 = (f32[128,128]{1,0:T(8,128)S(1)}, f32[128,128]{1,0:T(8,128)S(1)}, u32[]{:S(2)}, u32[]{:S(2)}) collective-permute-start(f32[128,128]{1,0:T(8,128)S(1)} %get-tuple-element.16), channel_id=1, source_target_pairs={{0,8},{1,9},{2,10},{3,11},{4,12},{5,13},{6,14},{7,15},{8,0},{9,1},... | collective-permute-start | bytes 196616 | tf_op jit(solution)/shard_map/ppermute | solution.py:372
  18.5 19.7 %collective-permute-start = (bf16[3,7,2,120,128]{4,3,2,1,0:T(8,128)(2,1)S(1)}, bf16[3,7,2,120,128]{4,3,2,1,0:T(8,128)(2,1)S(1)}, u32[]{:S(2)}, u32[]{:S(2)}) collective-permute-start(bf16[3,7,2,120,128]{4,3,2,1,0:T(8,128)(2,1)S(1)} %copy-done.1), channel_id=1, source_target_pairs={{0,1},{1,2},{2,3},{3,4},{4,5},{5,6},{6,7},{7,8},{8,9},{9,10},{10,1... | collective-permute-start | bytes 3870728 | tf_op jit(solution)/shard_map/ppermute | solution.py:385
  27.6 15.1 %collective-permute-start.7 = (f32[128,128]{1,0:T(8,128)S(1)}, f32[128,128]{1,0:T(8,128)S(1)}, u32[]{:S(2)}, u32[]{:S(2)}) collective-permute-start(f32[128,128]{1,0:T(8,128)S(1)} %add_add_fusion.refs_5_), channel_id=1, source_target_pairs={{0,3},{1,0},{2,1},{3,2},{4,7},{5,4},{6,5},{7,6},{8,11},{9,8},{10,9... | collective-permute-start | bytes 196616 | tf_op jit(solution)/shard_map/ppermute | solution.py:372
  29.8 12.9 %collective-permute-start.6 = (f32[128,128]{1,0:T(8,128)S(1)}, f32[128,128]{1,0:T(8,128)S(1)}, u32[]{:S(2)}, u32[]{:S(2)}) collective-permute-start(f32[128,128]{1,0:T(8,128)S(1)} %add_add_fusion.refs_5_), channel_id=1, source_target_pairs={{0,2},{1,3},{2,0},{3,1},{4,6},{5,7},{6,4},{7,5},{8,10},{9,11},{10,... | collective-permute-start | bytes 196616 | tf_op jit(solution)/shard_map/ppermute | solution.py:372
  30.1 12.6 %collective-permute-start.5 = (f32[128,128]{1,0:T(8,128)S(1)}, f32[128,128]{1,0:T(8,128)S(1)}, u32[]{:S(2)}, u32[]{:S(2)}) collective-permute-start(f32[128,128]{1,0:T(8,128)S(1)} %add_add_fusion.refs_5_), channel_id=1, source_target_pairs={{0,1},{1,2},{2,3},{3,0},{4,5},{5,6},{6,7},{7,4},{8,9},{9,10},{10,1... | collective-permute-start | bytes 196616 | tf_op jit(solution)/shard_map/ppermute | solution.py:372

commit v8 on v7

--- a/solution.py
+++ b/solution.py
@@ -69,7 +69,7 @@
 EDGE = tuple(range(AFTER)) + tuple(range(ROWS - BEFORE, ROWS))
 
 
-def edge_kernel(image_ref, mask_ref, top_ref, low_ref, _, rows_ref, masks_ref, turned_ref, in_sems, out_sems):
+def edge_kernel(cut, image_ref, mask_ref, top_ref, low0_ref, low1_ref, rows_ref, masks_ref, turned_ref, in_sems, out_sems):
     fetches = fetched(image_ref, mask_ref, rows_ref, masks_ref, in_sems, EDGE)
     stores = []
     for at, row in enumerate(EDGE):
@@ -79,10 +79,16 @@
             turned_ref[at, g, k] = value
 
         turned([rows_ref.at[at, 0], rows_ref.at[at, 1]], masks_ref[row : row + 1, :], SKEW[row], masks_ref.shape[1], put)
-        target = top_ref.at[row] if row < AFTER else low_ref.at[row - (ROWS - BEFORE)]
-        store = pltpu.make_async_copy(turned_ref.at[at], target, out_sems.at[at])
-        store.start()
-        stores.append(store)
+        groups = turned_ref.shape[1]
+        i = row - (ROWS - BEFORE)
+        if row < AFTER:
+            targets = ((top_ref.at[row], 0, groups),)
+        else:
+            targets = ((low0_ref.at[i], 0, cut), (low1_ref.at[i], cut, groups))
+        for target, start, stop in targets:
+            store = pltpu.make_async_copy(turned_ref.at[at, start:stop], target, out_sems.at[len(stores)])
+            store.start()
+            stores.append(store)
     for store in stores:
         store.wait()
 
@@ -91,24 +97,24 @@
     return jax.ShapeDtypeStruct((rows, groups, 2, count, LANES), jnp.bfloat16)
 
 
-def edge_rows(images, valid_mask, groups):
+def edge_rows(images, valid_mask, groups, cut):
     count = images.shape[2]
     far = pl.BlockSpec(memory_space=pl.ANY)
     return pl.pallas_call(
-        edge_kernel,
+        functools.partial(edge_kernel, cut),
         in_specs=[far, far],
         out_specs=[far] * 3,
         out_shape=[
             rows_shape(AFTER, groups, count),
-            rows_shape(BEFORE, groups, count),
-            jax.ShapeDtypeStruct((8, LANES), jnp.float32),
+            rows_shape(BEFORE, cut, count),
+            rows_shape(BEFORE, groups - cut, count),
         ],
         scratch_shapes=[
             pltpu.VMEM((len(EDGE),) + images.shape[1:], jnp.bfloat16),
             pltpu.VMEM(valid_mask.shape, jnp.int32),
             pltpu.VMEM((len(EDGE), groups, 2, count, LANES), jnp.bfloat16),
             pltpu.SemaphoreType.DMA((len(EDGE) + 1,)),
-            pltpu.SemaphoreType.DMA((len(EDGE),)),
+            pltpu.SemaphoreType.DMA((AFTER + 2 * BEFORE,)),
         ],
         compiler_params=pltpu.CompilerParams(vmem_limit_bytes=61 * 2**20),
         cost_estimate=pl.CostEstimate(flops=10**6, bytes_accessed=4 * 10**6, transcendentals=0),
@@ -116,35 +122,27 @@
     )(images, valid_mask)
 
 
-def middle_kernel(image_ref, mask_ref, _, mid_ref, gram_ref, rows_ref, masks_ref, turned_ref, z_ref, in_sems, out_sems):
-    groups = mid_ref.shape[1]
+def local_kernel(image_ref, mask_ref, all_ref, gram_ref, rows_ref, masks_ref, turned_ref, z_ref, in_sems, out_sems):
+    groups = all_ref.shape[1]
     count, columns = image_ref.shape[2:]
-    order = tuple(range(AFTER, ROWS - BEFORE)) + EDGE
-    fetches = fetched(image_ref, mask_ref, rows_ref, masks_ref, in_sems, order)
+    fetches = fetched(image_ref, mask_ref, rows_ref, masks_ref, in_sems, range(ROWS))
     z_ref[...] = jnp.zeros_like(z_ref)
-    zero = jnp.zeros((count, columns), jnp.bfloat16)
     stores = []
     total = None
     wide = groups * LANES
-    for at, row in enumerate(order):
-        fetches[at].wait()
-        mask = masks_ref[row : row + 1, :]
-        if AFTER <= row < ROWS - BEFORE:
-
-            def put(g, k, value):
-                turned_ref[at, g, k] = value
-                z_ref[pl.ds(k * LANES, count), pl.ds(at * wide + g * LANES, LANES)] = value
-
-            turned([rows_ref.at[at, 0], rows_ref.at[at, 1]], mask, SKEW[row], columns, put)
-            store = pltpu.make_async_copy(turned_ref.at[at], mid_ref.at[row - AFTER], out_sems.at[at])
-            store.start()
-            stores.append(store)
-        else:
-            keep = jnp.broadcast_to((mask != 0).astype(jnp.float32), (count, columns)).astype(jnp.bfloat16) != 0
-            for k in range(2):
-                z_ref[pl.ds(k * LANES, count), pl.ds(at * wide, columns)] = jnp.where(keep, rows_ref[at, k], zero)
-        if at % 2:
-            z = z_ref[:, pl.ds((at - 1) * wide, 2 * wide)]
+    for row in range(ROWS):
+        fetches[row].wait()
+
+        def put(g, k, value):
+            turned_ref[row, g, k] = value
+            z_ref[pl.ds(k * LANES, count), pl.ds(row * wide + g * LANES, LANES)] = value
+
+        turned([rows_ref.at[row, 0], rows_ref.at[row, 1]], masks_ref[row : row + 1, :], SKEW[row], columns, put)
+        store = pltpu.make_async_copy(turned_ref.at[row], all_ref.at[row], out_sems.at[row])
+        store.start()
+        stores.append(store)
+        if row % 2:
+            z = z_ref[:, pl.ds((row - 1) * wide, 2 * wide)]
             part = lax.dot_general(z, z, NT, preferred_element_type=jnp.float32)
             total = part if total is None else total + part
     real = total[:LANES, :LANES] + total[LANES:, LANES:]
@@ -156,27 +154,26 @@
         store.wait()
 
 
-def middle_rows(images, valid_mask, groups, behind):
+def local_rows(images, valid_mask, groups):
     count = images.shape[2]
-    rows = ROWS - AFTER - BEFORE
     far = pl.BlockSpec(memory_space=pl.ANY)
     return pl.pallas_call(
-        middle_kernel,
-        in_specs=[far, far, far],
+        local_kernel,
+        in_specs=[far, far],
         out_specs=[far, pl.BlockSpec(memory_space=pltpu.VMEM)],
-        out_shape=[rows_shape(rows, groups, count), jax.ShapeDtypeStruct((LANES, LANES), jnp.float32)],
+        out_shape=[rows_shape(ROWS, groups, count), jax.ShapeDtypeStruct((LANES, LANES), jnp.float32)],
         scratch_shapes=[
             pltpu.VMEM(images.shape, jnp.bfloat16),
             pltpu.VMEM(valid_mask.shape, jnp.int32),
-            pltpu.VMEM((rows, groups, 2, count, LANES), jnp.bfloat16),
+            pltpu.VMEM((ROWS, groups, 2, count, LANES), jnp.bfloat16),
             pltpu.VMEM((2 * LANES, ROWS * groups * LANES), jnp.bfloat16),
             pltpu.SemaphoreType.DMA((ROWS + 1,)),
-            pltpu.SemaphoreType.DMA((rows,)),
+            pltpu.SemaphoreType.DMA((ROWS,)),
         ],
-        compiler_params=pltpu.CompilerParams(vmem_limit_bytes=52 * 2**20),
+        compiler_params=pltpu.CompilerParams(vmem_limit_bytes=50 * 2**20),
         cost_estimate=pl.CostEstimate(flops=10**9, bytes_accessed=5 * 10**6, transcendentals=0),
-        name="middle_rows",
-    )(images, valid_mask, behind)
+        name="local_rows",
+    )(images, valid_mask)
 
 
 def added(terms):
@@ -205,11 +202,11 @@
 
 
 def looks_kernel(half, aliased, terms, slab, *refs):
-    other_ref, top_ref, mid_ref, low_ref = refs[:4]
-    refs = refs[4 + aliased :]
+    other_ref, all_ref = refs[:2]
+    refs = refs[2 + aliased :]
     term_refs, refs = refs[:terms], refs[terms:]
-    out_ref, extra_ref, w_ref = refs
-    count = top_ref.shape[3]
+    out_ref, extra_ref, w_ref, g_ref = refs
+    count = all_ref.shape[3]
 
     @pl.when(pl.program_id(0) == 0)
     def _():
@@ -223,14 +220,7 @@
         else:
             extra_ref[...] = jnp.zeros_like(extra_ref)
 
-    rows = {}
-    for r in range(ROWS):
-        if r < AFTER:
-            rows[r] = top_ref.at[r, 0]
-        elif r >= ROWS - BEFORE:
-            rows[r] = low_ref.at[r - (ROWS - BEFORE), 0]
-        else:
-            rows[r] = mid_ref.at[r - AFTER, 0]
+    rows = {r: all_ref.at[r, 0] for r in range(ROWS)}
     for r in range(other_ref.shape[0]):
         rows[ROWS + r if half else r - BEFORE] = other_ref.at[r, 0]
 
@@ -267,20 +257,9 @@
     on_eye = along % 8 == lax.broadcasted_iota(jnp.int32, eight, 0)
     block = along // 8
 
-    def normalised(real, imag, w, l):
-        picked = real[:8]
-        for v in range(1, count // 8):
-            picked = jnp.where(block == v, real[8 * v : 8 * v + 8], picked)
-        power = jnp.sum(jnp.where(on_eye, picked, 0.0), axis=0, keepdims=True)
-        across = lax.rsqrt(jnp.maximum(power, floor_power))
-        diagonal = jnp.where(on_eye, across, 0.0)
-        spread = jnp.concatenate([jnp.where(block == v, diagonal, 0.0) for v in range(count // 8)], axis=0)
-        scale = jnp.sum(spread, axis=1, keepdims=True) * across
-        out_ref[w, l, 0] = (real * scale).astype(jnp.bfloat16)[:, :count]
-        out_ref[w, l, 1] = (imag * scale).astype(jnp.bfloat16)[:, :count]
-
     outer_rows, windows = HALVES[half]
-    for l in range(PER):
+
+    def products(l):
         slot = l % 2
         for k in range(2):
             w_ref[slot, k, pl.ds(0, count), pl.ds(0, LANES)] = gathered(l, k, INNER)
@@ -297,22 +276,41 @@
                 reads.append(read[LANES + start : LANES + start + TILE])
         gram = lax.dot_general(jnp.concatenate(reads, axis=0), every, NT, preferred_element_type=jnp.float32)
         for w in range(2):
-            real, imag = [], []
             for start in range(0, LANES, TILE):
                 base = 2 * (w * LANES + start)
                 re, im = gram[base : base + TILE], gram[base + TILE : base + 2 * TILE]
-                real.append(re[:, :LANES] + im[:, LANES:])
-                imag.append(im[:, :LANES] - re[:, LANES:])
-            normalised(jnp.concatenate(real, axis=0)[:count], jnp.concatenate(imag, axis=0)[:count], w, l)
-
-
-def looked(half, other, top, mid, low, first, groups, looks, previous, terms, slab):
+                g_ref[slot, w, 0, pl.ds(start, TILE)] = re[:, :LANES] + im[:, LANES:]
+                g_ref[slot, w, 1, pl.ds(start, TILE)] = im[:, :LANES] - re[:, LANES:]
+
+    def normalised(l):
+        for w in range(2):
+            real, imag = g_ref.at[l % 2, w, 0], g_ref.at[l % 2, w, 1]
+            picked = real[0:8]
+            for v in range(1, count // 8):
+                picked = jnp.where(block == v, real[8 * v : 8 * v + 8], picked)
+            power = jnp.sum(jnp.where(on_eye, picked, 0.0), axis=0, keepdims=True)
+            across = lax.rsqrt(jnp.maximum(power, floor_power))
+            diagonal = jnp.where(on_eye, across, 0.0)
+            spread = jnp.concatenate([jnp.where(block == v, diagonal, 0.0) for v in range(count // 8)], axis=0)
+            scale = jnp.sum(spread, axis=1, keepdims=True) * across
+            out_ref[w, l, 0] = (real[0:count] * scale).astype(jnp.bfloat16)[:, :count]
+            out_ref[w, l, 1] = (imag[0:count] * scale).astype(jnp.bfloat16)[:, :count]
+
+    products(0)
+    for l in range(PER):
+        if l + 1 < PER:
+            products(l + 1)
+        normalised(l)
+
+
+def looked(half, other, rows, first, groups, looks, previous, terms, slab):
     count = other.shape[3]
 
     def spec(array):
-        return pl.BlockSpec((array.shape[0], 1) + array.shape[2:], lambda s: (0, s + first, 0, 0, 0))
-
-    operands = [other, top, mid, low]
+        offset = 0 if array is other else first
+        return pl.BlockSpec((array.shape[0], 1) + array.shape[2:], lambda s: (0, s + offset, 0, 0, 0))
+
+    operands = [other, rows]
     in_specs = [spec(a) for a in operands]
     aliases = {}
     if previous is not None:
@@ -340,10 +338,11 @@
         input_output_aliases=aliases,
         scratch_shapes=[
             pltpu.VMEM((2, 2, LANES, 2 * LANES), jnp.bfloat16),
+            pltpu.VMEM((2, 2, 2, LANES, LANES), jnp.float32),
         ],
-        compiler_params=pltpu.CompilerParams(vmem_limit_bytes=48 * 2**20),
+        compiler_params=pltpu.CompilerParams(vmem_limit_bytes=49 * 2**20),
         cost_estimate=pl.CostEstimate(
-            flops=20 * groups * PER * 2 * 512 * 256 * 256, bytes_accessed=groups * 10**6, transcendentals=0
+            flops=1 * groups * PER * 2 * 512 * 256 * 256, bytes_accessed=groups * 10**6, transcendentals=0
         ),
         name="looks",
     )(*operands)
@@ -380,20 +379,21 @@
     size = lax.axis_size("pix")
     forward = [(i, i + 1) for i in range(size - 1)]
     backward = [(i + 1, i) for i in range(size - 1)]
-    top, low, edge_done = edge_rows(images, valid_mask, groups)
+    top, low0, low1 = edge_rows(images, valid_mask, groups, cut)
     after = lax.ppermute(top, "pix", backward)
-    before = lax.ppermute(low, "pix", forward)
-    mid, total = middle_rows(images, valid_mask, groups, edge_done)
+    before0 = lax.ppermute(low0, "pix", forward)
+    before1 = lax.ppermute(low1, "pix", forward)
+    rows, total = local_rows(images, valid_mask, groups)
     steps = rounds(size)
     if steps is None:
         terms, steps = [lax.psum(total, "pix")], []
     else:
         terms = round_terms(total, "pix", *steps[0]) if steps else [total]
-    out, zeros = looked(1, after, top, mid, low, 0, groups, looks, None, [], False)
+    out, zeros = looked(1, after, rows, 0, groups, looks, None, [], False)
     for step in steps[1:]:
         terms = round_terms(added(terms) + zeros, "pix", *step)
-    out, _ = looked(0, before, top, mid, low, 0, cut, looks, out, [], False)
-    out, slab = looked(0, before, top, mid, low, cut, groups - cut, looks, out, terms, True)
+    out, _ = looked(0, before0, rows, 0, cut, looks, out, [], False)
+    out, slab = looked(0, before1, rows, cut, groups - cut, looks, out, terms, True)
     return (out, slab)
 
 

time: 46.7 us -> 46 us (0.985)
  the two profiles are of different devices: /device:TPU:8 before, /device:TPU:1 now
where the time goes in v8:
time: 46 us; the launch traced here: 45.8 us
  Pallas kernels  25.3 us (55%)
  starting transfers between devices  18.9 us (41%)
  local copies, waits for them, and re-layouts  0.74 us (2%)
  between operations  0.72 us (2%)
    pallas_call x3, Pallas kernels, looked(): pl.pallas_call(functools.partial(looks_kernel, half, previous is not None...  15.3 us
    ppermute x6, starting transfers between devices, round_terms(): terms.append(lax.ppermute(value, axis, pairs))  9.28 us
    pallas_call x1, Pallas kernels, local_rows(): pl.pallas_call(local_kernel, in_specs=[far, far], out_specs=[far, pl.Bloc...  7.12 us
    ppermute x1, starting transfers between devices, shards(): before0 = lax.ppermute(low0, 'pix', forward)  4.46 us
    ppermute x1, starting transfers between devices, shards(): before1 = lax.ppermute(low1, 'pix', forward)  3.23 us
    pallas_call x1, Pallas kernels, edge_rows(): pl.pallas_call(functools.partial(edge_kernel, cut), in_specs=[far, far],...  2.88 us
    ppermute x1, starting transfers between devices, shards(): after = lax.ppermute(top, 'pix', backward)  1.97 us
  transfers between devices with their start and end apart: 9, of which 0 were waited for; matrix products, arithmetic and copies ran while one was open for 0% of the time, Pallas kernels for 41%

profile of v8, /device:TPU:1, one launch (start us, length us, event | category | flops | bytes accessed | tf_op | source)
XLA Modules:
  0.0 45.8 jit_solution(13392702287806488532)
XLA Ops:
  0.6 2.9 %edge_rows.1 = (bf16[2,7,2,120,128]{4,3,2,1,0:T(8,128)(2,1)}, bf16[3,4,2,120,128]{4,3,2,1,0:T(8,128)(2,1)}, bf16[3,3,2,120,128]{4,3,2,1,0:T(8,128)(2,1)}) custom-call(bf16[8,2,120,840]{3,2,1,0:T(8,128)(2,1)} %image_ref.3, s32[8,840]{1,0:T(8,128)} %mask_ref.3), custom_call_target="tpu_custom_call" | custom-call | flops 1000000 | bytes 4000000 | tf_op jit(solution)/shard_map/edge_rows/pallas_call | solution.py:103
  3.5 2.0 %collective-permute-start.2 = (bf16[2,7,2,120,128]{4,3,2,1,0:T(8,128)(2,1)}, bf16[2,7,2,120,128]{4,3,2,1,0:T(8,128)(2,1)S(1)}, u32[]{:S(2)}, u32[]{:S(2)}) collective-permute-start(bf16[2,7,2,120,128]{4,3,2,1,0:T(8,128)(2,1)} %get-tuple-element.13), channel_id=1, source_target_pairs={{1,0},{2,1},{3,2},{4,3},{5,4},{6,5},{7,6},{8,7},{9,8},{10,9},{11,1... | collective-permute-start | bytes 2580488 | tf_op jit(solution)/shard_map/ppermute | solution.py:383
  5.5 4.5 %collective-permute-start.1 = (bf16[3,4,2,120,128]{4,3,2,1,0:T(8,128)(2,1)}, bf16[3,4,2,120,128]{4,3,2,1,0:T(8,128)(2,1)S(1)}, u32[]{:S(2)}, u32[]{:S(2)}) collective-permute-start(bf16[3,4,2,120,128]{4,3,2,1,0:T(8,128)(2,1)} %get-tuple-element.12), channel_id=1, source_target_pairs={{0,1},{1,2},{2,3},{3,4},{4,5},{5,6},{6,7},{7,8},{8,9},{9,10},{10,1... | collective-permute-start | bytes 2211848 | tf_op jit(solution)/shard_map/ppermute | solution.py:384
  10.0 0.0 copy-start
  10.0 0.7 %copy-done = s32[8,840]{1,0:T(8,128)S(1)} copy-done((s32[8,840]{1,0:T(8,128)S(1)}, s32[8,840]{1,0:T(8,128)}, u32[]{:S(2)}) %copy-start) | copy-done | bytes 26904
  10.7 7.1 %local_rows.1 = (bf16[8,7,2,120,128]{4,3,2,1,0:T(8,128)(2,1)S(1)}, f32[128,128]{1,0:T(8,128)S(1)}) custom-call(bf16[8,2,120,840]{3,2,1,0:T(8,128)(2,1)} %image_ref.3, s32[8,840]{1,0:T(8,128)S(1)} %copy-done), custom_call_target="tpu_custom_call" | custom-call | flops 1000000000 | bytes 5000000 | tf_op jit(solution)/shard_map/local_rows/pallas_call | solution.py:160
  17.8 3.4 %collective-permute-start.5 = (f32[128,128]{1,0:T(8,128)S(1)}, f32[128,128]{1,0:T(8,128)S(1)}, u32[]{:S(2)}, u32[]{:S(2)}) collective-permute-start(f32[128,128]{1,0:T(8,128)S(1)} %get-tuple-element.16), channel_id=1, source_target_pairs={{0,12},{1,13},{2,14},{3,15},{4,0},{5,1},{6,2},{7,3},{8,4},{9,5},{1... | collective-permute-start | bytes 196616 | tf_op jit(solution)/shard_map/ppermute | solution.py:371
  21.2 0.0 collective-permute-start.4
  21.2 0.5 collective-permute-start.3
  21.7 0.0 collective-permute-done.2.refs_0_
  21.7 3.2 %collective-permute-start = (bf16[3,3,2,120,128]{4,3,2,1,0:T(8,128)(2,1)}, bf16[3,3,2,120,128]{4,3,2,1,0:T(8,128)(2,1)S(1)}, u32[]{:S(2)}, u32[]{:S(2)}) collective-permute-start(bf16[3,3,2,120,128]{4,3,2,1,0:T(8,128)(2,1)} %get-tuple-element.10), channel_id=1, source_target_pairs={{0,1},{1,2},{2,3},{3,4},{4,5},{5,6},{6,7},{7,8},{8,9},{9,10},{10,1... | collective-permute-start | bytes 1658888 | tf_op jit(solution)/shard_map/ppermute | solution.py:385
  24.9 7.1 %looks.3 = (bf16[4,40,2,120,120]{4,3,2,1,0:T(8,128)(2,1)}, f32[128,128]{1,0:T(8,128)S(1)}) custom-call(bf16[2,7,2,120,128]{4,3,2,1,0:T(8,128)(2,1)S(1)} %collective-permute-done.2.refs_0_, bf16[8,7,2,120,128]{4,3,2,1,0:T(8,128)(2,1)S(1)} %get-tuple-element.11.refs_1_), custom_call_target="tpu_custom_call" | custom-call | flops 2818572288 | bytes 7000000 | tf_op jit(solution)/shard_map/looks/pallas_call | solution.py:332
  32.0 0.0 collective-permute-done.5
  32.0 0.0 collective-permute-done.4
  32.0 0.0 collective-permute-done.3
  32.0 0.1 collective-permute-start.8
  32.1 3.4 %collective-permute-start.7 = (f32[128,128]{1,0:T(8,128)S(1)}, f32[128,128]{1,0:T(8,128)S(1)}, u32[]{:S(2)}, u32[]{:S(2)}) collective-permute-start(f32[128,128]{1,0:T(8,128)S(1)} %add_add_fusion.refs_3_), channel_id=1, source_target_pairs={{0,2},{1,3},{2,0},{3,1},{4,6},{5,7},{6,4},{7,5},{8,10},{9,11},{10,... | collective-permute-start | bytes 196616 | tf_op jit(solution)/shard_map/ppermute | solution.py:371
  35.6 1.9 %collective-permute-start.6 = (f32[128,128]{1,0:T(8,128)S(1)}, f32[128,128]{1,0:T(8,128)S(1)}, u32[]{:S(2)}, u32[]{:S(2)}) collective-permute-start(f32[128,128]{1,0:T(8,128)S(1)} %add_add_fusion.refs_3_), channel_id=1, source_target_pairs={{0,1},{1,2},{2,3},{3,0},{4,5},{5,6},{6,7},{7,4},{8,9},{9,10},{10,1... | collective-permute-start | bytes 196616 | tf_op jit(solution)/shard_map/ppermute | solution.py:371
  37.5 0.0 collective-permute-done.1.refs_0_
  37.5 4.5 %looks.4 = (bf16[4,40,2,120,120]{4,3,2,1,0:T(8,128)(2,1)}, f32[128,128]{1,0:T(8,128)}) custom-call(bf16[3,4,2,120,128]{4,3,2,1,0:T(8,128)(2,1)S(1)} %collective-permute-done.1.refs_0_, bf16[8,7,2,120,128]{4,3,2,1,0:T(8,128)(2,1)S(1)} %get-tuple-element.11.refs_1_, ...), custom_call_target="tpu_custom_call", output_to_operand_aliasing={{0}: (2, {})} | custom-call | flops 1610612736 | bytes 4000000 | tf_op jit(solution)/shard_map/looks/pallas_call | solution.py:332
  42.0 0.0 collective-permute-done.refs_0_
  42.0 0.0 collective-permute-done.8.refs_6_
  42.0 0.0 collective-permute-done.7.refs_5_
  42.0 3.7 %looks.5 = (bf16[4,40,2,120,120]{4,3,2,1,0:T(8,128)(2,1)}, f32[2,120,120]{2,1,0:T(8,128)}) custom-call(bf16[3,3,2,120,128]{4,3,2,1,0:T(8,128)(2,1)S(1)} %collective-permute-done.refs_0_, bf16[8,7,2,120,128]{4,3,2,1,0:T(8,128)(2,1)S(1)} %get-tuple-element.11.refs_1_, ...), custom_call_target="tpu_custom_call", output_to_operand_aliasing={{0}: (2, {})} | custom-call | flops 1207959552 | bytes 3000000 | tf_op jit(solution)/shard_map/looks/pallas_call | solution.py:332
  (2 shorter events, 0.0 us)
Async XLA Ops:
  3.5 18.2 %collective-permute-start.2 = (bf16[2,7,2,120,128]{4,3,2,1,0:T(8,128)(2,1)}, bf16[2,7,2,120,128]{4,3,2,1,0:T(8,128)(2,1)S(1)}, u32[]{:S(2)}, u32[]{:S(2)}) collective-permute-start(bf16[2,7,2,120,128]{4,3,2,1,0:T(8,128)(2,1)} %get-tuple-element.13), channel_id=1, source_target_pairs={{1,0},{2,1},{3,2},{4,3},{5,4},{6,5},{7,6},{8,7},{9,8},{10,9},{11,1... | collective-permute-start | bytes 2580488 | tf_op jit(solution)/shard_map/ppermute | solution.py:383
  5.5 32.0 %collective-permute-start.1 = (bf16[3,4,2,120,128]{4,3,2,1,0:T(8,128)(2,1)}, bf16[3,4,2,120,128]{4,3,2,1,0:T(8,128)(2,1)S(1)}, u32[]{:S(2)}, u32[]{:S(2)}) collective-permute-start(bf16[3,4,2,120,128]{4,3,2,1,0:T(8,128)(2,1)} %get-tuple-element.12), channel_id=1, source_target_pairs={{0,1},{1,2},{2,3},{3,4},{4,5},{5,6},{6,7},{7,8},{8,9},{9,10},{10,1... | collective-permute-start | bytes 2211848 | tf_op jit(solution)/shard_map/ppermute | solution.py:384
  10.0 0.8 %copy-start = (s32[8,840]{1,0:T(8,128)S(1)}, s32[8,840]{1,0:T(8,128)}, u32[]{:S(2)}) copy-start(s32[8,840]{1,0:T(8,128)} %mask_ref.3) | copy-start | bytes 80644
  17.8 14.2 %collective-permute-start.5 = (f32[128,128]{1,0:T(8,128)S(1)}, f32[128,128]{1,0:T(8,128)S(1)}, u32[]{:S(2)}, u32[]{:S(2)}) collective-permute-start(f32[128,128]{1,0:T(8,128)S(1)} %get-tuple-element.16), channel_id=1, source_target_pairs={{0,12},{1,13},{2,14},{3,15},{4,0},{5,1},{6,2},{7,3},{8,4},{9,5},{1... | collective-permute-start | bytes 196616 | tf_op jit(solution)/shard_map/ppermute | solution.py:371
  21.2 10.8 %collective-permute-start.4 = (f32[128,128]{1,0:T(8,128)S(1)}, f32[128,128]{1,0:T(8,128)S(1)}, u32[]{:S(2)}, u32[]{:S(2)}) collective-permute-start(f32[128,128]{1,0:T(8,128)S(1)} %get-tuple-element.16), channel_id=1, source_target_pairs={{0,4},{1,5},{2,6},{3,7},{4,8},{5,9},{6,10},{7,11},{8,12},{9,13},{1... | collective-permute-start | bytes 196616 | tf_op jit(solution)/shard_map/ppermute | solution.py:371
  21.2 10.8 %collective-permute-start.3 = (f32[128,128]{1,0:T(8,128)S(1)}, f32[128,128]{1,0:T(8,128)S(1)}, u32[]{:S(2)}, u32[]{:S(2)}) collective-permute-start(f32[128,128]{1,0:T(8,128)S(1)} %get-tuple-element.16), channel_id=1, source_target_pairs={{0,8},{1,9},{2,10},{3,11},{4,12},{5,13},{6,14},{7,15},{8,0},{9,1},... | collective-permute-start | bytes 196616 | tf_op jit(solution)/shard_map/ppermute | solution.py:371
  21.7 20.3 %collective-permute-start = (bf16[3,3,2,120,128]{4,3,2,1,0:T(8,128)(2,1)}, bf16[3,3,2,120,128]{4,3,2,1,0:T(8,128)(2,1)S(1)}, u32[]{:S(2)}, u32[]{:S(2)}) collective-permute-start(bf16[3,3,2,120,128]{4,3,2,1,0:T(8,128)(2,1)} %get-tuple-element.10), channel_id=1, source_target_pairs={{0,1},{1,2},{2,3},{3,4},{4,5},{5,6},{6,7},{7,8},{8,9},{9,10},{10,1... | collective-permute-start | bytes 1658888 | tf_op jit(solution)/shard_map/ppermute | solution.py:385
  32.0 10.0 %collective-permute-start.8 = (f32[128,128]{1,0:T(8,128)S(1)}, f32[128,128]{1,0:T(8,128)S(1)}, u32[]{:S(2)}, u32[]{:S(2)}) collective-permute-start(f32[128,128]{1,0:T(8,128)S(1)} %add_add_fusion.refs_3_), channel_id=1, source_target_pairs={{0,3},{1,0},{2,1},{3,2},{4,7},{5,4},{6,5},{7,6},{8,11},{9,8},{10,9... | collective-permute-start | bytes 196616 | tf_op jit(solution)/shard_map/ppermute | solution.py:371
  32.1 9.9 %collective-permute-start.7 = (f32[128,128]{1,0:T(8,128)S(1)}, f32[128,128]{1,0:T(8,128)S(1)}, u32[]{:S(2)}, u32[]{:S(2)}) collective-permute-start(f32[128,128]{1,0:T(8,128)S(1)} %add_add_fusion.refs_3_), channel_id=1, source_target_pairs={{0,2},{1,3},{2,0},{3,1},{4,6},{5,7},{6,4},{7,5},{8,10},{9,11},{10,... | collective-permute-start | bytes 196616 | tf_op jit(solution)/shard_map/ppermute | solution.py:371
  35.6 6.5 %collective-permute-start.6 = (f32[128,128]{1,0:T(8,128)S(1)}, f32[128,128]{1,0:T(8,128)S(1)}, u32[]{:S(2)}, u32[]{:S(2)}) collective-permute-start(f32[128,128]{1,0:T(8,128)S(1)} %add_add_fusion.refs_3_), channel_id=1, source_target_pairs={{0,1},{1,2},{2,3},{3,0},{4,5},{5,6},{6,7},{7,4},{8,9},{9,10},{10,1... | collective-permute-start | bytes 196616 | tf_op jit(solution)/shard_map/ppermute | solution.py:371

commit v9 on v8

--- a/solution.py
+++ b/solution.py
@@ -16,7 +16,6 @@
 ROWS = 8
 SKEW = (5, 0, 1, 2, 3, 4, 1, 2)
 BEFORE, AFTER = 3, 2
-NT = (((1,), (1,)), ((), ()))
 
 
 def turned(image, mask, skew, columns, put):
@@ -122,55 +121,57 @@
     )(images, valid_mask)
 
 
-def local_kernel(image_ref, mask_ref, all_ref, gram_ref, rows_ref, masks_ref, turned_ref, z_ref, in_sems, out_sems):
+def local_kernel(image_ref, mask_ref, all_ref, gram_ref, rows_ref, masks_ref, y_ref, in_sems, out_sems):
     groups = all_ref.shape[1]
     count, columns = image_ref.shape[2:]
     fetches = fetched(image_ref, mask_ref, rows_ref, masks_ref, in_sems, range(ROWS))
-    z_ref[...] = jnp.zeros_like(z_ref)
+    rest = LANES - count
+    y_ref[:, :, 0:2, pl.ds(count, rest), :] = jnp.zeros((ROWS, groups, 2, rest, LANES), jnp.bfloat16)
     stores = []
     total = None
-    wide = groups * LANES
     for row in range(ROWS):
         fetches[row].wait()
 
         def put(g, k, value):
-            turned_ref[row, g, k] = value
-            z_ref[pl.ds(k * LANES, count), pl.ds(row * wide + g * LANES, LANES)] = value
+            y_ref[row, g, k, pl.ds(0, count), :] = value
 
         turned([rows_ref.at[row, 0], rows_ref.at[row, 1]], masks_ref[row : row + 1, :], SKEW[row], columns, put)
-        store = pltpu.make_async_copy(turned_ref.at[row], all_ref.at[row], out_sems.at[row])
+        for g in range(groups):
+            for k in range(2):
+                y_ref[row, g, 2 + k] = y_ref[row, g, k].T
+        store = pltpu.make_async_copy(y_ref.at[row], all_ref.at[row], out_sems.at[row])
         store.start()
         stores.append(store)
-        if row % 2:
-            z = z_ref[:, pl.ds((row - 1) * wide, 2 * wide)]
-            part = lax.dot_general(z, z, NT, preferred_element_type=jnp.float32)
-            total = part if total is None else total + part
+        left = [y_ref[row, g, 0:2].reshape(2 * LANES, LANES) for g in range(groups)]
+        right = [jnp.concatenate([y_ref[row, g, 2], y_ref[row, g, 3]], axis=1) for g in range(groups)]
+        left, right = jnp.concatenate(left, axis=1), jnp.concatenate(right, axis=0)
+        part = jnp.dot(left, right, preferred_element_type=jnp.float32)
+        total = part if total is None else total + part
     real = total[:LANES, :LANES] + total[LANES:, LANES:]
     imag = total[LANES:, :LANES] - total[:LANES, LANES:]
     i = lax.broadcasted_iota(jnp.int32, real.shape, 0)
     j = lax.broadcasted_iota(jnp.int32, real.shape, 1)
     gram_ref[...] = jnp.where(i <= j, real, imag)
-    for store in stores:
-        store.wait()
+    for copy in stores:
+        copy.wait()
 
 
 def local_rows(images, valid_mask, groups):
-    count = images.shape[2]
     far = pl.BlockSpec(memory_space=pl.ANY)
+    shape = (ROWS, groups, 4, LANES, LANES)
     return pl.pallas_call(
         local_kernel,
         in_specs=[far, far],
         out_specs=[far, pl.BlockSpec(memory_space=pltpu.VMEM)],
-        out_shape=[rows_shape(ROWS, groups, count), jax.ShapeDtypeStruct((LANES, LANES), jnp.float32)],
+        out_shape=[jax.ShapeDtypeStruct(shape, jnp.bfloat16), jax.ShapeDtypeStruct((LANES, LANES), jnp.float32)],
         scratch_shapes=[
             pltpu.VMEM(images.shape, jnp.bfloat16),
             pltpu.VMEM(valid_mask.shape, jnp.int32),
-            pltpu.VMEM((ROWS, groups, 2, count, LANES), jnp.bfloat16),
-            pltpu.VMEM((2 * LANES, ROWS * groups * LANES), jnp.bfloat16),
+            pltpu.VMEM(shape, jnp.bfloat16),
             pltpu.SemaphoreType.DMA((ROWS + 1,)),
             pltpu.SemaphoreType.DMA((ROWS,)),
         ],
-        compiler_params=pltpu.CompilerParams(vmem_limit_bytes=50 * 2**20),
+        compiler_params=pltpu.CompilerParams(vmem_limit_bytes=40 * 2**20),
         cost_estimate=pl.CostEstimate(flops=10**9, bytes_accessed=5 * 10**6, transcendentals=0),
         name="local_rows",
     )(images, valid_mask)
@@ -205,12 +206,12 @@
     other_ref, all_ref = refs[:2]
     refs = refs[2 + aliased :]
     term_refs, refs = refs[:terms], refs[terms:]
-    out_ref, extra_ref, w_ref, g_ref = refs
-    count = all_ref.shape[3]
+    out_ref, extra_ref, w_ref, g_ref, h_ref = refs
+    count = other_ref.shape[3]
 
     @pl.when(pl.program_id(0) == 0)
     def _():
-        w_ref[...] = jnp.zeros_like(w_ref)
+        h_ref[...] = jnp.zeros_like(h_ref)
         if slab:
             real, imag = slab_values([t[...] for t in term_refs])
             extra_ref[0] = real[:count, :count]
@@ -222,7 +223,10 @@
 
     rows = {r: all_ref.at[r, 0] for r in range(ROWS)}
     for r in range(other_ref.shape[0]):
-        rows[ROWS + r if half else r - BEFORE] = other_ref.at[r, 0]
+        for k in range(2):
+            h_ref[r, k, pl.ds(0, count), :] = other_ref[r, 0, k]
+            h_ref[r, 2 + k] = h_ref[r, k].T
+        rows[ROWS + r if half else r - BEFORE] = h_ref.at[r]
 
     lane = lax.broadcasted_iota(jnp.int32, (1, LANES), 1)
 
@@ -232,7 +236,7 @@
         return place < LOOK
 
     def widened(which):
-        return jnp.broadcast_to(which.astype(jnp.float32), (count, LANES)).astype(jnp.bfloat16) != 0
+        return jnp.broadcast_to(which.astype(jnp.float32), (LANES, LANES)).astype(jnp.bfloat16) != 0
 
     single = [lanes_of(t) for t in range(2 * PER - 1)]
     wide = [widened(s) for s in single]
@@ -252,6 +256,26 @@
             select = select | single[turn(l, r)]
         return select.astype(jnp.float32)
 
+    across_tile = lax.broadcasted_iota(jnp.int32, (TILE, 2 * LANES), 0).astype(jnp.float32).astype(jnp.bfloat16)
+
+    def tall(r, start):
+        return jnp.concatenate([rows[r][2, start : start + TILE], rows[r][3, start : start + TILE]], axis=1)
+
+    def stacked(l, which):
+        owners = [None] * LANES
+        for r in which:
+            for q in range(LOOK):
+                owners[(LOOK * turn(l, r) + q) % LANES] = r
+        tiles = []
+        for start in range(0, LANES, TILE):
+            here = owners[start : start + TILE]
+            found = [r for r in dict.fromkeys(here) if r is not None] or [which[0]]
+            value = tall(found[0], start)
+            for r in found[1:]:
+                value = jnp.where(across_tile < here.index(r), value, tall(r, start))
+            tiles.append(value)
+        return tiles
+
     eight = (8, LANES)
     along = lax.broadcasted_iota(jnp.int32, eight, 1)
     on_eye = along % 8 == lax.broadcasted_iota(jnp.int32, eight, 0)
@@ -262,8 +286,8 @@
     def products(l):
         slot = l % 2
         for k in range(2):
-            w_ref[slot, k, pl.ds(0, count), pl.ds(0, LANES)] = gathered(l, k, INNER)
-            w_ref[slot, k, pl.ds(0, count), pl.ds(LANES, LANES)] = gathered(l, k, outer_rows)
+            w_ref[slot, k, :, pl.ds(0, LANES)] = gathered(l, k, INNER)
+            w_ref[slot, k, :, pl.ds(LANES, LANES)] = gathered(l, k, outer_rows)
         every = w_ref[slot].reshape(2 * LANES, 2 * LANES)
         nothing = jnp.zeros_like(every)
         reads = []
@@ -274,7 +298,8 @@
             for start in range(0, LANES, TILE):
                 reads.append(read[start : start + TILE])
                 reads.append(read[LANES + start : LANES + start + TILE])
-        gram = lax.dot_general(jnp.concatenate(reads, axis=0), every, NT, preferred_element_type=jnp.float32)
+        right = jnp.concatenate(stacked(l, INNER) + stacked(l, outer_rows), axis=0)
+        gram = jnp.dot(jnp.concatenate(reads, axis=0), right, preferred_element_type=jnp.float32)
         for w in range(2):
             for start in range(0, LANES, TILE):
                 base = 2 * (w * LANES + start)
@@ -308,7 +333,8 @@
 
     def spec(array):
         offset = 0 if array is other else first
-        return pl.BlockSpec((array.shape[0], 1) + array.shape[2:], lambda s: (0, s + offset, 0, 0, 0))
+        rest = array.shape[2:]
+        return pl.BlockSpec((array.shape[0], 1) + rest, lambda s: (0, s + offset) + (0,) * len(rest))
 
     operands = [other, rows]
     in_specs = [spec(a) for a in operands]
@@ -339,8 +365,9 @@
         scratch_shapes=[
             pltpu.VMEM((2, 2, LANES, 2 * LANES), jnp.bfloat16),
             pltpu.VMEM((2, 2, 2, LANES, LANES), jnp.float32),
+            pltpu.VMEM((other.shape[0], 4, LANES, LANES), jnp.bfloat16),
         ],
-        compiler_params=pltpu.CompilerParams(vmem_limit_bytes=49 * 2**20),
+        compiler_params=pltpu.CompilerParams(vmem_limit_bytes=44 * 2**20),
         cost_estimate=pl.CostEstimate(
             flops=1 * groups * PER * 2 * 512 * 256 * 256, bytes_accessed=groups * 10**6, transcendentals=0
         ),

time: 46 us -> 51.9 us (1.13)
  Pallas kernels: 25.3 us -> 29.2 us
  local copies, waits for them, and re-layouts: 0.74 us -> 2.72 us
    pallas_call x3, Pallas kernels: 15.3 us -> 17.3 us  [looked(): pl.pallas_call(functools.partial(looks_kernel, half, previous is not None...]
    unnamed x2 -> x4, local copies, waits for them, and re-layouts: 0.74 us -> 2.72 us
    pallas_call x1, Pallas kernels: 7.12 us -> 8.95 us  [local_rows(): pl.pallas_call(local_kernel, in_specs=[far, far], out_specs=[far, pl.Bloc...]
  transfers between devices with their start and end apart: 9 -> 9, of which waited for: 0 -> 0; matrix products, arithmetic and copies ran while one was open for 0% -> 0% of each run, Pallas kernels for 41% -> 43%
where the time goes in v9:
time: 51.9 us; the launch traced here: 51.6 us
  Pallas kernels  29.2 us (56%)
  starting transfers between devices  18.9 us (36%)
  local copies, waits for them, and re-layouts  2.72 us (5%)
  between operations  0.72 us (1%)
    pallas_call x3, Pallas kernels, looked(): pl.pallas_call(functools.partial(looks_kernel, half, previous is not None...  17.3 us
    ppermute x6, starting transfers between devices, round_terms(): terms.append(lax.ppermute(value, axis, pairs))  9.29 us
    pallas_call x1, Pallas kernels, local_rows(): pl.pallas_call(local_kernel, in_specs=[far, far], out_specs=[far, pl.Bloc...  8.95 us
    ppermute x1, starting transfers between devices, shards(): before0 = lax.ppermute(low0, 'pix', forward)  4.46 us
    ppermute x1, starting transfers between devices, shards(): before1 = lax.ppermute(low1, 'pix', forward)  3.23 us
    pallas_call x1, Pallas kernels, edge_rows(): pl.pallas_call(functools.partial(edge_kernel, cut), in_specs=[far, far],...  2.88 us
    unnamed x4, local copies, waits for them, and re-layouts  2.72 us
    ppermute x1, starting transfers between devices, shards(): after = lax.ppermute(top, 'pix', backward)  1.97 us
  transfers between devices with their start and end apart: 9, of which 0 were waited for; matrix products, arithmetic and copies ran while one was open for 0% of the time, Pallas kernels for 43%

profile of v9, /device:TPU:1, one launch (start us, length us, event | category | flops | bytes accessed | tf_op | source)
XLA Modules:
  0.0 51.6 jit_solution(13954855219945426186)
XLA Ops:
  0.6 2.9 %edge_rows.1 = (bf16[2,7,2,120,128]{4,3,2,1,0:T(8,128)(2,1)}, bf16[3,4,2,120,128]{4,3,2,1,0:T(8,128)(2,1)}, bf16[3,3,2,120,128]{4,3,2,1,0:T(8,128)(2,1)}) custom-call(bf16[8,2,120,840]{3,2,1,0:T(8,128)(2,1)} %image_ref.3, s32[8,840]{1,0:T(8,128)} %mask_ref.3), custom_call_target="tpu_custom_call" | custom-call | flops 1000000 | bytes 4000000 | tf_op jit(solution)/shard_map/edge_rows/pallas_call | solution.py:102
  3.5 2.0 %collective-permute-start.2 = (bf16[2,7,2,120,128]{4,3,2,1,0:T(8,128)(2,1)}, bf16[2,7,2,120,128]{4,3,2,1,0:T(8,128)(2,1)S(1)}, u32[]{:S(2)}, u32[]{:S(2)}) collective-permute-start(bf16[2,7,2,120,128]{4,3,2,1,0:T(8,128)(2,1)} %get-tuple-element.13), channel_id=1, source_target_pairs={{1,0},{2,1},{3,2},{4,3},{5,4},{6,5},{7,6},{8,7},{9,8},{10,9},{11,1... | collective-permute-start | bytes 2580488 | tf_op jit(solution)/shard_map/ppermute | solution.py:410
  5.5 4.5 %collective-permute-start.1 = (bf16[3,4,2,120,128]{4,3,2,1,0:T(8,128)(2,1)}, bf16[3,4,2,120,128]{4,3,2,1,0:T(8,128)(2,1)S(1)}, u32[]{:S(2)}, u32[]{:S(2)}) collective-permute-start(bf16[3,4,2,120,128]{4,3,2,1,0:T(8,128)(2,1)} %get-tuple-element.12), channel_id=1, source_target_pairs={{0,1},{1,2},{2,3},{3,4},{4,5},{5,6},{6,7},{7,8},{8,9},{9,10},{10,1... | collective-permute-start | bytes 2211848 | tf_op jit(solution)/shard_map/ppermute | solution.py:411
  10.0 0.0 copy-start
  10.0 2.0 %copy-done = bf16[8,2,120,840]{3,2,1,0:T(8,128)(2,1)S(1)} copy-done((bf16[8,2,120,840]{3,2,1,0:T(8,128)(2,1)S(1)}, bf16[8,2,120,840]{3,2,1,0:T(8,128)(2,1)}, u32[]{:S(2)}) %copy-start) | copy-done | bytes 3225624
  11.9 0.7 %copy-done.1 = s32[8,840]{1,0:T(8,128)S(1)} copy-done((s32[8,840]{1,0:T(8,128)S(1)}, s32[8,840]{1,0:T(8,128)}, u32[]{:S(2)}) %copy-start.1) | copy-done | bytes 26904
  12.7 9.0 %local_rows.1 = (bf16[8,7,4,128,128]{4,3,2,1,0:T(8,128)(2,1)S(1)}, f32[128,128]{1,0:T(8,128)S(1)}) custom-call(bf16[8,2,120,840]{3,2,1,0:T(8,128)(2,1)S(1)} %copy-done, s32[8,840]{1,0:T(8,128)S(1)} %copy-done.1), custom_call_target="tpu_custom_call" | custom-call | flops 1000000000 | bytes 5000000 | tf_op jit(solution)/shard_map/local_rows/pallas_call | solution.py:162
  21.6 3.4 %collective-permute-start.5 = (f32[128,128]{1,0:T(8,128)S(1)}, f32[128,128]{1,0:T(8,128)S(1)}, u32[]{:S(2)}, u32[]{:S(2)}) collective-permute-start(f32[128,128]{1,0:T(8,128)S(1)} %get-tuple-element.16), channel_id=1, source_target_pairs={{0,12},{1,13},{2,14},{3,15},{4,0},{5,1},{6,2},{7,3},{8,4},{9,5},{1... | collective-permute-start | bytes 196616 | tf_op jit(solution)/shard_map/ppermute | solution.py:398
  25.0 0.0 collective-permute-start.4
  25.0 0.4 collective-permute-start.3
  25.5 0.0 collective-permute-done.2.refs_0_
  25.5 3.2 %collective-permute-start = (bf16[3,3,2,120,128]{4,3,2,1,0:T(8,128)(2,1)}, bf16[3,3,2,120,128]{4,3,2,1,0:T(8,128)(2,1)S(1)}, u32[]{:S(2)}, u32[]{:S(2)}) collective-permute-start(bf16[3,3,2,120,128]{4,3,2,1,0:T(8,128)(2,1)} %get-tuple-element.10), channel_id=1, source_target_pairs={{0,1},{1,2},{2,3},{3,4},{4,5},{5,6},{6,7},{7,8},{8,9},{9,10},{10,1... | collective-permute-start | bytes 1658888 | tf_op jit(solution)/shard_map/ppermute | solution.py:412
  28.7 8.1 %looks.3 = (bf16[4,40,2,120,120]{4,3,2,1,0:T(8,128)(2,1)}, f32[128,128]{1,0:T(8,128)S(1)}) custom-call(bf16[2,7,2,120,128]{4,3,2,1,0:T(8,128)(2,1)S(1)} %collective-permute-done.2.refs_0_, bf16[8,7,4,128,128]{4,3,2,1,0:T(8,128)(2,1)S(1)} %get-tuple-element.11.refs_1_), custom_call_target="tpu_custom_call" | custom-call | flops 2818572288 | bytes 7000000 | tf_op jit(solution)/shard_map/looks/pallas_call | solution.py:358
  36.8 0.0 collective-permute-done.5
  36.8 0.0 collective-permute-done.4
  36.8 0.0 collective-permute-done.3
  36.8 0.1 collective-permute-start.8
  36.9 3.5 %collective-permute-start.7 = (f32[128,128]{1,0:T(8,128)S(1)}, f32[128,128]{1,0:T(8,128)S(1)}, u32[]{:S(2)}, u32[]{:S(2)}) collective-permute-start(f32[128,128]{1,0:T(8,128)S(1)} %add_add_fusion.refs_3_), channel_id=1, source_target_pairs={{0,2},{1,3},{2,0},{3,1},{4,6},{5,7},{6,4},{7,5},{8,10},{9,11},{10,... | collective-permute-start | bytes 196616 | tf_op jit(solution)/shard_map/ppermute | solution.py:398
  40.3 1.9 %collective-permute-start.6 = (f32[128,128]{1,0:T(8,128)S(1)}, f32[128,128]{1,0:T(8,128)S(1)}, u32[]{:S(2)}, u32[]{:S(2)}) collective-permute-start(f32[128,128]{1,0:T(8,128)S(1)} %add_add_fusion.refs_3_), channel_id=1, source_target_pairs={{0,1},{1,2},{2,3},{3,0},{4,5},{5,6},{6,7},{7,4},{8,9},{9,10},{10,1... | collective-permute-start | bytes 196616 | tf_op jit(solution)/shard_map/ppermute | solution.py:398
  42.3 0.0 collective-permute-done.1.refs_0_
  42.3 5.1 %looks.4 = (bf16[4,40,2,120,120]{4,3,2,1,0:T(8,128)(2,1)}, f32[128,128]{1,0:T(8,128)}) custom-call(bf16[3,4,2,120,128]{4,3,2,1,0:T(8,128)(2,1)S(1)} %collective-permute-done.1.refs_0_, bf16[8,7,4,128,128]{4,3,2,1,0:T(8,128)(2,1)S(1)} %get-tuple-element.11.refs_1_, ...), custom_call_target="tpu_custom_call", output_to_operand_aliasing={{0}: (2, {})} | custom-call | flops 1610612736 | bytes 4000000 | tf_op jit(solution)/shard_map/looks/pallas_call | solution.py:358
  47.4 0.0 collective-permute-done.8.refs_6_
  47.4 0.0 collective-permute-done.7.refs_5_
  47.4 4.1 %looks.5 = (bf16[4,40,2,120,120]{4,3,2,1,0:T(8,128)(2,1)}, f32[2,120,120]{2,1,0:T(8,128)}) custom-call(bf16[3,3,2,120,128]{4,3,2,1,0:T(8,128)(2,1)S(1)} %collective-permute-done.refs_0_, bf16[8,7,4,128,128]{4,3,2,1,0:T(8,128)(2,1)S(1)} %get-tuple-element.11.refs_1_, ...), custom_call_target="tpu_custom_call", output_to_operand_aliasing={{0}: (2, {})} | custom-call | flops 1207959552 | bytes 3000000 | tf_op jit(solution)/shard_map/looks/pallas_call | solution.py:358
  (4 shorter events, 0.0 us)
Async XLA Ops:
  3.5 22.0 %collective-permute-start.2 = (bf16[2,7,2,120,128]{4,3,2,1,0:T(8,128)(2,1)}, bf16[2,7,2,120,128]{4,3,2,1,0:T(8,128)(2,1)S(1)}, u32[]{:S(2)}, u32[]{:S(2)}) collective-permute-start(bf16[2,7,2,120,128]{4,3,2,1,0:T(8,128)(2,1)} %get-tuple-element.13), channel_id=1, source_target_pairs={{1,0},{2,1},{3,2},{4,3},{5,4},{6,5},{7,6},{8,7},{9,8},{10,9},{11,1... | collective-permute-start | bytes 2580488 | tf_op jit(solution)/shard_map/ppermute | solution.py:410
  5.5 36.8 %collective-permute-start.1 = (bf16[3,4,2,120,128]{4,3,2,1,0:T(8,128)(2,1)}, bf16[3,4,2,120,128]{4,3,2,1,0:T(8,128)(2,1)S(1)}, u32[]{:S(2)}, u32[]{:S(2)}) collective-permute-start(bf16[3,4,2,120,128]{4,3,2,1,0:T(8,128)(2,1)} %get-tuple-element.12), channel_id=1, source_target_pairs={{0,1},{1,2},{2,3},{3,4},{4,5},{5,6},{6,7},{7,8},{8,9},{9,10},{10,1... | collective-permute-start | bytes 2211848 | tf_op jit(solution)/shard_map/ppermute | solution.py:411
  10.0 2.0 %copy-start = (bf16[8,2,120,840]{3,2,1,0:T(8,128)(2,1)S(1)}, bf16[8,2,120,840]{3,2,1,0:T(8,128)(2,1)}, u32[]{:S(2)}) copy-start(bf16[8,2,120,840]{3,2,1,0:T(8,128)(2,1)} %image_ref.3) | copy-start | bytes 9676804
  11.9 0.7 %copy-start.1 = (s32[8,840]{1,0:T(8,128)S(1)}, s32[8,840]{1,0:T(8,128)}, u32[]{:S(2)}) copy-start(s32[8,840]{1,0:T(8,128)} %mask_ref.3) | copy-start | bytes 80644
  21.6 15.1 %collective-permute-start.5 = (f32[128,128]{1,0:T(8,128)S(1)}, f32[128,128]{1,0:T(8,128)S(1)}, u32[]{:S(2)}, u32[]{:S(2)}) collective-permute-start(f32[128,128]{1,0:T(8,128)S(1)} %get-tuple-element.16), channel_id=1, source_target_pairs={{0,12},{1,13},{2,14},{3,15},{4,0},{5,1},{6,2},{7,3},{8,4},{9,5},{1... | collective-permute-start | bytes 196616 | tf_op jit(solution)/shard_map/ppermute | solution.py:398
  25.0 11.8 %collective-permute-start.4 = (f32[128,128]{1,0:T(8,128)S(1)}, f32[128,128]{1,0:T(8,128)S(1)}, u32[]{:S(2)}, u32[]{:S(2)}) collective-permute-start(f32[128,128]{1,0:T(8,128)S(1)} %get-tuple-element.16), channel_id=1, source_target_pairs={{0,4},{1,5},{2,6},{3,7},{4,8},{5,9},{6,10},{7,11},{8,12},{9,13},{1... | collective-permute-start | bytes 196616 | tf_op jit(solution)/shard_map/ppermute | solution.py:398
  25.0 11.8 %collective-permute-start.3 = (f32[128,128]{1,0:T(8,128)S(1)}, f32[128,128]{1,0:T(8,128)S(1)}, u32[]{:S(2)}, u32[]{:S(2)}) collective-permute-start(f32[128,128]{1,0:T(8,128)S(1)} %get-tuple-element.16), channel_id=1, source_target_pairs={{0,8},{1,9},{2,10},{3,11},{4,12},{5,13},{6,14},{7,15},{8,0},{9,1},... | collective-permute-start | bytes 196616 | tf_op jit(solution)/shard_map/ppermute | solution.py:398
  25.5 21.9 %collective-permute-start = (bf16[3,3,2,120,128]{4,3,2,1,0:T(8,128)(2,1)}, bf16[3,3,2,120,128]{4,3,2,1,0:T(8,128)(2,1)S(1)}, u32[]{:S(2)}, u32[]{:S(2)}) collective-permute-start(bf16[3,3,2,120,128]{4,3,2,1,0:T(8,128)(2,1)} %get-tuple-element.10), channel_id=1, source_target_pairs={{0,1},{1,2},{2,3},{3,4},{4,5},{5,6},{6,7},{7,8},{8,9},{9,10},{10,1... | collective-permute-start | bytes 1658888 | tf_op jit(solution)/shard_map/ppermute | solution.py:412
  36.8 10.6 %collective-permute-start.8 = (f32[128,128]{1,0:T(8,128)S(1)}, f32[128,128]{1,0:T(8,128)S(1)}, u32[]{:S(2)}, u32[]{:S(2)}) collective-permute-start(f32[128,128]{1,0:T(8,128)S(1)} %add_add_fusion.refs_3_), channel_id=1, source_target_pairs={{0,3},{1,0},{2,1},{3,2},{4,7},{5,4},{6,5},{7,6},{8,11},{9,8},{10,9... | collective-permute-start | bytes 196616 | tf_op jit(solution)/shard_map/ppermute | solution.py:398
  36.9 10.5 %collective-permute-start.7 = (f32[128,128]{1,0:T(8,128)S(1)}, f32[128,128]{1,0:T(8,128)S(1)}, u32[]{:S(2)}, u32[]{:S(2)}) collective-permute-start(f32[128,128]{1,0:T(8,128)S(1)} %add_add_fusion.refs_3_), channel_id=1, source_target_pairs={{0,2},{1,3},{2,0},{3,1},{4,6},{5,7},{6,4},{7,5},{8,10},{9,11},{10,... | collective-permute-start | bytes 196616 | tf_op jit(solution)/shard_map/ppermute | solution.py:398
  40.3 7.1 %collective-permute-start.6 = (f32[128,128]{1,0:T(8,128)S(1)}, f32[128,128]{1,0:T(8,128)S(1)}, u32[]{:S(2)}, u32[]{:S(2)}) collective-permute-start(f32[128,128]{1,0:T(8,128)S(1)} %add_add_fusion.refs_3_), channel_id=1, source_target_pairs={{0,1},{1,2},{2,3},{3,0},{4,5},{5,6},{6,7},{7,4},{8,9},{9,10},{10,1... | collective-permute-start | bytes 196616 | tf_op jit(solution)/shard_map/ppermute | solution.py:398

commit v10 on v8

--- a/solution.py
+++ b/solution.py
@@ -290,9 +290,10 @@
                 picked = jnp.where(block == v, real[8 * v : 8 * v + 8], picked)
             power = jnp.sum(jnp.where(on_eye, picked, 0.0), axis=0, keepdims=True)
             across = lax.rsqrt(jnp.maximum(power, floor_power))
-            diagonal = jnp.where(on_eye, across, 0.0)
-            spread = jnp.concatenate([jnp.where(block == v, diagonal, 0.0) for v in range(count // 8)], axis=0)
-            scale = jnp.sum(spread, axis=1, keepdims=True) * across
+            run = jnp.where(on_eye, across, 0.0)
+            for shift in (1, 2, 4):
+                run = run + pltpu.roll(run, shift, 1)
+            scale = jnp.concatenate([run[:, 8 * v + 7 : 8 * v + 8] * across for v in range(count // 8)], axis=0)
             out_ref[w, l, 0] = (real[0:count] * scale).astype(jnp.bfloat16)[:, :count]
             out_ref[w, l, 1] = (imag[0:count] * scale).astype(jnp.bfloat16)[:, :count]
 

time: 46 us -> 49.1 us (1.067)
  Pallas kernels: 25.3 us -> 28.3 us
    pallas_call x3, Pallas kernels: 15.3 us -> 18.3 us  [looked(): pl.pallas_call(functools.partial(looks_kernel, half, previous is not None...]
  transfers between devices with their start and end apart: 9 -> 9, of which waited for: 0 -> 0; matrix products, arithmetic and copies ran while one was open for 0% -> 0% of each run, Pallas kernels for 41% -> 43%
where the time goes in v10:
time: 49.1 us; the launch traced here: 48.8 us
  Pallas kernels  28.3 us (58%)
  starting transfers between devices  19 us (39%)
  local copies, waits for them, and re-layouts  0.74 us (2%)
  between operations  0.72 us (1%)
    pallas_call x3, Pallas kernels, looked(): pl.pallas_call(functools.partial(looks_kernel, half, previous is not None...  18.3 us
    ppermute x6, starting transfers between devices, round_terms(): terms.append(lax.ppermute(value, axis, pairs))  9.29 us
    pallas_call x1, Pallas kernels, local_rows(): pl.pallas_call(local_kernel, in_specs=[far, far], out_specs=[far, pl.Bloc...  7.12 us
    ppermute x1, starting transfers between devices, shards(): before0 = lax.ppermute(low0, 'pix', forward)  4.46 us
    ppermute x1, starting transfers between devices, shards(): before1 = lax.ppermute(low1, 'pix', forward)  3.23 us
    pallas_call x1, Pallas kernels, edge_rows(): pl.pallas_call(functools.partial(edge_kernel, cut), in_specs=[far, far],...  2.88 us
    ppermute x1, starting transfers between devices, shards(): after = lax.ppermute(top, 'pix', backward)  1.97 us
  transfers between devices with their start and end apart: 9, of which 0 were waited for; matrix products, arithmetic and copies ran while one was open for 0% of the time, Pallas kernels for 43%

profile of v10, /device:TPU:1, one launch (start us, length us, event | category | flops | bytes accessed | tf_op | source)
XLA Modules:
  0.0 48.8 jit_solution(7961472526231567200)
XLA Ops:
  0.6 2.9 %edge_rows.1 = (bf16[2,7,2,120,128]{4,3,2,1,0:T(8,128)(2,1)}, bf16[3,4,2,120,128]{4,3,2,1,0:T(8,128)(2,1)}, bf16[3,3,2,120,128]{4,3,2,1,0:T(8,128)(2,1)}) custom-call(bf16[8,2,120,840]{3,2,1,0:T(8,128)(2,1)} %image_ref.3, s32[8,840]{1,0:T(8,128)} %mask_ref.3), custom_call_target="tpu_custom_call" | custom-call | flops 1000000 | bytes 4000000 | tf_op jit(solution)/shard_map/edge_rows/pallas_call | solution.py:103
  3.5 2.0 %collective-permute-start.2 = (bf16[2,7,2,120,128]{4,3,2,1,0:T(8,128)(2,1)}, bf16[2,7,2,120,128]{4,3,2,1,0:T(8,128)(2,1)S(1)}, u32[]{:S(2)}, u32[]{:S(2)}) collective-permute-start(bf16[2,7,2,120,128]{4,3,2,1,0:T(8,128)(2,1)} %get-tuple-element.13), channel_id=1, source_target_pairs={{1,0},{2,1},{3,2},{4,3},{5,4},{6,5},{7,6},{8,7},{9,8},{10,9},{11,1... | collective-permute-start | bytes 2580488 | tf_op jit(solution)/shard_map/ppermute | solution.py:384
  5.5 4.5 %collective-permute-start.1 = (bf16[3,4,2,120,128]{4,3,2,1,0:T(8,128)(2,1)}, bf16[3,4,2,120,128]{4,3,2,1,0:T(8,128)(2,1)S(1)}, u32[]{:S(2)}, u32[]{:S(2)}) collective-permute-start(bf16[3,4,2,120,128]{4,3,2,1,0:T(8,128)(2,1)} %get-tuple-element.12), channel_id=1, source_target_pairs={{0,1},{1,2},{2,3},{3,4},{4,5},{5,6},{6,7},{7,8},{8,9},{9,10},{10,1... | collective-permute-start | bytes 2211848 | tf_op jit(solution)/shard_map/ppermute | solution.py:385
  10.0 0.0 copy-start
  10.0 0.7 %copy-done = s32[8,840]{1,0:T(8,128)S(1)} copy-done((s32[8,840]{1,0:T(8,128)S(1)}, s32[8,840]{1,0:T(8,128)}, u32[]{:S(2)}) %copy-start) | copy-done | bytes 26904
  10.7 7.1 %local_rows.1 = (bf16[8,7,2,120,128]{4,3,2,1,0:T(8,128)(2,1)S(1)}, f32[128,128]{1,0:T(8,128)S(1)}) custom-call(bf16[8,2,120,840]{3,2,1,0:T(8,128)(2,1)} %image_ref.3, s32[8,840]{1,0:T(8,128)S(1)} %copy-done), custom_call_target="tpu_custom_call" | custom-call | flops 1000000000 | bytes 5000000 | tf_op jit(solution)/shard_map/local_rows/pallas_call | solution.py:160
  17.8 3.4 %collective-permute-start.5 = (f32[128,128]{1,0:T(8,128)S(1)}, f32[128,128]{1,0:T(8,128)S(1)}, u32[]{:S(2)}, u32[]{:S(2)}) collective-permute-start(f32[128,128]{1,0:T(8,128)S(1)} %get-tuple-element.16), channel_id=1, source_target_pairs={{0,12},{1,13},{2,14},{3,15},{4,0},{5,1},{6,2},{7,3},{8,4},{9,5},{1... | collective-permute-start | bytes 196616 | tf_op jit(solution)/shard_map/ppermute | solution.py:372
  21.2 0.0 collective-permute-start.4
  21.2 0.5 collective-permute-start.3
  21.7 0.0 collective-permute-done.2.refs_0_
  21.7 3.2 %collective-permute-start = (bf16[3,3,2,120,128]{4,3,2,1,0:T(8,128)(2,1)}, bf16[3,3,2,120,128]{4,3,2,1,0:T(8,128)(2,1)S(1)}, u32[]{:S(2)}, u32[]{:S(2)}) collective-permute-start(bf16[3,3,2,120,128]{4,3,2,1,0:T(8,128)(2,1)} %get-tuple-element.10), channel_id=1, source_target_pairs={{0,1},{1,2},{2,3},{3,4},{4,5},{5,6},{6,7},{7,8},{8,9},{9,10},{10,1... | collective-permute-start | bytes 1658888 | tf_op jit(solution)/shard_map/ppermute | solution.py:386
  24.9 8.6 %looks.3 = (bf16[4,40,2,120,120]{4,3,2,1,0:T(8,128)(2,1)}, f32[128,128]{1,0:T(8,128)S(1)}) custom-call(bf16[2,7,2,120,128]{4,3,2,1,0:T(8,128)(2,1)S(1)} %collective-permute-done.2.refs_0_, bf16[8,7,2,120,128]{4,3,2,1,0:T(8,128)(2,1)S(1)} %get-tuple-element.11.refs_1_), custom_call_target="tpu_custom_call" | custom-call | flops 2818572288 | bytes 7000000 | tf_op jit(solution)/shard_map/looks/pallas_call | solution.py:333
  33.5 0.0 collective-permute-done.5
  33.5 0.0 collective-permute-done.4
  33.5 0.0 collective-permute-done.3
  33.5 0.1 collective-permute-start.8
  33.6 3.5 %collective-permute-start.7 = (f32[128,128]{1,0:T(8,128)S(1)}, f32[128,128]{1,0:T(8,128)S(1)}, u32[]{:S(2)}, u32[]{:S(2)}) collective-permute-start(f32[128,128]{1,0:T(8,128)S(1)} %add_add_fusion.refs_3_), channel_id=1, source_target_pairs={{0,2},{1,3},{2,0},{3,1},{4,6},{5,7},{6,4},{7,5},{8,10},{9,11},{10,... | collective-permute-start | bytes 196616 | tf_op jit(solution)/shard_map/ppermute | solution.py:372
  37.1 1.9 %collective-permute-start.6 = (f32[128,128]{1,0:T(8,128)S(1)}, f32[128,128]{1,0:T(8,128)S(1)}, u32[]{:S(2)}, u32[]{:S(2)}) collective-permute-start(f32[128,128]{1,0:T(8,128)S(1)} %add_add_fusion.refs_3_), channel_id=1, source_target_pairs={{0,1},{1,2},{2,3},{3,0},{4,5},{5,6},{6,7},{7,4},{8,9},{9,10},{10,1... | collective-permute-start | bytes 196616 | tf_op jit(solution)/shard_map/ppermute | solution.py:372
  39.0 0.0 collective-permute-done.1.refs_0_
  39.0 5.4 %looks.4 = (bf16[4,40,2,120,120]{4,3,2,1,0:T(8,128)(2,1)}, f32[128,128]{1,0:T(8,128)}) custom-call(bf16[3,4,2,120,128]{4,3,2,1,0:T(8,128)(2,1)S(1)} %collective-permute-done.1.refs_0_, bf16[8,7,2,120,128]{4,3,2,1,0:T(8,128)(2,1)S(1)} %get-tuple-element.11.refs_1_, ...), custom_call_target="tpu_custom_call", output_to_operand_aliasing={{0}: (2, {})} | custom-call | flops 1610612736 | bytes 4000000 | tf_op jit(solution)/shard_map/looks/pallas_call | solution.py:333
  44.4 0.0 collective-permute-done.refs_0_
  44.4 0.0 collective-permute-done.8.refs_6_
  44.4 0.0 collective-permute-done.6.refs_4_
  44.4 4.4 %looks.5 = (bf16[4,40,2,120,120]{4,3,2,1,0:T(8,128)(2,1)}, f32[2,120,120]{2,1,0:T(8,128)}) custom-call(bf16[3,3,2,120,128]{4,3,2,1,0:T(8,128)(2,1)S(1)} %collective-permute-done.refs_0_, bf16[8,7,2,120,128]{4,3,2,1,0:T(8,128)(2,1)S(1)} %get-tuple-element.11.refs_1_, ...), custom_call_target="tpu_custom_call", output_to_operand_aliasing={{0}: (2, {})} | custom-call | flops 1207959552 | bytes 3000000 | tf_op jit(solution)/shard_map/looks/pallas_call | solution.py:333
  (2 shorter events, 0.0 us)
Async XLA Ops:
  3.5 18.2 %collective-permute-start.2 = (bf16[2,7,2,120,128]{4,3,2,1,0:T(8,128)(2,1)}, bf16[2,7,2,120,128]{4,3,2,1,0:T(8,128)(2,1)S(1)}, u32[]{:S(2)}, u32[]{:S(2)}) collective-permute-start(bf16[2,7,2,120,128]{4,3,2,1,0:T(8,128)(2,1)} %get-tuple-element.13), channel_id=1, source_target_pairs={{1,0},{2,1},{3,2},{4,3},{5,4},{6,5},{7,6},{8,7},{9,8},{10,9},{11,1... | collective-permute-start | bytes 2580488 | tf_op jit(solution)/shard_map/ppermute | solution.py:384
  5.5 33.5 %collective-permute-start.1 = (bf16[3,4,2,120,128]{4,3,2,1,0:T(8,128)(2,1)}, bf16[3,4,2,120,128]{4,3,2,1,0:T(8,128)(2,1)S(1)}, u32[]{:S(2)}, u32[]{:S(2)}) collective-permute-start(bf16[3,4,2,120,128]{4,3,2,1,0:T(8,128)(2,1)} %get-tuple-element.12), channel_id=1, source_target_pairs={{0,1},{1,2},{2,3},{3,4},{4,5},{5,6},{6,7},{7,8},{8,9},{9,10},{10,1... | collective-permute-start | bytes 2211848 | tf_op jit(solution)/shard_map/ppermute | solution.py:385
  10.0 0.8 %copy-start = (s32[8,840]{1,0:T(8,128)S(1)}, s32[8,840]{1,0:T(8,128)}, u32[]{:S(2)}) copy-start(s32[8,840]{1,0:T(8,128)} %mask_ref.3) | copy-start | bytes 80644
  17.8 15.7 %collective-permute-start.5 = (f32[128,128]{1,0:T(8,128)S(1)}, f32[128,128]{1,0:T(8,128)S(1)}, u32[]{:S(2)}, u32[]{:S(2)}) collective-permute-start(f32[128,128]{1,0:T(8,128)S(1)} %get-tuple-element.16), channel_id=1, source_target_pairs={{0,12},{1,13},{2,14},{3,15},{4,0},{5,1},{6,2},{7,3},{8,4},{9,5},{1... | collective-permute-start | bytes 196616 | tf_op jit(solution)/shard_map/ppermute | solution.py:372
  21.2 12.3 %collective-permute-start.4 = (f32[128,128]{1,0:T(8,128)S(1)}, f32[128,128]{1,0:T(8,128)S(1)}, u32[]{:S(2)}, u32[]{:S(2)}) collective-permute-start(f32[128,128]{1,0:T(8,128)S(1)} %get-tuple-element.16), channel_id=1, source_target_pairs={{0,4},{1,5},{2,6},{3,7},{4,8},{5,9},{6,10},{7,11},{8,12},{9,13},{1... | collective-permute-start | bytes 196616 | tf_op jit(solution)/shard_map/ppermute | solution.py:372
  21.2 12.3 %collective-permute-start.3 = (f32[128,128]{1,0:T(8,128)S(1)}, f32[128,128]{1,0:T(8,128)S(1)}, u32[]{:S(2)}, u32[]{:S(2)}) collective-permute-start(f32[128,128]{1,0:T(8,128)S(1)} %get-tuple-element.16), channel_id=1, source_target_pairs={{0,8},{1,9},{2,10},{3,11},{4,12},{5,13},{6,14},{7,15},{8,0},{9,1},... | collective-permute-start | bytes 196616 | tf_op jit(solution)/shard_map/ppermute | solution.py:372
  21.7 22.7 %collective-permute-start = (bf16[3,3,2,120,128]{4,3,2,1,0:T(8,128)(2,1)}, bf16[3,3,2,120,128]{4,3,2,1,0:T(8,128)(2,1)S(1)}, u32[]{:S(2)}, u32[]{:S(2)}) collective-permute-start(bf16[3,3,2,120,128]{4,3,2,1,0:T(8,128)(2,1)} %get-tuple-element.10), channel_id=1, source_target_pairs={{0,1},{1,2},{2,3},{3,4},{4,5},{5,6},{6,7},{7,8},{8,9},{9,10},{10,1... | collective-permute-start | bytes 1658888 | tf_op jit(solution)/shard_map/ppermute | solution.py:386
  33.5 10.9 %collective-permute-start.8 = (f32[128,128]{1,0:T(8,128)S(1)}, f32[128,128]{1,0:T(8,128)S(1)}, u32[]{:S(2)}, u32[]{:S(2)}) collective-permute-start(f32[128,128]{1,0:T(8,128)S(1)} %add_add_fusion.refs_3_), channel_id=1, source_target_pairs={{0,3},{1,0},{2,1},{3,2},{4,7},{5,4},{6,5},{7,6},{8,11},{9,8},{10,9... | collective-permute-start | bytes 196616 | tf_op jit(solution)/shard_map/ppermute | solution.py:372
  33.6 10.8 %collective-permute-start.7 = (f32[128,128]{1,0:T(8,128)S(1)}, f32[128,128]{1,0:T(8,128)S(1)}, u32[]{:S(2)}, u32[]{:S(2)}) collective-permute-start(f32[128,128]{1,0:T(8,128)S(1)} %add_add_fusion.refs_3_), channel_id=1, source_target_pairs={{0,2},{1,3},{2,0},{3,1},{4,6},{5,7},{6,4},{7,5},{8,10},{9,11},{10,... | collective-permute-start | bytes 196616 | tf_op jit(solution)/shard_map/ppermute | solution.py:372
  37.1 7.4 %collective-permute-start.6 = (f32[128,128]{1,0:T(8,128)S(1)}, f32[128,128]{1,0:T(8,128)S(1)}, u32[]{:S(2)}, u32[]{:S(2)}) collective-permute-start(f32[128,128]{1,0:T(8,128)S(1)} %add_add_fusion.refs_3_), channel_id=1, source_target_pairs={{0,1},{1,2},{2,3},{3,0},{4,5},{5,6},{6,7},{7,4},{8,9},{9,10},{10,1... | collective-permute-start | bytes 196616 | tf_op jit(solution)/shard_map/ppermute | solution.py:372

commit v11 on v8

--- a/solution.py
+++ b/solution.py
@@ -205,12 +205,15 @@
     other_ref, all_ref = refs[:2]
     refs = refs[2 + aliased :]
     term_refs, refs = refs[:terms], refs[terms:]
-    out_ref, extra_ref, w_ref, g_ref = refs
+    out_ref, extra_ref, w_ref, g_ref, eye_ref = refs
     count = all_ref.shape[3]
 
     @pl.when(pl.program_id(0) == 0)
     def _():
         w_ref[...] = jnp.zeros_like(w_ref)
+        i = lax.broadcasted_iota(jnp.int32, eye_ref.shape, 0)
+        j = lax.broadcasted_iota(jnp.int32, eye_ref.shape, 1)
+        eye_ref[...] = jnp.where(i == j % LANES, 1.0, 0.0).astype(jnp.bfloat16)
         if slab:
             real, imag = slab_values([t[...] for t in term_refs])
             extra_ref[0] = real[:count, :count]
@@ -283,16 +286,23 @@
                 g_ref[slot, w, 1, pl.ds(start, TILE)] = im[:, :LANES] - re[:, LANES:]
 
     def normalised(l):
+        acrosses, terms_of = [], []
         for w in range(2):
-            real, imag = g_ref.at[l % 2, w, 0], g_ref.at[l % 2, w, 1]
+            real = g_ref.at[l % 2, w, 0]
             picked = real[0:8]
             for v in range(1, count // 8):
                 picked = jnp.where(block == v, real[8 * v : 8 * v + 8], picked)
             power = jnp.sum(jnp.where(on_eye, picked, 0.0), axis=0, keepdims=True)
             across = lax.rsqrt(jnp.maximum(power, floor_power))
-            diagonal = jnp.where(on_eye, across, 0.0)
-            spread = jnp.concatenate([jnp.where(block == v, diagonal, 0.0) for v in range(count // 8)], axis=0)
-            scale = jnp.sum(spread, axis=1, keepdims=True) * across
+            acrosses.append(across)
+            tile = jnp.broadcast_to(across, (TILE, LANES))
+            high = tile.astype(jnp.bfloat16)
+            rest = (tile - high.astype(jnp.float32)).astype(jnp.bfloat16)
+            terms_of += [jnp.concatenate([high, rest], axis=1)] * (LANES // TILE)
+        down = lax.dot_general(eye_ref[...], jnp.concatenate(terms_of, axis=0), NT, preferred_element_type=jnp.float32)
+        for w in range(2):
+            real, imag = g_ref.at[l % 2, w, 0], g_ref.at[l % 2, w, 1]
+            scale = down[0:count, w * LANES : (w + 1) * LANES] * acrosses[w]
             out_ref[w, l, 0] = (real[0:count] * scale).astype(jnp.bfloat16)[:, :count]
             out_ref[w, l, 1] = (imag[0:count] * scale).astype(jnp.bfloat16)[:, :count]
 
@@ -339,6 +349,7 @@
         scratch_shapes=[
             pltpu.VMEM((2, 2, LANES, 2 * LANES), jnp.bfloat16),
             pltpu.VMEM((2, 2, 2, LANES, LANES), jnp.float32),
+            pltpu.VMEM((LANES, 2 * LANES), jnp.bfloat16),
         ],
         compiler_params=pltpu.CompilerParams(vmem_limit_bytes=49 * 2**20),
         cost_estimate=pl.CostEstimate(

time: 46 us -> 55 us (1.20)
  Pallas kernels: 25.3 us -> 34.3 us
    pallas_call x3, Pallas kernels: 15.3 us -> 24.3 us  [looked(): pl.pallas_call(functools.partial(looks_kernel, half, previous is not None...]
  transfers between devices with their start and end apart: 9 -> 9, of which waited for: 0 -> 0; matrix products, arithmetic and copies ran while one was open for 0% -> 0% of each run, Pallas kernels for 41% -> 47%
where the time goes in v11:
time: 55 us; the launch traced here: 54.7 us
  Pallas kernels  34.3 us (62%)
  starting transfers between devices  18.9 us (34%)
  local copies, waits for them, and re-layouts  0.74 us (1%)
  between operations  0.72 us (1%)
    pallas_call x3, Pallas kernels, looked(): pl.pallas_call(functools.partial(looks_kernel, half, previous is not None...  24.3 us
    ppermute x6, starting transfers between devices, round_terms(): terms.append(lax.ppermute(value, axis, pairs))  9.28 us
    pallas_call x1, Pallas kernels, local_rows(): pl.pallas_call(local_kernel, in_specs=[far, far], out_specs=[far, pl.Bloc...  7.12 us
    ppermute x1, starting transfers between devices, shards(): before0 = lax.ppermute(low0, 'pix', forward)  4.46 us
    ppermute x1, starting transfers between devices, shards(): before1 = lax.ppermute(low1, 'pix', forward)  3.23 us
    pallas_call x1, Pallas kernels, edge_rows(): pl.pallas_call(functools.partial(edge_kernel, cut), in_specs=[far, far],...  2.88 us
    ppermute x1, starting transfers between devices, shards(): after = lax.ppermute(top, 'pix', backward)  1.97 us
  transfers between devices with their start and end apart: 9, of which 0 were waited for; matrix products, arithmetic and copies ran while one was open for 0% of the time, Pallas kernels for 47%

profile of v11, /device:TPU:1, one launch (start us, length us, event | category | flops | bytes accessed | tf_op | source)
XLA Modules:
  0.0 54.7 jit_solution(11842744908118702421)
XLA Ops:
  0.6 2.9 %edge_rows.1 = (bf16[2,7,2,120,128]{4,3,2,1,0:T(8,128)(2,1)}, bf16[3,4,2,120,128]{4,3,2,1,0:T(8,128)(2,1)}, bf16[3,3,2,120,128]{4,3,2,1,0:T(8,128)(2,1)}) custom-call(bf16[8,2,120,840]{3,2,1,0:T(8,128)(2,1)} %image_ref.3, s32[8,840]{1,0:T(8,128)} %mask_ref.3), custom_call_target="tpu_custom_call" | custom-call | flops 1000000 | bytes 4000000 | tf_op jit(solution)/shard_map/edge_rows/pallas_call | solution.py:103
  3.5 2.0 %collective-permute-start.2 = (bf16[2,7,2,120,128]{4,3,2,1,0:T(8,128)(2,1)}, bf16[2,7,2,120,128]{4,3,2,1,0:T(8,128)(2,1)S(1)}, u32[]{:S(2)}, u32[]{:S(2)}) collective-permute-start(bf16[2,7,2,120,128]{4,3,2,1,0:T(8,128)(2,1)} %get-tuple-element.13), channel_id=1, source_target_pairs={{1,0},{2,1},{3,2},{4,3},{5,4},{6,5},{7,6},{8,7},{9,8},{10,9},{11,1... | collective-permute-start | bytes 2580488 | tf_op jit(solution)/shard_map/ppermute | solution.py:394
  5.5 4.5 %collective-permute-start.1 = (bf16[3,4,2,120,128]{4,3,2,1,0:T(8,128)(2,1)}, bf16[3,4,2,120,128]{4,3,2,1,0:T(8,128)(2,1)S(1)}, u32[]{:S(2)}, u32[]{:S(2)}) collective-permute-start(bf16[3,4,2,120,128]{4,3,2,1,0:T(8,128)(2,1)} %get-tuple-element.12), channel_id=1, source_target_pairs={{0,1},{1,2},{2,3},{3,4},{4,5},{5,6},{6,7},{7,8},{8,9},{9,10},{10,1... | collective-permute-start | bytes 2211848 | tf_op jit(solution)/shard_map/ppermute | solution.py:395
  10.0 0.0 copy-start
  10.0 0.7 %copy-done = s32[8,840]{1,0:T(8,128)S(1)} copy-done((s32[8,840]{1,0:T(8,128)S(1)}, s32[8,840]{1,0:T(8,128)}, u32[]{:S(2)}) %copy-start) | copy-done | bytes 26904
  10.7 7.1 %local_rows.1 = (bf16[8,7,2,120,128]{4,3,2,1,0:T(8,128)(2,1)S(1)}, f32[128,128]{1,0:T(8,128)S(1)}) custom-call(bf16[8,2,120,840]{3,2,1,0:T(8,128)(2,1)} %image_ref.3, s32[8,840]{1,0:T(8,128)S(1)} %copy-done), custom_call_target="tpu_custom_call" | custom-call | flops 1000000000 | bytes 5000000 | tf_op jit(solution)/shard_map/local_rows/pallas_call | solution.py:160
  17.8 3.4 %collective-permute-start.5 = (f32[128,128]{1,0:T(8,128)S(1)}, f32[128,128]{1,0:T(8,128)S(1)}, u32[]{:S(2)}, u32[]{:S(2)}) collective-permute-start(f32[128,128]{1,0:T(8,128)S(1)} %get-tuple-element.16), channel_id=1, source_target_pairs={{0,12},{1,13},{2,14},{3,15},{4,0},{5,1},{6,2},{7,3},{8,4},{9,5},{1... | collective-permute-start | bytes 196616 | tf_op jit(solution)/shard_map/ppermute | solution.py:382
  21.2 0.0 collective-permute-start.4
  21.2 0.5 collective-permute-start.3
  21.7 0.0 collective-permute-done.2.refs_0_
  21.7 3.2 %collective-permute-start = (bf16[3,3,2,120,128]{4,3,2,1,0:T(8,128)(2,1)}, bf16[3,3,2,120,128]{4,3,2,1,0:T(8,128)(2,1)S(1)}, u32[]{:S(2)}, u32[]{:S(2)}) collective-permute-start(bf16[3,3,2,120,128]{4,3,2,1,0:T(8,128)(2,1)} %get-tuple-element.10), channel_id=1, source_target_pairs={{0,1},{1,2},{2,3},{3,4},{4,5},{5,6},{6,7},{7,8},{8,9},{9,10},{10,1... | collective-permute-start | bytes 1658888 | tf_op jit(solution)/shard_map/ppermute | solution.py:396
  24.9 11.6 %looks.3 = (bf16[4,40,2,120,120]{4,3,2,1,0:T(8,128)(2,1)}, f32[128,128]{1,0:T(8,128)S(1)}) custom-call(bf16[2,7,2,120,128]{4,3,2,1,0:T(8,128)(2,1)S(1)} %collective-permute-done.2.refs_0_, bf16[8,7,2,120,128]{4,3,2,1,0:T(8,128)(2,1)S(1)} %get-tuple-element.11.refs_1_), custom_call_target="tpu_custom_call" | custom-call | flops 2818572288 | bytes 7000000 | tf_op jit(solution)/shard_map/looks/pallas_call | solution.py:342
  36.5 0.0 collective-permute-done.5
  36.5 0.0 collective-permute-done.4
  36.5 0.0 collective-permute-done.3
  36.5 0.1 collective-permute-start.8
  36.6 3.4 %collective-permute-start.7 = (f32[128,128]{1,0:T(8,128)S(1)}, f32[128,128]{1,0:T(8,128)S(1)}, u32[]{:S(2)}, u32[]{:S(2)}) collective-permute-start(f32[128,128]{1,0:T(8,128)S(1)} %add_add_fusion.refs_3_), channel_id=1, source_target_pairs={{0,2},{1,3},{2,0},{3,1},{4,6},{5,7},{6,4},{7,5},{8,10},{9,11},{10,... | collective-permute-start | bytes 196616 | tf_op jit(solution)/shard_map/ppermute | solution.py:382
  40.0 1.9 %collective-permute-start.6 = (f32[128,128]{1,0:T(8,128)S(1)}, f32[128,128]{1,0:T(8,128)S(1)}, u32[]{:S(2)}, u32[]{:S(2)}) collective-permute-start(f32[128,128]{1,0:T(8,128)S(1)} %add_add_fusion.refs_3_), channel_id=1, source_target_pairs={{0,1},{1,2},{2,3},{3,0},{4,5},{5,6},{6,7},{7,4},{8,9},{9,10},{10,1... | collective-permute-start | bytes 196616 | tf_op jit(solution)/shard_map/ppermute | solution.py:382
  42.0 0.0 collective-permute-done.1.refs_0_
  42.0 7.1 %looks.4 = (bf16[4,40,2,120,120]{4,3,2,1,0:T(8,128)(2,1)}, f32[128,128]{1,0:T(8,128)}) custom-call(bf16[3,4,2,120,128]{4,3,2,1,0:T(8,128)(2,1)S(1)} %collective-permute-done.1.refs_0_, bf16[8,7,2,120,128]{4,3,2,1,0:T(8,128)(2,1)S(1)} %get-tuple-element.11.refs_1_, ...), custom_call_target="tpu_custom_call", output_to_operand_aliasing={{0}: (2, {})} | custom-call | flops 1610612736 | bytes 4000000 | tf_op jit(solution)/shard_map/looks/pallas_call | solution.py:342
  49.1 0.0 collective-permute-done.refs_0_
  49.1 0.0 collective-permute-done.8.refs_6_
  49.1 0.0 collective-permute-done.7.refs_5_
  49.1 5.6 %looks.5 = (bf16[4,40,2,120,120]{4,3,2,1,0:T(8,128)(2,1)}, f32[2,120,120]{2,1,0:T(8,128)}) custom-call(bf16[3,3,2,120,128]{4,3,2,1,0:T(8,128)(2,1)S(1)} %collective-permute-done.refs_0_, bf16[8,7,2,120,128]{4,3,2,1,0:T(8,128)(2,1)S(1)} %get-tuple-element.11.refs_1_, ...), custom_call_target="tpu_custom_call", output_to_operand_aliasing={{0}: (2, {})} | custom-call | flops 1207959552 | bytes 3000000 | tf_op jit(solution)/shard_map/looks/pallas_call | solution.py:342
  (2 shorter events, 0.0 us)
Async XLA Ops:
  3.5 18.2 %collective-permute-start.2 = (bf16[2,7,2,120,128]{4,3,2,1,0:T(8,128)(2,1)}, bf16[2,7,2,120,128]{4,3,2,1,0:T(8,128)(2,1)S(1)}, u32[]{:S(2)}, u32[]{:S(2)}) collective-permute-start(bf16[2,7,2,120,128]{4,3,2,1,0:T(8,128)(2,1)} %get-tuple-element.13), channel_id=1, source_target_pairs={{1,0},{2,1},{3,2},{4,3},{5,4},{6,5},{7,6},{8,7},{9,8},{10,9},{11,1... | collective-permute-start | bytes 2580488 | tf_op jit(solution)/shard_map/ppermute | solution.py:394
  5.5 36.5 %collective-permute-start.1 = (bf16[3,4,2,120,128]{4,3,2,1,0:T(8,128)(2,1)}, bf16[3,4,2,120,128]{4,3,2,1,0:T(8,128)(2,1)S(1)}, u32[]{:S(2)}, u32[]{:S(2)}) collective-permute-start(bf16[3,4,2,120,128]{4,3,2,1,0:T(8,128)(2,1)} %get-tuple-element.12), channel_id=1, source_target_pairs={{0,1},{1,2},{2,3},{3,4},{4,5},{5,6},{6,7},{7,8},{8,9},{9,10},{10,1... | collective-permute-start | bytes 2211848 | tf_op jit(solution)/shard_map/ppermute | solution.py:395
  10.0 0.8 %copy-start = (s32[8,840]{1,0:T(8,128)S(1)}, s32[8,840]{1,0:T(8,128)}, u32[]{:S(2)}) copy-start(s32[8,840]{1,0:T(8,128)} %mask_ref.3) | copy-start | bytes 80644
  17.8 18.7 %collective-permute-start.5 = (f32[128,128]{1,0:T(8,128)S(1)}, f32[128,128]{1,0:T(8,128)S(1)}, u32[]{:S(2)}, u32[]{:S(2)}) collective-permute-start(f32[128,128]{1,0:T(8,128)S(1)} %get-tuple-element.16), channel_id=1, source_target_pairs={{0,12},{1,13},{2,14},{3,15},{4,0},{5,1},{6,2},{7,3},{8,4},{9,5},{1... | collective-permute-start | bytes 196616 | tf_op jit(solution)/shard_map/ppermute | solution.py:382
  21.2 15.3 %collective-permute-start.4 = (f32[128,128]{1,0:T(8,128)S(1)}, f32[128,128]{1,0:T(8,128)S(1)}, u32[]{:S(2)}, u32[]{:S(2)}) collective-permute-start(f32[128,128]{1,0:T(8,128)S(1)} %get-tuple-element.16), channel_id=1, source_target_pairs={{0,4},{1,5},{2,6},{3,7},{4,8},{5,9},{6,10},{7,11},{8,12},{9,13},{1... | collective-permute-start | bytes 196616 | tf_op jit(solution)/shard_map/ppermute | solution.py:382
  21.2 15.3 %collective-permute-start.3 = (f32[128,128]{1,0:T(8,128)S(1)}, f32[128,128]{1,0:T(8,128)S(1)}, u32[]{:S(2)}, u32[]{:S(2)}) collective-permute-start(f32[128,128]{1,0:T(8,128)S(1)} %get-tuple-element.16), channel_id=1, source_target_pairs={{0,8},{1,9},{2,10},{3,11},{4,12},{5,13},{6,14},{7,15},{8,0},{9,1},... | collective-permute-start | bytes 196616 | tf_op jit(solution)/shard_map/ppermute | solution.py:382
  21.7 27.4 %collective-permute-start = (bf16[3,3,2,120,128]{4,3,2,1,0:T(8,128)(2,1)}, bf16[3,3,2,120,128]{4,3,2,1,0:T(8,128)(2,1)S(1)}, u32[]{:S(2)}, u32[]{:S(2)}) collective-permute-start(bf16[3,3,2,120,128]{4,3,2,1,0:T(8,128)(2,1)} %get-tuple-element.10), channel_id=1, source_target_pairs={{0,1},{1,2},{2,3},{3,4},{4,5},{5,6},{6,7},{7,8},{8,9},{9,10},{10,1... | collective-permute-start | bytes 1658888 | tf_op jit(solution)/shard_map/ppermute | solution.py:396
  36.5 12.5 %collective-permute-start.8 = (f32[128,128]{1,0:T(8,128)S(1)}, f32[128,128]{1,0:T(8,128)S(1)}, u32[]{:S(2)}, u32[]{:S(2)}) collective-permute-start(f32[128,128]{1,0:T(8,128)S(1)} %add_add_fusion.refs_3_), channel_id=1, source_target_pairs={{0,3},{1,0},{2,1},{3,2},{4,7},{5,4},{6,5},{7,6},{8,11},{9,8},{10,9... | collective-permute-start | bytes 196616 | tf_op jit(solution)/shard_map/ppermute | solution.py:382
  36.6 12.5 %collective-permute-start.7 = (f32[128,128]{1,0:T(8,128)S(1)}, f32[128,128]{1,0:T(8,128)S(1)}, u32[]{:S(2)}, u32[]{:S(2)}) collective-permute-start(f32[128,128]{1,0:T(8,128)S(1)} %add_add_fusion.refs_3_), channel_id=1, source_target_pairs={{0,2},{1,3},{2,0},{3,1},{4,6},{5,7},{6,4},{7,5},{8,10},{9,11},{10,... | collective-permute-start | bytes 196616 | tf_op jit(solution)/shard_map/ppermute | solution.py:382
  40.0 9.0 %collective-permute-start.6 = (f32[128,128]{1,0:T(8,128)S(1)}, f32[128,128]{1,0:T(8,128)S(1)}, u32[]{:S(2)}, u32[]{:S(2)}) collective-permute-start(f32[128,128]{1,0:T(8,128)S(1)} %add_add_fusion.refs_3_), channel_id=1, source_target_pairs={{0,1},{1,2},{2,3},{3,0},{4,5},{5,6},{6,7},{7,4},{8,9},{9,10},{10,1... | collective-permute-start | bytes 196616 | tf_op jit(solution)/shard_map/ppermute | solution.py:382

commit v12 on v8

--- a/solution.py
+++ b/solution.py
@@ -14,7 +14,7 @@
 PER = LANES // LOOK
 SPAN = PER * LOOK
 ROWS = 8
-SKEW = (5, 0, 1, 2, 3, 4, 1, 2)
+SKEW = (3, 4, 5, 4, 5, 0, 1, 2)
 BEFORE, AFTER = 3, 2
 NT = (((1,), (1,)), ((), ()))
 
@@ -194,35 +194,35 @@
     return real / scaled, imag / scaled
 
 
-INNER = (1, 2, 3, 4, 5)
-HALVES = (
-    ((-3, -2, -1, 0), (((1, 2, 3), None), (None, (-1, 0)))),
-    ((6, 7, 8, 9), ((None, (6, 7)), ((3, 4, 5), None))),
-)
-
-
-def looks_kernel(half, aliased, terms, slab, *refs):
-    other_ref, all_ref = refs[:2]
-    refs = refs[2 + aliased :]
+TILES = ((-3, -2, -1, 0, 1, 2), (3, 4, 5, 6, 7, 8))
+LAST = ROWS + AFTER - 1
+WINDOWS = tuple(tuple(range(2 * w - 3, 2 * w + 4)) for w in range(ROWS // 2))
+
+
+def looks_kernel(aliased, terms, *refs):
+    before_ref, all_ref, after_ref = refs[:3]
+    refs = refs[3 + aliased :]
     term_refs, refs = refs[:terms], refs[terms:]
-    out_ref, extra_ref, w_ref, g_ref = refs
+    if terms:
+        out_ref, slab_ref, w_ref, g_ref, last_ref, e_ref = refs
+    else:
+        out_ref, w_ref, g_ref, last_ref, e_ref = refs
     count = all_ref.shape[3]
 
     @pl.when(pl.program_id(0) == 0)
     def _():
         w_ref[...] = jnp.zeros_like(w_ref)
-        if slab:
+        last_ref[...] = jnp.zeros_like(last_ref)
+        if terms:
             real, imag = slab_values([t[...] for t in term_refs])
-            extra_ref[0] = real[:count, :count]
-            extra_ref[1] = imag[:count, :count]
-        elif terms:
-            extra_ref[...] = added([t[...] for t in term_refs])
-        else:
-            extra_ref[...] = jnp.zeros_like(extra_ref)
+            slab_ref[0] = real[:count, :count]
+            slab_ref[1] = imag[:count, :count]
 
     rows = {r: all_ref.at[r, 0] for r in range(ROWS)}
-    for r in range(other_ref.shape[0]):
-        rows[ROWS + r if half else r - BEFORE] = other_ref.at[r, 0]
+    for r in range(BEFORE):
+        rows[r - BEFORE] = before_ref.at[r, 0]
+    for r in range(AFTER):
+        rows[ROWS + r] = after_ref.at[r, 0]
 
     lane = lax.broadcasted_iota(jnp.int32, (1, LANES), 1)
 
@@ -247,43 +247,69 @@
         return out
 
     def kept(l, which):
-        select = single[turn(l, which[0])]
-        for r in which[1:]:
+        select = jnp.zeros((1, LANES), jnp.bool_)
+        for r in which:
             select = select | single[turn(l, r)]
         return select.astype(jnp.float32)
+
+    def masked(value, lanes):
+        lanes = jnp.broadcast_to(lanes, value.shape).astype(jnp.bfloat16) != 0
+        value = jnp.where(lanes, value, jnp.zeros_like(value))
+        parts = []
+        for start in range(0, LANES, TILE):
+            parts += [value[start : start + TILE], value[LANES + start : LANES + start + TILE]]
+        return parts
+
+    def combined(gram, base, put):
+        for start in range(0, LANES, TILE):
+            at = base + 2 * start
+            re, im = gram[at : at + TILE], gram[at + TILE : at + 2 * TILE]
+            put(start, re[:, :LANES] + im[:, LANES:], im[:, :LANES] - re[:, LANES:])
+
+    for k in range(2):
+        last_ref[k, pl.ds(0, count), :] = rows[LAST][k]
+    last = last_ref[...].reshape(2 * LANES, LANES)
+    reads = []
+    for l in range(PER):
+        reads += masked(last, kept(l, (LAST,)))
+    last_gram = lax.dot_general(jnp.concatenate(reads, axis=0), last, NT, preferred_element_type=jnp.float32)
+    for l in range(PER):
+
+        def put_last(start, real, imag):
+            e_ref[l, 0, pl.ds(start, TILE)] = real
+            e_ref[l, 1, pl.ds(start, TILE)] = imag
+
+        combined(last_gram, 2 * LANES * l, put_last)
 
     eight = (8, LANES)
     along = lax.broadcasted_iota(jnp.int32, eight, 1)
     on_eye = along % 8 == lax.broadcasted_iota(jnp.int32, eight, 0)
     block = along // 8
 
-    outer_rows, windows = HALVES[half]
-
     def products(l):
         slot = l % 2
         for k in range(2):
-            w_ref[slot, k, pl.ds(0, count), pl.ds(0, LANES)] = gathered(l, k, INNER)
-            w_ref[slot, k, pl.ds(0, count), pl.ds(LANES, LANES)] = gathered(l, k, outer_rows)
+            for t, which in enumerate(TILES):
+                w_ref[slot, k, pl.ds(0, count), pl.ds(t * LANES, LANES)] = gathered(l, k, which)
         every = w_ref[slot].reshape(2 * LANES, 2 * LANES)
-        nothing = jnp.zeros_like(every)
         reads = []
-        for inner_rows, rest_rows in windows:
-            lanes = jnp.concatenate([kept(l, inner_rows or INNER), kept(l, rest_rows or outer_rows)], axis=1)
-            lanes = jnp.broadcast_to(lanes, every.shape).astype(jnp.bfloat16) != 0
-            read = jnp.where(lanes, every, nothing)
-            for start in range(0, LANES, TILE):
-                reads.append(read[start : start + TILE])
-                reads.append(read[LANES + start : LANES + start + TILE])
+        for window in WINDOWS:
+            lanes = [kept(l, [r for r in which if r in window]) for which in TILES]
+            reads += masked(every, jnp.concatenate(lanes, axis=1))
         gram = lax.dot_general(jnp.concatenate(reads, axis=0), every, NT, preferred_element_type=jnp.float32)
-        for w in range(2):
-            for start in range(0, LANES, TILE):
-                base = 2 * (w * LANES + start)
-                re, im = gram[base : base + TILE], gram[base + TILE : base + 2 * TILE]
-                g_ref[slot, w, 0, pl.ds(start, TILE)] = re[:, :LANES] + im[:, LANES:]
-                g_ref[slot, w, 1, pl.ds(start, TILE)] = im[:, :LANES] - re[:, LANES:]
+        for w, window in enumerate(WINDOWS):
+
+            def put(start, real, imag):
+                if LAST in window:
+                    real = real + e_ref[l, 0, pl.ds(start, TILE)]
+                    imag = imag + e_ref[l, 1, pl.ds(start, TILE)]
+                g_ref[slot, w, 0, pl.ds(start, TILE)] = real
+                g_ref[slot, w, 1, pl.ds(start, TILE)] = imag
+
+            combined(gram, 2 * LANES * w, put)
 
     def normalised(l):
-        for w in range(2):
+        for w in range(len(WINDOWS)):
             real, imag = g_ref.at[l % 2, w, 0], g_ref.at[l % 2, w, 1]
             picked = real[0:8]
             for v in range(1, count // 8):
@@ -303,15 +329,14 @@
         normalised(l)
 
 
-def looked(half, other, rows, first, groups, looks, previous, terms, slab):
-    count = other.shape[3]
-
-    def spec(array):
-        offset = 0 if array is other else first
+def looked(before, rows, after, first, groups, looks, previous, terms):
+    count = rows.shape[3]
+
+    def spec(array, offset):
         return pl.BlockSpec((array.shape[0], 1) + array.shape[2:], lambda s: (0, s + offset, 0, 0, 0))
 
-    operands = [other, rows]
-    in_specs = [spec(a) for a in operands]
+    operands = [before, rows, after]
+    in_specs = [spec(before, 0), spec(rows, first), spec(after, first)]
     aliases = {}
     if previous is not None:
         aliases = {len(operands): 0}
@@ -320,17 +345,13 @@
     for term in terms:
         operands.append(term)
         in_specs.append(pl.BlockSpec(term.shape, lambda s: (0, 0)))
-    extra = (2, count, count) if slab else (LANES, LANES)
-    out_specs = [
-        pl.BlockSpec((2, PER, 2, count, count), lambda s: (half, s + first, 0, 0, 0)),
-        pl.BlockSpec(extra, lambda s: (0,) * len(extra)),
-    ]
-    out_shape = [
-        jax.ShapeDtypeStruct((ROWS // 2, looks, 2, count, count), jnp.bfloat16),
-        jax.ShapeDtypeStruct(extra, jnp.float32),
-    ]
+    out_specs = [pl.BlockSpec((ROWS // 2, PER, 2, count, count), lambda s: (0, s + first, 0, 0, 0))]
+    out_shape = [jax.ShapeDtypeStruct((ROWS // 2, looks, 2, count, count), jnp.bfloat16)]
+    if terms:
+        out_specs.append(pl.BlockSpec((2, count, count), lambda s: (0, 0, 0)))
+        out_shape.append(jax.ShapeDtypeStruct((2, count, count), jnp.float32))
     return pl.pallas_call(
-        functools.partial(looks_kernel, half, previous is not None, len(terms), slab),
+        functools.partial(looks_kernel, previous is not None, len(terms)),
         grid=(groups,),
         in_specs=in_specs,
         out_specs=out_specs,
@@ -338,11 +359,13 @@
         input_output_aliases=aliases,
         scratch_shapes=[
             pltpu.VMEM((2, 2, LANES, 2 * LANES), jnp.bfloat16),
-            pltpu.VMEM((2, 2, 2, LANES, LANES), jnp.float32),
+            pltpu.VMEM((2, ROWS // 2, 2, LANES, LANES), jnp.float32),
+            pltpu.VMEM((2, LANES, LANES), jnp.bfloat16),
+            pltpu.VMEM((PER, 2, LANES, LANES), jnp.float32),
         ],
         compiler_params=pltpu.CompilerParams(vmem_limit_bytes=49 * 2**20),
         cost_estimate=pl.CostEstimate(
-            flops=1 * groups * PER * 2 * 512 * 256 * 256, bytes_accessed=groups * 10**6, transcendentals=0
+            flops=1 * groups * PER * 2 * 1024 * 256 * 256, bytes_accessed=2 * groups * 10**6, transcendentals=0
         ),
         name="looks",
     )(*operands)
@@ -384,16 +407,14 @@
     before0 = lax.ppermute(low0, "pix", forward)
     before1 = lax.ppermute(low1, "pix", forward)
     rows, total = local_rows(images, valid_mask, groups)
+    terms = [total]
     steps = rounds(size)
     if steps is None:
         terms, steps = [lax.psum(total, "pix")], []
-    else:
-        terms = round_terms(total, "pix", *steps[0]) if steps else [total]
-    out, zeros = looked(1, after, rows, 0, groups, looks, None, [], False)
-    for step in steps[1:]:
-        terms = round_terms(added(terms) + zeros, "pix", *step)
-    out, _ = looked(0, before0, rows, 0, cut, looks, out, [], False)
-    out, slab = looked(0, before1, rows, cut, groups - cut, looks, out, terms, True)
+    for step in steps:
+        terms = round_terms(added(terms), "pix", *step)
+    (out,) = looked(before0, rows, after, 0, cut, looks, None, [])
+    out, slab = looked(before1, rows, after, cut, groups - cut, looks, out, terms)
     return (out, slab)
 
 

time: 46 us -> 45.3 us (0.985)
  waiting for transfers between devices: 0.02 us -> 4.1 us
  starting transfers between devices: 18.9 us -> 15.7 us
  Pallas kernels: 25.3 us -> 23.8 us
    ppermute x6, waiting for transfers between devices: 0.02 us -> 4.09 us  [round_terms(): terms.append(lax.ppermute(value, axis, pairs))]
    ppermute x6, starting transfers between devices: 9.28 us -> 6.37 us  [round_terms(): terms.append(lax.ppermute(value, axis, pairs))]
    pallas_call x3 -> x2, Pallas kernels: 15.3 us -> 13.8 us  [looked(): pl.pallas_call(functools.partial(looks_kernel, previous is not None, len(...]
  transfers between devices with their start and end apart: 9 -> 9, of which waited for: 0 -> 3; matrix products, arithmetic and copies ran while one was open for 0% -> 0% of each run, Pallas kernels for 41% -> 33%
where the time goes in v12:
time: 45.3 us; the launch traced here: 45 us
  Pallas kernels  23.8 us (53%)
  starting transfers between devices  15.7 us (35%)
  waiting for transfers between devices  4.1 us (9%)
  local copies, waits for them, and re-layouts  0.74 us (2%)
  between operations  0.7 us (2%)
    pallas_call x2, Pallas kernels, looked(): pl.pallas_call(functools.partial(looks_kernel, previous is not None, len(...  13.8 us
    pallas_call x1, Pallas kernels, local_rows(): pl.pallas_call(local_kernel, in_specs=[far, far], out_specs=[far, pl.Bloc...  7.12 us
    ppermute x6, starting transfers between devices, round_terms(): terms.append(lax.ppermute(value, axis, pairs))  6.37 us
    ppermute x1, starting transfers between devices, shards(): before0 = lax.ppermute(low0, 'pix', forward)  4.46 us
    ppermute x6, waiting for transfers between devices, round_terms(): terms.append(lax.ppermute(value, axis, pairs))  4.09 us
    ppermute x1, starting transfers between devices, shards(): before1 = lax.ppermute(low1, 'pix', forward)  2.9 us
    pallas_call x1, Pallas kernels, edge_rows(): pl.pallas_call(functools.partial(edge_kernel, cut), in_specs=[far, far],...  2.87 us
    ppermute x1, starting transfers between devices, shards(): after = lax.ppermute(top, 'pix', backward)  1.97 us
  transfers between devices with their start and end apart: 9, of which 3 were waited for; matrix products, arithmetic and copies ran while one was open for 0% of the time, Pallas kernels for 33%

profile of v12, /device:TPU:1, one launch (start us, length us, event | category | flops | bytes accessed | tf_op | source)
XLA Modules:
  0.0 45.0 jit_solution(7736132414145061296)
XLA Ops:
  0.6 2.9 %edge_rows.1 = (bf16[2,7,2,120,128]{4,3,2,1,0:T(8,128)(2,1)}, bf16[3,4,2,120,128]{4,3,2,1,0:T(8,128)(2,1)}, bf16[3,3,2,120,128]{4,3,2,1,0:T(8,128)(2,1)}) custom-call(bf16[8,2,120,840]{3,2,1,0:T(8,128)(2,1)} %image_ref.3, s32[8,840]{1,0:T(8,128)} %mask_ref.3), custom_call_target="tpu_custom_call" | custom-call | flops 1000000 | bytes 4000000 | tf_op jit(solution)/shard_map/edge_rows/pallas_call | solution.py:103
  3.5 2.0 %collective-permute-start.1 = (bf16[2,7,2,120,128]{4,3,2,1,0:T(8,128)(2,1)}, bf16[2,7,2,120,128]{4,3,2,1,0:T(8,128)(2,1)S(1)}, u32[]{:S(2)}, u32[]{:S(2)}) collective-permute-start(bf16[2,7,2,120,128]{4,3,2,1,0:T(8,128)(2,1)} %get-tuple-element.9), channel_id=1, source_target_pairs={{1,0},{2,1},{3,2},{4,3},{5,4},{6,5},{7,6},{8,7},{9,8},{10,9},{11,1... | collective-permute-start | bytes 2580488 | tf_op jit(solution)/shard_map/ppermute | solution.py:406
  5.5 4.5 %collective-permute-start.2 = (bf16[3,4,2,120,128]{4,3,2,1,0:T(8,128)(2,1)}, bf16[3,4,2,120,128]{4,3,2,1,0:T(8,128)(2,1)S(1)}, u32[]{:S(2)}, u32[]{:S(2)}) collective-permute-start(bf16[3,4,2,120,128]{4,3,2,1,0:T(8,128)(2,1)} %get-tuple-element.10), channel_id=1, source_target_pairs={{0,1},{1,2},{2,3},{3,4},{4,5},{5,6},{6,7},{7,8},{8,9},{9,10},{10,1... | collective-permute-start | bytes 2211848 | tf_op jit(solution)/shard_map/ppermute | solution.py:407
  10.0 0.0 copy-start
  10.0 0.7 %copy-done = s32[8,840]{1,0:T(8,128)S(1)} copy-done((s32[8,840]{1,0:T(8,128)S(1)}, s32[8,840]{1,0:T(8,128)}, u32[]{:S(2)}) %copy-start) | copy-done | bytes 26904
  10.7 7.1 %local_rows.1 = (bf16[8,7,2,120,128]{4,3,2,1,0:T(8,128)(2,1)S(1)}, f32[128,128]{1,0:T(8,128)S(1)}) custom-call(bf16[8,2,120,840]{3,2,1,0:T(8,128)(2,1)} %image_ref.3, s32[8,840]{1,0:T(8,128)S(1)} %copy-done), custom_call_target="tpu_custom_call" | custom-call | flops 1000000000 | bytes 5000000 | tf_op jit(solution)/shard_map/local_rows/pallas_call | solution.py:160
  17.8 3.4 %collective-permute-start.5 = (f32[128,128]{1,0:T(8,128)S(1)}, f32[128,128]{1,0:T(8,128)S(1)}, u32[]{:S(2)}, u32[]{:S(2)}) collective-permute-start(f32[128,128]{1,0:T(8,128)S(1)} %get-tuple-element.11), channel_id=1, source_target_pairs={{0,12},{1,13},{2,14},{3,15},{4,0},{5,1},{6,2},{7,3},{8,4},{9,5},{1... | collective-permute-start | bytes 196616 | tf_op jit(solution)/shard_map/ppermute | solution.py:394
  21.2 0.0 collective-permute-start.4
  21.2 0.5 collective-permute-start.3
  21.7 1.3 %collective-permute-done.5 = f32[128,128]{1,0:T(8,128)S(1)} collective-permute-done((f32[128,128]{1,0:T(8,128)S(1)}, f32[128,128]{1,0:T(8,128)S(1)}, u32[]{:S(2)}, u32[]{:S(2)}) %collective-permute-start.5) | collective-permute-done | bytes 65568 | tf_op jit(solution)/shard_map/ppermute | solution.py:394
  22.9 2.9 %collective-permute-start = (bf16[3,3,2,120,128]{4,3,2,1,0:T(8,128)(2,1)}, bf16[3,3,2,120,128]{4,3,2,1,0:T(8,128)(2,1)S(1)}, u32[]{:S(2)}, u32[]{:S(2)}) collective-permute-start(bf16[3,3,2,120,128]{4,3,2,1,0:T(8,128)(2,1)} %get-tuple-element.7), channel_id=1, source_target_pairs={{0,1},{1,2},{2,3},{3,4},{4,5},{5,6},{6,7},{7,8},{8,9},{9,10},{10,1... | collective-permute-start | bytes 1658888 | tf_op jit(solution)/shard_map/ppermute | solution.py:408
  25.8 0.9 %collective-permute-done.4 = f32[128,128]{1,0:T(8,128)S(1)} collective-permute-done((f32[128,128]{1,0:T(8,128)S(1)}, f32[128,128]{1,0:T(8,128)S(1)}, u32[]{:S(2)}, u32[]{:S(2)}) %collective-permute-start.4) | collective-permute-done | bytes 65568 | tf_op jit(solution)/shard_map/ppermute | solution.py:394
  26.8 1.9 %collective-permute-done.3 = f32[128,128]{1,0:T(8,128)S(1)} collective-permute-done((f32[128,128]{1,0:T(8,128)S(1)}, f32[128,128]{1,0:T(8,128)S(1)}, u32[]{:S(2)}, u32[]{:S(2)}) %collective-permute-start.3) | collective-permute-done | bytes 65568 | tf_op jit(solution)/shard_map/ppermute | solution.py:394
  28.7 0.8 %collective-permute-start.8 = (f32[128,128]{1,0:T(8,128)S(1)}, f32[128,128]{1,0:T(8,128)S(1)}, u32[]{:S(2)}, u32[]{:S(2)}) collective-permute-start(f32[128,128]{1,0:T(8,128)S(1)} %add_add_fusion.refs_4_), channel_id=1, source_target_pairs={{0,3},{1,0},{2,1},{3,2},{4,7},{5,4},{6,5},{7,6},{8,11},{9,8},{10,9... | collective-permute-start | bytes 196616 | tf_op jit(solution)/shard_map/ppermute | solution.py:394
  29.5 0.2 collective-permute-start.7
  29.7 0.0 collective-permute-done.2.refs_0_
  29.7 1.5 %collective-permute-start.6 = (f32[128,128]{1,0:T(8,128)S(1)}, f32[128,128]{1,0:T(8,128)S(1)}, u32[]{:S(2)}, u32[]{:S(2)}) collective-permute-start(f32[128,128]{1,0:T(8,128)S(1)} %add_add_fusion.refs_4_), channel_id=1, source_target_pairs={{0,1},{1,2},{2,3},{3,0},{4,5},{5,6},{6,7},{7,4},{8,9},{9,10},{10,1... | collective-permute-start | bytes 196616 | tf_op jit(solution)/shard_map/ppermute | solution.py:394
  31.2 0.0 collective-permute-done.1.refs_2_
  31.2 7.7 %looks.2.refs_3_ = bf16[4,40,2,120,120]{4,3,2,1,0:T(8,128)(2,1)} custom-call(bf16[3,4,2,120,128]{4,3,2,1,0:T(8,128)(2,1)S(1)} %collective-permute-done.2.refs_0_, bf16[8,7,2,120,128]{4,3,2,1,0:T(8,128)(2,1)S(1)} %get-tuple-element.8.refs_1_, bf16[2,7,2,120,128]{4,3,2,1,0:T(8,128)(2,1)S(1)} %collective-permute-done.1.refs_2_), custom_call_target="tpu_custom_call" | custom-call | flops 3221225472 | bytes 8000000 | tf_op jit(solution)/shard_map/looks/pallas_call | solution.py:353
  38.9 0.0 collective-permute-done.8.refs_7_
  38.9 0.0 collective-permute-done.7.refs_6_
  38.9 0.0 collective-permute-done.6.refs_5_
  38.9 0.0 collective-permute-done.refs_0_
  38.9 6.1 %looks.3 = (bf16[4,40,2,120,120]{4,3,2,1,0:T(8,128)(2,1)}, f32[2,120,120]{2,1,0:T(8,128)}) custom-call(bf16[3,3,2,120,128]{4,3,2,1,0:T(8,128)(2,1)S(1)} %collective-permute-done.refs_0_, bf16[8,7,2,120,128]{4,3,2,1,0:T(8,128)(2,1)S(1)} %get-tuple-element.8.refs_1_, ...), custom_call_target="tpu_custom_call", output_to_operand_aliasing={{0}: (3, {})} | custom-call | flops 2415919104 | bytes 6000000 | tf_op jit(solution)/shard_map/looks/pallas_call | solution.py:353
  (1 shorter events, 0.0 us)
Async XLA Ops:
  3.5 27.7 %collective-permute-start.1 = (bf16[2,7,2,120,128]{4,3,2,1,0:T(8,128)(2,1)}, bf16[2,7,2,120,128]{4,3,2,1,0:T(8,128)(2,1)S(1)}, u32[]{:S(2)}, u32[]{:S(2)}) collective-permute-start(bf16[2,7,2,120,128]{4,3,2,1,0:T(8,128)(2,1)} %get-tuple-element.9), channel_id=1, source_target_pairs={{1,0},{2,1},{3,2},{4,3},{5,4},{6,5},{7,6},{8,7},{9,8},{10,9},{11,1... | collective-permute-start | bytes 2580488 | tf_op jit(solution)/shard_map/ppermute | solution.py:406
  5.5 24.2 %collective-permute-start.2 = (bf16[3,4,2,120,128]{4,3,2,1,0:T(8,128)(2,1)}, bf16[3,4,2,120,128]{4,3,2,1,0:T(8,128)(2,1)S(1)}, u32[]{:S(2)}, u32[]{:S(2)}) collective-permute-start(bf16[3,4,2,120,128]{4,3,2,1,0:T(8,128)(2,1)} %get-tuple-element.10), channel_id=1, source_target_pairs={{0,1},{1,2},{2,3},{3,4},{4,5},{5,6},{6,7},{7,8},{8,9},{9,10},{10,1... | collective-permute-start | bytes 2211848 | tf_op jit(solution)/shard_map/ppermute | solution.py:407
  10.0 0.8 %copy-start = (s32[8,840]{1,0:T(8,128)S(1)}, s32[8,840]{1,0:T(8,128)}, u32[]{:S(2)}) copy-start(s32[8,840]{1,0:T(8,128)} %mask_ref.3) | copy-start | bytes 80644
  17.8 5.1 %collective-permute-start.5 = (f32[128,128]{1,0:T(8,128)S(1)}, f32[128,128]{1,0:T(8,128)S(1)}, u32[]{:S(2)}, u32[]{:S(2)}) collective-permute-start(f32[128,128]{1,0:T(8,128)S(1)} %get-tuple-element.11), channel_id=1, source_target_pairs={{0,12},{1,13},{2,14},{3,15},{4,0},{5,1},{6,2},{7,3},{8,4},{9,5},{1... | collective-permute-start | bytes 196616 | tf_op jit(solution)/shard_map/ppermute | solution.py:394
  21.2 5.6 %collective-permute-start.4 = (f32[128,128]{1,0:T(8,128)S(1)}, f32[128,128]{1,0:T(8,128)S(1)}, u32[]{:S(2)}, u32[]{:S(2)}) collective-permute-start(f32[128,128]{1,0:T(8,128)S(1)} %get-tuple-element.11), channel_id=1, source_target_pairs={{0,4},{1,5},{2,6},{3,7},{4,8},{5,9},{6,10},{7,11},{8,12},{9,13},{1... | collective-permute-start | bytes 196616 | tf_op jit(solution)/shard_map/ppermute | solution.py:394
  21.2 7.4 %collective-permute-start.3 = (f32[128,128]{1,0:T(8,128)S(1)}, f32[128,128]{1,0:T(8,128)S(1)}, u32[]{:S(2)}, u32[]{:S(2)}) collective-permute-start(f32[128,128]{1,0:T(8,128)S(1)} %get-tuple-element.11), channel_id=1, source_target_pairs={{0,8},{1,9},{2,10},{3,11},{4,12},{5,13},{6,14},{7,15},{8,0},{9,1},... | collective-permute-start | bytes 196616 | tf_op jit(solution)/shard_map/ppermute | solution.py:394
  22.9 16.0 %collective-permute-start = (bf16[3,3,2,120,128]{4,3,2,1,0:T(8,128)(2,1)}, bf16[3,3,2,120,128]{4,3,2,1,0:T(8,128)(2,1)S(1)}, u32[]{:S(2)}, u32[]{:S(2)}) collective-permute-start(bf16[3,3,2,120,128]{4,3,2,1,0:T(8,128)(2,1)} %get-tuple-element.7), channel_id=1, source_target_pairs={{0,1},{1,2},{2,3},{3,4},{4,5},{5,6},{6,7},{7,8},{8,9},{9,10},{10,1... | collective-permute-start | bytes 1658888 | tf_op jit(solution)/shard_map/ppermute | solution.py:408
  28.7 10.2 %collective-permute-start.8 = (f32[128,128]{1,0:T(8,128)S(1)}, f32[128,128]{1,0:T(8,128)S(1)}, u32[]{:S(2)}, u32[]{:S(2)}) collective-permute-start(f32[128,128]{1,0:T(8,128)S(1)} %add_add_fusion.refs_4_), channel_id=1, source_target_pairs={{0,3},{1,0},{2,1},{3,2},{4,7},{5,4},{6,5},{7,6},{8,11},{9,8},{10,9... | collective-permute-start | bytes 196616 | tf_op jit(solution)/shard_map/ppermute | solution.py:394
  29.5 9.4 %collective-permute-start.7 = (f32[128,128]{1,0:T(8,128)S(1)}, f32[128,128]{1,0:T(8,128)S(1)}, u32[]{:S(2)}, u32[]{:S(2)}) collective-permute-start(f32[128,128]{1,0:T(8,128)S(1)} %add_add_fusion.refs_4_), channel_id=1, source_target_pairs={{0,2},{1,3},{2,0},{3,1},{4,6},{5,7},{6,4},{7,5},{8,10},{9,11},{10,... | collective-permute-start | bytes 196616 | tf_op jit(solution)/shard_map/ppermute | solution.py:394
  29.7 9.2 %collective-permute-start.6 = (f32[128,128]{1,0:T(8,128)S(1)}, f32[128,128]{1,0:T(8,128)S(1)}, u32[]{:S(2)}, u32[]{:S(2)}) collective-permute-start(f32[128,128]{1,0:T(8,128)S(1)} %add_add_fusion.refs_4_), channel_id=1, source_target_pairs={{0,1},{1,2},{2,3},{3,0},{4,5},{5,6},{6,7},{7,4},{8,9},{9,10},{10,1... | collective-permute-start | bytes 196616 | tf_op jit(solution)/shard_map/ppermute | solution.py:394

commit v13 on v8

--- a/solution.py
+++ b/solution.py
@@ -69,7 +69,7 @@
 EDGE = tuple(range(AFTER)) + tuple(range(ROWS - BEFORE, ROWS))
 
 
-def edge_kernel(cut, image_ref, mask_ref, top_ref, low0_ref, low1_ref, rows_ref, masks_ref, turned_ref, in_sems, out_sems):
+def edge_kernel(image_ref, mask_ref, top_ref, low_ref, rows_ref, masks_ref, turned_ref, in_sems, out_sems):
     fetches = fetched(image_ref, mask_ref, rows_ref, masks_ref, in_sems, EDGE)
     stores = []
     for at, row in enumerate(EDGE):
@@ -79,16 +79,10 @@
             turned_ref[at, g, k] = value
 
         turned([rows_ref.at[at, 0], rows_ref.at[at, 1]], masks_ref[row : row + 1, :], SKEW[row], masks_ref.shape[1], put)
-        groups = turned_ref.shape[1]
-        i = row - (ROWS - BEFORE)
-        if row < AFTER:
-            targets = ((top_ref.at[row], 0, groups),)
-        else:
-            targets = ((low0_ref.at[i], 0, cut), (low1_ref.at[i], cut, groups))
-        for target, start, stop in targets:
-            store = pltpu.make_async_copy(turned_ref.at[at, start:stop], target, out_sems.at[len(stores)])
-            store.start()
-            stores.append(store)
+        target = top_ref.at[row] if row < AFTER else low_ref.at[row - (ROWS - BEFORE)]
+        store = pltpu.make_async_copy(turned_ref.at[at], target, out_sems.at[at])
+        store.start()
+        stores.append(store)
     for store in stores:
         store.wait()
 
@@ -97,24 +91,23 @@
     return jax.ShapeDtypeStruct((rows, groups, 2, count, LANES), jnp.bfloat16)
 
 
-def edge_rows(images, valid_mask, groups, cut):
+def edge_rows(images, valid_mask, groups):
     count = images.shape[2]
     far = pl.BlockSpec(memory_space=pl.ANY)
     return pl.pallas_call(
-        functools.partial(edge_kernel, cut),
+        edge_kernel,
         in_specs=[far, far],
-        out_specs=[far] * 3,
+        out_specs=[far] * 2,
         out_shape=[
             rows_shape(AFTER, groups, count),
-            rows_shape(BEFORE, cut, count),
-            rows_shape(BEFORE, groups - cut, count),
+            rows_shape(BEFORE, groups, count),
         ],
         scratch_shapes=[
             pltpu.VMEM((len(EDGE),) + images.shape[1:], jnp.bfloat16),
             pltpu.VMEM(valid_mask.shape, jnp.int32),
             pltpu.VMEM((len(EDGE), groups, 2, count, LANES), jnp.bfloat16),
             pltpu.SemaphoreType.DMA((len(EDGE) + 1,)),
-            pltpu.SemaphoreType.DMA((AFTER + 2 * BEFORE,)),
+            pltpu.SemaphoreType.DMA((len(EDGE),)),
         ],
         compiler_params=pltpu.CompilerParams(vmem_limit_bytes=61 * 2**20),
         cost_estimate=pl.CostEstimate(flops=10**6, bytes_accessed=4 * 10**6, transcendentals=0),
@@ -266,19 +259,17 @@
             w_ref[slot, k, pl.ds(0, count), pl.ds(LANES, LANES)] = gathered(l, k, outer_rows)
         every = w_ref[slot].reshape(2 * LANES, 2 * LANES)
         nothing = jnp.zeros_like(every)
-        reads = []
-        for inner_rows, rest_rows in windows:
+        for w, (inner_rows, rest_rows) in enumerate(windows):
             lanes = jnp.concatenate([kept(l, inner_rows or INNER), kept(l, rest_rows or outer_rows)], axis=1)
             lanes = jnp.broadcast_to(lanes, every.shape).astype(jnp.bfloat16) != 0
             read = jnp.where(lanes, every, nothing)
+            reads = []
             for start in range(0, LANES, TILE):
                 reads.append(read[start : start + TILE])
                 reads.append(read[LANES + start : LANES + start + TILE])
-        gram = lax.dot_general(jnp.concatenate(reads, axis=0), every, NT, preferred_element_type=jnp.float32)
-        for w in range(2):
+            gram = lax.dot_general(jnp.concatenate(reads, axis=0), every, NT, preferred_element_type=jnp.float32)
             for start in range(0, LANES, TILE):
-                base = 2 * (w * LANES + start)
-                re, im = gram[base : base + TILE], gram[base + TILE : base + 2 * TILE]
+                re, im = gram[2 * start : 2 * start + TILE], gram[2 * start + TILE : 2 * start + 2 * TILE]
                 g_ref[slot, w, 0, pl.ds(start, TILE)] = re[:, :LANES] + im[:, LANES:]
                 g_ref[slot, w, 1, pl.ds(start, TILE)] = im[:, :LANES] - re[:, LANES:]
 
@@ -307,8 +298,7 @@
     count = other.shape[3]
 
     def spec(array):
-        offset = 0 if array is other else first
-        return pl.BlockSpec((array.shape[0], 1) + array.shape[2:], lambda s: (0, s + offset, 0, 0, 0))
+        return pl.BlockSpec((array.shape[0], 1) + array.shape[2:], lambda s: (0, s + first, 0, 0, 0))
 
     operands = [other, rows]
     in_specs = [spec(a) for a in operands]
@@ -379,10 +369,9 @@
     size = lax.axis_size("pix")
     forward = [(i, i + 1) for i in range(size - 1)]
     backward = [(i + 1, i) for i in range(size - 1)]
-    top, low0, low1 = edge_rows(images, valid_mask, groups, cut)
+    top, low = edge_rows(images, valid_mask, groups)
     after = lax.ppermute(top, "pix", backward)
-    before0 = lax.ppermute(low0, "pix", forward)
-    before1 = lax.ppermute(low1, "pix", forward)
+    before = lax.ppermute(low, "pix", forward)
     rows, total = local_rows(images, valid_mask, groups)
     steps = rounds(size)
     if steps is None:
@@ -392,8 +381,8 @@
     out, zeros = looked(1, after, rows, 0, groups, looks, None, [], False)
     for step in steps[1:]:
         terms = round_terms(added(terms) + zeros, "pix", *step)
-    out, _ = looked(0, before0, rows, 0, cut, looks, out, [], False)
-    out, slab = looked(0, before1, rows, cut, groups - cut, looks, out, terms, True)
+    out, _ = looked(0, before, rows, 0, cut, looks, out, [], False)
+    out, slab = looked(0, before, rows, cut, groups - cut, looks, out, terms, True)
     return (out, slab)
 
 

time: 46 us -> 51.2 us (1.11)
  the two profiles are of different devices: /device:TPU:1 before, /device:TPU:27 now
where the time goes in v13:
time: 51.2 us; the launch traced here: 51.1 us
  Pallas kernels  27 us (53%)
  starting transfers between devices  19.4 us (38%)
  waiting for transfers between devices  3.99 us (8%)
  between operations  0.7 us (1%)
    pallas_call x3, Pallas kernels, looked(): pl.pallas_call(functools.partial(looks_kernel, half, previous is not None...  17 us
    ppermute x6, starting transfers between devices, round_terms(): terms.append(lax.ppermute(value, axis, pairs))  15.4 us
    pallas_call x1, Pallas kernels, local_rows(): pl.pallas_call(local_kernel, in_specs=[far, far], out_specs=[far, pl.Bloc...  7.15 us
    ppermute x6, waiting for transfers between devices, round_terms(): terms.append(lax.ppermute(value, axis, pairs))  3.99 us
    pallas_call x1, Pallas kernels, edge_rows(): pl.pallas_call(edge_kernel, in_specs=[far, far], out_specs=[far] * 2, out...  2.86 us
    ppermute x1, starting transfers between devices, shards(): after = lax.ppermute(top, 'pix', backward)  2.63 us
    ppermute x1, starting transfers between devices, shards(): before = lax.ppermute(low, 'pix', forward)  1.29 us
  transfers between devices with their start and end apart: 8, of which 3 were waited for; matrix products, arithmetic and copies ran while one was open for 0% of the time, Pallas kernels for 39%

profile of v13, /device:TPU:27, one launch (start us, length us, event | category | flops | bytes accessed | tf_op | source)
XLA Modules:
  0.0 51.1 jit_solution(3418760868274933967)
XLA Ops:
  0.6 0.0 copy-start
  0.6 2.9 %edge_rows.1 = (bf16[2,7,2,120,128]{4,3,2,1,0:T(8,128)(2,1)}, bf16[3,7,2,120,128]{4,3,2,1,0:T(8,128)(2,1)}) custom-call(bf16[8,2,120,840]{3,2,1,0:T(8,128)(2,1)} %image_ref.3, s32[8,840]{1,0:T(8,128)} %mask_ref.3), custom_call_target="tpu_custom_call" | custom-call | flops 1000000 | bytes 4000000 | tf_op jit(solution)/shard_map/edge_rows/pallas_call | solution.py:97
  3.5 2.6 %collective-permute-start.1 = (bf16[2,7,2,120,128]{4,3,2,1,0:T(8,128)(2,1)}, bf16[2,7,2,120,128]{4,3,2,1,0:T(8,128)(2,1)S(1)}, u32[]{:S(2)}, u32[]{:S(2)}) collective-permute-start(bf16[2,7,2,120,128]{4,3,2,1,0:T(8,128)(2,1)} %get-tuple-element.11), channel_id=1, source_target_pairs={{1,0},{2,1},{3,2},{4,3},{5,4},{6,5},{7,6},{8,7},{9,8},{10,9},{11,1... | collective-permute-start | bytes 2580488 | tf_op jit(solution)/shard_map/ppermute | solution.py:373
  6.1 1.3 %collective-permute-start = (bf16[3,7,2,120,128]{4,3,2,1,0:T(8,128)(2,1)}, bf16[3,7,2,120,128]{4,3,2,1,0:T(8,128)(2,1)S(1)}, u32[]{:S(2)}, u32[]{:S(2)}) collective-permute-start(bf16[3,7,2,120,128]{4,3,2,1,0:T(8,128)(2,1)} %get-tuple-element.9), channel_id=1, source_target_pairs={{0,1},{1,2},{2,3},{3,4},{4,5},{5,6},{6,7},{7,8},{8,9},{9,10},{10,1... | collective-permute-start | bytes 3870728 | tf_op jit(solution)/shard_map/ppermute | solution.py:374
  7.4 0.0 copy-done
  7.5 7.1 %local_rows.1 = (bf16[8,7,2,120,128]{4,3,2,1,0:T(8,128)(2,1)S(1)}, f32[128,128]{1,0:T(8,128)S(1)}) custom-call(bf16[8,2,120,840]{3,2,1,0:T(8,128)(2,1)} %image_ref.3, s32[8,840]{1,0:T(8,128)S(1)} %copy-done), custom_call_target="tpu_custom_call" | custom-call | flops 1000000000 | bytes 5000000 | tf_op jit(solution)/shard_map/local_rows/pallas_call | solution.py:153
  14.6 2.8 %collective-permute-start.4 = (f32[128,128]{1,0:T(8,128)S(1)}, f32[128,128]{1,0:T(8,128)S(1)}, u32[]{:S(2)}, u32[]{:S(2)}) collective-permute-start(f32[128,128]{1,0:T(8,128)S(1)} %get-tuple-element.14), channel_id=1, source_target_pairs={{0,12},{1,13},{2,14},{3,15},{4,0},{5,1},{6,2},{7,3},{8,4},{9,5},{1... | collective-permute-start | bytes 196616 | tf_op jit(solution)/shard_map/ppermute | solution.py:361
  17.4 0.6 %collective-permute-start.3 = (f32[128,128]{1,0:T(8,128)S(1)}, f32[128,128]{1,0:T(8,128)S(1)}, u32[]{:S(2)}, u32[]{:S(2)}) collective-permute-start(f32[128,128]{1,0:T(8,128)S(1)} %get-tuple-element.14), channel_id=1, source_target_pairs={{0,4},{1,5},{2,6},{3,7},{4,8},{5,9},{6,10},{7,11},{8,12},{9,13},{1... | collective-permute-start | bytes 196616 | tf_op jit(solution)/shard_map/ppermute | solution.py:361
  17.9 0.8 %collective-permute-start.2 = (f32[128,128]{1,0:T(8,128)S(1)}, f32[128,128]{1,0:T(8,128)S(1)}, u32[]{:S(2)}, u32[]{:S(2)}) collective-permute-start(f32[128,128]{1,0:T(8,128)S(1)} %get-tuple-element.14), channel_id=1, source_target_pairs={{0,8},{1,9},{2,10},{3,11},{4,12},{5,13},{6,14},{7,15},{8,0},{9,1},... | collective-permute-start | bytes 196616 | tf_op jit(solution)/shard_map/ppermute | solution.py:361
  18.7 0.0 collective-permute-done.1.refs_0_
  18.7 8.0 %looks.3 = (bf16[4,40,2,120,120]{4,3,2,1,0:T(8,128)(2,1)}, f32[128,128]{1,0:T(8,128)S(1)}) custom-call(bf16[2,7,2,120,128]{4,3,2,1,0:T(8,128)(2,1)S(1)} %collective-permute-done.1.refs_0_, bf16[8,7,2,120,128]{4,3,2,1,0:T(8,128)(2,1)S(1)} %get-tuple-element.10.refs_1_), custom_call_target="tpu_custom_call" | custom-call | flops 2818572288 | bytes 7000000 | tf_op jit(solution)/shard_map/looks/pallas_call | solution.py:322
  26.7 1.2 %collective-permute-done.4 = f32[128,128]{1,0:T(8,128)S(1)} collective-permute-done((f32[128,128]{1,0:T(8,128)S(1)}, f32[128,128]{1,0:T(8,128)S(1)}, u32[]{:S(2)}, u32[]{:S(2)}) %collective-permute-start.4) | collective-permute-done | bytes 65568 | tf_op jit(solution)/shard_map/ppermute | solution.py:361
  27.8 0.8 %collective-permute-done.3 = f32[128,128]{1,0:T(8,128)S(1)} collective-permute-done((f32[128,128]{1,0:T(8,128)S(1)}, f32[128,128]{1,0:T(8,128)S(1)}, u32[]{:S(2)}, u32[]{:S(2)}) %collective-permute-start.3) | collective-permute-done | bytes 65568 | tf_op jit(solution)/shard_map/ppermute | solution.py:361
  28.7 2.0 %collective-permute-done.2 = f32[128,128]{1,0:T(8,128)S(1)} collective-permute-done((f32[128,128]{1,0:T(8,128)S(1)}, f32[128,128]{1,0:T(8,128)S(1)}, u32[]{:S(2)}, u32[]{:S(2)}) %collective-permute-start.2) | collective-permute-done | bytes 65568 | tf_op jit(solution)/shard_map/ppermute | solution.py:361
  30.7 7.9 %collective-permute-start.7 = (f32[128,128]{1,0:T(8,128)S(1)}, f32[128,128]{1,0:T(8,128)S(1)}, u32[]{:S(2)}, u32[]{:S(2)}) collective-permute-start(f32[128,128]{1,0:T(8,128)S(1)} %add_add_fusion.refs_3_), channel_id=1, source_target_pairs={{0,3},{1,0},{2,1},{3,2},{4,7},{5,4},{6,5},{7,6},{8,11},{9,8},{10,9... | collective-permute-start | bytes 196616 | tf_op jit(solution)/shard_map/ppermute | solution.py:361
  38.6 1.5 %collective-permute-start.6 = (f32[128,128]{1,0:T(8,128)S(1)}, f32[128,128]{1,0:T(8,128)S(1)}, u32[]{:S(2)}, u32[]{:S(2)}) collective-permute-start(f32[128,128]{1,0:T(8,128)S(1)} %add_add_fusion.refs_3_), channel_id=1, source_target_pairs={{0,2},{1,3},{2,0},{3,1},{4,6},{5,7},{6,4},{7,5},{8,10},{9,11},{10,... | collective-permute-start | bytes 196616 | tf_op jit(solution)/shard_map/ppermute | solution.py:361
  40.1 1.9 %collective-permute-start.5 = (f32[128,128]{1,0:T(8,128)S(1)}, f32[128,128]{1,0:T(8,128)S(1)}, u32[]{:S(2)}, u32[]{:S(2)}) collective-permute-start(f32[128,128]{1,0:T(8,128)S(1)} %add_add_fusion.refs_3_), channel_id=1, source_target_pairs={{0,1},{1,2},{2,3},{3,0},{4,5},{5,6},{6,7},{7,4},{8,9},{9,10},{10,1... | collective-permute-start | bytes 196616 | tf_op jit(solution)/shard_map/ppermute | solution.py:361
  42.0 0.0 collective-permute-done.refs_0_
  42.0 5.0 %looks.4 = (bf16[4,40,2,120,120]{4,3,2,1,0:T(8,128)(2,1)}, f32[128,128]{1,0:T(8,128)}) custom-call(bf16[3,7,2,120,128]{4,3,2,1,0:T(8,128)(2,1)S(1)} %collective-permute-done.refs_0_, bf16[8,7,2,120,128]{4,3,2,1,0:T(8,128)(2,1)S(1)} %get-tuple-element.10.refs_1_, bf16[4,40,2,120,120]{4,3,2,1,0:T(8,128)(2,1)} %get-tuple-element.12.refs_2_), custom_call_target="tpu_custom_call", output_to_operand_aliasing={{0}: (2, {})} | custom-call | flops 1610612736 | bytes 4000000 | tf_op jit(solution)/shard_map/looks/pallas_call | solution.py:322
  47.0 0.0 collective-permute-done.7.refs_6_
  47.0 0.0 collective-permute-done.6.refs_5_
  47.0 0.0 collective-permute-done.5.refs_4_
  47.0 4.1 %looks.5 = (bf16[4,40,2,120,120]{4,3,2,1,0:T(8,128)(2,1)}, f32[2,120,120]{2,1,0:T(8,128)}) custom-call(bf16[3,7,2,120,128]{4,3,2,1,0:T(8,128)(2,1)S(1)} %collective-permute-done.refs_0_, bf16[8,7,2,120,128]{4,3,2,1,0:T(8,128)(2,1)S(1)} %get-tuple-element.10.refs_1_, ...), custom_call_target="tpu_custom_call", output_to_operand_aliasing={{0}: (2, {})} | custom-call | flops 1207959552 | bytes 3000000 | tf_op jit(solution)/shard_map/looks/pallas_call | solution.py:322
  (1 shorter events, 0.0 us)
Async XLA Ops:
  0.6 6.8 %copy-start = (s32[8,840]{1,0:T(8,128)S(1)}, s32[8,840]{1,0:T(8,128)}, u32[]{:S(2)}) copy-start(s32[8,840]{1,0:T(8,128)} %mask_ref.3) | copy-start | bytes 80644
  3.5 15.2 %collective-permute-start.1 = (bf16[2,7,2,120,128]{4,3,2,1,0:T(8,128)(2,1)}, bf16[2,7,2,120,128]{4,3,2,1,0:T(8,128)(2,1)S(1)}, u32[]{:S(2)}, u32[]{:S(2)}) collective-permute-start(bf16[2,7,2,120,128]{4,3,2,1,0:T(8,128)(2,1)} %get-tuple-element.11), channel_id=1, source_target_pairs={{1,0},{2,1},{3,2},{4,3},{5,4},{6,5},{7,6},{8,7},{9,8},{10,9},{11,1... | collective-permute-start | bytes 2580488 | tf_op jit(solution)/shard_map/ppermute | solution.py:373
  6.1 35.9 %collective-permute-start = (bf16[3,7,2,120,128]{4,3,2,1,0:T(8,128)(2,1)}, bf16[3,7,2,120,128]{4,3,2,1,0:T(8,128)(2,1)S(1)}, u32[]{:S(2)}, u32[]{:S(2)}) collective-permute-start(bf16[3,7,2,120,128]{4,3,2,1,0:T(8,128)(2,1)} %get-tuple-element.9), channel_id=1, source_target_pairs={{0,1},{1,2},{2,3},{3,4},{4,5},{5,6},{6,7},{7,8},{8,9},{9,10},{10,1... | collective-permute-start | bytes 3870728 | tf_op jit(solution)/shard_map/ppermute | solution.py:374
  14.6 13.2 %collective-permute-start.4 = (f32[128,128]{1,0:T(8,128)S(1)}, f32[128,128]{1,0:T(8,128)S(1)}, u32[]{:S(2)}, u32[]{:S(2)}) collective-permute-start(f32[128,128]{1,0:T(8,128)S(1)} %get-tuple-element.14), channel_id=1, source_target_pairs={{0,12},{1,13},{2,14},{3,15},{4,0},{5,1},{6,2},{7,3},{8,4},{9,5},{1... | collective-permute-start | bytes 196616 | tf_op jit(solution)/shard_map/ppermute | solution.py:361
  17.4 11.3 %collective-permute-start.3 = (f32[128,128]{1,0:T(8,128)S(1)}, f32[128,128]{1,0:T(8,128)S(1)}, u32[]{:S(2)}, u32[]{:S(2)}) collective-permute-start(f32[128,128]{1,0:T(8,128)S(1)} %get-tuple-element.14), channel_id=1, source_target_pairs={{0,4},{1,5},{2,6},{3,7},{4,8},{5,9},{6,10},{7,11},{8,12},{9,13},{1... | collective-permute-start | bytes 196616 | tf_op jit(solution)/shard_map/ppermute | solution.py:361
  17.9 12.7 %collective-permute-start.2 = (f32[128,128]{1,0:T(8,128)S(1)}, f32[128,128]{1,0:T(8,128)S(1)}, u32[]{:S(2)}, u32[]{:S(2)}) collective-permute-start(f32[128,128]{1,0:T(8,128)S(1)} %get-tuple-element.14), channel_id=1, source_target_pairs={{0,8},{1,9},{2,10},{3,11},{4,12},{5,13},{6,14},{7,15},{8,0},{9,1},... | collective-permute-start | bytes 196616 | tf_op jit(solution)/shard_map/ppermute | solution.py:361
  30.7 16.3 %collective-permute-start.7 = (f32[128,128]{1,0:T(8,128)S(1)}, f32[128,128]{1,0:T(8,128)S(1)}, u32[]{:S(2)}, u32[]{:S(2)}) collective-permute-start(f32[128,128]{1,0:T(8,128)S(1)} %add_add_fusion.refs_3_), channel_id=1, source_target_pairs={{0,3},{1,0},{2,1},{3,2},{4,7},{5,4},{6,5},{7,6},{8,11},{9,8},{10,9... | collective-permute-start | bytes 196616 | tf_op jit(solution)/shard_map/ppermute | solution.py:361
  38.6 8.4 %collective-permute-start.6 = (f32[128,128]{1,0:T(8,128)S(1)}, f32[128,128]{1,0:T(8,128)S(1)}, u32[]{:S(2)}, u32[]{:S(2)}) collective-permute-start(f32[128,128]{1,0:T(8,128)S(1)} %add_add_fusion.refs_3_), channel_id=1, source_target_pairs={{0,2},{1,3},{2,0},{3,1},{4,6},{5,7},{6,4},{7,5},{8,10},{9,11},{10,... | collective-permute-start | bytes 196616 | tf_op jit(solution)/shard_map/ppermute | solution.py:361
  40.1 6.9 %collective-permute-start.5 = (f32[128,128]{1,0:T(8,128)S(1)}, f32[128,128]{1,0:T(8,128)S(1)}, u32[]{:S(2)}, u32[]{:S(2)}) collective-permute-start(f32[128,128]{1,0:T(8,128)S(1)} %add_add_fusion.refs_3_), channel_id=1, source_target_pairs={{0,1},{1,2},{2,3},{3,0},{4,5},{5,6},{6,7},{7,4},{8,9},{9,10},{10,1... | collective-permute-start | bytes 196616 | tf_op jit(solution)/shard_map/ppermute | solution.py:361

commit v14 on v7

--- a/solution.py
+++ b/solution.py
@@ -69,7 +69,7 @@
 EDGE = tuple(range(AFTER)) + tuple(range(ROWS - BEFORE, ROWS))
 
 
-def edge_kernel(image_ref, mask_ref, top_ref, low_ref, _, rows_ref, masks_ref, turned_ref, in_sems, out_sems):
+def edge_kernel(image_ref, mask_ref, top_ref, low_ref, rows_ref, masks_ref, turned_ref, in_sems, out_sems):
     fetches = fetched(image_ref, mask_ref, rows_ref, masks_ref, in_sems, EDGE)
     stores = []
     for at, row in enumerate(EDGE):
@@ -97,11 +97,10 @@
     return pl.pallas_call(
         edge_kernel,
         in_specs=[far, far],
-        out_specs=[far] * 3,
+        out_specs=[far] * 2,
         out_shape=[
             rows_shape(AFTER, groups, count),
             rows_shape(BEFORE, groups, count),
-            jax.ShapeDtypeStruct((8, LANES), jnp.float32),
         ],
         scratch_shapes=[
             pltpu.VMEM((len(EDGE),) + images.shape[1:], jnp.bfloat16),
@@ -116,14 +115,16 @@
     )(images, valid_mask)
 
 
-def middle_kernel(image_ref, mask_ref, _, mid_ref, gram_ref, rows_ref, masks_ref, turned_ref, z_ref, in_sems, out_sems):
+def middle_kernel(image_ref, mask_ref, low_ref, mid_ref, gram_ref, again_ref, *scratch):
+    rows_ref, masks_ref, turned_ref, z_ref, in_sems, out_sems = scratch
     groups = mid_ref.shape[1]
     count, columns = image_ref.shape[2:]
     order = tuple(range(AFTER, ROWS - BEFORE)) + EDGE
     fetches = fetched(image_ref, mask_ref, rows_ref, masks_ref, in_sems, order)
+    stores = [pltpu.make_async_copy(low_ref, again_ref, out_sems.at[ROWS - AFTER - BEFORE])]
+    stores[0].start()
     z_ref[...] = jnp.zeros_like(z_ref)
     zero = jnp.zeros((count, columns), jnp.bfloat16)
-    stores = []
     total = None
     wide = groups * LANES
     for at, row in enumerate(order):
@@ -156,27 +157,32 @@
         store.wait()
 
 
-def middle_rows(images, valid_mask, groups, behind):
+def middle_rows(images, valid_mask, low):
     count = images.shape[2]
+    groups = low.shape[1]
     rows = ROWS - AFTER - BEFORE
     far = pl.BlockSpec(memory_space=pl.ANY)
     return pl.pallas_call(
         middle_kernel,
         in_specs=[far, far, far],
-        out_specs=[far, pl.BlockSpec(memory_space=pltpu.VMEM)],
-        out_shape=[rows_shape(rows, groups, count), jax.ShapeDtypeStruct((LANES, LANES), jnp.float32)],
+        out_specs=[far, pl.BlockSpec(memory_space=pltpu.VMEM), far],
+        out_shape=[
+            rows_shape(rows, groups, count),
+            jax.ShapeDtypeStruct((LANES, LANES), jnp.float32),
+            jax.ShapeDtypeStruct(low.shape, low.dtype),
+        ],
         scratch_shapes=[
             pltpu.VMEM(images.shape, jnp.bfloat16),
             pltpu.VMEM(valid_mask.shape, jnp.int32),
             pltpu.VMEM((rows, groups, 2, count, LANES), jnp.bfloat16),
             pltpu.VMEM((2 * LANES, ROWS * groups * LANES), jnp.bfloat16),
             pltpu.SemaphoreType.DMA((ROWS + 1,)),
-            pltpu.SemaphoreType.DMA((rows,)),
+            pltpu.SemaphoreType.DMA((rows + 1,)),
         ],
-        compiler_params=pltpu.CompilerParams(vmem_limit_bytes=52 * 2**20),
+        compiler_params=pltpu.CompilerParams(vmem_limit_bytes=51 * 2**20),
         cost_estimate=pl.CostEstimate(flops=10**9, bytes_accessed=5 * 10**6, transcendentals=0),
         name="middle_rows",
-    )(images, valid_mask, behind)
+    )(images, valid_mask, low)
 
 
 def added(terms):
@@ -343,7 +349,7 @@
         ],
         compiler_params=pltpu.CompilerParams(vmem_limit_bytes=48 * 2**20),
         cost_estimate=pl.CostEstimate(
-            flops=20 * groups * PER * 2 * 512 * 256 * 256, bytes_accessed=groups * 10**6, transcendentals=0
+            flops=2 * groups * PER * 2 * 512 * 256 * 256, bytes_accessed=groups * 10**6, transcendentals=0
         ),
         name="looks",
     )(*operands)
@@ -380,10 +386,10 @@
     size = lax.axis_size("pix")
     forward = [(i, i + 1) for i in range(size - 1)]
     backward = [(i + 1, i) for i in range(size - 1)]
-    top, low, edge_done = edge_rows(images, valid_mask, groups)
+    top, low = edge_rows(images, valid_mask, groups)
     after = lax.ppermute(top, "pix", backward)
+    mid, total, low = middle_rows(images, valid_mask, low)
     before = lax.ppermute(low, "pix", forward)
-    mid, total = middle_rows(images, valid_mask, groups, edge_done)
     steps = rounds(size)
     if steps is None:
         terms, steps = [lax.psum(total, "pix")], []

time: 46.7 us -> 47.4 us (1.015)
  the two profiles are of different devices: /device:TPU:8 before, /device:TPU:25 now
where the time goes in v14:
time: 47.4 us; the launch traced here: 47.2 us
  Pallas kernels  23.3 us (49%)
  starting transfers between devices  20.7 us (44%)
  waiting for transfers between devices  2.43 us (5%)
  between operations  0.72 us (2%)
    pallas_call x3, Pallas kernels, looked(): pl.pallas_call(functools.partial(looks_kernel, half, previous is not None...  15.4 us
    ppermute x6, starting transfers between devices, round_terms(): terms.append(lax.ppermute(value, axis, pairs))  15 us
    pallas_call x1, Pallas kernels, middle_rows(): pl.pallas_call(middle_kernel, in_specs=[far, far, far], out_specs=[far, p...  4.99 us
    ppermute x1, starting transfers between devices, shards(): before = lax.ppermute(low, 'pix', forward)  3.02 us
    pallas_call x1, Pallas kernels, edge_rows(): pl.pallas_call(edge_kernel, in_specs=[far, far], out_specs=[far] * 2, out...  2.84 us
    ppermute x1, starting transfers between devices, shards(): after = lax.ppermute(top, 'pix', backward)  2.71 us
    ppermute x1, waiting for transfers between devices, shards(): after = lax.ppermute(top, 'pix', backward)  2.41 us
  transfers between devices with their start and end apart: 8, of which 1 were waited for; matrix products, arithmetic and copies ran while one was open for 0% of the time, Pallas kernels for 35%

profile of v14, /device:TPU:25, one launch (start us, length us, event | category | flops | bytes accessed | tf_op | source)
XLA Modules:
  0.0 47.2 jit_solution(16625402442172111480)
XLA Ops:
  0.6 0.0 copy-start.1
  0.6 2.8 %edge_rows.1 = (bf16[2,7,2,120,128]{4,3,2,1,0:T(8,128)(2,1)}, bf16[3,7,2,120,128]{4,3,2,1,0:T(8,128)(2,1)}) custom-call(bf16[8,2,120,840]{3,2,1,0:T(8,128)(2,1)} %image_ref.3, s32[8,840]{1,0:T(8,128)} %mask_ref.3), custom_call_target="tpu_custom_call" | custom-call | flops 1000000 | bytes 4000000 | tf_op jit(solution)/shard_map/edge_rows/pallas_call | solution.py:97
  3.5 0.0 copy-start
  3.5 2.7 %collective-permute-start.1 = (bf16[2,7,2,120,128]{4,3,2,1,0:T(8,128)(2,1)}, bf16[2,7,2,120,128]{4,3,2,1,0:T(8,128)(2,1)S(1)}, u32[]{:S(2)}, u32[]{:S(2)}) collective-permute-start(bf16[2,7,2,120,128]{4,3,2,1,0:T(8,128)(2,1)} %get-tuple-element.12.refs_1_), channel_id=1, source_target_pairs={{1,0},{2,1},{3,2},{4,3},{5,4},{6,5},{7,6},{8,7},{9,8},{10,9},{11,1... | collective-permute-start | bytes 2580488 | tf_op jit(solution)/shard_map/ppermute | solution.py:390
  6.2 0.0 copy-done.1
  6.2 5.0 %middle_rows.1 = (bf16[3,7,2,120,128]{4,3,2,1,0:T(8,128)(2,1)S(1)}, f32[128,128]{1,0:T(8,128)S(1)}, bf16[3,7,2,120,128]{4,3,2,1,0:T(8,128)(2,1)S(1)}) custom-call(bf16[8,2,120,840]{3,2,1,0:T(8,128)(2,1)} %image_ref.3, s32[8,840]{1,0:T(8,128)S(1)} %copy-done.1, bf16[3,7,2,120,128]{4,3,2,1,0:T(8,128)(2,1)} %get-tuple-element.10.low_ref), custom_call_target="tpu_custom_call" | custom-call | flops 1000000000 | bytes 5000000 | tf_op jit(solution)/shard_map/middle_rows/pallas_call | solution.py:165
  11.2 3.0 %collective-permute-start = (bf16[3,7,2,120,128]{4,3,2,1,0:T(8,128)(2,1)S(1)}, bf16[3,7,2,120,128]{4,3,2,1,0:T(8,128)(2,1)S(1)}, u32[]{:S(2)}, u32[]{:S(2)}) collective-permute-start(bf16[3,7,2,120,128]{4,3,2,1,0:T(8,128)(2,1)S(1)} %get-tuple-element.11.refs_3_), channel_id=1, source_target_pairs={{0,1},{1,2},{2,3},{3,4},{4,5},{5,6},{6,7},{7,8},{8,9},{9,10},{10,1... | collective-permute-start | bytes 3870728 | tf_op jit(solution)/shard_map/ppermute | solution.py:392
  14.3 0.2 collective-permute-start.4
  14.5 3.1 %collective-permute-start.3 = (f32[128,128]{1,0:T(8,128)S(1)}, f32[128,128]{1,0:T(8,128)S(1)}, u32[]{:S(2)}, u32[]{:S(2)}) collective-permute-start(f32[128,128]{1,0:T(8,128)S(1)} %get-tuple-element.16), channel_id=1, source_target_pairs={{0,4},{1,5},{2,6},{3,7},{4,8},{5,9},{6,10},{7,11},{8,12},{9,13},{1... | collective-permute-start | bytes 196616 | tf_op jit(solution)/shard_map/ppermute | solution.py:378
  17.6 0.0 collective-permute-start.2
  17.6 2.4 %collective-permute-done.1.refs_0_ = bf16[2,7,2,120,128]{4,3,2,1,0:T(8,128)(2,1)S(1)} collective-permute-done((bf16[2,7,2,120,128]{4,3,2,1,0:T(8,128)(2,1)}, bf16[2,7,2,120,128]{4,3,2,1,0:T(8,128)(2,1)S(1)}, u32[]{:S(2)}, u32[]{:S(2)}) %collective-permute-start.1) | collective-permute-done | bytes 860192 | tf_op jit(solution)/shard_map/ppermute | solution.py:390
  20.0 7.1 %looks.3 = (bf16[4,40,2,120,120]{4,3,2,1,0:T(8,128)(2,1)}, f32[128,128]{1,0:T(8,128)S(1)}) custom-call(bf16[2,7,2,120,128]{4,3,2,1,0:T(8,128)(2,1)S(1)} %collective-permute-done.1.refs_0_, bf16[2,7,2,120,128]{4,3,2,1,0:T(8,128)(2,1)S(1)} %copy-done, bf16[3,7,2,120,128]{4,3,2,1,0:T(8,128)(2,1)S(1)} %get-tuple-element.13.refs_2_, ...), custom_call_target="tpu_custom_call" | custom-call | flops 5637144576 | bytes 7000000 | tf_op jit(solution)/shard_map/looks/pallas_call | solution.py:340
  27.1 0.0 collective-permute-done.4
  27.1 0.0 collective-permute-done.3
  27.1 0.0 collective-permute-done.2
  27.2 0.1 collective-permute-start.7
  27.2 9.7 %collective-permute-start.6 = (f32[128,128]{1,0:T(8,128)S(1)}, f32[128,128]{1,0:T(8,128)S(1)}, u32[]{:S(2)}, u32[]{:S(2)}) collective-permute-start(f32[128,128]{1,0:T(8,128)S(1)} %add_add_fusion.refs_5_), channel_id=1, source_target_pairs={{0,2},{1,3},{2,0},{3,1},{4,6},{5,7},{6,4},{7,5},{8,10},{9,11},{10,... | collective-permute-start | bytes 196616 | tf_op jit(solution)/shard_map/ppermute | solution.py:378
  36.9 1.9 %collective-permute-start.5 = (f32[128,128]{1,0:T(8,128)S(1)}, f32[128,128]{1,0:T(8,128)S(1)}, u32[]{:S(2)}, u32[]{:S(2)}) collective-permute-start(f32[128,128]{1,0:T(8,128)S(1)} %add_add_fusion.refs_5_), channel_id=1, source_target_pairs={{0,1},{1,2},{2,3},{3,0},{4,5},{5,6},{6,7},{7,4},{8,9},{9,10},{10,1... | collective-permute-start | bytes 196616 | tf_op jit(solution)/shard_map/ppermute | solution.py:378
  38.9 0.0 collective-permute-done.refs_0_
  38.9 4.5 %looks.4 = (bf16[4,40,2,120,120]{4,3,2,1,0:T(8,128)(2,1)}, f32[128,128]{1,0:T(8,128)}) custom-call(bf16[3,7,2,120,128]{4,3,2,1,0:T(8,128)(2,1)S(1)} %collective-permute-done.refs_0_, bf16[2,7,2,120,128]{4,3,2,1,0:T(8,128)(2,1)S(1)} %copy-done, bf16[3,7,2,120,128]{4,3,2,1,0:T(8,128)(2,1)S(1)} %get-tuple-element.13.refs_2_, ...), custom_call_target="tpu_custom_call", output_to_operand_aliasing={{0}: (4, {})} | custom-call | flops 3221225472 | bytes 4000000 | tf_op jit(solution)/shard_map/looks/pallas_call | solution.py:340
  43.4 0.0 collective-permute-done.7.refs_8_
  43.4 0.0 collective-permute-done.6.refs_7_
  43.4 0.0 collective-permute-done.5.refs_6_
  43.4 3.7 %looks.5 = (bf16[4,40,2,120,120]{4,3,2,1,0:T(8,128)(2,1)}, f32[2,120,120]{2,1,0:T(8,128)}) custom-call(bf16[3,7,2,120,128]{4,3,2,1,0:T(8,128)(2,1)S(1)} %collective-permute-done.refs_0_, bf16[2,7,2,120,128]{4,3,2,1,0:T(8,128)(2,1)S(1)} %copy-done, bf16[3,7,2,120,128]{4,3,2,1,0:T(8,128)(2,1)S(1)} %get-tuple-element.13.refs_2_, ...), custom_call_target="tpu_custom_call", output_to_operand_aliasing={{0}: (4, {})} | custom-call | flops 2415919104 | bytes 3000000 | tf_op jit(solution)/shard_map/looks/pallas_call | solution.py:340
  (2 shorter events, 0.0 us)
Async XLA Ops:
  0.6 5.6 %copy-start.1 = (s32[8,840]{1,0:T(8,128)S(1)}, s32[8,840]{1,0:T(8,128)}, u32[]{:S(2)}) copy-start(s32[8,840]{1,0:T(8,128)} %mask_ref.3) | copy-start | bytes 80644
  3.5 16.5 %copy-start = (bf16[2,7,2,120,128]{4,3,2,1,0:T(8,128)(2,1)S(1)}, bf16[2,7,2,120,128]{4,3,2,1,0:T(8,128)(2,1)}, u32[]{:S(2)}) copy-start(bf16[2,7,2,120,128]{4,3,2,1,0:T(8,128)(2,1)} %get-tuple-element.12.refs_1_) | copy-start | bytes 2580484
  3.5 16.5 %collective-permute-start.1 = (bf16[2,7,2,120,128]{4,3,2,1,0:T(8,128)(2,1)}, bf16[2,7,2,120,128]{4,3,2,1,0:T(8,128)(2,1)S(1)}, u32[]{:S(2)}, u32[]{:S(2)}) collective-permute-start(bf16[2,7,2,120,128]{4,3,2,1,0:T(8,128)(2,1)} %get-tuple-element.12.refs_1_), channel_id=1, source_target_pairs={{1,0},{2,1},{3,2},{4,3},{5,4},{6,5},{7,6},{8,7},{9,8},{10,9},{11,1... | collective-permute-start | bytes 2580488 | tf_op jit(solution)/shard_map/ppermute | solution.py:390
  11.2 27.6 %collective-permute-start = (bf16[3,7,2,120,128]{4,3,2,1,0:T(8,128)(2,1)S(1)}, bf16[3,7,2,120,128]{4,3,2,1,0:T(8,128)(2,1)S(1)}, u32[]{:S(2)}, u32[]{:S(2)}) collective-permute-start(bf16[3,7,2,120,128]{4,3,2,1,0:T(8,128)(2,1)S(1)} %get-tuple-element.11.refs_3_), channel_id=1, source_target_pairs={{0,1},{1,2},{2,3},{3,4},{4,5},{5,6},{6,7},{7,8},{8,9},{9,10},{10,1... | collective-permute-start | bytes 3870728 | tf_op jit(solution)/shard_map/ppermute | solution.py:392
  14.3 12.9 %collective-permute-start.4 = (f32[128,128]{1,0:T(8,128)S(1)}, f32[128,128]{1,0:T(8,128)S(1)}, u32[]{:S(2)}, u32[]{:S(2)}) collective-permute-start(f32[128,128]{1,0:T(8,128)S(1)} %get-tuple-element.16), channel_id=1, source_target_pairs={{0,12},{1,13},{2,14},{3,15},{4,0},{5,1},{6,2},{7,3},{8,4},{9,5},{1... | collective-permute-start | bytes 196616 | tf_op jit(solution)/shard_map/ppermute | solution.py:378
  14.5 12.7 %collective-permute-start.3 = (f32[128,128]{1,0:T(8,128)S(1)}, f32[128,128]{1,0:T(8,128)S(1)}, u32[]{:S(2)}, u32[]{:S(2)}) collective-permute-start(f32[128,128]{1,0:T(8,128)S(1)} %get-tuple-element.16), channel_id=1, source_target_pairs={{0,4},{1,5},{2,6},{3,7},{4,8},{5,9},{6,10},{7,11},{8,12},{9,13},{1... | collective-permute-start | bytes 196616 | tf_op jit(solution)/shard_map/ppermute | solution.py:378
  17.6 9.6 %collective-permute-start.2 = (f32[128,128]{1,0:T(8,128)S(1)}, f32[128,128]{1,0:T(8,128)S(1)}, u32[]{:S(2)}, u32[]{:S(2)}) collective-permute-start(f32[128,128]{1,0:T(8,128)S(1)} %get-tuple-element.16), channel_id=1, source_target_pairs={{0,8},{1,9},{2,10},{3,11},{4,12},{5,13},{6,14},{7,15},{8,0},{9,1},... | collective-permute-start | bytes 196616 | tf_op jit(solution)/shard_map/ppermute | solution.py:378
  27.2 16.2 %collective-permute-start.7 = (f32[128,128]{1,0:T(8,128)S(1)}, f32[128,128]{1,0:T(8,128)S(1)}, u32[]{:S(2)}, u32[]{:S(2)}) collective-permute-start(f32[128,128]{1,0:T(8,128)S(1)} %add_add_fusion.refs_5_), channel_id=1, source_target_pairs={{0,3},{1,0},{2,1},{3,2},{4,7},{5,4},{6,5},{7,6},{8,11},{9,8},{10,9... | collective-permute-start | bytes 196616 | tf_op jit(solution)/shard_map/ppermute | solution.py:378
  27.2 16.2 %collective-permute-start.6 = (f32[128,128]{1,0:T(8,128)S(1)}, f32[128,128]{1,0:T(8,128)S(1)}, u32[]{:S(2)}, u32[]{:S(2)}) collective-permute-start(f32[128,128]{1,0:T(8,128)S(1)} %add_add_fusion.refs_5_), channel_id=1, source_target_pairs={{0,2},{1,3},{2,0},{3,1},{4,6},{5,7},{6,4},{7,5},{8,10},{9,11},{10,... | collective-permute-start | bytes 196616 | tf_op jit(solution)/shard_map/ppermute | solution.py:378
  36.9 6.5 %collective-permute-start.5 = (f32[128,128]{1,0:T(8,128)S(1)}, f32[128,128]{1,0:T(8,128)S(1)}, u32[]{:S(2)}, u32[]{:S(2)}) collective-permute-start(f32[128,128]{1,0:T(8,128)S(1)} %add_add_fusion.refs_5_), channel_id=1, source_target_pairs={{0,1},{1,2},{2,3},{3,0},{4,5},{5,6},{6,7},{7,4},{8,9},{9,10},{10,1... | collective-permute-start | bytes 196616 | tf_op jit(solution)/shard_map/ppermute | solution.py:378

commit v15 on v14

--- a/solution.py
+++ b/solution.py
@@ -115,14 +115,17 @@
     )(images, valid_mask)
 
 
-def middle_kernel(image_ref, mask_ref, low_ref, mid_ref, gram_ref, again_ref, *scratch):
+def middle_kernel(cut, image_ref, mask_ref, low_ref, mid_ref, gram_ref, again_ref, first_ref, second_ref, *scratch):
     rows_ref, masks_ref, turned_ref, z_ref, in_sems, out_sems = scratch
     groups = mid_ref.shape[1]
     count, columns = image_ref.shape[2:]
     order = tuple(range(AFTER, ROWS - BEFORE)) + EDGE
     fetches = fetched(image_ref, mask_ref, rows_ref, masks_ref, in_sems, order)
-    stores = [pltpu.make_async_copy(low_ref, again_ref, out_sems.at[ROWS - AFTER - BEFORE])]
-    stores[0].start()
+    stores = []
+    for target, start, stop in ((first_ref, 0, cut), (second_ref, cut, groups), (again_ref, 0, groups)):
+        sem = out_sems.at[ROWS - AFTER - BEFORE + len(stores)]
+        stores.append(pltpu.make_async_copy(low_ref.at[:, start:stop], target, sem))
+        stores[-1].start()
     z_ref[...] = jnp.zeros_like(z_ref)
     zero = jnp.zeros((count, columns), jnp.bfloat16)
     total = None
@@ -157,19 +160,21 @@
         store.wait()
 
 
-def middle_rows(images, valid_mask, low):
+def middle_rows(images, valid_mask, low, cut):
     count = images.shape[2]
     groups = low.shape[1]
     rows = ROWS - AFTER - BEFORE
     far = pl.BlockSpec(memory_space=pl.ANY)
     return pl.pallas_call(
-        middle_kernel,
+        functools.partial(middle_kernel, cut),
         in_specs=[far, far, far],
-        out_specs=[far, pl.BlockSpec(memory_space=pltpu.VMEM), far],
+        out_specs=[far, pl.BlockSpec(memory_space=pltpu.VMEM), far, far, far],
         out_shape=[
             rows_shape(rows, groups, count),
             jax.ShapeDtypeStruct((LANES, LANES), jnp.float32),
             jax.ShapeDtypeStruct(low.shape, low.dtype),
+            rows_shape(BEFORE, cut, count),
+            rows_shape(BEFORE, groups - cut, count),
         ],
         scratch_shapes=[
             pltpu.VMEM(images.shape, jnp.bfloat16),
@@ -177,9 +182,9 @@
             pltpu.VMEM((rows, groups, 2, count, LANES), jnp.bfloat16),
             pltpu.VMEM((2 * LANES, ROWS * groups * LANES), jnp.bfloat16),
             pltpu.SemaphoreType.DMA((ROWS + 1,)),
-            pltpu.SemaphoreType.DMA((rows + 1,)),
+            pltpu.SemaphoreType.DMA((rows + 3,)),
         ],
-        compiler_params=pltpu.CompilerParams(vmem_limit_bytes=51 * 2**20),
+        compiler_params=pltpu.CompilerParams(vmem_limit_bytes=49 * 2**20),
         cost_estimate=pl.CostEstimate(flops=10**9, bytes_accessed=5 * 10**6, transcendentals=0),
         name="middle_rows",
     )(images, valid_mask, low)
@@ -316,7 +321,8 @@
     count = other.shape[3]
 
     def spec(array):
-        return pl.BlockSpec((array.shape[0], 1) + array.shape[2:], lambda s: (0, s + first, 0, 0, 0))
+        offset = 0 if array is other else first
+        return pl.BlockSpec((array.shape[0], 1) + array.shape[2:], lambda s: (0, s + offset, 0, 0, 0))
 
     operands = [other, top, mid, low]
     in_specs = [spec(a) for a in operands]
@@ -388,18 +394,19 @@
     backward = [(i + 1, i) for i in range(size - 1)]
     top, low = edge_rows(images, valid_mask, groups)
     after = lax.ppermute(top, "pix", backward)
-    mid, total, low = middle_rows(images, valid_mask, low)
-    before = lax.ppermute(low, "pix", forward)
+    mid, total, low, low0, low1 = middle_rows(images, valid_mask, low, cut)
+    before0 = lax.ppermute(low0, "pix", forward)
+    before1 = lax.ppermute(low1, "pix", forward)
     steps = rounds(size)
     if steps is None:
         terms, steps = [lax.psum(total, "pix")], []
     else:
         terms = round_terms(total, "pix", *steps[0]) if steps else [total]
-    out, zeros = looked(1, after, top, mid, low, 0, groups, looks, None, [], False)
+    out, _ = looked(1, after, top, mid, low, 0, groups, looks, None, [], False)
+    out, zeros = looked(0, before0, top, mid, low, 0, cut, looks, out, [], False)
     for step in steps[1:]:
         terms = round_terms(added(terms) + zeros, "pix", *step)
-    out, _ = looked(0, before, top, mid, low, 0, cut, looks, out, [], False)
-    out, slab = looked(0, before, top, mid, low, cut, groups - cut, looks, out, terms, True)
+    out, slab = looked(0, before1, top, mid, low, cut, groups - cut, looks, out, terms, True)
     return (out, slab)
 
 

time: 47.4 us -> 45.4 us (0.958)
  the two profiles are of different devices: /device:TPU:25 before, /device:TPU:1 now
where the time goes in v15:
time: 45.4 us; the launch traced here: 45 us
  Pallas kernels  23.3 us (51%)
  starting transfers between devices  17.1 us (38%)
  waiting for transfers between devices  3.9 us (9%)
  between operations  0.72 us (2%)
    pallas_call x3, Pallas kernels, looked(): pl.pallas_call(functools.partial(looks_kernel, half, previous is not None...  15.4 us
    ppermute x6, starting transfers between devices, round_terms(): terms.append(lax.ppermute(value, axis, pairs))  7.29 us
    pallas_call x1, Pallas kernels, middle_rows(): pl.pallas_call(functools.partial(middle_kernel, cut), in_specs=[far, far,...  5.02 us
    ppermute x1, starting transfers between devices, shards(): before0 = lax.ppermute(low0, 'pix', forward)  4.46 us
    ppermute x6, waiting for transfers between devices, round_terms(): terms.append(lax.ppermute(value, axis, pairs))  3.89 us
    ppermute x1, starting transfers between devices, shards(): before1 = lax.ppermute(low1, 'pix', forward)  3.24 us
    pallas_call x1, Pallas kernels, edge_rows(): pl.pallas_call(edge_kernel, in_specs=[far, far], out_specs=[far] * 2, out...  2.84 us
    ppermute x1, starting transfers between devices, shards(): after = lax.ppermute(top, 'pix', backward)  2.1 us
  transfers between devices with their start and end apart: 9, of which 3 were waited for; matrix products, arithmetic and copies ran while one was open for 0% of the time, Pallas kernels for 37%

profile of v15, /device:TPU:1, one launch (start us, length us, event | category | flops | bytes accessed | tf_op | source)
XLA Modules:
  0.0 45.0 jit_solution(4721884982953453039)
XLA Ops:
  0.6 0.0 copy-start.1
  0.6 2.8 %edge_rows.1 = (bf16[2,7,2,120,128]{4,3,2,1,0:T(8,128)(2,1)}, bf16[3,7,2,120,128]{4,3,2,1,0:T(8,128)(2,1)}) custom-call(bf16[8,2,120,840]{3,2,1,0:T(8,128)(2,1)} %image_ref.3, s32[8,840]{1,0:T(8,128)} %mask_ref.3), custom_call_target="tpu_custom_call" | custom-call | flops 1000000 | bytes 4000000 | tf_op jit(solution)/shard_map/edge_rows/pallas_call | solution.py:97
  3.5 2.1 %collective-permute-start.2 = (bf16[2,7,2,120,128]{4,3,2,1,0:T(8,128)(2,1)}, bf16[2,7,2,120,128]{4,3,2,1,0:T(8,128)(2,1)S(1)}, u32[]{:S(2)}, u32[]{:S(2)}) collective-permute-start(bf16[2,7,2,120,128]{4,3,2,1,0:T(8,128)(2,1)} %get-tuple-element.14.refs_1_), channel_id=1, source_target_pairs={{1,0},{2,1},{3,2},{4,3},{5,4},{6,5},{7,6},{8,7},{9,8},{10,9},{11,1... | collective-permute-start | bytes 2580488 | tf_op jit(solution)/shard_map/ppermute | solution.py:396
  5.6 5.0 %middle_rows.1 = (bf16[3,7,2,120,128]{4,3,2,1,0:T(8,128)(2,1)S(1)}, f32[128,128]{1,0:T(8,128)S(1)}, bf16[3,7,2,120,128]{4,3,2,1,0:T(8,128)(2,1)S(1)}, bf16[3,4,2...) custom-call(bf16[8,2,120,840]{3,2,1,0:T(8,128)(2,1)} %image_ref.3, s32[8,840]{1,0:T(8,128)S(1)} %copy-done.1, ...), custom_call_target="tpu_custom_call" | custom-call | flops 1000000000 | bytes 5000000 | tf_op jit(solution)/shard_map/middle_rows/pallas_call | solution.py:168
  10.6 4.5 %collective-permute-start.1 = (bf16[3,4,2,120,128]{4,3,2,1,0:T(8,128)(2,1)S(1)}, bf16[3,4,2,120,128]{4,3,2,1,0:T(8,128)(2,1)S(1)}, u32[]{:S(2)}, u32[]{:S(2)}) collective-permute-start(bf16[3,4,2,120,128]{4,3,2,1,0:T(8,128)(2,1)S(1)} %get-tuple-element.17), channel_id=1, source_target_pairs={{0,1},{1,2},{2,3},{3,4},{4,5},{5,6},{6,7},{7,8},{8,9},{9,10},{10,1... | collective-permute-start | bytes 2211848 | tf_op jit(solution)/shard_map/ppermute | solution.py:398
  15.1 2.4 %collective-permute-start.3 = (f32[128,128]{1,0:T(8,128)S(1)}, f32[128,128]{1,0:T(8,128)S(1)}, u32[]{:S(2)}, u32[]{:S(2)}) collective-permute-start(f32[128,128]{1,0:T(8,128)S(1)} %get-tuple-element.20), channel_id=1, source_target_pairs={{0,8},{1,9},{2,10},{3,11},{4,12},{5,13},{6,14},{7,15},{8,0},{9,1},... | collective-permute-start | bytes 196616 | tf_op jit(solution)/shard_map/ppermute | solution.py:384
  17.5 1.3 %collective-permute-start.4 = (f32[128,128]{1,0:T(8,128)S(1)}, f32[128,128]{1,0:T(8,128)S(1)}, u32[]{:S(2)}, u32[]{:S(2)}) collective-permute-start(f32[128,128]{1,0:T(8,128)S(1)} %get-tuple-element.20), channel_id=1, source_target_pairs={{0,4},{1,5},{2,6},{3,7},{4,8},{5,9},{6,10},{7,11},{8,12},{9,13},{1... | collective-permute-start | bytes 196616 | tf_op jit(solution)/shard_map/ppermute | solution.py:384
  18.8 2.0 %collective-permute-start.5 = (f32[128,128]{1,0:T(8,128)S(1)}, f32[128,128]{1,0:T(8,128)S(1)}, u32[]{:S(2)}, u32[]{:S(2)}) collective-permute-start(f32[128,128]{1,0:T(8,128)S(1)} %get-tuple-element.20), channel_id=1, source_target_pairs={{0,12},{1,13},{2,14},{3,15},{4,0},{5,1},{6,2},{7,3},{8,4},{9,5},{1... | collective-permute-start | bytes 196616 | tf_op jit(solution)/shard_map/ppermute | solution.py:384
  20.7 0.0 collective-permute-done.2.refs_0_
  20.8 3.2 %collective-permute-start = (bf16[3,3,2,120,128]{4,3,2,1,0:T(8,128)(2,1)S(1)}, bf16[3,3,2,120,128]{4,3,2,1,0:T(8,128)(2,1)S(1)}, u32[]{:S(2)}, u32[]{:S(2)}) collective-permute-start(bf16[3,3,2,120,128]{4,3,2,1,0:T(8,128)(2,1)S(1)} %get-tuple-element.13), channel_id=1, source_target_pairs={{0,1},{1,2},{2,3},{3,4},{4,5},{5,6},{6,7},{7,8},{8,9},{9,10},{10,1... | collective-permute-start | bytes 1658888 | tf_op jit(solution)/shard_map/ppermute | solution.py:399
  24.0 7.2 %looks.3 = (bf16[4,40,2,120,120]{4,3,2,1,0:T(8,128)(2,1)}, f32[128,128]{1,0:T(8,128)}) custom-call(bf16[2,7,2,120,128]{4,3,2,1,0:T(8,128)(2,1)S(1)} %collective-permute-done.2.refs_0_, bf16[2,7,2,120,128]{4,3,2,1,0:T(8,128)(2,1)S(1)} %copy-done, bf16[3,7,2,120,128]{4,3,2,1,0:T(8,128)(2,1)S(1)} %get-tuple-element.15.refs_2_, ...), custom_call_target="tpu_custom_call" | custom-call | flops 5637144576 | bytes 7000000 | tf_op jit(solution)/shard_map/looks/pallas_call | solution.py:346
  31.2 0.0 collective-permute-done.1.refs_0_
  31.2 4.5 %looks.4 = (bf16[4,40,2,120,120]{4,3,2,1,0:T(8,128)(2,1)}, f32[128,128]{1,0:T(8,128)S(1)}) custom-call(bf16[3,4,2,120,128]{4,3,2,1,0:T(8,128)(2,1)S(1)} %collective-permute-done.1.refs_0_, bf16[2,7,2,120,128]{4,3,2,1,0:T(8,128)(2,1)S(1)} %copy-done, bf16[3,7,2,120,128]{4,3,2,1,0:T(8,128)(2,1)S(1)} %get-tuple-element.15.refs_2_, ...), custom_call_target="tpu_custom_call", output_to_operand_aliasing={{0}: (4, {})} | custom-call | flops 3221225472 | bytes 4000000 | tf_op jit(solution)/shard_map/looks/pallas_call | solution.py:346
  35.7 0.0 collective-permute-done.3
  35.7 0.0 collective-permute-done.4
  35.7 0.0 collective-permute-done.5
  35.8 1.2 %collective-permute-start.6 = (f32[128,128]{1,0:T(8,128)S(1)}, f32[128,128]{1,0:T(8,128)S(1)}, u32[]{:S(2)}, u32[]{:S(2)}) collective-permute-start(f32[128,128]{1,0:T(8,128)S(1)} %add_add_fusion.refs_5_), channel_id=1, source_target_pairs={{0,1},{1,2},{2,3},{3,0},{4,5},{5,6},{6,7},{7,4},{8,9},{9,10},{10,1... | collective-permute-start | bytes 196616 | tf_op jit(solution)/shard_map/ppermute | solution.py:384
  36.9 0.0 collective-permute-start.7
  36.9 0.5 %collective-permute-start.8 = (f32[128,128]{1,0:T(8,128)S(1)}, f32[128,128]{1,0:T(8,128)S(1)}, u32[]{:S(2)}, u32[]{:S(2)}) collective-permute-start(f32[128,128]{1,0:T(8,128)S(1)} %add_add_fusion.refs_5_), channel_id=1, source_target_pairs={{0,3},{1,0},{2,1},{3,2},{4,7},{5,4},{6,5},{7,6},{8,11},{9,8},{10,9... | collective-permute-start | bytes 196616 | tf_op jit(solution)/shard_map/ppermute | solution.py:384
  37.4 0.0 collective-permute-done.refs_0_
  37.4 0.9 %collective-permute-done.6.refs_6_ = f32[128,128]{1,0:T(8,128)S(1)} collective-permute-done((f32[128,128]{1,0:T(8,128)S(1)}, f32[128,128]{1,0:T(8,128)S(1)}, u32[]{:S(2)}, u32[]{:S(2)}) %collective-permute-start.6) | collective-permute-done | bytes 65568 | tf_op jit(solution)/shard_map/ppermute | solution.py:384
  38.3 2.5 %collective-permute-done.7.refs_7_ = f32[128,128]{1,0:T(8,128)S(1)} collective-permute-done((f32[128,128]{1,0:T(8,128)S(1)}, f32[128,128]{1,0:T(8,128)S(1)}, u32[]{:S(2)}, u32[]{:S(2)}) %collective-permute-start.7) | collective-permute-done | bytes 65568 | tf_op jit(solution)/shard_map/ppermute | solution.py:384
  40.8 0.5 %collective-permute-done.8.refs_8_ = f32[128,128]{1,0:T(8,128)S(1)} collective-permute-done((f32[128,128]{1,0:T(8,128)S(1)}, f32[128,128]{1,0:T(8,128)S(1)}, u32[]{:S(2)}, u32[]{:S(2)}) %collective-permute-start.8) | collective-permute-done | bytes 65568 | tf_op jit(solution)/shard_map/ppermute | solution.py:384
  41.3 3.7 %looks.5 = (bf16[4,40,2,120,120]{4,3,2,1,0:T(8,128)(2,1)}, f32[2,120,120]{2,1,0:T(8,128)}) custom-call(bf16[3,3,2,120,128]{4,3,2,1,0:T(8,128)(2,1)S(1)} %collective-permute-done.refs_0_, bf16[2,7,2,120,128]{4,3,2,1,0:T(8,128)(2,1)S(1)} %copy-done, bf16[3,7,2,120,128]{4,3,2,1,0:T(8,128)(2,1)S(1)} %get-tuple-element.15.refs_2_, ...), custom_call_target="tpu_custom_call", output_to_operand_aliasing={{0}: (4, {})} | custom-call | flops 2415919104 | bytes 3000000 | tf_op jit(solution)/shard_map/looks/pallas_call | solution.py:346
  (4 shorter events, 0.0 us)
Async XLA Ops:
  0.6 5.0 %copy-start.1 = (s32[8,840]{1,0:T(8,128)S(1)}, s32[8,840]{1,0:T(8,128)}, u32[]{:S(2)}) copy-start(s32[8,840]{1,0:T(8,128)} %mask_ref.3) | copy-start | bytes 80644
  3.5 20.5 %copy-start = (bf16[2,7,2,120,128]{4,3,2,1,0:T(8,128)(2,1)S(1)}, bf16[2,7,2,120,128]{4,3,2,1,0:T(8,128)(2,1)}, u32[]{:S(2)}) copy-start(bf16[2,7,2,120,128]{4,3,2,1,0:T(8,128)(2,1)} %get-tuple-element.14.refs_1_) | copy-start | bytes 2580484
  3.5 17.3 %collective-permute-start.2 = (bf16[2,7,2,120,128]{4,3,2,1,0:T(8,128)(2,1)}, bf16[2,7,2,120,128]{4,3,2,1,0:T(8,128)(2,1)S(1)}, u32[]{:S(2)}, u32[]{:S(2)}) collective-permute-start(bf16[2,7,2,120,128]{4,3,2,1,0:T(8,128)(2,1)} %get-tuple-element.14.refs_1_), channel_id=1, source_target_pairs={{1,0},{2,1},{3,2},{4,3},{5,4},{6,5},{7,6},{8,7},{9,8},{10,9},{11,1... | collective-permute-start | bytes 2580488 | tf_op jit(solution)/shard_map/ppermute | solution.py:396
  10.6 20.5 %collective-permute-start.1 = (bf16[3,4,2,120,128]{4,3,2,1,0:T(8,128)(2,1)S(1)}, bf16[3,4,2,120,128]{4,3,2,1,0:T(8,128)(2,1)S(1)}, u32[]{:S(2)}, u32[]{:S(2)}) collective-permute-start(bf16[3,4,2,120,128]{4,3,2,1,0:T(8,128)(2,1)S(1)} %get-tuple-element.17), channel_id=1, source_target_pairs={{0,1},{1,2},{2,3},{3,4},{4,5},{5,6},{6,7},{7,8},{8,9},{9,10},{10,1... | collective-permute-start | bytes 2211848 | tf_op jit(solution)/shard_map/ppermute | solution.py:398
  15.1 20.6 %collective-permute-start.3 = (f32[128,128]{1,0:T(8,128)S(1)}, f32[128,128]{1,0:T(8,128)S(1)}, u32[]{:S(2)}, u32[]{:S(2)}) collective-permute-start(f32[128,128]{1,0:T(8,128)S(1)} %get-tuple-element.20), channel_id=1, source_target_pairs={{0,8},{1,9},{2,10},{3,11},{4,12},{5,13},{6,14},{7,15},{8,0},{9,1},... | collective-permute-start | bytes 196616 | tf_op jit(solution)/shard_map/ppermute | solution.py:384
  17.5 18.2 %collective-permute-start.4 = (f32[128,128]{1,0:T(8,128)S(1)}, f32[128,128]{1,0:T(8,128)S(1)}, u32[]{:S(2)}, u32[]{:S(2)}) collective-permute-start(f32[128,128]{1,0:T(8,128)S(1)} %get-tuple-element.20), channel_id=1, source_target_pairs={{0,4},{1,5},{2,6},{3,7},{4,8},{5,9},{6,10},{7,11},{8,12},{9,13},{1... | collective-permute-start | bytes 196616 | tf_op jit(solution)/shard_map/ppermute | solution.py:384
  18.8 16.9 %collective-permute-start.5 = (f32[128,128]{1,0:T(8,128)S(1)}, f32[128,128]{1,0:T(8,128)S(1)}, u32[]{:S(2)}, u32[]{:S(2)}) collective-permute-start(f32[128,128]{1,0:T(8,128)S(1)} %get-tuple-element.20), channel_id=1, source_target_pairs={{0,12},{1,13},{2,14},{3,15},{4,0},{5,1},{6,2},{7,3},{8,4},{9,5},{1... | collective-permute-start | bytes 196616 | tf_op jit(solution)/shard_map/ppermute | solution.py:384
  20.8 16.7 %collective-permute-start = (bf16[3,3,2,120,128]{4,3,2,1,0:T(8,128)(2,1)S(1)}, bf16[3,3,2,120,128]{4,3,2,1,0:T(8,128)(2,1)S(1)}, u32[]{:S(2)}, u32[]{:S(2)}) collective-permute-start(bf16[3,3,2,120,128]{4,3,2,1,0:T(8,128)(2,1)S(1)} %get-tuple-element.13), channel_id=1, source_target_pairs={{0,1},{1,2},{2,3},{3,4},{4,5},{5,6},{6,7},{7,8},{8,9},{9,10},{10,1... | collective-permute-start | bytes 1658888 | tf_op jit(solution)/shard_map/ppermute | solution.py:399
  35.8 2.5 %collective-permute-start.6 = (f32[128,128]{1,0:T(8,128)S(1)}, f32[128,128]{1,0:T(8,128)S(1)}, u32[]{:S(2)}, u32[]{:S(2)}) collective-permute-start(f32[128,128]{1,0:T(8,128)S(1)} %add_add_fusion.refs_5_), channel_id=1, source_target_pairs={{0,1},{1,2},{2,3},{3,0},{4,5},{5,6},{6,7},{7,4},{8,9},{9,10},{10,1... | collective-permute-start | bytes 196616 | tf_op jit(solution)/shard_map/ppermute | solution.py:384
  36.9 3.8 %collective-permute-start.7 = (f32[128,128]{1,0:T(8,128)S(1)}, f32[128,128]{1,0:T(8,128)S(1)}, u32[]{:S(2)}, u32[]{:S(2)}) collective-permute-start(f32[128,128]{1,0:T(8,128)S(1)} %add_add_fusion.refs_5_), channel_id=1, source_target_pairs={{0,2},{1,3},{2,0},{3,1},{4,6},{5,7},{6,4},{7,5},{8,10},{9,11},{10,... | collective-permute-start | bytes 196616 | tf_op jit(solution)/shard_map/ppermute | solution.py:384
  36.9 4.4 %collective-permute-start.8 = (f32[128,128]{1,0:T(8,128)S(1)}, f32[128,128]{1,0:T(8,128)S(1)}, u32[]{:S(2)}, u32[]{:S(2)}) collective-permute-start(f32[128,128]{1,0:T(8,128)S(1)} %add_add_fusion.refs_5_), channel_id=1, source_target_pairs={{0,3},{1,0},{2,1},{3,2},{4,7},{5,4},{6,5},{7,6},{8,11},{9,8},{10,9... | collective-permute-start | bytes 196616 | tf_op jit(solution)/shard_map/ppermute | solution.py:384

commit v16 on v15

--- a/solution.py
+++ b/solution.py
@@ -355,7 +355,7 @@
         ],
         compiler_params=pltpu.CompilerParams(vmem_limit_bytes=48 * 2**20),
         cost_estimate=pl.CostEstimate(
-            flops=2 * groups * PER * 2 * 512 * 256 * 256, bytes_accessed=groups * 10**6, transcendentals=0
+            flops=groups * PER * 2 * 512 * 256 * 256, bytes_accessed=groups * 10**6, transcendentals=0
         ),
         name="looks",
     )(*operands)
@@ -402,10 +402,10 @@
         terms, steps = [lax.psum(total, "pix")], []
     else:
         terms = round_terms(total, "pix", *steps[0]) if steps else [total]
-    out, _ = looked(1, after, top, mid, low, 0, groups, looks, None, [], False)
-    out, zeros = looked(0, before0, top, mid, low, 0, cut, looks, out, [], False)
+    out, zeros = looked(1, after, top, mid, low, 0, groups, looks, None, [], False)
     for step in steps[1:]:
         terms = round_terms(added(terms) + zeros, "pix", *step)
+    out, _ = looked(0, before0, top, mid, low, 0, cut, looks, out, [], False)
     out, slab = looked(0, before1, top, mid, low, cut, groups - cut, looks, out, terms, True)
     return (out, slab)
 

time: 45.4 us -> 43.4 us (0.956)
  waiting for transfers between devices: 3.9 us -> 0.02 us
  starting transfers between devices: 17.1 us -> 19.1 us
    ppermute x6, waiting for transfers between devices: 3.89 us -> 0.02 us  [round_terms(): terms.append(lax.ppermute(value, axis, pairs))]
    ppermute x6, starting transfers between devices: 7.29 us -> 9.28 us  [round_terms(): terms.append(lax.ppermute(value, axis, pairs))]
  transfers between devices with their start and end apart: 9 -> 9, of which waited for: 3 -> 0; matrix products, arithmetic and copies ran while one was open for 0% -> 0% of each run, Pallas kernels for 37% -> 39%
where the time goes in v16:
time: 43.4 us; the launch traced here: 43.2 us
  Pallas kernels  23.3 us (54%)
  starting transfers between devices  19.1 us (44%)
  between operations  0.74 us (2%)
    pallas_call x3, Pallas kernels, looked(): pl.pallas_call(functools.partial(looks_kernel, half, previous is not None...  15.5 us
    ppermute x6, starting transfers between devices, round_terms(): terms.append(lax.ppermute(value, axis, pairs))  9.28 us
    pallas_call x1, Pallas kernels, middle_rows(): pl.pallas_call(functools.partial(middle_kernel, cut), in_specs=[far, far,...  5.02 us
    ppermute x1, starting transfers between devices, shards(): before0 = lax.ppermute(low0, 'pix', forward)  4.46 us
    ppermute x1, starting transfers between devices, shards(): before1 = lax.ppermute(low1, 'pix', forward)  3.24 us
    pallas_call x1, Pallas kernels, edge_rows(): pl.pallas_call(edge_kernel, in_specs=[far, far], out_specs=[far] * 2, out...  2.84 us
    ppermute x1, starting transfers between devices, shards(): after = lax.ppermute(top, 'pix', backward)  2.1 us
  transfers between devices with their start and end apart: 9, of which 0 were waited for; matrix products, arithmetic and copies ran while one was open for 0% of the time, Pallas kernels for 39%

profile of v16, /device:TPU:1, one launch (start us, length us, event | category | flops | bytes accessed | tf_op | source)
XLA Modules:
  0.0 43.2 jit_solution(15390931037966529461)
XLA Ops:
  0.6 2.8 %edge_rows.1 = (bf16[2,7,2,120,128]{4,3,2,1,0:T(8,128)(2,1)}, bf16[3,7,2,120,128]{4,3,2,1,0:T(8,128)(2,1)}) custom-call(bf16[8,2,120,840]{3,2,1,0:T(8,128)(2,1)} %image_ref.3, s32[8,840]{1,0:T(8,128)} %mask_ref.3), custom_call_target="tpu_custom_call" | custom-call | flops 1000000 | bytes 4000000 | tf_op jit(solution)/shard_map/edge_rows/pallas_call | solution.py:97
  3.5 0.0 copy-start
  3.5 2.1 %collective-permute-start.2 = (bf16[2,7,2,120,128]{4,3,2,1,0:T(8,128)(2,1)}, bf16[2,7,2,120,128]{4,3,2,1,0:T(8,128)(2,1)S(1)}, u32[]{:S(2)}, u32[]{:S(2)}) collective-permute-start(bf16[2,7,2,120,128]{4,3,2,1,0:T(8,128)(2,1)} %get-tuple-element.14.refs_1_), channel_id=1, source_target_pairs={{1,0},{2,1},{3,2},{4,3},{5,4},{6,5},{7,6},{8,7},{9,8},{10,9},{11,1... | collective-permute-start | bytes 2580488 | tf_op jit(solution)/shard_map/ppermute | solution.py:396
  5.6 5.0 %middle_rows.1 = (bf16[3,7,2,120,128]{4,3,2,1,0:T(8,128)(2,1)S(1)}, f32[128,128]{1,0:T(8,128)S(1)}, bf16[3,7,2,120,128]{4,3,2,1,0:T(8,128)(2,1)S(1)}, bf16[3,4,2...) custom-call(bf16[8,2,120,840]{3,2,1,0:T(8,128)(2,1)} %image_ref.3, s32[8,840]{1,0:T(8,128)S(1)} %copy-done.1, ...), custom_call_target="tpu_custom_call" | custom-call | flops 1000000000 | bytes 5000000 | tf_op jit(solution)/shard_map/middle_rows/pallas_call | solution.py:168
  10.6 4.5 %collective-permute-start.1 = (bf16[3,4,2,120,128]{4,3,2,1,0:T(8,128)(2,1)S(1)}, bf16[3,4,2,120,128]{4,3,2,1,0:T(8,128)(2,1)S(1)}, u32[]{:S(2)}, u32[]{:S(2)}) collective-permute-start(bf16[3,4,2,120,128]{4,3,2,1,0:T(8,128)(2,1)S(1)} %get-tuple-element.17), channel_id=1, source_target_pairs={{0,1},{1,2},{2,3},{3,4},{4,5},{5,6},{6,7},{7,8},{8,9},{9,10},{10,1... | collective-permute-start | bytes 2211848 | tf_op jit(solution)/shard_map/ppermute | solution.py:398
  15.1 3.4 %collective-permute-start.5 = (f32[128,128]{1,0:T(8,128)S(1)}, f32[128,128]{1,0:T(8,128)S(1)}, u32[]{:S(2)}, u32[]{:S(2)}) collective-permute-start(f32[128,128]{1,0:T(8,128)S(1)} %get-tuple-element.20), channel_id=1, source_target_pairs={{0,12},{1,13},{2,14},{3,15},{4,0},{5,1},{6,2},{7,3},{8,4},{9,5},{1... | collective-permute-start | bytes 196616 | tf_op jit(solution)/shard_map/ppermute | solution.py:384
  18.5 0.0 collective-permute-start.4
  18.5 0.5 %collective-permute-start.3 = (f32[128,128]{1,0:T(8,128)S(1)}, f32[128,128]{1,0:T(8,128)S(1)}, u32[]{:S(2)}, u32[]{:S(2)}) collective-permute-start(f32[128,128]{1,0:T(8,128)S(1)} %get-tuple-element.20), channel_id=1, source_target_pairs={{0,8},{1,9},{2,10},{3,11},{4,12},{5,13},{6,14},{7,15},{8,0},{9,1},... | collective-permute-start | bytes 196616 | tf_op jit(solution)/shard_map/ppermute | solution.py:384
  18.9 0.0 collective-permute-done.2.refs_0_
  18.9 3.2 %collective-permute-start = (bf16[3,3,2,120,128]{4,3,2,1,0:T(8,128)(2,1)S(1)}, bf16[3,3,2,120,128]{4,3,2,1,0:T(8,128)(2,1)S(1)}, u32[]{:S(2)}, u32[]{:S(2)}) collective-permute-start(bf16[3,3,2,120,128]{4,3,2,1,0:T(8,128)(2,1)S(1)} %get-tuple-element.13), channel_id=1, source_target_pairs={{0,1},{1,2},{2,3},{3,4},{4,5},{5,6},{6,7},{7,8},{8,9},{9,10},{10,1... | collective-permute-start | bytes 1658888 | tf_op jit(solution)/shard_map/ppermute | solution.py:399
  22.2 7.2 %looks.3 = (bf16[4,40,2,120,120]{4,3,2,1,0:T(8,128)(2,1)}, f32[128,128]{1,0:T(8,128)S(1)}) custom-call(bf16[2,7,2,120,128]{4,3,2,1,0:T(8,128)(2,1)S(1)} %collective-permute-done.2.refs_0_, bf16[2,7,2,120,128]{4,3,2,1,0:T(8,128)(2,1)S(1)} %copy-done, bf16[3,7,2,120,128]{4,3,2,1,0:T(8,128)(2,1)S(1)} %get-tuple-element.15.refs_2_, ...), custom_call_target="tpu_custom_call" | custom-call | flops 2818572288 | bytes 7000000 | tf_op jit(solution)/shard_map/looks/pallas_call | solution.py:346
  29.4 0.0 collective-permute-done.5
  29.4 0.0 collective-permute-done.4
  29.4 0.0 collective-permute-done.3
  29.4 0.1 collective-permute-start.8
  29.5 3.4 %collective-permute-start.7 = (f32[128,128]{1,0:T(8,128)S(1)}, f32[128,128]{1,0:T(8,128)S(1)}, u32[]{:S(2)}, u32[]{:S(2)}) collective-permute-start(f32[128,128]{1,0:T(8,128)S(1)} %add_add_fusion.refs_5_), channel_id=1, source_target_pairs={{0,2},{1,3},{2,0},{3,1},{4,6},{5,7},{6,4},{7,5},{8,10},{9,11},{10,... | collective-permute-start | bytes 196616 | tf_op jit(solution)/shard_map/ppermute | solution.py:384
  32.9 1.9 %collective-permute-start.6 = (f32[128,128]{1,0:T(8,128)S(1)}, f32[128,128]{1,0:T(8,128)S(1)}, u32[]{:S(2)}, u32[]{:S(2)}) collective-permute-start(f32[128,128]{1,0:T(8,128)S(1)} %add_add_fusion.refs_5_), channel_id=1, source_target_pairs={{0,1},{1,2},{2,3},{3,0},{4,5},{5,6},{6,7},{7,4},{8,9},{9,10},{10,1... | collective-permute-start | bytes 196616 | tf_op jit(solution)/shard_map/ppermute | solution.py:384
  34.9 0.0 collective-permute-done.1.refs_0_
  34.9 4.5 %looks.4 = (bf16[4,40,2,120,120]{4,3,2,1,0:T(8,128)(2,1)}, f32[128,128]{1,0:T(8,128)}) custom-call(bf16[3,4,2,120,128]{4,3,2,1,0:T(8,128)(2,1)S(1)} %collective-permute-done.1.refs_0_, bf16[2,7,2,120,128]{4,3,2,1,0:T(8,128)(2,1)S(1)} %copy-done, bf16[3,7,2,120,128]{4,3,2,1,0:T(8,128)(2,1)S(1)} %get-tuple-element.15.refs_2_, ...), custom_call_target="tpu_custom_call", output_to_operand_aliasing={{0}: (4, {})} | custom-call | flops 1610612736 | bytes 4000000 | tf_op jit(solution)/shard_map/looks/pallas_call | solution.py:346
  39.4 0.0 collective-permute-done.refs_0_
  39.4 0.0 collective-permute-done.8.refs_8_
  39.4 0.0 collective-permute-done.7.refs_7_
  39.4 0.0 collective-permute-done.6.refs_6_
  39.4 3.8 %looks.5 = (bf16[4,40,2,120,120]{4,3,2,1,0:T(8,128)(2,1)}, f32[2,120,120]{2,1,0:T(8,128)}) custom-call(bf16[3,3,2,120,128]{4,3,2,1,0:T(8,128)(2,1)S(1)} %collective-permute-done.refs_0_, bf16[2,7,2,120,128]{4,3,2,1,0:T(8,128)(2,1)S(1)} %copy-done, bf16[3,7,2,120,128]{4,3,2,1,0:T(8,128)(2,1)S(1)} %get-tuple-element.15.refs_2_, ...), custom_call_target="tpu_custom_call", output_to_operand_aliasing={{0}: (4, {})} | custom-call | flops 1207959552 | bytes 3000000 | tf_op jit(solution)/shard_map/looks/pallas_call | solution.py:346
  (4 shorter events, 0.0 us)
Async XLA Ops:
  0.6 5.0 %copy-start.1 = (s32[8,840]{1,0:T(8,128)S(1)}, s32[8,840]{1,0:T(8,128)}, u32[]{:S(2)}) copy-start(s32[8,840]{1,0:T(8,128)} %mask_ref.3) | copy-start | bytes 80644
  3.5 18.7 %copy-start = (bf16[2,7,2,120,128]{4,3,2,1,0:T(8,128)(2,1)S(1)}, bf16[2,7,2,120,128]{4,3,2,1,0:T(8,128)(2,1)}, u32[]{:S(2)}) copy-start(bf16[2,7,2,120,128]{4,3,2,1,0:T(8,128)(2,1)} %get-tuple-element.14.refs_1_) | copy-start | bytes 2580484
  3.5 15.4 %collective-permute-start.2 = (bf16[2,7,2,120,128]{4,3,2,1,0:T(8,128)(2,1)}, bf16[2,7,2,120,128]{4,3,2,1,0:T(8,128)(2,1)S(1)}, u32[]{:S(2)}, u32[]{:S(2)}) collective-permute-start(bf16[2,7,2,120,128]{4,3,2,1,0:T(8,128)(2,1)} %get-tuple-element.14.refs_1_), channel_id=1, source_target_pairs={{1,0},{2,1},{3,2},{4,3},{5,4},{6,5},{7,6},{8,7},{9,8},{10,9},{11,1... | collective-permute-start | bytes 2580488 | tf_op jit(solution)/shard_map/ppermute | solution.py:396
  10.6 24.2 %collective-permute-start.1 = (bf16[3,4,2,120,128]{4,3,2,1,0:T(8,128)(2,1)S(1)}, bf16[3,4,2,120,128]{4,3,2,1,0:T(8,128)(2,1)S(1)}, u32[]{:S(2)}, u32[]{:S(2)}) collective-permute-start(bf16[3,4,2,120,128]{4,3,2,1,0:T(8,128)(2,1)S(1)} %get-tuple-element.17), channel_id=1, source_target_pairs={{0,1},{1,2},{2,3},{3,4},{4,5},{5,6},{6,7},{7,8},{8,9},{9,10},{10,1... | collective-permute-start | bytes 2211848 | tf_op jit(solution)/shard_map/ppermute | solution.py:398
  15.1 14.3 %collective-permute-start.5 = (f32[128,128]{1,0:T(8,128)S(1)}, f32[128,128]{1,0:T(8,128)S(1)}, u32[]{:S(2)}, u32[]{:S(2)}) collective-permute-start(f32[128,128]{1,0:T(8,128)S(1)} %get-tuple-element.20), channel_id=1, source_target_pairs={{0,12},{1,13},{2,14},{3,15},{4,0},{5,1},{6,2},{7,3},{8,4},{9,5},{1... | collective-permute-start | bytes 196616 | tf_op jit(solution)/shard_map/ppermute | solution.py:384
  18.5 10.9 %collective-permute-start.4 = (f32[128,128]{1,0:T(8,128)S(1)}, f32[128,128]{1,0:T(8,128)S(1)}, u32[]{:S(2)}, u32[]{:S(2)}) collective-permute-start(f32[128,128]{1,0:T(8,128)S(1)} %get-tuple-element.20), channel_id=1, source_target_pairs={{0,4},{1,5},{2,6},{3,7},{4,8},{5,9},{6,10},{7,11},{8,12},{9,13},{1... | collective-permute-start | bytes 196616 | tf_op jit(solution)/shard_map/ppermute | solution.py:384
  18.5 10.9 %collective-permute-start.3 = (f32[128,128]{1,0:T(8,128)S(1)}, f32[128,128]{1,0:T(8,128)S(1)}, u32[]{:S(2)}, u32[]{:S(2)}) collective-permute-start(f32[128,128]{1,0:T(8,128)S(1)} %get-tuple-element.20), channel_id=1, source_target_pairs={{0,8},{1,9},{2,10},{3,11},{4,12},{5,13},{6,14},{7,15},{8,0},{9,1},... | collective-permute-start | bytes 196616 | tf_op jit(solution)/shard_map/ppermute | solution.py:384
  18.9 20.5 %collective-permute-start = (bf16[3,3,2,120,128]{4,3,2,1,0:T(8,128)(2,1)S(1)}, bf16[3,3,2,120,128]{4,3,2,1,0:T(8,128)(2,1)S(1)}, u32[]{:S(2)}, u32[]{:S(2)}) collective-permute-start(bf16[3,3,2,120,128]{4,3,2,1,0:T(8,128)(2,1)S(1)} %get-tuple-element.13), channel_id=1, source_target_pairs={{0,1},{1,2},{2,3},{3,4},{4,5},{5,6},{6,7},{7,8},{8,9},{9,10},{10,1... | collective-permute-start | bytes 1658888 | tf_op jit(solution)/shard_map/ppermute | solution.py:399
  29.4 10.0 %collective-permute-start.8 = (f32[128,128]{1,0:T(8,128)S(1)}, f32[128,128]{1,0:T(8,128)S(1)}, u32[]{:S(2)}, u32[]{:S(2)}) collective-permute-start(f32[128,128]{1,0:T(8,128)S(1)} %add_add_fusion.refs_5_), channel_id=1, source_target_pairs={{0,3},{1,0},{2,1},{3,2},{4,7},{5,4},{6,5},{7,6},{8,11},{9,8},{10,9... | collective-permute-start | bytes 196616 | tf_op jit(solution)/shard_map/ppermute | solution.py:384
  29.5 10.0 %collective-permute-start.7 = (f32[128,128]{1,0:T(8,128)S(1)}, f32[128,128]{1,0:T(8,128)S(1)}, u32[]{:S(2)}, u32[]{:S(2)}) collective-permute-start(f32[128,128]{1,0:T(8,128)S(1)} %add_add_fusion.refs_5_), channel_id=1, source_target_pairs={{0,2},{1,3},{2,0},{3,1},{4,6},{5,7},{6,4},{7,5},{8,10},{9,11},{10,... | collective-permute-start | bytes 196616 | tf_op jit(solution)/shard_map/ppermute | solution.py:384
  32.9 6.5 %collective-permute-start.6 = (f32[128,128]{1,0:T(8,128)S(1)}, f32[128,128]{1,0:T(8,128)S(1)}, u32[]{:S(2)}, u32[]{:S(2)}) collective-permute-start(f32[128,128]{1,0:T(8,128)S(1)} %add_add_fusion.refs_5_), channel_id=1, source_target_pairs={{0,1},{1,2},{2,3},{3,0},{4,5},{5,6},{6,7},{7,4},{8,9},{9,10},{10,1... | collective-permute-start | bytes 196616 | tf_op jit(solution)/shard_map/ppermute | solution.py:384

commit v17 on v16

--- a/solution.py
+++ b/solution.py
@@ -303,18 +303,20 @@
             lanes = jnp.concatenate([kept(l, inner_rows or INNER), kept(l, rest_rows or outer_rows)], axis=1)
             lanes = jnp.broadcast_to(lanes, every.shape).astype(jnp.bfloat16) != 0
             read = jnp.where(lanes, every, nothing)
-            for start in range(0, LANES, TILE):
-                reads.append(read[start : start + TILE])
-                reads.append(read[LANES + start : LANES + start + TILE])
+            for start in range(0, count, TILE):
+                stop = min(start + TILE, count)
+                reads.append(read[start:stop])
+                reads.append(read[LANES + start : LANES + stop])
         gram = lax.dot_general(jnp.concatenate(reads, axis=0), every, NT, preferred_element_type=jnp.float32)
         for w in range(2):
             real, imag = [], []
-            for start in range(0, LANES, TILE):
-                base = 2 * (w * LANES + start)
-                re, im = gram[base : base + TILE], gram[base + TILE : base + 2 * TILE]
+            for start in range(0, count, TILE):
+                height = min(TILE, count - start)
+                base = 2 * (w * count + start)
+                re, im = gram[base : base + height], gram[base + height : base + 2 * height]
                 real.append(re[:, :LANES] + im[:, LANES:])
                 imag.append(im[:, :LANES] - re[:, LANES:])
-            normalised(jnp.concatenate(real, axis=0)[:count], jnp.concatenate(imag, axis=0)[:count], w, l)
+            normalised(jnp.concatenate(real, axis=0), jnp.concatenate(imag, axis=0), w, l)
 
 
 def looked(half, other, top, mid, low, first, groups, looks, previous, terms, slab):

time: 43.4 us -> 43.4 us (level)
  no operation moved by 1% of the time
where the time goes in v17:
time: 43.4 us; the launch traced here: 43.2 us
  Pallas kernels  23.4 us (54%)
  starting transfers between devices  19.1 us (44%)
  between operations  0.74 us (2%)
    pallas_call x3, Pallas kernels, looked(): pl.pallas_call(functools.partial(looks_kernel, half, previous is not None...  15.5 us
    ppermute x6, starting transfers between devices, round_terms(): terms.append(lax.ppermute(value, axis, pairs))  9.28 us
    pallas_call x1, Pallas kernels, middle_rows(): pl.pallas_call(functools.partial(middle_kernel, cut), in_specs=[far, far,...  5.02 us
    ppermute x1, starting transfers between devices, shards(): before0 = lax.ppermute(low0, 'pix', forward)  4.46 us
    ppermute x1, starting transfers between devices, shards(): before1 = lax.ppermute(low1, 'pix', forward)  3.24 us
    pallas_call x1, Pallas kernels, edge_rows(): pl.pallas_call(edge_kernel, in_specs=[far, far], out_specs=[far] * 2, out...  2.84 us
    ppermute x1, starting transfers between devices, shards(): after = lax.ppermute(top, 'pix', backward)  2.1 us
  transfers between devices with their start and end apart: 9, of which 0 were waited for; matrix products, arithmetic and copies ran while one was open for 0% of the time, Pallas kernels for 39%

profile of v17, /device:TPU:1, one launch (start us, length us, event | category | flops | bytes accessed | tf_op | source)
XLA Modules:
  0.0 43.2 jit_solution(3804678427082622583)
XLA Ops:
  0.6 0.0 copy-start.1
  0.6 2.8 %edge_rows.1 = (bf16[2,7,2,120,128]{4,3,2,1,0:T(8,128)(2,1)}, bf16[3,7,2,120,128]{4,3,2,1,0:T(8,128)(2,1)}) custom-call(bf16[8,2,120,840]{3,2,1,0:T(8,128)(2,1)} %image_ref.3, s32[8,840]{1,0:T(8,128)} %mask_ref.3), custom_call_target="tpu_custom_call" | custom-call | flops 1000000 | bytes 4000000 | tf_op jit(solution)/shard_map/edge_rows/pallas_call | solution.py:97
  3.5 2.1 %collective-permute-start.2 = (bf16[2,7,2,120,128]{4,3,2,1,0:T(8,128)(2,1)}, bf16[2,7,2,120,128]{4,3,2,1,0:T(8,128)(2,1)S(1)}, u32[]{:S(2)}, u32[]{:S(2)}) collective-permute-start(bf16[2,7,2,120,128]{4,3,2,1,0:T(8,128)(2,1)} %get-tuple-element.14.refs_1_), channel_id=1, source_target_pairs={{1,0},{2,1},{3,2},{4,3},{5,4},{6,5},{7,6},{8,7},{9,8},{10,9},{11,1... | collective-permute-start | bytes 2580488 | tf_op jit(solution)/shard_map/ppermute | solution.py:398
  5.6 5.0 %middle_rows.1 = (bf16[3,7,2,120,128]{4,3,2,1,0:T(8,128)(2,1)S(1)}, f32[128,128]{1,0:T(8,128)S(1)}, bf16[3,7,2,120,128]{4,3,2,1,0:T(8,128)(2,1)S(1)}, bf16[3,4,2...) custom-call(bf16[8,2,120,840]{3,2,1,0:T(8,128)(2,1)} %image_ref.3, s32[8,840]{1,0:T(8,128)S(1)} %copy-done.1, ...), custom_call_target="tpu_custom_call" | custom-call | flops 1000000000 | bytes 5000000 | tf_op jit(solution)/shard_map/middle_rows/pallas_call | solution.py:168
  10.6 4.5 %collective-permute-start.1 = (bf16[3,4,2,120,128]{4,3,2,1,0:T(8,128)(2,1)S(1)}, bf16[3,4,2,120,128]{4,3,2,1,0:T(8,128)(2,1)S(1)}, u32[]{:S(2)}, u32[]{:S(2)}) collective-permute-start(bf16[3,4,2,120,128]{4,3,2,1,0:T(8,128)(2,1)S(1)} %get-tuple-element.17), channel_id=1, source_target_pairs={{0,1},{1,2},{2,3},{3,4},{4,5},{5,6},{6,7},{7,8},{8,9},{9,10},{10,1... | collective-permute-start | bytes 2211848 | tf_op jit(solution)/shard_map/ppermute | solution.py:400
  15.1 3.4 %collective-permute-start.5 = (f32[128,128]{1,0:T(8,128)S(1)}, f32[128,128]{1,0:T(8,128)S(1)}, u32[]{:S(2)}, u32[]{:S(2)}) collective-permute-start(f32[128,128]{1,0:T(8,128)S(1)} %get-tuple-element.20), channel_id=1, source_target_pairs={{0,12},{1,13},{2,14},{3,15},{4,0},{5,1},{6,2},{7,3},{8,4},{9,5},{1... | collective-permute-start | bytes 196616 | tf_op jit(solution)/shard_map/ppermute | solution.py:386
  18.5 0.0 collective-permute-start.4
  18.5 0.5 %collective-permute-start.3 = (f32[128,128]{1,0:T(8,128)S(1)}, f32[128,128]{1,0:T(8,128)S(1)}, u32[]{:S(2)}, u32[]{:S(2)}) collective-permute-start(f32[128,128]{1,0:T(8,128)S(1)} %get-tuple-element.20), channel_id=1, source_target_pairs={{0,8},{1,9},{2,10},{3,11},{4,12},{5,13},{6,14},{7,15},{8,0},{9,1},... | collective-permute-start | bytes 196616 | tf_op jit(solution)/shard_map/ppermute | solution.py:386
  18.9 0.0 collective-permute-done.2.refs_0_
  18.9 3.2 %collective-permute-start = (bf16[3,3,2,120,128]{4,3,2,1,0:T(8,128)(2,1)S(1)}, bf16[3,3,2,120,128]{4,3,2,1,0:T(8,128)(2,1)S(1)}, u32[]{:S(2)}, u32[]{:S(2)}) collective-permute-start(bf16[3,3,2,120,128]{4,3,2,1,0:T(8,128)(2,1)S(1)} %get-tuple-element.13), channel_id=1, source_target_pairs={{0,1},{1,2},{2,3},{3,4},{4,5},{5,6},{6,7},{7,8},{8,9},{9,10},{10,1... | collective-permute-start | bytes 1658888 | tf_op jit(solution)/shard_map/ppermute | solution.py:401
  22.2 7.2 %looks.3 = (bf16[4,40,2,120,120]{4,3,2,1,0:T(8,128)(2,1)}, f32[128,128]{1,0:T(8,128)S(1)}) custom-call(bf16[2,7,2,120,128]{4,3,2,1,0:T(8,128)(2,1)S(1)} %collective-permute-done.2.refs_0_, bf16[2,7,2,120,128]{4,3,2,1,0:T(8,128)(2,1)S(1)} %copy-done, bf16[3,7,2,120,128]{4,3,2,1,0:T(8,128)(2,1)S(1)} %get-tuple-element.15.refs_2_, ...), custom_call_target="tpu_custom_call" | custom-call | flops 2818572288 | bytes 7000000 | tf_op jit(solution)/shard_map/looks/pallas_call | solution.py:348
  29.4 0.0 collective-permute-done.5
  29.4 0.0 collective-permute-done.4
  29.4 0.0 collective-permute-done.3
  29.5 0.1 collective-permute-start.8
  29.5 3.5 %collective-permute-start.7 = (f32[128,128]{1,0:T(8,128)S(1)}, f32[128,128]{1,0:T(8,128)S(1)}, u32[]{:S(2)}, u32[]{:S(2)}) collective-permute-start(f32[128,128]{1,0:T(8,128)S(1)} %add_add_fusion.refs_5_), channel_id=1, source_target_pairs={{0,2},{1,3},{2,0},{3,1},{4,6},{5,7},{6,4},{7,5},{8,10},{9,11},{10,... | collective-permute-start | bytes 196616 | tf_op jit(solution)/shard_map/ppermute | solution.py:386
  33.0 1.9 %collective-permute-start.6 = (f32[128,128]{1,0:T(8,128)S(1)}, f32[128,128]{1,0:T(8,128)S(1)}, u32[]{:S(2)}, u32[]{:S(2)}) collective-permute-start(f32[128,128]{1,0:T(8,128)S(1)} %add_add_fusion.refs_5_), channel_id=1, source_target_pairs={{0,1},{1,2},{2,3},{3,0},{4,5},{5,6},{6,7},{7,4},{8,9},{9,10},{10,1... | collective-permute-start | bytes 196616 | tf_op jit(solution)/shard_map/ppermute | solution.py:386
  34.9 0.0 collective-permute-done.1.refs_0_
  34.9 4.5 %looks.4 = (bf16[4,40,2,120,120]{4,3,2,1,0:T(8,128)(2,1)}, f32[128,128]{1,0:T(8,128)}) custom-call(bf16[3,4,2,120,128]{4,3,2,1,0:T(8,128)(2,1)S(1)} %collective-permute-done.1.refs_0_, bf16[2,7,2,120,128]{4,3,2,1,0:T(8,128)(2,1)S(1)} %copy-done, bf16[3,7,2,120,128]{4,3,2,1,0:T(8,128)(2,1)S(1)} %get-tuple-element.15.refs_2_, ...), custom_call_target="tpu_custom_call", output_to_operand_aliasing={{0}: (4, {})} | custom-call | flops 1610612736 | bytes 4000000 | tf_op jit(solution)/shard_map/looks/pallas_call | solution.py:348
  39.5 0.0 collective-permute-done.refs_0_
  39.5 0.0 collective-permute-done.8.refs_8_
  39.5 0.0 collective-permute-done.7.refs_7_
  39.5 0.0 collective-permute-done.6.refs_6_
  39.5 3.7 %looks.5 = (bf16[4,40,2,120,120]{4,3,2,1,0:T(8,128)(2,1)}, f32[2,120,120]{2,1,0:T(8,128)}) custom-call(bf16[3,3,2,120,128]{4,3,2,1,0:T(8,128)(2,1)S(1)} %collective-permute-done.refs_0_, bf16[2,7,2,120,128]{4,3,2,1,0:T(8,128)(2,1)S(1)} %copy-done, bf16[3,7,2,120,128]{4,3,2,1,0:T(8,128)(2,1)S(1)} %get-tuple-element.15.refs_2_, ...), custom_call_target="tpu_custom_call", output_to_operand_aliasing={{0}: (4, {})} | custom-call | flops 1207959552 | bytes 3000000 | tf_op jit(solution)/shard_map/looks/pallas_call | solution.py:348
  (4 shorter events, 0.0 us)
Async XLA Ops:
  0.6 5.0 %copy-start.1 = (s32[8,840]{1,0:T(8,128)S(1)}, s32[8,840]{1,0:T(8,128)}, u32[]{:S(2)}) copy-start(s32[8,840]{1,0:T(8,128)} %mask_ref.3) | copy-start | bytes 80644
  3.5 18.7 %copy-start = (bf16[2,7,2,120,128]{4,3,2,1,0:T(8,128)(2,1)S(1)}, bf16[2,7,2,120,128]{4,3,2,1,0:T(8,128)(2,1)}, u32[]{:S(2)}) copy-start(bf16[2,7,2,120,128]{4,3,2,1,0:T(8,128)(2,1)} %get-tuple-element.14.refs_1_) | copy-start | bytes 2580484
  3.5 15.4 %collective-permute-start.2 = (bf16[2,7,2,120,128]{4,3,2,1,0:T(8,128)(2,1)}, bf16[2,7,2,120,128]{4,3,2,1,0:T(8,128)(2,1)S(1)}, u32[]{:S(2)}, u32[]{:S(2)}) collective-permute-start(bf16[2,7,2,120,128]{4,3,2,1,0:T(8,128)(2,1)} %get-tuple-element.14.refs_1_), channel_id=1, source_target_pairs={{1,0},{2,1},{3,2},{4,3},{5,4},{6,5},{7,6},{8,7},{9,8},{10,9},{11,1... | collective-permute-start | bytes 2580488 | tf_op jit(solution)/shard_map/ppermute | solution.py:398
  10.6 24.3 %collective-permute-start.1 = (bf16[3,4,2,120,128]{4,3,2,1,0:T(8,128)(2,1)S(1)}, bf16[3,4,2,120,128]{4,3,2,1,0:T(8,128)(2,1)S(1)}, u32[]{:S(2)}, u32[]{:S(2)}) collective-permute-start(bf16[3,4,2,120,128]{4,3,2,1,0:T(8,128)(2,1)S(1)} %get-tuple-element.17), channel_id=1, source_target_pairs={{0,1},{1,2},{2,3},{3,4},{4,5},{5,6},{6,7},{7,8},{8,9},{9,10},{10,1... | collective-permute-start | bytes 2211848 | tf_op jit(solution)/shard_map/ppermute | solution.py:400
  15.1 14.3 %collective-permute-start.5 = (f32[128,128]{1,0:T(8,128)S(1)}, f32[128,128]{1,0:T(8,128)S(1)}, u32[]{:S(2)}, u32[]{:S(2)}) collective-permute-start(f32[128,128]{1,0:T(8,128)S(1)} %get-tuple-element.20), channel_id=1, source_target_pairs={{0,12},{1,13},{2,14},{3,15},{4,0},{5,1},{6,2},{7,3},{8,4},{9,5},{1... | collective-permute-start | bytes 196616 | tf_op jit(solution)/shard_map/ppermute | solution.py:386
  18.5 10.9 %collective-permute-start.4 = (f32[128,128]{1,0:T(8,128)S(1)}, f32[128,128]{1,0:T(8,128)S(1)}, u32[]{:S(2)}, u32[]{:S(2)}) collective-permute-start(f32[128,128]{1,0:T(8,128)S(1)} %get-tuple-element.20), channel_id=1, source_target_pairs={{0,4},{1,5},{2,6},{3,7},{4,8},{5,9},{6,10},{7,11},{8,12},{9,13},{1... | collective-permute-start | bytes 196616 | tf_op jit(solution)/shard_map/ppermute | solution.py:386
  18.5 10.9 %collective-permute-start.3 = (f32[128,128]{1,0:T(8,128)S(1)}, f32[128,128]{1,0:T(8,128)S(1)}, u32[]{:S(2)}, u32[]{:S(2)}) collective-permute-start(f32[128,128]{1,0:T(8,128)S(1)} %get-tuple-element.20), channel_id=1, source_target_pairs={{0,8},{1,9},{2,10},{3,11},{4,12},{5,13},{6,14},{7,15},{8,0},{9,1},... | collective-permute-start | bytes 196616 | tf_op jit(solution)/shard_map/ppermute | solution.py:386
  18.9 20.5 %collective-permute-start = (bf16[3,3,2,120,128]{4,3,2,1,0:T(8,128)(2,1)S(1)}, bf16[3,3,2,120,128]{4,3,2,1,0:T(8,128)(2,1)S(1)}, u32[]{:S(2)}, u32[]{:S(2)}) collective-permute-start(bf16[3,3,2,120,128]{4,3,2,1,0:T(8,128)(2,1)S(1)} %get-tuple-element.13), channel_id=1, source_target_pairs={{0,1},{1,2},{2,3},{3,4},{4,5},{5,6},{6,7},{7,8},{8,9},{9,10},{10,1... | collective-permute-start | bytes 1658888 | tf_op jit(solution)/shard_map/ppermute | solution.py:401
  29.5 10.0 %collective-permute-start.8 = (f32[128,128]{1,0:T(8,128)S(1)}, f32[128,128]{1,0:T(8,128)S(1)}, u32[]{:S(2)}, u32[]{:S(2)}) collective-permute-start(f32[128,128]{1,0:T(8,128)S(1)} %add_add_fusion.refs_5_), channel_id=1, source_target_pairs={{0,3},{1,0},{2,1},{3,2},{4,7},{5,4},{6,5},{7,6},{8,11},{9,8},{10,9... | collective-permute-start | bytes 196616 | tf_op jit(solution)/shard_map/ppermute | solution.py:386
  29.5 10.0 %collective-permute-start.7 = (f32[128,128]{1,0:T(8,128)S(1)}, f32[128,128]{1,0:T(8,128)S(1)}, u32[]{:S(2)}, u32[]{:S(2)}) collective-permute-start(f32[128,128]{1,0:T(8,128)S(1)} %add_add_fusion.refs_5_), channel_id=1, source_target_pairs={{0,2},{1,3},{2,0},{3,1},{4,6},{5,7},{6,4},{7,5},{8,10},{9,11},{10,... | collective-permute-start | bytes 196616 | tf_op jit(solution)/shard_map/ppermute | solution.py:386
  33.0 6.5 %collective-permute-start.6 = (f32[128,128]{1,0:T(8,128)S(1)}, f32[128,128]{1,0:T(8,128)S(1)}, u32[]{:S(2)}, u32[]{:S(2)}) collective-permute-start(f32[128,128]{1,0:T(8,128)S(1)} %add_add_fusion.refs_5_), channel_id=1, source_target_pairs={{0,1},{1,2},{2,3},{3,0},{4,5},{5,6},{6,7},{7,4},{8,9},{9,10},{10,1... | collective-permute-start | bytes 196616 | tf_op jit(solution)/shard_map/ppermute | solution.py:386

commit v18 on v17

--- a/solution.py
+++ b/solution.py
@@ -390,7 +390,7 @@
 def shards(images, valid_mask):
     looks = images.shape[3] // LOOK
     groups = -(-looks // PER)
-    cut = -(-groups // 2)
+    cut = groups // 2
     size = lax.axis_size("pix")
     forward = [(i, i + 1) for i in range(size - 1)]
     backward = [(i + 1, i) for i in range(size - 1)]

time: 43.4 us -> 47.5 us (1.094)
  the two profiles are of different devices: /device:TPU:1 before, /device:TPU:29 now
where the time goes in v18:
time: 47.5 us; the launch traced here: 47.3 us
  Pallas kernels  23.3 us (49%)
  starting transfers between devices  20.3 us (43%)
  waiting for transfers between devices  2.87 us (6%)
  between operations  0.73 us (2%)
    pallas_call x3, Pallas kernels, looked(): pl.pallas_call(functools.partial(looks_kernel, half, previous is not None...  15.5 us
    ppermute x6, starting transfers between devices, round_terms(): terms.append(lax.ppermute(value, axis, pairs))  12.1 us
    pallas_call x1, Pallas kernels, middle_rows(): pl.pallas_call(functools.partial(middle_kernel, cut), in_specs=[far, far,...  5.01 us
    ppermute x1, starting transfers between devices, shards(): before1 = lax.ppermute(low1, 'pix', forward)  3.02 us
    ppermute x1, waiting for transfers between devices, shards(): after = lax.ppermute(top, 'pix', backward)  2.85 us
    pallas_call x1, Pallas kernels, edge_rows(): pl.pallas_call(edge_kernel, in_specs=[far, far], out_specs=[far] * 2, out...  2.84 us
    ppermute x1, starting transfers between devices, shards(): after = lax.ppermute(top, 'pix', backward)  2.71 us
    ppermute x1, starting transfers between devices, shards(): before0 = lax.ppermute(low0, 'pix', forward)  2.46 us
  transfers between devices with their start and end apart: 9, of which 1 were waited for; matrix products, arithmetic and copies ran while one was open for 0% of the time, Pallas kernels for 33%

profile of v18, /device:TPU:29, one launch (start us, length us, event | category | flops | bytes accessed | tf_op | source)
XLA Modules:
  0.0 47.3 jit_solution(12850565354651356042)
XLA Ops:
  0.6 2.8 %edge_rows.1 = (bf16[2,7,2,120,128]{4,3,2,1,0:T(8,128)(2,1)}, bf16[3,7,2,120,128]{4,3,2,1,0:T(8,128)(2,1)}) custom-call(bf16[8,2,120,840]{3,2,1,0:T(8,128)(2,1)} %image_ref.3, s32[8,840]{1,0:T(8,128)} %mask_ref.3), custom_call_target="tpu_custom_call" | custom-call | flops 1000000 | bytes 4000000 | tf_op jit(solution)/shard_map/edge_rows/pallas_call | solution.py:97
  3.5 2.7 %collective-permute-start.2 = (bf16[2,7,2,120,128]{4,3,2,1,0:T(8,128)(2,1)}, bf16[2,7,2,120,128]{4,3,2,1,0:T(8,128)(2,1)S(1)}, u32[]{:S(2)}, u32[]{:S(2)}) collective-permute-start(bf16[2,7,2,120,128]{4,3,2,1,0:T(8,128)(2,1)} %get-tuple-element.14.refs_1_), channel_id=1, source_target_pairs={{1,0},{2,1},{3,2},{4,3},{5,4},{6,5},{7,6},{8,7},{9,8},{10,9},{11,1... | collective-permute-start | bytes 2580488 | tf_op jit(solution)/shard_map/ppermute | solution.py:398
  6.2 5.0 %middle_rows.1 = (bf16[3,7,2,120,128]{4,3,2,1,0:T(8,128)(2,1)S(1)}, f32[128,128]{1,0:T(8,128)S(1)}, bf16[3,7,2,120,128]{4,3,2,1,0:T(8,128)(2,1)S(1)}, bf16[3,3,2...) custom-call(bf16[8,2,120,840]{3,2,1,0:T(8,128)(2,1)} %image_ref.3, s32[8,840]{1,0:T(8,128)S(1)} %copy-done.1, ...), custom_call_target="tpu_custom_call" | custom-call | flops 1000000000 | bytes 5000000 | tf_op jit(solution)/shard_map/middle_rows/pallas_call | solution.py:168
  11.3 3.0 %collective-permute-start = (bf16[3,4,2,120,128]{4,3,2,1,0:T(8,128)(2,1)S(1)}, bf16[3,4,2,120,128]{4,3,2,1,0:T(8,128)(2,1)S(1)}, u32[]{:S(2)}, u32[]{:S(2)}) collective-permute-start(bf16[3,4,2,120,128]{4,3,2,1,0:T(8,128)(2,1)S(1)} %get-tuple-element.13), channel_id=1, source_target_pairs={{0,1},{1,2},{2,3},{3,4},{4,5},{5,6},{6,7},{7,8},{8,9},{9,10},{10,1... | collective-permute-start | bytes 2211848 | tf_op jit(solution)/shard_map/ppermute | solution.py:401
  14.3 2.5 %collective-permute-start.1 = (bf16[3,3,2,120,128]{4,3,2,1,0:T(8,128)(2,1)S(1)}, bf16[3,3,2,120,128]{4,3,2,1,0:T(8,128)(2,1)S(1)}, u32[]{:S(2)}, u32[]{:S(2)}) collective-permute-start(bf16[3,3,2,120,128]{4,3,2,1,0:T(8,128)(2,1)S(1)} %get-tuple-element.17), channel_id=1, source_target_pairs={{0,1},{1,2},{2,3},{3,4},{4,5},{5,6},{6,7},{7,8},{8,9},{9,10},{10,1... | collective-permute-start | bytes 1658888 | tf_op jit(solution)/shard_map/ppermute | solution.py:400
  16.7 0.2 collective-permute-start.5
  16.9 3.1 %collective-permute-start.4 = (f32[128,128]{1,0:T(8,128)S(1)}, f32[128,128]{1,0:T(8,128)S(1)}, u32[]{:S(2)}, u32[]{:S(2)}) collective-permute-start(f32[128,128]{1,0:T(8,128)S(1)} %get-tuple-element.20), channel_id=1, source_target_pairs={{0,4},{1,5},{2,6},{3,7},{4,8},{5,9},{6,10},{7,11},{8,12},{9,13},{1... | collective-permute-start | bytes 196616 | tf_op jit(solution)/shard_map/ppermute | solution.py:386
  20.1 2.8 %collective-permute-done.2.refs_0_ = bf16[2,7,2,120,128]{4,3,2,1,0:T(8,128)(2,1)S(1)} collective-permute-done((bf16[2,7,2,120,128]{4,3,2,1,0:T(8,128)(2,1)}, bf16[2,7,2,120,128]{4,3,2,1,0:T(8,128)(2,1)S(1)}, u32[]{:S(2)}, u32[]{:S(2)}) %collective-permute-start.2) | collective-permute-done | bytes 860192 | tf_op jit(solution)/shard_map/ppermute | solution.py:398
  22.9 0.6 %collective-permute-start.3 = (f32[128,128]{1,0:T(8,128)S(1)}, f32[128,128]{1,0:T(8,128)S(1)}, u32[]{:S(2)}, u32[]{:S(2)}) collective-permute-start(f32[128,128]{1,0:T(8,128)S(1)} %get-tuple-element.20), channel_id=1, source_target_pairs={{0,8},{1,9},{2,10},{3,11},{4,12},{5,13},{6,14},{7,15},{8,0},{9,1},... | collective-permute-start | bytes 196616 | tf_op jit(solution)/shard_map/ppermute | solution.py:386
  23.5 0.0 copy-done
  23.5 7.2 %looks.3 = (bf16[4,40,2,120,120]{4,3,2,1,0:T(8,128)(2,1)}, f32[128,128]{1,0:T(8,128)S(1)}) custom-call(bf16[2,7,2,120,128]{4,3,2,1,0:T(8,128)(2,1)S(1)} %collective-permute-done.2.refs_0_, bf16[2,7,2,120,128]{4,3,2,1,0:T(8,128)(2,1)S(1)} %copy-done, bf16[3,7,2,120,128]{4,3,2,1,0:T(8,128)(2,1)S(1)} %get-tuple-element.15.refs_2_, ...), custom_call_target="tpu_custom_call" | custom-call | flops 2818572288 | bytes 7000000 | tf_op jit(solution)/shard_map/looks/pallas_call | solution.py:348
  30.7 0.0 collective-permute-done.5
  30.7 0.0 collective-permute-done.4
  30.7 0.0 collective-permute-done.3
  30.7 0.1 collective-permute-start.8
  30.8 6.2 %collective-permute-start.7 = (f32[128,128]{1,0:T(8,128)S(1)}, f32[128,128]{1,0:T(8,128)S(1)}, u32[]{:S(2)}, u32[]{:S(2)}) collective-permute-start(f32[128,128]{1,0:T(8,128)S(1)} %add_add_fusion.refs_5_), channel_id=1, source_target_pairs={{0,2},{1,3},{2,0},{3,1},{4,6},{5,7},{6,4},{7,5},{8,10},{9,11},{10,... | collective-permute-start | bytes 196616 | tf_op jit(solution)/shard_map/ppermute | solution.py:386
  37.0 1.9 %collective-permute-start.6 = (f32[128,128]{1,0:T(8,128)S(1)}, f32[128,128]{1,0:T(8,128)S(1)}, u32[]{:S(2)}, u32[]{:S(2)}) collective-permute-start(f32[128,128]{1,0:T(8,128)S(1)} %add_add_fusion.refs_5_), channel_id=1, source_target_pairs={{0,1},{1,2},{2,3},{3,0},{4,5},{5,6},{6,7},{7,4},{8,9},{9,10},{10,1... | collective-permute-start | bytes 196616 | tf_op jit(solution)/shard_map/ppermute | solution.py:386
  38.9 0.0 collective-permute-done.1.refs_0_
  38.9 3.6 %looks.4 = (bf16[4,40,2,120,120]{4,3,2,1,0:T(8,128)(2,1)}, f32[128,128]{1,0:T(8,128)}) custom-call(bf16[3,3,2,120,128]{4,3,2,1,0:T(8,128)(2,1)S(1)} %collective-permute-done.1.refs_0_, bf16[2,7,2,120,128]{4,3,2,1,0:T(8,128)(2,1)S(1)} %copy-done, bf16[3,7,2,120,128]{4,3,2,1,0:T(8,128)(2,1)S(1)} %get-tuple-element.15.refs_2_, ...), custom_call_target="tpu_custom_call", output_to_operand_aliasing={{0}: (4, {})} | custom-call | flops 1207959552 | bytes 3000000 | tf_op jit(solution)/shard_map/looks/pallas_call | solution.py:348
  42.6 0.0 collective-permute-done.refs_0_
  42.6 0.0 collective-permute-done.8.refs_8_
  42.6 0.0 collective-permute-done.7.refs_7_
  42.6 0.0 collective-permute-done.6.refs_6_
  42.6 4.7 %looks.5 = (bf16[4,40,2,120,120]{4,3,2,1,0:T(8,128)(2,1)}, f32[2,120,120]{2,1,0:T(8,128)}) custom-call(bf16[3,4,2,120,128]{4,3,2,1,0:T(8,128)(2,1)S(1)} %collective-permute-done.refs_0_, bf16[2,7,2,120,128]{4,3,2,1,0:T(8,128)(2,1)S(1)} %copy-done, bf16[3,7,2,120,128]{4,3,2,1,0:T(8,128)(2,1)S(1)} %get-tuple-element.15.refs_2_, ...), custom_call_target="tpu_custom_call", output_to_operand_aliasing={{0}: (4, {})} | custom-call | flops 1610612736 | bytes 4000000 | tf_op jit(solution)/shard_map/looks/pallas_call | solution.py:348
  (4 shorter events, 0.0 us)
Async XLA Ops:
  0.6 5.6 %copy-start.1 = (s32[8,840]{1,0:T(8,128)S(1)}, s32[8,840]{1,0:T(8,128)}, u32[]{:S(2)}) copy-start(s32[8,840]{1,0:T(8,128)} %mask_ref.3) | copy-start | bytes 80644
  3.5 20.0 %copy-start = (bf16[2,7,2,120,128]{4,3,2,1,0:T(8,128)(2,1)S(1)}, bf16[2,7,2,120,128]{4,3,2,1,0:T(8,128)(2,1)}, u32[]{:S(2)}) copy-start(bf16[2,7,2,120,128]{4,3,2,1,0:T(8,128)(2,1)} %get-tuple-element.14.refs_1_) | copy-start | bytes 2580484
  3.5 19.4 %collective-permute-start.2 = (bf16[2,7,2,120,128]{4,3,2,1,0:T(8,128)(2,1)}, bf16[2,7,2,120,128]{4,3,2,1,0:T(8,128)(2,1)S(1)}, u32[]{:S(2)}, u32[]{:S(2)}) collective-permute-start(bf16[2,7,2,120,128]{4,3,2,1,0:T(8,128)(2,1)} %get-tuple-element.14.refs_1_), channel_id=1, source_target_pairs={{1,0},{2,1},{3,2},{4,3},{5,4},{6,5},{7,6},{8,7},{9,8},{10,9},{11,1... | collective-permute-start | bytes 2580488 | tf_op jit(solution)/shard_map/ppermute | solution.py:398
  11.3 31.3 %collective-permute-start = (bf16[3,4,2,120,128]{4,3,2,1,0:T(8,128)(2,1)S(1)}, bf16[3,4,2,120,128]{4,3,2,1,0:T(8,128)(2,1)S(1)}, u32[]{:S(2)}, u32[]{:S(2)}) collective-permute-start(bf16[3,4,2,120,128]{4,3,2,1,0:T(8,128)(2,1)S(1)} %get-tuple-element.13), channel_id=1, source_target_pairs={{0,1},{1,2},{2,3},{3,4},{4,5},{5,6},{6,7},{7,8},{8,9},{9,10},{10,1... | collective-permute-start | bytes 2211848 | tf_op jit(solution)/shard_map/ppermute | solution.py:401
  14.3 24.6 %collective-permute-start.1 = (bf16[3,3,2,120,128]{4,3,2,1,0:T(8,128)(2,1)S(1)}, bf16[3,3,2,120,128]{4,3,2,1,0:T(8,128)(2,1)S(1)}, u32[]{:S(2)}, u32[]{:S(2)}) collective-permute-start(bf16[3,3,2,120,128]{4,3,2,1,0:T(8,128)(2,1)S(1)} %get-tuple-element.17), channel_id=1, source_target_pairs={{0,1},{1,2},{2,3},{3,4},{4,5},{5,6},{6,7},{7,8},{8,9},{9,10},{10,1... | collective-permute-start | bytes 1658888 | tf_op jit(solution)/shard_map/ppermute | solution.py:400
  16.7 14.0 %collective-permute-start.5 = (f32[128,128]{1,0:T(8,128)S(1)}, f32[128,128]{1,0:T(8,128)S(1)}, u32[]{:S(2)}, u32[]{:S(2)}) collective-permute-start(f32[128,128]{1,0:T(8,128)S(1)} %get-tuple-element.20), channel_id=1, source_target_pairs={{0,12},{1,13},{2,14},{3,15},{4,0},{5,1},{6,2},{7,3},{8,4},{9,5},{1... | collective-permute-start | bytes 196616 | tf_op jit(solution)/shard_map/ppermute | solution.py:386
  16.9 13.8 %collective-permute-start.4 = (f32[128,128]{1,0:T(8,128)S(1)}, f32[128,128]{1,0:T(8,128)S(1)}, u32[]{:S(2)}, u32[]{:S(2)}) collective-permute-start(f32[128,128]{1,0:T(8,128)S(1)} %get-tuple-element.20), channel_id=1, source_target_pairs={{0,4},{1,5},{2,6},{3,7},{4,8},{5,9},{6,10},{7,11},{8,12},{9,13},{1... | collective-permute-start | bytes 196616 | tf_op jit(solution)/shard_map/ppermute | solution.py:386
  22.9 7.8 %collective-permute-start.3 = (f32[128,128]{1,0:T(8,128)S(1)}, f32[128,128]{1,0:T(8,128)S(1)}, u32[]{:S(2)}, u32[]{:S(2)}) collective-permute-start(f32[128,128]{1,0:T(8,128)S(1)} %get-tuple-element.20), channel_id=1, source_target_pairs={{0,8},{1,9},{2,10},{3,11},{4,12},{5,13},{6,14},{7,15},{8,0},{9,1},... | collective-permute-start | bytes 196616 | tf_op jit(solution)/shard_map/ppermute | solution.py:386
  30.7 11.8 %collective-permute-start.8 = (f32[128,128]{1,0:T(8,128)S(1)}, f32[128,128]{1,0:T(8,128)S(1)}, u32[]{:S(2)}, u32[]{:S(2)}) collective-permute-start(f32[128,128]{1,0:T(8,128)S(1)} %add_add_fusion.refs_5_), channel_id=1, source_target_pairs={{0,3},{1,0},{2,1},{3,2},{4,7},{5,4},{6,5},{7,6},{8,11},{9,8},{10,9... | collective-permute-start | bytes 196616 | tf_op jit(solution)/shard_map/ppermute | solution.py:386
  30.8 11.8 %collective-permute-start.7 = (f32[128,128]{1,0:T(8,128)S(1)}, f32[128,128]{1,0:T(8,128)S(1)}, u32[]{:S(2)}, u32[]{:S(2)}) collective-permute-start(f32[128,128]{1,0:T(8,128)S(1)} %add_add_fusion.refs_5_), channel_id=1, source_target_pairs={{0,2},{1,3},{2,0},{3,1},{4,6},{5,7},{6,4},{7,5},{8,10},{9,11},{10,... | collective-permute-start | bytes 196616 | tf_op jit(solution)/shard_map/ppermute | solution.py:386
  37.0 5.6 %collective-permute-start.6 = (f32[128,128]{1,0:T(8,128)S(1)}, f32[128,128]{1,0:T(8,128)S(1)}, u32[]{:S(2)}, u32[]{:S(2)}) collective-permute-start(f32[128,128]{1,0:T(8,128)S(1)} %add_add_fusion.refs_5_), channel_id=1, source_target_pairs={{0,1},{1,2},{2,3},{3,0},{4,5},{5,6},{6,7},{7,4},{8,9},{9,10},{10,1... | collective-permute-start | bytes 196616 | tf_op jit(solution)/shard_map/ppermute | solution.py:386
